TPU v7x, 256 devices: a whole 4x4x8 slice. The times are simulated.
256 devices in a mesh: aa: 8 (over x, y_hi), ba: 32 (over z, y_lo, core).
Axes of the slice: x: 4, y: 4 (y_hi: 2, y_lo: 2; y = y_hi * 2 + y_lo), z: 8, core: 2. Of those that a mesh axis runs over, the one named last changes fastest.
Arguments:
- ligand_slab: bfloat16 [64, 128, 16384], P(None, 'aa', 'ba'), may hold values from -6 to 6
- protein_slab: bfloat16 [64, 1024, 16384], P(None, 'ba', 'aa'), may hold values from -6 to 6
- protein_orbitals: bfloat16 [1024, 16384], P(None, 'ba'), may hold values from -0.046875 to 0.046875
- ligand_orbitals: bfloat16 [128, 16384], P(None, 'aa'), may hold values from -0.046875 to 0.046875
Outputs:
- pair_exchange: float32 [128, 1024], P('aa', 'ba')
- ligand_back: float32 [16384, 128], P(('aa', 'ba'))
- protein_back: float32 [16384, 1024], P(('ba', 'aa'))
All inputs are finite; a program needn't handle non-finite values.
Results may differ from a plain program's by a relative error of at most 0.0024.
Values may be sent and summed in bfloat16 or wider, within the bound.
No kernel may reach another device: no remote copies, remote signals or barrier semaphores. Data moves between devices by JAX's collectives and lax.ppermute only.
A program may use at most 192 MiB of HBM per device.

v0:
```python
import math

import jax
import jax.numpy as jnp
from jax import lax
from jax.sharding import PartitionSpec as P


def on_device(ligand_slab, protein_slab, protein_orbitals, ligand_orbitals):
    fit_count = ligand_slab.shape[0]
    lig_local = ligand_slab.shape[1]
    pro_local = protein_slab.shape[1]
    lig_total = ligand_orbitals.shape[0]
    pro_total = protein_orbitals.shape[0]
    cross_a_all = lax.psum(
        jnp.einsum(
            "qam,bm->qab", ligand_slab, protein_orbitals, preferred_element_type=jnp.float32
        ),
        "ba",
    )
    cross_b_all = lax.psum(
        jnp.einsum(
            "an,qbn->qba", ligand_orbitals, protein_slab, preferred_element_type=jnp.float32
        ),
        "aa",
    )
    own_a = lax.dynamic_slice_in_dim(cross_a_all, lax.axis_index("ba") * pro_local, pro_local, 2)
    own_b = lax.dynamic_slice_in_dim(cross_b_all, lax.axis_index("aa") * lig_local, lig_local, 2)
    own_b = jnp.transpose(own_b, (0, 2, 1))
    rounded_a = cross_a_all.astype(jnp.bfloat16)
    rounded_b = cross_b_all.astype(jnp.bfloat16)
    form_a = "qam,qab->mb"
    form_b = "qbn,qba->na"
    pair_exchange = -jnp.sum(own_a * own_b, axis=0) / math.sqrt(fit_count)
    scale_protein = 1.0 / math.sqrt(fit_count * lig_total)
    scale_ligand = 1.0 / math.sqrt(fit_count * pro_total)
    slab_part = ligand_slab
    protein_back = lax.psum_scatter(
        jnp.einsum(form_a, slab_part, rounded_a, preferred_element_type=jnp.float32)
        * scale_protein,
        "aa",
        scatter_dimension=0,
        tiled=True,
    )
    slab_part = protein_slab
    ligand_back = lax.psum_scatter(
        jnp.einsum(form_b, slab_part, rounded_b, preferred_element_type=jnp.float32) * scale_ligand,
        "ba",
        scatter_dimension=0,
        tiled=True,
    )
    return (pair_exchange, ligand_back, protein_back)


def solution(mesh):
    placed = (P(None, "aa", "ba"), P(None, "ba", "aa"), P(None, "ba"), P(None, "aa"))
    return jax.shard_map(
        on_device,
        mesh=mesh,
        in_specs=placed,
        out_specs=(P("aa", "ba"), P(("aa", "ba"), None), P(("ba", "aa"), None)),
        check_vma=False,
    )
```

profile of v0, /device:TPU:1, one launch (start us, length us, event | category | flops | bytes accessed | tf_op | source)
XLA Modules:
  0.0 1048.9 jit_solution(15083016670717883467)
XLA Ops:
  7.2 0.0 copy-start
  7.2 0.0 copy-start.2
  7.2 0.0 all-reduce.5.cloned.1.call-start
  7.2 6.9 fusion.10
  14.2 0.0 all-reduce.5.cloned.1.call-update
  14.2 0.0 all-reduce.3.cloned.1.call-start
  14.2 0.0 copy-done
  14.3 0.0 copy-done.2
  14.3 13.6 %fusion.8 = f32[64,16,1024]{1,2,0:T(8,128)} fusion(bf16[64,16,512]{2,1,0:T(8,128)(2,1)S(1)} %copy-done, bf16[1024,512]{1,0:T(8,128)(2,1)S(1)} %copy-done.2), kind=kOutput, calls=%fused_computation.9 | convolution fusion | flops 1073741824 | bytes 6291456 | tf_op jit(solution)/shard_map/qam,bm->qab/dot_general | solution.py:16
  27.9 0.0 all-reduce.3.cloned.1.call-update
  27.9 0.0 reduce-scatter.7.cloned.1.call-start
  27.9 79.1 %all-reduce.5.cloned.1.call-done = f32[64,32,128]{2,1,0:T(8,128)} async-done(((f32[64,32,128]{2,1,0:T(8,128)}), f32[64,32,128]{2,1,0:T(8,128)}) %all-reduce.5.cloned.1.call-update) | async-done | bytes 1048592 | tf_op jit(solution)/shard_map/psum | solution.py:21
  107.0 5.0 fusion.3
  112.0 1.3 copy.32
  113.4 0.0 reduce-scatter.7.cloned.1.call-update
  113.4 0.0 copy-start.1
  113.4 0.0 reduce-scatter.9.cloned.1.call-start
  113.5 726.4 %all-reduce.3.cloned.1.call-done = f32[64,16,1024]{1,2,0:T(8,128)} async-done(((f32[64,16,1024]{1,2,0:T(8,128)}), f32[64,16,1024]{1,2,0:T(8,128)}) %all-reduce.3.cloned.1.call-update) | async-done | bytes 4194320 | tf_op jit(solution)/shard_map/psum | solution.py:15
  839.9 13.9 %fusion.4 = f32[512,1024]{0,1:T(8,128)} fusion(bf16[64,16,512]{2,1,0:T(8,128)(2,1)S(1)} %copy-done, f32[64,16,1024]{1,2,0:T(8,128)} %all-reduce.3.cloned.1.call-done), kind=kOutput, calls=%fused_computation.6 | convolution fusion | flops 1075314688 | bytes 7340032 | tf_op jit(solution)/shard_map/qam,qab->mb/dot_general | solution.py:39
  853.9 2.9 copy.34
  856.8 0.0 reduce-scatter.9.cloned.1.call-update
  856.8 0.0 copy-done.1
  856.8 1.6 fusion.7
  858.4 0.7 copy.27
  859.1 97.4 %reduce-scatter.7.cloned.1.call-done = f32[64,128]{1,0:T(8,128)} async-done(((f32[2048,128]{1,0:T(8,128)}), f32[64,128]{1,0:T(8,128)}) %reduce-scatter.7.cloned.1.call-update) | async-done | bytes 32784
  956.5 85.9 %reduce-scatter.9.cloned.1.call-done = f32[64,1024]{1,0:T(8,128)} async-done(((f32[512,1024]{1,0:T(8,128)}), f32[64,1024]{1,0:T(8,128)}) %reduce-scatter.9.cloned.1.call-update) | async-done | bytes 262160
  (1 shorter events, 0.0 us)
Async XLA Ops:
  7.2 7.1 copy-start
  7.2 7.1 copy-start.2
  7.2 99.9 %all-reduce.5.cloned.1.call-start = ((), (), s32[]{:S(2)}) async-start(), calls=%async_computation.3 | async-start | bytes 2097152 | tf_op jit(solution)/shard_map/psum | solution.py:21
  14.2 825.7 %all-reduce.3.cloned.1.call-start = ((), (), s32[]{:S(2)}) async-start(), calls=%async_computation.2 | async-start | bytes 67108864 | tf_op jit(solution)/shard_map/psum | solution.py:15
  27.9 928.6 %reduce-scatter.7.cloned.1.call-start = ((), (), s32[]{:S(2)}) async-start(), calls=%async_computation.4 | async-start | bytes 1081344
  113.4 743.4 %copy-start.1 = (f32[64,32,128]{2,1,0:T(8,128)S(1)}, f32[64,32,128]{2,1,0:T(8,128)}, u32[]{:S(2)}) copy-start(f32[64,32,128]{2,1,0:T(8,128)} %all-reduce.5.cloned.1.call-done) | copy-start | bytes 3145732
  113.4 928.9 %reduce-scatter.9.cloned.1.call-start = ((), (), s32[]{:S(2)}) async-start(), calls=%async_computation.5 | async-start | bytes 2359296
Sparse Core Ops, SparseCore 0:
  14.3 92.6 all-reduce.4
  109.7 730.1 all-reduce.2
  843.0 113.4 reduce-scatter.6
  961.5 80.8 reduce-scatter.8
where the time goes:
time: 1050 us
  waiting for transfers between devices  989 us (94%)
  matrix products  39.5 us (4%)
  between operations  13.8 us (1%)
    psum x1, waiting for transfers between devices, on_device(): lax.psum(jnp.einsum('qam,bm->qab', ligand_slab, protein_orbitals, preferr...  726 us
    unnamed x6, waiting for transfers between devices  183 us
    psum x1, waiting for transfers between devices, on_device(): lax.psum(jnp.einsum('an,qbn->qba', ligand_orbitals, protein_slab, preferr...  79.1 us
  transfers between devices with their start and end apart: 4, of which 4 were waited for; matrix products, arithmetic and copies ran while one was open for 4% of the time, Pallas kernels for 0%

commit v1 on v0

v1 whole, which is shorter than its diff:
```python
import math

import jax
import jax.numpy as jnp
from jax import lax
from jax.sharding import Mesh, PartitionSpec as P

AXES = ("x", "yh", "z", "yl", "c")
AA = ("x", "yh")
ZY = ("z", "yl")
F32 = jnp.float32
BF16 = jnp.bfloat16


def flat_perm(sizes, shift):
    first, second = sizes
    return [
        (i * second + j, ((i + shift[0]) % first) * second + (j + shift[1]) % second)
        for i in range(first)
        for j in range(second)
    ]


def shifts(sizes):
    return [(i, j) for i in range(sizes[0]) for j in range(sizes[1]) if (i, j) != (0, 0)]


def scatter_sum(pieces, axes, sizes):
    me = [lax.axis_index(name) for name in axes]
    total = lax.dynamic_index_in_dim(pieces, me[0] * sizes[1] + me[1], 0, keepdims=False)
    for shift in shifts(sizes):
        target = lax.rem(me[0] + shift[0], sizes[0]) * sizes[1] + lax.rem(me[1] + shift[1], sizes[1])
        piece = lax.dynamic_index_in_dim(pieces, target, 0, keepdims=False)
        total = total + lax.ppermute(piece, axes, flat_perm(sizes, shift))
    return total


def scatter_sum_all(pieces, axes):
    return jnp.sum(lax.all_to_all(pieces, axes, 0, 0, tiled=True), axis=0)


def gather(block, axes, sizes):
    me = [lax.axis_index(name) for name in axes]
    out = jnp.zeros((sizes[0] * sizes[1],) + block.shape, block.dtype)
    out = lax.dynamic_update_index_in_dim(out, block, me[0] * sizes[1] + me[1], 0)
    for shift in shifts(sizes):
        source = lax.rem(me[0] + sizes[0] - shift[0], sizes[0]) * sizes[1] + lax.rem(
            me[1] + sizes[1] - shift[1], sizes[1]
        )
        got = lax.ppermute(block, axes, flat_perm(sizes, shift))
        out = lax.dynamic_update_index_in_dim(out, got, source, 0)
    return out


def swap(block):
    return lax.ppermute(block, "c", [(0, 1), (1, 0)])


def dot(left, right, contract):
    return lax.dot_general(left, right, (contract, ((), ())), preferred_element_type=F32)


def on_device(ligand_slab, protein_slab, protein_orbitals, ligand_orbitals, *, sizes):
    aa = tuple(sizes[name] for name in AA)
    zy = tuple(sizes[name] for name in ZY)
    n_aa, n_zy = aa[0] * aa[1], zy[0] * zy[1]
    fit, lig, mus = ligand_slab.shape
    _, pro, nus = protein_slab.shape
    lig_total, pro_total = ligand_orbitals.shape[0], protein_orbitals.shape[0]
    core = lax.axis_index("c")

    x_own = ligand_slab.reshape(fit * lig, mus)
    y = protein_slab.reshape(fit * pro, nus)
    orb = protein_orbitals.reshape(n_zy, 2, pro, mus)
    orb_own = lax.dynamic_index_in_dim(orb, core, 1, keepdims=False).reshape(n_zy * pro, mus)
    orb_send = lax.dynamic_index_in_dim(orb, 1 - core, 1, keepdims=False).reshape(n_zy * pro, mus)
    x_other = swap(x_own)
    orb_other = swap(orb_send)

    b_part = dot(ligand_orbitals, y, ((1,), (1,)))
    b_own = scatter_sum(b_part.reshape(n_aa, lig, fit * pro), AA, aa)

    a_part = dot(orb_own, x_own, ((1,), (1,))) + dot(orb_other, x_other, ((1,), (1,)))
    a_own = scatter_sum_all(a_part.reshape(n_zy, pro, fit * lig), ZY)

    b_all = gather(b_own.astype(BF16), AA, aa).reshape(n_aa * lig, fit * pro)
    a_all = gather(a_own.astype(BF16), ZY, zy).reshape(n_zy * pro, fit * lig)

    pair = jnp.sum(
        jnp.transpose(a_own.reshape(pro, fit, lig), (1, 2, 0))
        * jnp.transpose(b_own.reshape(lig, fit, pro), (1, 0, 2)),
        axis=0,
    )
    pair_exchange = -pair / math.sqrt(fit)

    scale_ligand = 1.0 / math.sqrt(fit * pro_total)
    back_b = dot(y, b_all, ((0,), (1,))) * scale_ligand
    back_b = back_b.reshape(n_zy, 2, nus // (2 * n_zy), lig_total)
    keep = lax.dynamic_index_in_dim(back_b, core, 1, keepdims=False)
    send = lax.dynamic_index_in_dim(back_b, 1 - core, 1, keepdims=False)
    ligand_back = scatter_sum_all(keep + swap(send), ZY)

    scale_protein = 1.0 / math.sqrt(fit * lig_total)
    half = n_zy * pro
    back_other = dot(x_other, a_all, ((0,), (1,))) * scale_protein
    back_own = dot(x_own, a_all, ((0,), (1,))) * scale_protein
    away = scatter_sum_all(back_other.reshape(n_aa, mus // n_aa, half), AA)
    here = scatter_sum_all(back_own.reshape(n_aa, mus // n_aa, half), AA)
    there = swap(away)
    rows = mus // n_aa
    here = here.reshape(rows, n_zy, 1, pro)
    there = there.reshape(rows, n_zy, 1, pro)
    protein_back = jnp.where(
        core == 0,
        jnp.concatenate([here, there], axis=2),
        jnp.concatenate([there, here], axis=2),
    ).reshape(rows, pro_total)
    return (pair_exchange, ligand_back, protein_back)


def solution(mesh):
    sizes = {"x": mesh.shape["aa"] // 2, "yh": 2, "z": mesh.shape["ba"] // 4, "yl": 2, "c": 2}
    fine = Mesh(mesh.devices.reshape([sizes[name] for name in AXES]), AXES)
    aa, ba = AA, ("z", "yl", "c")
    placed = (P(None, aa, ba), P(None, ba, aa), P(None, ba), P(None, aa))

    def body(*args):
        return on_device(*args, sizes=sizes)

    return jax.shard_map(
        body,
        mesh=fine,
        in_specs=placed,
        out_specs=(P(aa, ba), P(aa + ba, None), P(ba + aa, None)),
        check_vma=False,
    )
```

time: 1050 us -> 208 us (0.20)
  waiting for transfers between devices: 989 us -> 63 us
  starting transfers between devices: 0.16 us -> 103 us
  matrix products: 39.5 us -> 23.7 us
  between operations: 13.8 us -> 1.14 us
    psum x2 -> x0, waiting for transfers between devices: 806 us -> none  [the longest x1 726 us: on_device(): lax.psum(jnp.einsum('qam,bm->qab', ligand_slab, protein_orbitals, preferr...]
    unnamed x6 -> x0, waiting for transfers between devices: 183 us -> none
    ppermute x0 -> x33, starting transfers between devices: none -> 76.2 us  [the longest x22 49.8 us: gather(): got = lax.ppermute(block, axes, flat_perm(sizes, shift))]
    all_to_all x0 -> x4, waiting for transfers between devices: none -> 43.1 us  [scatter_sum_all(): return jnp.sum(lax.all_to_all(pieces, axes, 0, 0, tiled=True), axis=0)]
    all_to_all x0 -> x4, starting transfers between devices: none -> 27 us  [scatter_sum_all(): return jnp.sum(lax.all_to_all(pieces, axes, 0, 0, tiled=True), axis=0)]
    ppermute x0 -> x33, waiting for transfers between devices: none -> 20 us  [the longest x22 15.1 us: gather(): got = lax.ppermute(block, axes, flat_perm(sizes, shift))]
    dot_general x4 -> x6, matrix products: 39.5 us -> 23.7 us  [dot(): lax.dot_general(left, right, (contract, ((), ())), preferred_element_type...]
  transfers between devices with their start and end apart: 4 -> 37, of which waited for: 4 -> 10; matrix products, arithmetic and copies ran while one was open for 4% -> 19% of each run, Pallas kernels for 0% -> 0%
where the time goes in v1:
time: 208 us
  starting transfers between devices  103 us (50%)
  waiting for transfers between devices  63 us (30%)
  matrix products  23.7 us (11%)
  local copies, waits for them, and re-layouts  9.83 us (5%)
  other arithmetic  6.74 us (3%)
    ppermute x22, starting transfers between devices, gather(): got = lax.ppermute(block, axes, flat_perm(sizes, shift))  49.8 us
    all_to_all x4, waiting for transfers between devices, scatter_sum_all(): return jnp.sum(lax.all_to_all(pieces, axes, 0, 0, tiled=True), axis=0)  43.1 us
    all_to_all x4, starting transfers between devices, scatter_sum_all(): return jnp.sum(lax.all_to_all(pieces, axes, 0, 0, tiled=True), axis=0)  27 us
    dot_general x6, matrix products, dot(): lax.dot_general(left, right, (contract, ((), ())), preferred_element_type...  23.7 us
    ppermute x22, waiting for transfers between devices, gather(): got = lax.ppermute(block, axes, flat_perm(sizes, shift))  15.1 us
    ppermute x4, starting transfers between devices, swap(): return lax.ppermute(block, 'c', [(0, 1), (1, 0)])  13.2 us
    ppermute x7, starting transfers between devices, scatter_sum(): total = total + lax.ppermute(piece, axes, flat_perm(sizes, shift))  13.1 us
    ppermute x7, waiting for transfers between devices, scatter_sum(): total = total + lax.ppermute(piece, axes, flat_perm(sizes, shift))  4.82 us
  transfers between devices with their start and end apart: 37, of which 10 were waited for; matrix products, arithmetic and copies ran while one was open for 19% of the time, Pallas kernels for 0%

profile of v1, /device:TPU:1, one launch (start us, length us, event | category | flops | bytes accessed | tf_op | source)
XLA Modules:
  0.0 207.6 jit_solution(16945357042298177573)
XLA Ops:
  0.7 3.3 %collective-permute-start.1 = (bf16[1024,512]{1,0:T(8,128)(2,1)}, bf16[1024,512]{1,0:T(8,128)(2,1)}, u32[]{:S(2)}, u32[]{:S(2)}) collective-permute-start(bf16[1024,512]{1,0:T(8,128)(2,1)} %bitcast.133), channel_id=1, source_target_pairs={{0,1},{1,0},{2,3},{3,2},{4,5},{5,4},{6,7},{7,6},{8,9},{9,8},{10,11... | collective-permute-start | bytes 3145736 | tf_op jit(solution)/shard_map/ppermute | solution.py:56
  4.0 6.3 %fusion.10 = f32[8,16,2048]{2,1,0:T(8,128)S(1)} fusion(bf16[8,16,2048]{2,1,0:T(8,128)(2,1)S(1)} %bitcast.123, bf16[2048,2048,1]{1,0,2:T(8,128)(2,1)} %bitcast.124), kind=kOutput, calls=%fused_computation.52 | convolution fusion | flops 1073741824 | bytes 9961472 | tf_op jit(solution)/shard_map/dot_general | solution.py:60
  11.2 3.6 %collective-permute-start.8 = (f32[16,2048]{1,0:T(8,128)}, f32[16,2048]{1,0:T(8,128)S(1)}, u32[]{:S(2)}, u32[]{:S(2)}) collective-permute-start(f32[16,2048]{1,0:T(8,128)} %get-tuple-element.18), channel_id=1, source_target_pairs={{0,224},{32,192},{64,32},{96,0},{128,96},{160,64},{192,160},{224,1... | collective-permute-start | bytes 393224 | tf_op jit(solution)/shard_map/ppermute | solution.py:34
  21.2 3.2 %collective-permute-start.4 = (f32[16,2048]{1,0:T(8,128)S(1)}, f32[16,2048]{1,0:T(8,128)}, u32[]{:S(2)}, u32[]{:S(2)}) collective-permute-start(f32[16,2048]{1,0:T(8,128)S(1)} %get-tuple-element.22), channel_id=1, source_target_pairs={{0,96},{32,64},{64,160},{96,128},{128,224},{160,192},{192,32},{224... | collective-permute-start | bytes 393224 | tf_op jit(solution)/shard_map/ppermute | solution.py:34
  24.8 2.6 %collective-permute-start.2 = (f32[16,2048]{1,0:T(8,128)S(1)}, f32[16,2048]{1,0:T(8,128)}, u32[]{:S(2)}, u32[]{:S(2)}) collective-permute-start(f32[16,2048]{1,0:T(8,128)S(1)} %get-tuple-element.17), channel_id=1, source_target_pairs={{0,32},{32,0},{64,96},{96,64},{128,160},{160,128},{192,224},{224,1... | collective-permute-start | bytes 393224 | tf_op jit(solution)/shard_map/ppermute | solution.py:34
  29.5 4.8 %collective-permute-done.3 = f32[16,2048]{1,0:T(8,128)} collective-permute-done((f32[16,2048]{1,0:T(8,128)S(1)}, f32[16,2048]{1,0:T(8,128)}, u32[]{:S(2)}, u32[]{:S(2)}) %collective-permute-start.3) | collective-permute-done | bytes 131104 | tf_op jit(solution)/shard_map/ppermute | solution.py:34
  36.2 3.8 %collective-permute-start.10 = (bf16[16,2048]{1,0:T(8,128)(2,1)}, bf16[16,2048]{1,0:T(8,128)(2,1)S(1)}, u32[]{:S(2)}, u32[]{:S(2)}) collective-permute-start(bf16[16,2048]{1,0:T(8,128)(2,1)} %get-tuple-element.15), channel_id=1, source_target_pairs={{0,64},{32,96},{64,128},{96,160},{128,192},{160,224},{192,0},{224,... | collective-permute-start | bytes 196616 | tf_op jit(solution)/shard_map/ppermute | solution.py:50
  40.1 3.3 %collective-permute-start.12 = (bf16[16,2048]{1,0:T(8,128)(2,1)}, bf16[16,2048]{1,0:T(8,128)(2,1)S(1)}, u32[]{:S(2)}, u32[]{:S(2)}) collective-permute-start(bf16[16,2048]{1,0:T(8,128)(2,1)} %get-tuple-element.15), channel_id=1, source_target_pairs={{0,128},{32,160},{64,192},{96,224},{128,0},{160,32},{192,64},{224,... | collective-permute-start | bytes 196616 | tf_op jit(solution)/shard_map/ppermute | solution.py:50
  45.5 3.5 %convolution_add_fusion = f32[512,1024]{1,0:T(8,128)} fusion(f32[512,1024]{1,0:T(8,128)S(1)} %fusion.9, bf16[512,512]{1,0:T(8,128)(2,1)} %collective-permute-done, bf16[1024,512]{1,0:T(8,128)(2,1)} %collective-permute-done.1), kind=kOutput, calls=%fused_computation.2 | convolution fusion | flops 537395200 | bytes 5767168 | tf_op jit(solution)/shard_map/dot_general | solution.py:60
  49.0 8.4 %all-to-all-start = ((f32[16,32,1024]{2,1,0:T(8,128)}), f32[16,32,1024]{2,1,0:T(8,128)S(1)}, u32[]{:S(2)}, u32[]{:S(2)}) async-start(f32[16,32,1024]{2,1,0:T(8,128)} %bitcast.126), calls=%async_computation | async-start | bytes 4194304 | tf_op jit(solution)/shard_map/all_to_all | solution.py:39
  57.4 2.6 %collective-permute-start.14 = (bf16[16,2048]{1,0:T(8,128)(2,1)}, bf16[16,2048]{1,0:T(8,128)(2,1)S(1)}, u32[]{:S(2)}, u32[]{:S(2)}) collective-permute-start(bf16[16,2048]{1,0:T(8,128)(2,1)} %get-tuple-element.15), channel_id=1, source_target_pairs={{0,192},{32,224},{64,0},{96,32},{128,64},{160,96},{192,128},{224,1... | collective-permute-start | bytes 196616 | tf_op jit(solution)/shard_map/ppermute | solution.py:50
  62.5 4.5 %collective-permute-done.15 = bf16[16,2048]{1,0:T(8,128)(2,1)S(1)} collective-permute-done((bf16[16,2048]{1,0:T(8,128)(2,1)}, bf16[16,2048]{1,0:T(8,128)(2,1)S(1)}, u32[]{:S(2)}, u32[]{:S(2)}) %collective-permute-start.15) | collective-permute-done | bytes 65568 | tf_op jit(solution)/shard_map/ppermute | solution.py:50
  67.0 5.7 %fusion = f32[2048,128]{0,1:T(8,128)} fusion(bf16[128,2048]{1,0:T(8,128)(2,1)S(1)} %bitcast.129, bf16[2048,2048]{1,0:T(8,128)(2,1)} %bitcast.125), kind=kOutput, calls=%fused_computation.1 | convolution fusion | flops 1074003968 | bytes 9961472 | tf_op jit(solution)/shard_map/dot_general | solution.py:60
  72.7 2.5 %copy.18 = f32[2048,128]{1,0:T(8,128)} copy(f32[2048,128]{0,1:T(8,128)} %fusion) | data formatting | bytes 2097152 | tf_op jit(solution)/shard_map/mul | solution.py:97
  77.1 6.2 %collective-permute-start.16 = (f32[16,64,128]{2,1,0:T(8,128)}, f32[16,64,128]{2,1,0:T(8,128)S(1)}, u32[]{:S(2)}, u32[]{:S(2)}) collective-permute-start(f32[16,64,128]{2,1,0:T(8,128)} %dynamic-slice_bitcast_fusion), channel_id=1, source_target_pairs={{0,1},{1,0},{2,3},{3,2},{4,5},{5,4},{6,7},{7,6},{8,9},{9,8},{10,11... | collective-permute-start | bytes 1572872 | tf_op jit(solution)/shard_map/ppermute | solution.py:56
  83.4 20.3 %all-to-all-done = f32[16,32,1024]{2,1,0:T(8,128)S(1)} async-done(((f32[16,32,1024]{2,1,0:T(8,128)}), f32[16,32,1024]{2,1,0:T(8,128)S(1)}, u32[]{:S(2)}, u32[]{:S(2)}) %all-to-all-start) | async-done | bytes 2097184 | tf_op jit(solution)/shard_map/all_to_all | solution.py:39
  106.3 7.7 %all-to-all-start.1 = ((f32[16,64,128]{2,1,0:T(8,128)}), f32[16,64,128]{2,1,0:T(8,128)S(1)}, u32[]{:S(2)}, u32[]{:S(2)}) async-start(f32[16,64,128]{2,1,0:T(8,128)} %bitcast_add_fusion), calls=%async_computation.1 | async-start | bytes 1048576 | tf_op jit(solution)/shard_map/all_to_all | solution.py:39
  117.5 3.3 %collective-permute-start.20 = (bf16[32,1024]{1,0:T(8,128)(2,1)S(1)}, bf16[32,1024]{1,0:T(8,128)(2,1)S(1)}, u32[]{:S(2)}, u32[]{:S(2)}) collective-permute-start(bf16[32,1024]{1,0:T(8,128)(2,1)S(1)} %get-tuple-element.13), channel_id=1, source_target_pairs={{0,8},{2,10},{4,12},{6,14},{8,16},{10,18},{12,20},{14,22},{16,24},... | collective-permute-start | bytes 196616 | tf_op jit(solution)/shard_map/ppermute | solution.py:50
  122.3 5.0 %collective-permute-done.18 = bf16[32,1024]{1,0:T(8,128)(2,1)S(1)} collective-permute-done((bf16[32,1024]{1,0:T(8,128)(2,1)S(1)}, bf16[32,1024]{1,0:T(8,128)(2,1)S(1)}, u32[]{:S(2)}, u32[]{:S(2)}) %collective-permute-start.18) | collective-permute-done | bytes 65568 | tf_op jit(solution)/shard_map/ppermute | solution.py:50
  127.3 4.1 %collective-permute-start.23 = (bf16[32,1024]{1,0:T(8,128)(2,1)S(1)}, bf16[32,1024]{1,0:T(8,128)(2,1)S(1)}, u32[]{:S(2)}, u32[]{:S(2)}) collective-permute-start(bf16[32,1024]{1,0:T(8,128)(2,1)S(1)} %get-tuple-element.13), channel_id=1, source_target_pairs={{0,14},{2,12},{4,18},{6,16},{8,22},{10,20},{12,26},{14,24},{16,30}... | collective-permute-start | bytes 196616 | tf_op jit(solution)/shard_map/ppermute | solution.py:50
  131.4 3.2 %collective-permute-start.24 = (bf16[32,1024]{1,0:T(8,128)(2,1)S(1)}, bf16[32,1024]{1,0:T(8,128)(2,1)S(1)}, u32[]{:S(2)}, u32[]{:S(2)}) collective-permute-start(bf16[32,1024]{1,0:T(8,128)(2,1)S(1)} %get-tuple-element.13), channel_id=1, source_target_pairs={{0,16},{2,18},{4,20},{6,22},{8,24},{10,26},{12,28},{14,30},{16,0},... | collective-permute-start | bytes 196616 | tf_op jit(solution)/shard_map/ppermute | solution.py:50
  134.6 2.8 %collective-permute-start.25 = (bf16[32,1024]{1,0:T(8,128)(2,1)S(1)}, bf16[32,1024]{1,0:T(8,128)(2,1)S(1)}, u32[]{:S(2)}, u32[]{:S(2)}) collective-permute-start(bf16[32,1024]{1,0:T(8,128)(2,1)S(1)} %get-tuple-element.13), channel_id=1, source_target_pairs={{0,18},{2,16},{4,22},{6,20},{8,26},{10,24},{12,30},{14,28},{16,2},... | collective-permute-start | bytes 196616 | tf_op jit(solution)/shard_map/ppermute | solution.py:50
  139.5 4.4 %collective-permute-start.27 = (bf16[32,1024]{1,0:T(8,128)(2,1)S(1)}, bf16[32,1024]{1,0:T(8,128)(2,1)S(1)}, u32[]{:S(2)}, u32[]{:S(2)}) collective-permute-start(bf16[32,1024]{1,0:T(8,128)(2,1)S(1)} %get-tuple-element.13), channel_id=1, source_target_pairs={{0,22},{2,20},{4,26},{6,24},{8,30},{10,28},{12,2},{14,0},{16,6},{1... | collective-permute-start | bytes 196616 | tf_op jit(solution)/shard_map/ppermute | solution.py:50
  146.0 7.1 %collective-permute-start.29 = (bf16[32,1024]{1,0:T(8,128)(2,1)S(1)}, bf16[32,1024]{1,0:T(8,128)(2,1)S(1)}, u32[]{:S(2)}, u32[]{:S(2)}) collective-permute-start(bf16[32,1024]{1,0:T(8,128)(2,1)S(1)} %get-tuple-element.13), channel_id=1, source_target_pairs={{0,26},{2,24},{4,30},{6,28},{8,2},{10,0},{12,6},{14,4},{16,10},{18... | collective-permute-start | bytes 196616 | tf_op jit(solution)/shard_map/ppermute | solution.py:50
  153.2 2.2 %collective-permute-start.31 = (bf16[32,1024]{1,0:T(8,128)(2,1)S(1)}, bf16[32,1024]{1,0:T(8,128)(2,1)S(1)}, u32[]{:S(2)}, u32[]{:S(2)}) collective-permute-start(bf16[32,1024]{1,0:T(8,128)(2,1)S(1)} %get-tuple-element.13), channel_id=1, source_target_pairs={{0,30},{2,28},{4,2},{6,0},{8,6},{10,4},{12,10},{14,8},{16,14},{18,... | collective-permute-start | bytes 196616 | tf_op jit(solution)/shard_map/ppermute | solution.py:50
  157.2 3.8 %collective-permute-done.31 = bf16[32,1024]{1,0:T(8,128)(2,1)S(1)} collective-permute-done((bf16[32,1024]{1,0:T(8,128)(2,1)S(1)}, bf16[32,1024]{1,0:T(8,128)(2,1)S(1)}, u32[]{:S(2)}, u32[]{:S(2)}) %collective-permute-start.31) | collective-permute-done | bytes 65568 | tf_op jit(solution)/shard_map/ppermute | solution.py:50
  161.0 3.3 %convolution_multiply_fusion.1 = f32[512,512]{0,1:T(8,128)} fusion(bf16[512,1024]{1,0:T(8,128)(2,1)S(1)} %bitcast.138, bf16[1024,512]{1,0:T(8,128)(2,1)} %collective-permute-done.1), kind=kOutput, calls=%fused_computation.3 | convolution fusion | flops 537133056 | bytes 3145728 | tf_op jit(solution)/shard_map/dot_general | solution.py:60
  164.3 6.9 %all-to-all-start.3 = ((f32[8,64,512]{2,1,0:T(8,128)}), f32[8,64,512]{2,1,0:T(8,128)S(1)}, u32[]{:S(2)}, u32[]{:S(2)}) async-start(f32[8,64,512]{2,1,0:T(8,128)} %bitcast.137), calls=%async_computation.3 | async-start | bytes 2097152 | tf_op jit(solution)/shard_map/all_to_all | solution.py:39
  171.2 3.0 %convolution_multiply_fusion.2 = f32[512,512]{0,1:T(8,128)} fusion(bf16[512,1024]{1,0:T(8,128)(2,1)} %bitcast.139, bf16[1024,512]{1,0:T(8,128)(2,1)S(1)} %bitcast.135), kind=kOutput, calls=%fused_computation.4 | convolution fusion | flops 537133056 | bytes 3145728 | tf_op jit(solution)/shard_map/dot_general | solution.py:60
  174.2 12.6 %all-to-all-done.3 = f32[8,64,512]{2,1,0:T(8,128)S(1)} async-done(((f32[8,64,512]{2,1,0:T(8,128)}), f32[8,64,512]{2,1,0:T(8,128)S(1)}, u32[]{:S(2)}, u32[]{:S(2)}) %all-to-all-start.3) | async-done | bytes 1048608 | tf_op jit(solution)/shard_map/all_to_all | solution.py:39
  186.8 4.0 %all-to-all-start.2 = ((f32[8,64,512]{2,1,0:T(8,128)}), f32[8,64,512]{2,1,0:T(8,128)S(1)}, u32[]{:S(2)}, u32[]{:S(2)}) async-start(f32[8,64,512]{2,1,0:T(8,128)} %bitcast.136), calls=%async_computation.2 | async-start | bytes 2097152 | tf_op jit(solution)/shard_map/all_to_all | solution.py:39
  196.1 10.1 %all-to-all-done.2 = f32[8,64,512]{2,1,0:T(8,128)S(1)} async-done(((f32[8,64,512]{2,1,0:T(8,128)}), f32[8,64,512]{2,1,0:T(8,128)S(1)}, u32[]{:S(2)}, u32[]{:S(2)}) %all-to-all-start.2) | async-done | bytes 1048608 | tf_op jit(solution)/shard_map/all_to_all | solution.py:39
  (106 shorter events, 38.3 us)
Async XLA Ops:
  0.7 42.7 %collective-permute-start.1 = (bf16[1024,512]{1,0:T(8,128)(2,1)}, bf16[1024,512]{1,0:T(8,128)(2,1)}, u32[]{:S(2)}, u32[]{:S(2)}) collective-permute-start(bf16[1024,512]{1,0:T(8,128)(2,1)} %bitcast.133), channel_id=1, source_target_pairs={{0,1},{1,0},{2,3},{3,2},{4,5},{5,4},{6,7},{7,6},{8,9},{9,8},{10,11... | collective-permute-start | bytes 3145736 | tf_op jit(solution)/shard_map/ppermute | solution.py:56
  11.2 7.8 %collective-permute-start.8 = (f32[16,2048]{1,0:T(8,128)}, f32[16,2048]{1,0:T(8,128)S(1)}, u32[]{:S(2)}, u32[]{:S(2)}) collective-permute-start(f32[16,2048]{1,0:T(8,128)} %get-tuple-element.18), channel_id=1, source_target_pairs={{0,224},{32,192},{64,32},{96,0},{128,96},{160,64},{192,160},{224,1... | collective-permute-start | bytes 393224 | tf_op jit(solution)/shard_map/ppermute | solution.py:34
  15.4 9.0 %collective-permute-start.6 = (f32[16,2048]{1,0:T(8,128)}, f32[16,2048]{1,0:T(8,128)S(1)}, u32[]{:S(2)}, u32[]{:S(2)}) collective-permute-start(f32[16,2048]{1,0:T(8,128)} %get-tuple-element.20), channel_id=1, source_target_pairs={{0,160},{32,128},{64,224},{96,192},{128,32},{160,0},{192,96},{224,... | collective-permute-start | bytes 393224 | tf_op jit(solution)/shard_map/ppermute | solution.py:34
  16.9 7.9 %collective-permute-start.5 = (f32[16,2048]{1,0:T(8,128)}, f32[16,2048]{1,0:T(8,128)S(1)}, u32[]{:S(2)}, u32[]{:S(2)}) collective-permute-start(f32[16,2048]{1,0:T(8,128)} %get-tuple-element.21), channel_id=1, source_target_pairs={{0,128},{32,160},{64,192},{96,224},{128,0},{160,32},{192,64},{224,... | collective-permute-start | bytes 393224 | tf_op jit(solution)/shard_map/ppermute | solution.py:34
  19.1 21.0 %collective-permute-start = (bf16[512,512]{1,0:T(8,128)(2,1)}, bf16[512,512]{1,0:T(8,128)(2,1)}, u32[]{:S(2)}, u32[]{:S(2)}) collective-permute-start(bf16[512,512]{1,0:T(8,128)(2,1)} %bitcast.3), channel_id=1, source_target_pairs={{0,1},{1,0},{2,3},{3,2},{4,5},{5,4},{6,7},{7,6},{8,9},{9,8},{10,11... | collective-permute-start | bytes 1572872 | tf_op jit(solution)/shard_map/ppermute | solution.py:56
  21.2 8.2 %collective-permute-start.4 = (f32[16,2048]{1,0:T(8,128)S(1)}, f32[16,2048]{1,0:T(8,128)}, u32[]{:S(2)}, u32[]{:S(2)}) collective-permute-start(f32[16,2048]{1,0:T(8,128)S(1)} %get-tuple-element.22), channel_id=1, source_target_pairs={{0,96},{32,64},{64,160},{96,128},{128,224},{160,192},{192,32},{224... | collective-permute-start | bytes 393224 | tf_op jit(solution)/shard_map/ppermute | solution.py:34
  24.4 9.8 %collective-permute-start.3 = (f32[16,2048]{1,0:T(8,128)S(1)}, f32[16,2048]{1,0:T(8,128)}, u32[]{:S(2)}, u32[]{:S(2)}) collective-permute-start(f32[16,2048]{1,0:T(8,128)S(1)} %get-tuple-element.23), channel_id=1, source_target_pairs={{0,64},{32,96},{64,128},{96,160},{128,192},{160,224},{192,0},{224,... | collective-permute-start | bytes 393224 | tf_op jit(solution)/shard_map/ppermute | solution.py:34
  24.8 9.4 %collective-permute-start.2 = (f32[16,2048]{1,0:T(8,128)S(1)}, f32[16,2048]{1,0:T(8,128)}, u32[]{:S(2)}, u32[]{:S(2)}) collective-permute-start(f32[16,2048]{1,0:T(8,128)S(1)} %get-tuple-element.17), channel_id=1, source_target_pairs={{0,32},{32,0},{64,96},{96,64},{128,160},{160,128},{192,224},{224,1... | collective-permute-start | bytes 393224 | tf_op jit(solution)/shard_map/ppermute | solution.py:34
  36.2 21.2 %collective-permute-start.9 = (bf16[16,2048]{1,0:T(8,128)(2,1)}, bf16[16,2048]{1,0:T(8,128)(2,1)}, u32[]{:S(2)}, u32[]{:S(2)}) collective-permute-start(bf16[16,2048]{1,0:T(8,128)(2,1)} %get-tuple-element.15), channel_id=1, source_target_pairs={{0,32},{32,0},{64,96},{96,64},{128,160},{160,128},{192,224},{224,1... | collective-permute-start | bytes 196616 | tf_op jit(solution)/shard_map/ppermute | solution.py:50
  36.2 24.7 %collective-permute-start.10 = (bf16[16,2048]{1,0:T(8,128)(2,1)}, bf16[16,2048]{1,0:T(8,128)(2,1)S(1)}, u32[]{:S(2)}, u32[]{:S(2)}) collective-permute-start(bf16[16,2048]{1,0:T(8,128)(2,1)} %get-tuple-element.15), channel_id=1, source_target_pairs={{0,64},{32,96},{64,128},{96,160},{128,192},{160,224},{192,0},{224,... | collective-permute-start | bytes 196616 | tf_op jit(solution)/shard_map/ppermute | solution.py:50
  40.0 22.4 %collective-permute-start.11 = (bf16[16,2048]{1,0:T(8,128)(2,1)}, bf16[16,2048]{1,0:T(8,128)(2,1)S(1)}, u32[]{:S(2)}, u32[]{:S(2)}) collective-permute-start(bf16[16,2048]{1,0:T(8,128)(2,1)} %get-tuple-element.15), channel_id=1, source_target_pairs={{0,96},{32,64},{64,160},{96,128},{128,224},{160,192},{192,32},{224... | collective-permute-start | bytes 196616 | tf_op jit(solution)/shard_map/ppermute | solution.py:50
  40.1 22.4 %collective-permute-start.12 = (bf16[16,2048]{1,0:T(8,128)(2,1)}, bf16[16,2048]{1,0:T(8,128)(2,1)S(1)}, u32[]{:S(2)}, u32[]{:S(2)}) collective-permute-start(bf16[16,2048]{1,0:T(8,128)(2,1)} %get-tuple-element.15), channel_id=1, source_target_pairs={{0,128},{32,160},{64,192},{96,224},{128,0},{160,32},{192,64},{224,... | collective-permute-start | bytes 196616 | tf_op jit(solution)/shard_map/ppermute | solution.py:50
  43.4 19.1 %collective-permute-start.13 = (bf16[16,2048]{1,0:T(8,128)(2,1)}, bf16[16,2048]{1,0:T(8,128)(2,1)S(1)}, u32[]{:S(2)}, u32[]{:S(2)}) collective-permute-start(bf16[16,2048]{1,0:T(8,128)(2,1)} %get-tuple-element.15), channel_id=1, source_target_pairs={{0,160},{32,128},{64,224},{96,192},{128,32},{160,0},{192,96},{224,... | collective-permute-start | bytes 196616 | tf_op jit(solution)/shard_map/ppermute | solution.py:50
  49.0 54.7 %all-to-all-start = ((f32[16,32,1024]{2,1,0:T(8,128)}), f32[16,32,1024]{2,1,0:T(8,128)S(1)}, u32[]{:S(2)}, u32[]{:S(2)}) async-start(f32[16,32,1024]{2,1,0:T(8,128)} %bitcast.126), calls=%async_computation | async-start | bytes 4194304 | tf_op jit(solution)/shard_map/all_to_all | solution.py:39
  77.1 27.3 %collective-permute-start.16 = (f32[16,64,128]{2,1,0:T(8,128)}, f32[16,64,128]{2,1,0:T(8,128)S(1)}, u32[]{:S(2)}, u32[]{:S(2)}) collective-permute-start(f32[16,64,128]{2,1,0:T(8,128)} %dynamic-slice_bitcast_fusion), channel_id=1, source_target_pairs={{0,1},{1,0},{2,3},{3,2},{4,5},{5,4},{6,7},{7,6},{8,9},{9,8},{10,11... | collective-permute-start | bytes 1572872 | tf_op jit(solution)/shard_map/ppermute | solution.py:56
  104.0 17.1 %collective-permute-start.17 = (bf16[32,1024]{1,0:T(8,128)(2,1)S(1)}, bf16[32,1024]{1,0:T(8,128)(2,1)S(1)}, u32[]{:S(2)}, u32[]{:S(2)}) collective-permute-start(bf16[32,1024]{1,0:T(8,128)(2,1)S(1)} %get-tuple-element.13), channel_id=1, source_target_pairs={{0,2},{2,0},{4,6},{6,4},{8,10},{10,8},{12,14},{14,12},{16,18},{18,... | collective-permute-start | bytes 196616 | tf_op jit(solution)/shard_map/ppermute | solution.py:50
  106.3 58.0 %all-to-all-start.1 = ((f32[16,64,128]{2,1,0:T(8,128)}), f32[16,64,128]{2,1,0:T(8,128)S(1)}, u32[]{:S(2)}, u32[]{:S(2)}) async-start(f32[16,64,128]{2,1,0:T(8,128)} %bitcast_add_fusion), calls=%async_computation.1 | async-start | bytes 1048576 | tf_op jit(solution)/shard_map/all_to_all | solution.py:39
  114.1 13.2 %collective-permute-start.18 = (bf16[32,1024]{1,0:T(8,128)(2,1)S(1)}, bf16[32,1024]{1,0:T(8,128)(2,1)S(1)}, u32[]{:S(2)}, u32[]{:S(2)}) collective-permute-start(bf16[32,1024]{1,0:T(8,128)(2,1)S(1)} %get-tuple-element.13), channel_id=1, source_target_pairs={{0,4},{2,6},{4,8},{6,10},{8,12},{10,14},{12,16},{14,18},{16,20},{1... | collective-permute-start | bytes 196616 | tf_op jit(solution)/shard_map/ppermute | solution.py:50
  115.5 16.0 %collective-permute-start.19 = (bf16[32,1024]{1,0:T(8,128)(2,1)S(1)}, bf16[32,1024]{1,0:T(8,128)(2,1)S(1)}, u32[]{:S(2)}, u32[]{:S(2)}) collective-permute-start(bf16[32,1024]{1,0:T(8,128)(2,1)S(1)} %get-tuple-element.13), channel_id=1, source_target_pairs={{0,6},{2,4},{4,10},{6,8},{8,14},{10,12},{12,18},{14,16},{16,22},{1... | collective-permute-start | bytes 196616 | tf_op jit(solution)/shard_map/ppermute | solution.py:50
  117.5 17.1 %collective-permute-start.20 = (bf16[32,1024]{1,0:T(8,128)(2,1)S(1)}, bf16[32,1024]{1,0:T(8,128)(2,1)S(1)}, u32[]{:S(2)}, u32[]{:S(2)}) collective-permute-start(bf16[32,1024]{1,0:T(8,128)(2,1)S(1)} %get-tuple-element.13), channel_id=1, source_target_pairs={{0,8},{2,10},{4,12},{6,14},{8,16},{10,18},{12,20},{14,22},{16,24},... | collective-permute-start | bytes 196616 | tf_op jit(solution)/shard_map/ppermute | solution.py:50
  120.8 16.6 %collective-permute-start.21 = (bf16[32,1024]{1,0:T(8,128)(2,1)S(1)}, bf16[32,1024]{1,0:T(8,128)(2,1)S(1)}, u32[]{:S(2)}, u32[]{:S(2)}) collective-permute-start(bf16[32,1024]{1,0:T(8,128)(2,1)S(1)} %get-tuple-element.13), channel_id=1, source_target_pairs={{0,10},{2,8},{4,14},{6,12},{8,18},{10,16},{12,22},{14,20},{16,26},... | collective-permute-start | bytes 196616 | tf_op jit(solution)/shard_map/ppermute | solution.py:50
  121.1 18.3 %collective-permute-start.22 = (bf16[32,1024]{1,0:T(8,128)(2,1)S(1)}, bf16[32,1024]{1,0:T(8,128)(2,1)S(1)}, u32[]{:S(2)}, u32[]{:S(2)}) collective-permute-start(bf16[32,1024]{1,0:T(8,128)(2,1)S(1)} %get-tuple-element.13), channel_id=1, source_target_pairs={{0,12},{2,14},{4,16},{6,18},{8,20},{10,22},{12,24},{14,26},{16,28}... | collective-permute-start | bytes 196616 | tf_op jit(solution)/shard_map/ppermute | solution.py:50
  127.3 16.5 %collective-permute-start.23 = (bf16[32,1024]{1,0:T(8,128)(2,1)S(1)}, bf16[32,1024]{1,0:T(8,128)(2,1)S(1)}, u32[]{:S(2)}, u32[]{:S(2)}) collective-permute-start(bf16[32,1024]{1,0:T(8,128)(2,1)S(1)} %get-tuple-element.13), channel_id=1, source_target_pairs={{0,14},{2,12},{4,18},{6,16},{8,22},{10,20},{12,26},{14,24},{16,30}... | collective-permute-start | bytes 196616 | tf_op jit(solution)/shard_map/ppermute | solution.py:50
  131.4 14.6 %collective-permute-start.24 = (bf16[32,1024]{1,0:T(8,128)(2,1)S(1)}, bf16[32,1024]{1,0:T(8,128)(2,1)S(1)}, u32[]{:S(2)}, u32[]{:S(2)}) collective-permute-start(bf16[32,1024]{1,0:T(8,128)(2,1)S(1)} %get-tuple-element.13), channel_id=1, source_target_pairs={{0,16},{2,18},{4,20},{6,22},{8,24},{10,26},{12,28},{14,30},{16,0},... | collective-permute-start | bytes 196616 | tf_op jit(solution)/shard_map/ppermute | solution.py:50
  134.6 18.5 %collective-permute-start.25 = (bf16[32,1024]{1,0:T(8,128)(2,1)S(1)}, bf16[32,1024]{1,0:T(8,128)(2,1)S(1)}, u32[]{:S(2)}, u32[]{:S(2)}) collective-permute-start(bf16[32,1024]{1,0:T(8,128)(2,1)S(1)} %get-tuple-element.13), channel_id=1, source_target_pairs={{0,18},{2,16},{4,22},{6,20},{8,26},{10,24},{12,30},{14,28},{16,2},... | collective-permute-start | bytes 196616 | tf_op jit(solution)/shard_map/ppermute | solution.py:50
  137.5 15.8 %collective-permute-start.26 = (bf16[32,1024]{1,0:T(8,128)(2,1)S(1)}, bf16[32,1024]{1,0:T(8,128)(2,1)S(1)}, u32[]{:S(2)}, u32[]{:S(2)}) collective-permute-start(bf16[32,1024]{1,0:T(8,128)(2,1)S(1)} %get-tuple-element.13), channel_id=1, source_target_pairs={{0,20},{2,22},{4,24},{6,26},{8,28},{10,30},{12,0},{14,2},{16,4},{1... | collective-permute-start | bytes 196616 | tf_op jit(solution)/shard_map/ppermute | solution.py:50
  139.5 16.0 %collective-permute-start.27 = (bf16[32,1024]{1,0:T(8,128)(2,1)S(1)}, bf16[32,1024]{1,0:T(8,128)(2,1)S(1)}, u32[]{:S(2)}, u32[]{:S(2)}) collective-permute-start(bf16[32,1024]{1,0:T(8,128)(2,1)S(1)} %get-tuple-element.13), channel_id=1, source_target_pairs={{0,22},{2,20},{4,26},{6,24},{8,30},{10,28},{12,2},{14,0},{16,6},{1... | collective-permute-start | bytes 196616 | tf_op jit(solution)/shard_map/ppermute | solution.py:50
  143.9 11.6 %collective-permute-start.28 = (bf16[32,1024]{1,0:T(8,128)(2,1)S(1)}, bf16[32,1024]{1,0:T(8,128)(2,1)S(1)}, u32[]{:S(2)}, u32[]{:S(2)}) collective-permute-start(bf16[32,1024]{1,0:T(8,128)(2,1)S(1)} %get-tuple-element.13), channel_id=1, source_target_pairs={{0,24},{2,26},{4,28},{6,30},{8,0},{10,2},{12,4},{14,6},{16,8},{18,... | collective-permute-start | bytes 196616 | tf_op jit(solution)/shard_map/ppermute | solution.py:50
  146.0 10.3 %collective-permute-start.29 = (bf16[32,1024]{1,0:T(8,128)(2,1)S(1)}, bf16[32,1024]{1,0:T(8,128)(2,1)S(1)}, u32[]{:S(2)}, u32[]{:S(2)}) collective-permute-start(bf16[32,1024]{1,0:T(8,128)(2,1)S(1)} %get-tuple-element.13), channel_id=1, source_target_pairs={{0,26},{2,24},{4,30},{6,28},{8,2},{10,0},{12,6},{14,4},{16,10},{18... | collective-permute-start | bytes 196616 | tf_op jit(solution)/shard_map/ppermute | solution.py:50
  164.3 22.4 %all-to-all-start.3 = ((f32[8,64,512]{2,1,0:T(8,128)}), f32[8,64,512]{2,1,0:T(8,128)S(1)}, u32[]{:S(2)}, u32[]{:S(2)}) async-start(f32[8,64,512]{2,1,0:T(8,128)} %bitcast.137), calls=%async_computation.3 | async-start | bytes 2097152 | tf_op jit(solution)/shard_map/all_to_all | solution.py:39
  186.8 19.5 %all-to-all-start.2 = ((f32[8,64,512]{2,1,0:T(8,128)}), f32[8,64,512]{2,1,0:T(8,128)S(1)}, u32[]{:S(2)}, u32[]{:S(2)}) async-start(f32[8,64,512]{2,1,0:T(8,128)} %bitcast.136), calls=%async_computation.2 | async-start | bytes 2097152 | tf_op jit(solution)/shard_map/all_to_all | solution.py:39
  194.0 12.5 %collective-permute-start.32 = (f32[64,512]{1,0:T(8,128)S(1)}, f32[64,512]{1,0:T(8,128)S(1)}, u32[]{:S(2)}, u32[]{:S(2)}) collective-permute-start(f32[64,512]{1,0:T(8,128)S(1)} %reduce_sum.49), channel_id=1, source_target_pairs={{0,1},{1,0},{2,3},{3,2},{4,5},{5,4},{6,7},{7,6},{8,9},{9,8},{10,11... | collective-permute-start | bytes 393224 | tf_op jit(solution)/shard_map/ppermute | solution.py:56
  (12 other events, 157.4 us)

commit v2 on v1

v2 whole, which is shorter than its diff:
```python
import math

import jax
import jax.numpy as jnp
from jax import lax
from jax.sharding import Mesh, PartitionSpec as P

AXES = ("x", "yh", "z", "yl", "c")
AA = ("x", "yh")
ZY = ("z", "yl")
F32 = jnp.float32
F16 = jnp.float16
BF16 = jnp.bfloat16
LANES = 128


def exchange(pieces, axes):
    return lax.all_to_all(pieces, axes, 0, 0, tiled=True)


def scatter_sum(pieces, axes):
    return jnp.sum(exchange(pieces, axes).astype(F32), axis=0)


def gather(block, axes, count):
    return exchange(jnp.broadcast_to(block[None], (count,) + block.shape), axes)


def swap(block):
    return lax.ppermute(block, "c", [(0, 1), (1, 0)])


def dot(left, right, contract):
    return lax.dot_general(left, right, (contract, ((), ())), preferred_element_type=F32)


def largest(*arrays):
    tops = [jnp.max(jnp.abs(array)).astype(F32) for array in arrays]
    return jnp.maximum(*tops)


def on_device(ligand_slab, protein_slab, protein_orbitals, ligand_orbitals, *, sizes):
    n_aa = sizes["x"] * sizes["yh"]
    n_zy = sizes["z"] * sizes["yl"]
    fit, lig, mus = ligand_slab.shape
    _, pro, nus = protein_slab.shape
    lig_total, pro_total = ligand_orbitals.shape[0], protein_orbitals.shape[0]
    core = lax.axis_index("c")
    wide = fit * lig

    x_own = ligand_slab.reshape(wide, mus)
    y = protein_slab.reshape(fit * pro, nus)
    orb = protein_orbitals.reshape(n_zy, 2, pro, mus)
    orb_own = lax.dynamic_index_in_dim(orb, core, 1, keepdims=False).reshape(n_zy * pro, mus)
    orb_send = lax.dynamic_index_in_dim(orb, 1 - core, 1, keepdims=False).reshape(n_zy * pro, mus)
    orb_other = swap(orb_send)
    x_other = swap(x_own)

    a_part = dot(orb_own, x_own, ((1,), (1,))) + dot(orb_other, x_other, ((1,), (1,)))
    bound = (2.0 * mus) * largest(x_own, x_other) * largest(orb_own, orb_other)
    code = jnp.ceil(jnp.log2(jnp.maximum(bound, 1e-30))) + 1.0
    a_sent = (a_part * jnp.exp2(15.0 - code)).astype(F16)
    a_sent = jnp.concatenate([a_sent, jnp.broadcast_to(code.astype(F16), (n_zy * pro, LANES))], axis=1)
    a_got = exchange(a_sent.reshape(n_zy, pro, wide + LANES), ZY)
    codes = a_got[:, :1, wide : wide + 1].astype(F32)
    a_own = jnp.sum(a_got[:, :, :wide].astype(F32) * jnp.exp2(codes - 15.0), axis=0)
    a_all = gather(a_own.astype(BF16), ZY, n_zy).reshape(n_zy * pro, wide)

    b_part = dot(ligand_orbitals, y, ((1,), (1,)))
    b_own = scatter_sum(b_part.reshape(n_aa, lig, fit * pro), AA)
    b_all = gather(b_own.astype(BF16), AA, n_aa).reshape(n_aa * lig, fit * pro)

    pair = jnp.sum(
        jnp.transpose(a_own.reshape(pro, fit, lig), (1, 2, 0))
        * jnp.transpose(b_own.reshape(lig, fit, pro), (1, 0, 2)),
        axis=0,
    )
    pair_exchange = -pair / math.sqrt(fit)

    scale_ligand = 1.0 / math.sqrt(fit * pro_total)
    back_b = dot(y, b_all, ((0,), (1,))) * scale_ligand
    back_b = back_b.reshape(n_zy, 2, nus // (2 * n_zy), lig_total)
    keep = lax.dynamic_index_in_dim(back_b, core, 1, keepdims=False)
    send = lax.dynamic_index_in_dim(back_b, 1 - core, 1, keepdims=False)
    ligand_back = scatter_sum((keep + swap(send)).astype(BF16), ZY)

    scale_protein = 1.0 / math.sqrt(fit * lig_total)
    half = n_zy * pro
    rows = mus // n_aa
    x_chip = jnp.stack(
        [x_own.T.reshape(n_aa, rows, wide), x_other.T.reshape(n_aa, rows, wide)], axis=1
    ).reshape(2 * mus, wide)
    back_a = (dot(x_chip, a_all, ((1,), (1,))) * scale_protein).astype(BF16)
    here, away = scatter_sum(back_a.reshape(n_aa, 2, rows, half), AA)
    there = swap(away)
    here = here.reshape(rows, n_zy, 1, pro)
    there = there.reshape(rows, n_zy, 1, pro)
    protein_back = jnp.where(
        core == 0,
        jnp.concatenate([here, there], axis=2),
        jnp.concatenate([there, here], axis=2),
    ).reshape(rows, pro_total)
    return (pair_exchange, ligand_back, protein_back)


def solution(mesh):
    sizes = {"x": mesh.shape["aa"] // 2, "yh": 2, "z": mesh.shape["ba"] // 4, "yl": 2, "c": 2}
    fine = Mesh(mesh.devices.reshape([sizes[name] for name in AXES]), AXES)
    aa, ba = AA, ("z", "yl", "c")
    placed = (P(None, aa, ba), P(None, ba, aa), P(None, ba), P(None, aa))

    def body(*args):
        return on_device(*args, sizes=sizes)

    return jax.shard_map(
        body,
        mesh=fine,
        in_specs=placed,
        out_specs=(P(aa, ba), P(aa + ba, None), P(ba + aa, None)),
        check_vma=False,
    )
```

time: 208 us -> 161 us (0.77)
  starting transfers between devices: 103 us -> 46.6 us
  other arithmetic: 6.74 us -> 12.1 us
  local copies, waits for them, and re-layouts: 9.83 us -> 13.1 us
  between operations: 1.14 us -> 3.53 us
    ppermute x29 -> x0, starting transfers between devices: 62.9 us -> none  [the longest x22 49.8 us: gather(): got = lax.ppermute(block, axes, flat_perm(sizes, shift))]
    ppermute x29 -> x0, waiting for transfers between devices: 20 us -> none  [the longest x22 15.1 us: gather(): got = lax.ppermute(block, axes, flat_perm(sizes, shift))]
    all_to_all x4 -> x6, waiting for transfers between devices: 43.1 us -> 62.4 us  [exchange(): return lax.all_to_all(pieces, axes, 0, 0, tiled=True)]
    all_to_all x4 -> x6, starting transfers between devices: 27 us -> 38 us  [exchange(): return lax.all_to_all(pieces, axes, 0, 0, tiled=True)]
    reduce_max x0 -> x4, other arithmetic: none -> 5.2 us  [largest(): tops = [jnp.max(jnp.abs(array)).astype(F32) for array in arrays]]
    ppermute x4, starting transfers between devices: 13.2 us -> 8.56 us  [swap(): return lax.ppermute(block, 'c', [(0, 1), (1, 0)])]
    reduce_sum x4, other arithmetic: 0.92 us -> 3.66 us  [the longest x3 2.1 us: scatter_sum(): return jnp.sum(exchange(pieces, axes).astype(F32), axis=0)]
    transpose x0 -> x2, local copies, waits for them, and re-layouts: none -> 2.66 us  [the longest x1 1.33 us: on_device(): x_own.T.reshape(n_aa, rows, wide)]
  transfers between devices with their start and end apart: 37 -> 10, of which waited for: 10 -> 7; matrix products, arithmetic and copies ran while one was open for 19% -> 25% of each run, Pallas kernels for 0% -> 0%
where the time goes in v2:
time: 161 us; the launch traced here: 160 us
  waiting for transfers between devices  62.7 us (39%)
  starting transfers between devices  46.6 us (29%)
  matrix products  21.9 us (14%)
  local copies, waits for them, and re-layouts  13.1 us (8%)
  other arithmetic  12.1 us (8%)
  between operations  3.53 us (2%)
    all_to_all x6, waiting for transfers between devices, exchange(): return lax.all_to_all(pieces, axes, 0, 0, tiled=True)  62.4 us
    all_to_all x6, starting transfers between devices, exchange(): return lax.all_to_all(pieces, axes, 0, 0, tiled=True)  38 us
    dot_general x5, matrix products, dot(): lax.dot_general(left, right, (contract, ((), ())), preferred_element_type...  21.9 us
    ppermute x4, starting transfers between devices, swap(): return lax.ppermute(block, 'c', [(0, 1), (1, 0)])  8.56 us
    reduce_max x4, other arithmetic, largest(): tops = [jnp.max(jnp.abs(array)).astype(F32) for array in arrays]  5.2 us
  transfers between devices with their start and end apart: 10, of which 7 were waited for; matrix products, arithmetic and copies ran while one was open for 25% of the time, Pallas kernels for 0%

profile of v2, /device:TPU:1, one launch (start us, length us, event | category | flops | bytes accessed | tf_op | source)
XLA Modules:
  0.0 159.9 jit_solution(14659761329615913664)
XLA Ops:
  0.7 3.0 %abs_reduce_fusion.3 = (bf16[]{:T(256)}, bf16[16,1,32,512]{3,2,1,0:T(8,128)(2,1)}, bf16[16,1,32,512]{3,2,1,0:T(8,128)(2,1)}) fusion(bf16[16,2,32,512]{3,2,1,0:T(8,128)(2,1)} %bitcast.68, s32[]{:T(128)S(6)} %select_n.22, s32[]{:T(128)S(6)} %select_n.23), kind=kLoop, calls=%fused_computation.17 | loop fusion | flops 524287 | bytes 2097162 | tf_op jit(solution)/shard_map/reduce_max | solution.py:38
  3.7 3.2 %collective-permute-start = (bf16[512,512]{1,0:T(8,128)(2,1)}, bf16[512,512]{1,0:T(8,128)(2,1)S(1)}, u32[]{:S(2)}, u32[]{:S(2)}) collective-permute-start(bf16[512,512]{1,0:T(8,128)(2,1)} %bitcast.3), channel_id=1, source_target_pairs={{0,1},{1,0},{2,3},{3,2},{4,5},{5,4},{6,7},{7,6},{8,9},{9,8},{10,11... | collective-permute-start | bytes 1572872 | tf_op jit(solution)/shard_map/ppermute | solution.py:30
  7.0 7.3 %fusion.5 = f32[8,16,2048]{2,1,0:T(8,128)} fusion(bf16[8,16,2048]{2,1,0:T(8,128)(2,1)S(1)} %bitcast.51, bf16[2048,2048,1]{1,0,2:T(8,128)(2,1)} %bitcast.52), kind=kOutput, calls=%fused_computation.25 | convolution fusion | flops 1073741824 | bytes 9961472 | tf_op jit(solution)/shard_map/dot_general | solution.py:34
  14.2 4.9 %all-to-all-start.1 = ((f32[8,16,2048]{2,1,0:T(8,128)}), f32[8,16,2048]{2,1,0:T(8,128)}, u32[]{:S(2)}, u32[]{:S(2)}) async-start(f32[8,16,2048]{2,1,0:T(8,128)} %fusion.5), calls=%async_computation.1 | async-start | bytes 2097152 | tf_op jit(solution)/shard_map/all_to_all | solution.py:18
  19.9 3.1 %fusion.4 = f32[512,1024]{1,0:T(8,128)} fusion(bf16[512,512]{1,0:T(8,128)(2,1)} %bitcast.66, bf16[1024,512]{1,0:T(8,128)(2,1)S(1)} %bitcast.55), kind=kOutput, calls=%fused_computation.24 | convolution fusion | flops 536870912 | bytes 3670016 | tf_op jit(solution)/shard_map/dot_general | solution.py:34
  27.1 2.3 %multiply_convert_fusion.1 = f16[512,1024]{1,0:T(8,128)(2,1)S(1)} fusion(f32[512,1024]{1,0:T(8,128)} %fusion.4, bf16[512,512]{1,0:T(8,128)(2,1)S(1)} %collective-permute-done, bf16[1024,512]{1,0:T(8,128)(2,1)S(1)} %collective-permute-done.1, f32[]{:T(128)S(6)} %exp2.13), kind=kOutput, calls=%fused_computation.6 | convolution fusion | flops 538443776 | bytes 4718596 | tf_op jit(solution)/shard_map/dot_general | solution.py:34
  29.5 1.3 concatenate.9
  30.8 4.0 %all-to-all-done.1 = f32[8,16,2048]{2,1,0:T(8,128)} async-done(((f32[8,16,2048]{2,1,0:T(8,128)}), f32[8,16,2048]{2,1,0:T(8,128)}, u32[]{:S(2)}, u32[]{:S(2)}) %all-to-all-start.1) | async-done | bytes 1048608 | tf_op jit(solution)/shard_map/all_to_all | solution.py:18
  34.8 8.5 %all-to-all-start = ((f16[16,32,1152]{2,1,0:T(8,128)(2,1)}), f16[16,32,1152]{2,1,0:T(8,128)(2,1)}, u32[]{:S(2)}, u32[]{:S(2)}) async-start(f16[16,32,1152]{2,1,0:T(8,128)(2,1)} %bitcast.58), calls=%async_computation | async-start | bytes 2359296 | tf_op jit(solution)/shard_map/all_to_all | solution.py:18
  43.3 1.3 reduce_sum.46
  44.6 25.9 %all-to-all-done = f16[16,32,1152]{2,1,0:T(8,128)(2,1)} async-done(((f16[16,32,1152]{2,1,0:T(8,128)(2,1)}), f16[16,32,1152]{2,1,0:T(8,128)(2,1)}, u32[]{:S(2)}, u32[]{:S(2)}) %all-to-all-start) | async-done | bytes 1179680 | tf_op jit(solution)/shard_map/all_to_all | solution.py:18
  70.5 0.9 broadcast_in_dim.4
  71.4 5.0 %all-to-all-start.2 = ((bf16[8,16,2048]{2,1,0:T(8,128)(2,1)}), bf16[8,16,2048]{2,1,0:T(8,128)(2,1)S(1)}, u32[]{:S(2)}, u32[]{:S(2)}) async-start(bf16[8,16,2048]{2,1,0:T(8,128)(2,1)} %broadcast_in_dim.4), calls=%async_computation.2 | async-start | bytes 1048576 | tf_op jit(solution)/shard_map/all_to_all | solution.py:18
  77.3 1.6 multiply_reduce_fusion
  78.9 6.1 %all-to-all-done.2 = bf16[8,16,2048]{2,1,0:T(8,128)(2,1)S(1)} async-done(((bf16[8,16,2048]{2,1,0:T(8,128)(2,1)}), bf16[8,16,2048]{2,1,0:T(8,128)(2,1)S(1)}, u32[]{:S(2)}, u32[]{:S(2)}) %all-to-all-start.2) | async-done | bytes 524320 | tf_op jit(solution)/shard_map/all_to_all | solution.py:18
  85.0 1.2 broadcast_in_dim.5
  86.1 8.9 %all-to-all-start.4 = ((bf16[16,32,1024]{2,1,0:T(8,128)(2,1)}), bf16[16,32,1024]{2,1,0:T(8,128)(2,1)}, u32[]{:S(2)}, u32[]{:S(2)}) async-start(bf16[16,32,1024]{2,1,0:T(8,128)(2,1)} %broadcast_in_dim.5), calls=%async_computation.4 | async-start | bytes 2097152 | tf_op jit(solution)/shard_map/all_to_all | solution.py:18
  95.0 5.6 %fusion = f32[2048,128]{0,1:T(8,128)} fusion(bf16[128,2048]{1,0:T(8,128)(2,1)S(1)} %bitcast.63, bf16[2048,2048]{1,0:T(8,128)(2,1)} %bitcast.53), kind=kOutput, calls=%fused_computation.1 | convolution fusion | flops 1074003968 | bytes 9961472 | tf_op jit(solution)/shard_map/dot_general | solution.py:34
  100.6 2.5 %copy.51 = f32[2048,128]{1,0:T(8,128)} copy(f32[2048,128]{0,1:T(8,128)} %fusion) | data formatting | bytes 2097152 | tf_op jit(solution)/shard_map/mul | solution.py:81
  103.2 1.9 %dynamic-slice_bitcast_fusion = f32[16,64,128]{2,1,0:T(8,128)} fusion(f32[16,2,64,128]{3,2,1,0:T(8,128)} %bitcast.59, s32[]{:T(128)S(6)} %select_n.23), kind=kLoop, calls=%fused_computation.15 | loop fusion | bytes 1048580 | tf_op jit(solution)/shard_map/jit(dynamic_index_in_dim)/squeeze | solution.py:84
  105.1 1.6 collective-permute-start.2
  106.7 1.3 copy.52
  108.0 1.3 copy.53
  110.1 9.4 %all-to-all-done.4 = bf16[16,32,1024]{2,1,0:T(8,128)(2,1)} async-done(((bf16[16,32,1024]{2,1,0:T(8,128)(2,1)}), bf16[16,32,1024]{2,1,0:T(8,128)(2,1)}, u32[]{:S(2)}, u32[]{:S(2)}) %all-to-all-start.4) | async-done | bytes 1048608 | tf_op jit(solution)/shard_map/all_to_all | solution.py:18
  119.5 7.2 %all-to-all-start.3 = ((bf16[16,64,128]{2,1,0:T(8,128)(2,1)}), bf16[16,64,128]{2,1,0:T(8,128)(2,1)S(1)}, u32[]{:S(2)}, u32[]{:S(2)}) async-start(bf16[16,64,128]{2,1,0:T(8,128)(2,1)} %fusion.1), calls=%async_computation.3 | async-start | bytes 524288 | tf_op jit(solution)/shard_map/all_to_all | solution.py:18
  126.7 1.4 pad_maximum_fusion
  128.4 3.5 %multiply_convert_fusion = bf16[1024,512]{1,0:T(8,128)(2,1)} fusion(bf16[1024,1024]{1,0:T(8,128)(2,1)S(1)} %bitcast.65, bf16[512,1024]{1,0:T(8,128)(2,1)} %bitcast.22), kind=kOutput, calls=%fused_computation.4 | convolution fusion | flops 1074790400 | bytes 4194304 | tf_op jit(solution)/shard_map/dot_general | solution.py:34
  131.9 4.9 %all-to-all-done.3 = bf16[16,64,128]{2,1,0:T(8,128)(2,1)S(1)} async-done(((bf16[16,64,128]{2,1,0:T(8,128)(2,1)}), bf16[16,64,128]{2,1,0:T(8,128)(2,1)S(1)}, u32[]{:S(2)}, u32[]{:S(2)}) %all-to-all-start.3) | async-done | bytes 262176 | tf_op jit(solution)/shard_map/all_to_all | solution.py:18
  136.9 3.6 %all-to-all-start.5 = ((bf16[8,2,64,512]{3,2,1,0:T(8,128)(2,1)}), bf16[8,2,64,512]{3,2,1,0:T(8,128)(2,1)S(1)}, u32[]{:S(2)}, u32[]{:S(2)}) async-start(bf16[8,2,64,512]{3,2,1,0:T(8,128)(2,1)} %bitcast.23), calls=%async_computation.5 | async-start | bytes 2097152 | tf_op jit(solution)/shard_map/all_to_all | solution.py:18
  141.8 12.1 %all-to-all-done.5 = bf16[8,2,64,512]{3,2,1,0:T(8,128)(2,1)S(1)} async-done(((bf16[8,2,64,512]{3,2,1,0:T(8,128)(2,1)}), bf16[8,2,64,512]{3,2,1,0:T(8,128)(2,1)S(1)}, u32[]{:S(2)}, u32[]{:S(2)}) %all-to-all-start.5) | async-done | bytes 1048608 | tf_op jit(solution)/shard_map/all_to_all | solution.py:18
  154.0 3.7 %collective-permute-start.3 = (f32[64,512]{1,0:T(8,128)S(1)}, f32[64,512]{1,0:T(8,128)S(1)}, u32[]{:S(2)}, u32[]{:S(2)}) collective-permute-start(f32[64,512]{1,0:T(8,128)S(1)} %get-tuple-element.22), channel_id=1, source_target_pairs={{0,1},{1,0},{2,3},{3,2},{4,5},{5,4},{6,7},{7,6},{8,9},{9,8},{10,11... | collective-permute-start | bytes 393224 | tf_op jit(solution)/shard_map/ppermute | solution.py:30
  159.0 0.9 copy.58
  (34 shorter events, 6.8 us)
Async XLA Ops:
  0.6 6.3 %copy-start = (bf16[128,2048]{1,0:T(8,128)(2,1)S(1)}, bf16[128,2048]{1,0:T(8,128)(2,1)}, u32[]{:S(2)}) copy-start(bf16[128,2048]{1,0:T(8,128)(2,1)} %param.7) | copy-start | bytes 1572868
  0.6 6.3 %copy-start.1 = (bf16[64,16,512]{2,1,0:T(8,128)(2,1)S(1)}, bf16[64,16,512]{2,1,0:T(8,128)(2,1)}, u32[]{:S(2)}) copy-start(bf16[64,16,512]{2,1,0:T(8,128)(2,1)} %param.4) | copy-start | bytes 3145732
  3.7 19.3 %collective-permute-start = (bf16[512,512]{1,0:T(8,128)(2,1)}, bf16[512,512]{1,0:T(8,128)(2,1)S(1)}, u32[]{:S(2)}, u32[]{:S(2)}) collective-permute-start(bf16[512,512]{1,0:T(8,128)(2,1)} %bitcast.3), channel_id=1, source_target_pairs={{0,1},{1,0},{2,3},{3,2},{4,5},{5,4},{6,7},{7,6},{8,9},{9,8},{10,11... | collective-permute-start | bytes 1572872 | tf_op jit(solution)/shard_map/ppermute | solution.py:30
  6.9 18.1 %collective-permute-start.1 = (bf16[1024,512]{1,0:T(8,128)(2,1)S(1)}, bf16[1024,512]{1,0:T(8,128)(2,1)S(1)}, u32[]{:S(2)}, u32[]{:S(2)}) collective-permute-start(bf16[1024,512]{1,0:T(8,128)(2,1)S(1)} %bitcast.54), channel_id=1, source_target_pairs={{0,1},{1,0},{2,3},{3,2},{4,5},{5,4},{6,7},{7,6},{8,9},{9,8},{10,11... | collective-permute-start | bytes 3145736 | tf_op jit(solution)/shard_map/ppermute | solution.py:30
  14.2 20.6 %all-to-all-start.1 = ((f32[8,16,2048]{2,1,0:T(8,128)}), f32[8,16,2048]{2,1,0:T(8,128)}, u32[]{:S(2)}, u32[]{:S(2)}) async-start(f32[8,16,2048]{2,1,0:T(8,128)} %fusion.5), calls=%async_computation.1 | async-start | bytes 2097152 | tf_op jit(solution)/shard_map/all_to_all | solution.py:18
  34.8 35.7 %all-to-all-start = ((f16[16,32,1152]{2,1,0:T(8,128)(2,1)}), f16[16,32,1152]{2,1,0:T(8,128)(2,1)}, u32[]{:S(2)}, u32[]{:S(2)}) async-start(f16[16,32,1152]{2,1,0:T(8,128)(2,1)} %bitcast.58), calls=%async_computation | async-start | bytes 2359296 | tf_op jit(solution)/shard_map/all_to_all | solution.py:18
  71.4 13.6 %all-to-all-start.2 = ((bf16[8,16,2048]{2,1,0:T(8,128)(2,1)}), bf16[8,16,2048]{2,1,0:T(8,128)(2,1)S(1)}, u32[]{:S(2)}, u32[]{:S(2)}) async-start(bf16[8,16,2048]{2,1,0:T(8,128)(2,1)} %broadcast_in_dim.4), calls=%async_computation.2 | async-start | bytes 1048576 | tf_op jit(solution)/shard_map/all_to_all | solution.py:18
  86.1 33.4 %all-to-all-start.4 = ((bf16[16,32,1024]{2,1,0:T(8,128)(2,1)}), bf16[16,32,1024]{2,1,0:T(8,128)(2,1)}, u32[]{:S(2)}, u32[]{:S(2)}) async-start(bf16[16,32,1024]{2,1,0:T(8,128)(2,1)} %broadcast_in_dim.5), calls=%async_computation.4 | async-start | bytes 2097152 | tf_op jit(solution)/shard_map/all_to_all | solution.py:18
  105.1 4.2 %collective-permute-start.2 = (f32[16,64,128]{2,1,0:T(8,128)}, f32[16,64,128]{2,1,0:T(8,128)S(1)}, u32[]{:S(2)}, u32[]{:S(2)}) collective-permute-start(f32[16,64,128]{2,1,0:T(8,128)} %dynamic-slice_bitcast_fusion), channel_id=1, source_target_pairs={{0,1},{1,0},{2,3},{3,2},{4,5},{5,4},{6,7},{7,6},{8,9},{9,8},{10,11... | collective-permute-start | bytes 1572872 | tf_op jit(solution)/shard_map/ppermute | solution.py:30
  108.0 1.3 copy-start.2
  109.3 17.4 %copy-start.3 = (bf16[512,1024]{1,0:T(8,128)(2,1)S(1)}, bf16[512,1024]{1,0:T(8,128)(2,1)}, u32[]{:S(2)}) copy-start(bf16[512,1024]{1,0:T(8,128)(2,1)} %copy.52) | copy-start | bytes 3145732
  119.5 17.3 %all-to-all-start.3 = ((bf16[16,64,128]{2,1,0:T(8,128)(2,1)}), bf16[16,64,128]{2,1,0:T(8,128)(2,1)S(1)}, u32[]{:S(2)}, u32[]{:S(2)}) async-start(bf16[16,64,128]{2,1,0:T(8,128)(2,1)} %fusion.1), calls=%async_computation.3 | async-start | bytes 524288 | tf_op jit(solution)/shard_map/all_to_all | solution.py:18
  136.9 17.0 %all-to-all-start.5 = ((bf16[8,2,64,512]{3,2,1,0:T(8,128)(2,1)}), bf16[8,2,64,512]{3,2,1,0:T(8,128)(2,1)S(1)}, u32[]{:S(2)}, u32[]{:S(2)}) async-start(bf16[8,2,64,512]{3,2,1,0:T(8,128)(2,1)} %bitcast.23), calls=%async_computation.5 | async-start | bytes 2097152 | tf_op jit(solution)/shard_map/all_to_all | solution.py:18
  154.0 4.7 %collective-permute-start.3 = (f32[64,512]{1,0:T(8,128)S(1)}, f32[64,512]{1,0:T(8,128)S(1)}, u32[]{:S(2)}, u32[]{:S(2)}) collective-permute-start(f32[64,512]{1,0:T(8,128)S(1)} %get-tuple-element.22), channel_id=1, source_target_pairs={{0,1},{1,0},{2,3},{3,2},{4,5},{5,4},{6,7},{7,6},{8,9},{9,8},{10,11... | collective-permute-start | bytes 393224 | tf_op jit(solution)/shard_map/ppermute | solution.py:30

commit v3 on v2

--- a/solution.py
+++ b/solution.py
@@ -7,11 +7,8 @@
 
 AXES = ("x", "yh", "z", "yl", "c")
 AA = ("x", "yh")
-ZY = ("z", "yl")
 F32 = jnp.float32
-F16 = jnp.float16
 BF16 = jnp.bfloat16
-LANES = 128
 
 
 def exchange(pieces, axes):
@@ -26,22 +23,80 @@
     return exchange(jnp.broadcast_to(block[None], (count,) + block.shape), axes)
 
 
-def swap(block):
-    return lax.ppermute(block, "c", [(0, 1), (1, 0)])
-
-
 def dot(left, right, contract):
     return lax.dot_general(left, right, (contract, ((), ())), preferred_element_type=F32)
 
 
-def largest(*arrays):
-    tops = [jnp.max(jnp.abs(array)).astype(F32) for array in arrays]
-    return jnp.maximum(*tops)
+def pick(pieces, index, count):
+    return lax.dynamic_index_in_dim(pieces, lax.rem(index + count, count), 0, keepdims=False)
+
+
+def ring_sum(pieces, axis, count):
+    me = lax.axis_index(axis)
+    up = [(i, (i + 1) % count) for i in range(count)]
+    down = [(i, (i - 1) % count) for i in range(count)]
+    far = count // 2
+    mid = pieces.shape[1] // 2
+    away = pick(pieces, me + far, count)
+    right = lax.ppermute(away[:mid], axis, up)
+    left = lax.ppermute(away[mid:], axis, down)
+    for hop in range(far - 1, 0, -1):
+        to_right = pick(pieces, me + hop, count)
+        to_left = pick(pieces, me - hop, count)
+        if hop == far - 1:
+            to_right = jnp.concatenate([to_right[:mid] + right, to_right[mid:]], axis=0)
+            to_left = jnp.concatenate([to_left[:mid], to_left[mid:] + left], axis=0)
+        else:
+            to_right = to_right + right
+            to_left = to_left + left
+        right = lax.ppermute(to_right, axis, up)
+        left = lax.ppermute(to_left, axis, down)
+    return pick(pieces, me, count) + (right + left)
+
+
+def ring_gather(block, axis, count):
+    me = lax.axis_index(axis)
+    up = [(i, (i + 1) % count) for i in range(count)]
+    down = [(i, (i - 1) % count) for i in range(count)]
+    far = count // 2
+    mid = block.shape[0] // 2
+    out = jnp.zeros((count,) + block.shape, block.dtype)
+
+    def put(out, part, index):
+        return lax.dynamic_update_index_in_dim(out, part, lax.rem(index + count, count), 0)
+
+    out = put(out, block, me)
+    right = left = block
+    for hop in range(1, far):
+        right = lax.ppermute(right, axis, up)
+        left = lax.ppermute(left, axis, down)
+        out = put(out, right, me - hop)
+        out = put(out, left, me + hop)
+    right = lax.ppermute(right[:mid], axis, up)
+    left = lax.ppermute(left[mid:], axis, down)
+    return put(out, jnp.concatenate([right, left], axis=0), me + far)
+
+
+def other(block, axis):
+    return lax.ppermute(block, axis, [(0, 1), (1, 0)])
+
+
+def pair_sum(pieces, axis):
+    me = lax.axis_index(axis)
+    keep = lax.dynamic_index_in_dim(pieces, me, 1, keepdims=False)
+    send = lax.dynamic_index_in_dim(pieces, 1 - me, 1, keepdims=False)
+    return keep + other(send, axis)
+
+
+def pair_gather(block, axis):
+    got = other(block, axis)
+    return jnp.where(lax.axis_index(axis) == 0, jnp.stack([block, got]), jnp.stack([got, block]))
 
 
 def on_device(ligand_slab, protein_slab, protein_orbitals, ligand_orbitals, *, sizes):
     n_aa = sizes["x"] * sizes["yh"]
-    n_zy = sizes["z"] * sizes["yl"]
+    n_z = sizes["z"]
+    n_zy = n_z * sizes["yl"]
     fit, lig, mus = ligand_slab.shape
     _, pro, nus = protein_slab.shape
     lig_total, pro_total = ligand_orbitals.shape[0], protein_orbitals.shape[0]
@@ -53,18 +108,14 @@
     orb = protein_orbitals.reshape(n_zy, 2, pro, mus)
     orb_own = lax.dynamic_index_in_dim(orb, core, 1, keepdims=False).reshape(n_zy * pro, mus)
     orb_send = lax.dynamic_index_in_dim(orb, 1 - core, 1, keepdims=False).reshape(n_zy * pro, mus)
-    orb_other = swap(orb_send)
-    x_other = swap(x_own)
+    orb_other = other(orb_send, "c")
+    x_other = other(x_own, "c")
 
     a_part = dot(orb_own, x_own, ((1,), (1,))) + dot(orb_other, x_other, ((1,), (1,)))
-    bound = (2.0 * mus) * largest(x_own, x_other) * largest(orb_own, orb_other)
-    code = jnp.ceil(jnp.log2(jnp.maximum(bound, 1e-30))) + 1.0
-    a_sent = (a_part * jnp.exp2(15.0 - code)).astype(F16)
-    a_sent = jnp.concatenate([a_sent, jnp.broadcast_to(code.astype(F16), (n_zy * pro, LANES))], axis=1)
-    a_got = exchange(a_sent.reshape(n_zy, pro, wide + LANES), ZY)
-    codes = a_got[:, :1, wide : wide + 1].astype(F32)
-    a_own = jnp.sum(a_got[:, :, :wide].astype(F32) * jnp.exp2(codes - 15.0), axis=0)
-    a_all = gather(a_own.astype(BF16), ZY, n_zy).reshape(n_zy * pro, wide)
+    a_z = ring_sum(a_part.reshape(n_z, 2 * pro, wide), "z", n_z)
+    a_own = pair_sum(a_z.reshape(1, 2, pro, wide), "yl").reshape(pro, wide)
+    a_pair = pair_gather(a_own.astype(BF16), "yl").reshape(2 * pro, wide)
+    a_all = ring_gather(a_pair, "z", n_z).reshape(n_zy * pro, wide)
 
     b_part = dot(ligand_orbitals, y, ((1,), (1,)))
     b_own = scatter_sum(b_part.reshape(n_aa, lig, fit * pro), AA)
@@ -79,10 +130,10 @@
 
     scale_ligand = 1.0 / math.sqrt(fit * pro_total)
     back_b = dot(y, b_all, ((0,), (1,))) * scale_ligand
-    back_b = back_b.reshape(n_zy, 2, nus // (2 * n_zy), lig_total)
-    keep = lax.dynamic_index_in_dim(back_b, core, 1, keepdims=False)
-    send = lax.dynamic_index_in_dim(back_b, 1 - core, 1, keepdims=False)
-    ligand_back = scatter_sum((keep + swap(send)).astype(BF16), ZY)
+    rows_b = nus // (2 * n_zy)
+    back_b = pair_sum(back_b.reshape(n_zy, 2, rows_b, lig_total), "c")
+    back_b = ring_sum(back_b.reshape(n_z, 2 * rows_b, lig_total), "z", n_z)
+    ligand_back = pair_sum(back_b.reshape(1, 2, rows_b, lig_total), "yl").reshape(rows_b, lig_total)
 
     scale_protein = 1.0 / math.sqrt(fit * lig_total)
     half = n_zy * pro
@@ -92,7 +143,7 @@
     ).reshape(2 * mus, wide)
     back_a = (dot(x_chip, a_all, ((1,), (1,))) * scale_protein).astype(BF16)
     here, away = scatter_sum(back_a.reshape(n_aa, 2, rows, half), AA)
-    there = swap(away)
+    there = other(away, "c")
     here = here.reshape(rows, n_zy, 1, pro)
     there = there.reshape(rows, n_zy, 1, pro)
     protein_back = jnp.where(

time: 161 us -> 156 us (0.969)
  starting transfers between devices: 46.6 us -> 68.2 us
  waiting for transfers between devices: 62.7 us -> 45.3 us
  matrix products: 21.9 us -> 17.9 us
  between operations: 3.53 us -> 1.05 us
  other arithmetic: 12.1 us -> 9.86 us
    all_to_all x6 -> x3, waiting for transfers between devices: 62.4 us -> 11.1 us  [exchange(): return lax.all_to_all(pieces, axes, 0, 0, tiled=True)]
    ppermute x4 -> x31, starting transfers between devices: 8.56 us -> 55.3 us  [the longest x7 18.4 us: other(): return lax.ppermute(block, axis, [(0, 1), (1, 0)])]
    ppermute x4 -> x31, waiting for transfers between devices: 0.27 us -> 34.2 us  [the longest x6 13.7 us: ring_sum(): right = lax.ppermute(to_right, axis, up)]
    all_to_all x6 -> x3, starting transfers between devices: 38 us -> 12.9 us  [exchange(): return lax.all_to_all(pieces, axes, 0, 0, tiled=True)]
    reduce_max x4 -> x0, other arithmetic: 5.2 us -> none  [largest(): tops = [jnp.max(jnp.abs(array)).astype(F32) for array in arrays]]
    add x0 -> x11, other arithmetic: none -> 5.1 us  [the longest x4 2.72 us: ring_sum(): to_left = to_left + left]
    dot_general x5, matrix products: 21.9 us -> 17.9 us  [dot(): lax.dot_general(left, right, (contract, ((), ())), preferred_element_type...]
  transfers between devices with their start and end apart: 10 -> 34, of which waited for: 7 -> 20; matrix products, arithmetic and copies ran while one was open for 25% -> 25% of each run, Pallas kernels for 0% -> 0%
where the time goes in v3:
time: 156 us; the launch traced here: 155 us
  starting transfers between devices  68.2 us (44%)
  waiting for transfers between devices  45.3 us (29%)
  matrix products  17.9 us (11%)
  local copies, waits for them, and re-layouts  13.1 us (8%)
  other arithmetic  9.86 us (6%)
    ppermute x7, starting transfers between devices, other(): return lax.ppermute(block, axis, [(0, 1), (1, 0)])  18.4 us
    ppermute x6, starting transfers between devices, ring_sum(): left = lax.ppermute(to_left, axis, down)  18 us
    dot_general x5, matrix products, dot(): lax.dot_general(left, right, (contract, ((), ())), preferred_element_type...  17.9 us
    ppermute x6, waiting for transfers between devices, ring_sum(): right = lax.ppermute(to_right, axis, up)  13.7 us
    all_to_all x3, starting transfers between devices, exchange(): return lax.all_to_all(pieces, axes, 0, 0, tiled=True)  12.9 us
    all_to_all x3, waiting for transfers between devices, exchange(): return lax.all_to_all(pieces, axes, 0, 0, tiled=True)  11.1 us
    ppermute x2, starting transfers between devices, ring_sum(): left = lax.ppermute(away[mid:], axis, down)  6.86 us
    ppermute x3, starting transfers between devices, ring_gather(): left = lax.ppermute(left, axis, down)  6.73 us
  transfers between devices with their start and end apart: 34, of which 20 were waited for; matrix products, arithmetic and copies ran while one was open for 25% of the time, Pallas kernels for 0%

profile of v3, /device:TPU:1, one launch (start us, length us, event | category | flops | bytes accessed | tf_op | source)
XLA Modules:
  0.0 155.4 jit_solution(2951901450466101730)
XLA Ops:
  0.6 3.3 %collective-permute-start.1 = (bf16[1024,512]{1,0:T(8,128)(2,1)}, bf16[1024,512]{1,0:T(8,128)(2,1)}, u32[]{:S(2)}, u32[]{:S(2)}) collective-permute-start(bf16[1024,512]{1,0:T(8,128)(2,1)} %bitcast.146), channel_id=1, source_target_pairs={{0,1},{1,0},{2,3},{3,2},{4,5},{5,4},{6,7},{7,6},{8,9},{9,8},{10,11... | collective-permute-start | bytes 3145736 | tf_op jit(solution)/shard_map/ppermute | solution.py:81
  5.4 7.2 %fusion.11 = f32[8,16,2048]{2,1,0:T(8,128)} fusion(bf16[8,16,2048]{2,1,0:T(8,128)(2,1)S(1)} %bitcast.137, bf16[2048,2048,1]{1,0,2:T(8,128)(2,1)} %bitcast.138), kind=kOutput, calls=%fused_computation.63 | convolution fusion | flops 1073741824 | bytes 9961472 | tf_op jit(solution)/shard_map/dot_general | solution.py:27
  12.7 5.0 %all-to-all-start = ((f32[8,16,2048]{2,1,0:T(8,128)}), f32[8,16,2048]{2,1,0:T(8,128)}, u32[]{:S(2)}, u32[]{:S(2)}) async-start(f32[8,16,2048]{2,1,0:T(8,128)} %fusion.11), calls=%async_computation | async-start | bytes 2097152 | tf_op jit(solution)/shard_map/all_to_all | solution.py:15
  18.5 2.0 %convolution_add_fusion = f32[512,1024]{1,0:T(8,128)S(1)} fusion(f32[512,1024]{1,0:T(8,128)S(1)} %fusion.10, bf16[512,512]{1,0:T(8,128)(2,1)S(1)} %collective-permute-done, bf16[1024,512]{1,0:T(8,128)(2,1)} %collective-permute-done.1), kind=kOutput, calls=%fused_computation.5 | convolution fusion | flops 537395200 | bytes 5767168 | tf_op jit(solution)/shard_map/dot_general | solution.py:27
  21.2 5.6 %collective-permute-start.6 = (f32[32,1024]{1,0:T(8,128)}, f32[32,1024]{1,0:T(8,128)}, u32[]{:S(2)}, u32[]{:S(2)}) collective-permute-start(f32[32,1024]{1,0:T(8,128)} %get-tuple-element.18), channel_id=1, source_target_pairs={{0,28},{4,0},{8,4},{12,8},{16,12},{20,16},{24,20},{28,24},{1,29},{... | collective-permute-start | bytes 393224 | tf_op jit(solution)/shard_map/ppermute | solution.py:42
  26.8 6.7 %all-to-all-done = f32[8,16,2048]{2,1,0:T(8,128)} async-done(((f32[8,16,2048]{2,1,0:T(8,128)}), f32[8,16,2048]{2,1,0:T(8,128)}, u32[]{:S(2)}, u32[]{:S(2)}) %all-to-all-start) | async-done | bytes 1048608 | tf_op jit(solution)/shard_map/all_to_all | solution.py:15
  35.6 4.1 %all-to-all-start.1 = ((bf16[8,16,2048]{2,1,0:T(8,128)(2,1)}), bf16[8,16,2048]{2,1,0:T(8,128)(2,1)S(1)}, u32[]{:S(2)}, u32[]{:S(2)}) async-start(bf16[8,16,2048]{2,1,0:T(8,128)(2,1)} %broadcast_in_dim.32), calls=%async_computation.1 | async-start | bytes 1048576 | tf_op jit(solution)/shard_map/all_to_all | solution.py:15
  41.4 5.6 %collective-permute-start.7 = (f32[64,1024]{1,0:T(8,128)}, f32[64,1024]{1,0:T(8,128)}, u32[]{:S(2)}, u32[]{:S(2)}) collective-permute-start(f32[64,1024]{1,0:T(8,128)} %pad_maximum_fusion.2), channel_id=1, source_target_pairs={{0,28},{4,0},{8,4},{12,8},{16,12},{20,16},{24,20},{28,24},{1,29},{... | collective-permute-start | bytes 786440 | tf_op jit(solution)/shard_map/ppermute | solution.py:53
  47.8 2.0 %all-to-all-done.1 = bf16[8,16,2048]{2,1,0:T(8,128)(2,1)S(1)} async-done(((bf16[8,16,2048]{2,1,0:T(8,128)(2,1)}), bf16[8,16,2048]{2,1,0:T(8,128)(2,1)S(1)}, u32[]{:S(2)}, u32[]{:S(2)}) %all-to-all-start.1) | async-done | bytes 524320 | tf_op jit(solution)/shard_map/all_to_all | solution.py:15
  49.8 5.6 %fusion = f32[2048,128]{0,1:T(8,128)} fusion(bf16[128,2048]{1,0:T(8,128)(2,1)S(1)} %bitcast.153, bf16[2048,2048]{1,0:T(8,128)(2,1)} %bitcast.139), kind=kOutput, calls=%fused_computation.1 | convolution fusion | flops 1074003968 | bytes 9961472 | tf_op jit(solution)/shard_map/dot_general | solution.py:27
  55.4 2.5 %copy.25 = f32[2048,128]{1,0:T(8,128)} copy(f32[2048,128]{0,1:T(8,128)} %fusion) | data formatting | bytes 2097152 | tf_op jit(solution)/shard_map/mul | solution.py:132
  62.5 5.6 %collective-permute-start.8 = (f32[64,1024]{1,0:T(8,128)}, f32[64,1024]{1,0:T(8,128)}, u32[]{:S(2)}, u32[]{:S(2)}) collective-permute-start(f32[64,1024]{1,0:T(8,128)} %bitcast_add_fusion.1), channel_id=1, source_target_pairs={{0,28},{4,0},{8,4},{12,8},{16,12},{20,16},{24,20},{28,24},{1,29},{... | collective-permute-start | bytes 786440 | tf_op jit(solution)/shard_map/ppermute | solution.py:53
  68.1 2.3 %copy.26 = bf16[512,1024]{1,0:T(8,128)(2,1)} copy(bf16[512,1024]{0,1:T(8,128)(2,1)} %bitcast.147) | data formatting | bytes 2097152 | tf_op jit(solution)/shard_map/transpose | solution.py:142
  70.4 2.3 %copy.27 = bf16[512,1024]{1,0:T(8,128)(2,1)} copy(bf16[512,1024]{0,1:T(8,128)(2,1)} %bitcast.48) | data formatting | bytes 2097152 | tf_op jit(solution)/shard_map/transpose | solution.py:142
  75.3 3.7 %collective-permute-start.9 = (f32[64,1024]{1,0:T(8,128)S(1)}, f32[64,1024]{1,0:T(8,128)S(1)}, u32[]{:S(2)}, u32[]{:S(2)}) collective-permute-start(f32[64,1024]{1,0:T(8,128)S(1)} %get-tuple-element.14), channel_id=1, source_target_pairs={{0,28},{4,0},{8,4},{12,8},{16,12},{20,16},{24,20},{28,24},{1,29},{... | collective-permute-start | bytes 786440 | tf_op jit(solution)/shard_map/ppermute | solution.py:53
  81.8 2.8 %collective-permute-done.4 = f32[64,1024]{1,0:T(8,128)S(1)} collective-permute-done((f32[64,1024]{1,0:T(8,128)S(1)}, f32[64,1024]{1,0:T(8,128)S(1)}, u32[]{:S(2)}, u32[]{:S(2)}) %collective-permute-start.4) | collective-permute-done | bytes 262176 | tf_op jit(solution)/shard_map/ppermute | solution.py:52
  85.6 6.7 %collective-permute-done.5 = f32[64,1024]{1,0:T(8,128)S(1)} collective-permute-done((f32[64,1024]{1,0:T(8,128)S(1)}, f32[64,1024]{1,0:T(8,128)S(1)}, u32[]{:S(2)}, u32[]{:S(2)}) %collective-permute-start.5) | collective-permute-done | bytes 262176 | tf_op jit(solution)/shard_map/ppermute | solution.py:52
  94.3 1.9 %collective-permute-done.10 = f32[1,32,1024]{2,1,0:T(8,128)S(1)} collective-permute-done((f32[1,32,1024]{2,1,0:T(8,128)S(1)}, f32[1,32,1024]{2,1,0:T(8,128)S(1)}, u32[]{:S(2)}, u32[]{:S(2)}) %collective-permute-start.10) | collective-permute-done | bytes 131104 | tf_op jit(solution)/shard_map/ppermute | solution.py:81
  97.3 2.5 %collective-permute-done.21 = bf16[32,1024]{1,0:T(8,128)(2,1)S(1)} collective-permute-done((bf16[32,1024]{1,0:T(8,128)(2,1)S(1)}, bf16[32,1024]{1,0:T(8,128)(2,1)S(1)}, u32[]{:S(2)}, u32[]{:S(2)}) %collective-permute-start.21) | collective-permute-done | bytes 65568 | tf_op jit(solution)/shard_map/ppermute | solution.py:81
  100.4 2.7 %collective-permute-start.19 = (f32[128,128]{1,0:T(8,128)S(1)}, f32[128,128]{1,0:T(8,128)S(1)}, u32[]{:S(2)}, u32[]{:S(2)}) collective-permute-start(f32[128,128]{1,0:T(8,128)S(1)} %get-tuple-element.24), channel_id=1, source_target_pairs={{0,28},{4,0},{8,4},{12,8},{16,12},{20,16},{24,20},{28,24},{1,29},{... | collective-permute-start | bytes 196616 | tf_op jit(solution)/shard_map/ppermute | solution.py:53
  104.9 2.0 %collective-permute-done.23 = bf16[64,1024]{1,0:T(8,128)(2,1)S(1)} collective-permute-done((bf16[64,1024]{1,0:T(8,128)(2,1)S(1)}, bf16[64,1024]{1,0:T(8,128)(2,1)S(1)}, u32[]{:S(2)}, u32[]{:S(2)}) %collective-permute-start.23) | collective-permute-done | bytes 131104 | tf_op jit(solution)/shard_map/ppermute | solution.py:72
  106.9 2.3 %collective-permute-start.25 = (bf16[64,1024]{1,0:T(8,128)(2,1)S(1)}, bf16[64,1024]{1,0:T(8,128)(2,1)S(1)}, u32[]{:S(2)}, u32[]{:S(2)}) collective-permute-start(bf16[64,1024]{1,0:T(8,128)(2,1)S(1)} %collective-permute-done.23), channel_id=1, source_target_pairs={{0,28},{4,0},{8,4},{12,8},{16,12},{20,16},{24,20},{28,24},{1,29},{... | collective-permute-start | bytes 393224 | tf_op jit(solution)/shard_map/ppermute | solution.py:72
  109.1 2.4 %collective-permute-done.24 = bf16[64,1024]{1,0:T(8,128)(2,1)S(1)} collective-permute-done((bf16[64,1024]{1,0:T(8,128)(2,1)S(1)}, bf16[64,1024]{1,0:T(8,128)(2,1)S(1)}, u32[]{:S(2)}, u32[]{:S(2)}) %collective-permute-start.24) | collective-permute-done | bytes 131104 | tf_op jit(solution)/shard_map/ppermute | solution.py:71
  112.0 3.4 %collective-permute-start.27 = (bf16[64,1024]{1,0:T(8,128)(2,1)S(1)}, bf16[64,1024]{1,0:T(8,128)(2,1)S(1)}, u32[]{:S(2)}, u32[]{:S(2)}) collective-permute-start(bf16[64,1024]{1,0:T(8,128)(2,1)S(1)} %collective-permute-done.25), channel_id=1, source_target_pairs={{0,28},{4,0},{8,4},{12,8},{16,12},{20,16},{24,20},{28,24},{1,29},{... | collective-permute-start | bytes 393224 | tf_op jit(solution)/shard_map/ppermute | solution.py:72
  115.5 1.9 %collective-permute-done.27 = bf16[64,1024]{1,0:T(8,128)(2,1)S(1)} collective-permute-done((bf16[64,1024]{1,0:T(8,128)(2,1)S(1)}, bf16[64,1024]{1,0:T(8,128)(2,1)S(1)}, u32[]{:S(2)}, u32[]{:S(2)}) %collective-permute-start.27) | collective-permute-done | bytes 131104 | tf_op jit(solution)/shard_map/ppermute | solution.py:72
  117.4 3.1 %collective-permute-start.29 = (bf16[32,1024]{1,0:T(8,128)(2,1)S(1)}, bf16[32,1024]{1,0:T(8,128)(2,1)S(1)}, u32[]{:S(2)}, u32[]{:S(2)}) collective-permute-start(bf16[32,1024]{1,0:T(8,128)(2,1)S(1)} %slice.105), channel_id=1, source_target_pairs={{0,28},{4,0},{8,4},{12,8},{16,12},{20,16},{24,20},{28,24},{1,29},{... | collective-permute-start | bytes 196616 | tf_op jit(solution)/shard_map/ppermute | solution.py:76
  121.8 3.1 %collective-permute-done.28 = bf16[32,1024]{1,0:T(8,128)(2,1)S(1)} collective-permute-done((bf16[32,1024]{1,0:T(8,128)(2,1)S(1)}, bf16[32,1024]{1,0:T(8,128)(2,1)S(1)}, u32[]{:S(2)}, u32[]{:S(2)}) %collective-permute-start.28) | collective-permute-done | bytes 65568 | tf_op jit(solution)/shard_map/ppermute | solution.py:75
  124.9 2.3 %multiply_convert_fusion = bf16[1024,512]{1,0:T(8,128)(2,1)} fusion(bf16[1024,1024]{1,0:T(8,128)(2,1)S(1)} %bitcast.161, bf16[512,1024]{1,0:T(8,128)(2,1)S(1)} %bitcast.164), kind=kOutput, calls=%fused_computation.4 | convolution fusion | flops 1074790400 | bytes 4194304 | tf_op jit(solution)/shard_map/dot_general | solution.py:27
  127.2 3.8 %all-to-all-start.2 = ((bf16[8,2,64,512]{3,2,1,0:T(8,128)(2,1)}), bf16[8,2,64,512]{3,2,1,0:T(8,128)(2,1)S(1)}, u32[]{:S(2)}, u32[]{:S(2)}) async-start(bf16[8,2,64,512]{3,2,1,0:T(8,128)(2,1)} %bitcast.63), calls=%async_computation.2 | async-start | bytes 2097152 | tf_op jit(solution)/shard_map/all_to_all | solution.py:15
  131.1 4.3 %collective-permute-done.15 = f32[128,128]{1,0:T(8,128)S(1)} collective-permute-done((f32[128,128]{1,0:T(8,128)S(1)}, f32[128,128]{1,0:T(8,128)S(1)}, u32[]{:S(2)}, u32[]{:S(2)}) %collective-permute-start.15) | collective-permute-done | bytes 65568 | tf_op jit(solution)/shard_map/ppermute | solution.py:52
  139.5 2.5 %all-to-all-done.2 = bf16[8,2,64,512]{3,2,1,0:T(8,128)(2,1)S(1)} async-done(((bf16[8,2,64,512]{3,2,1,0:T(8,128)(2,1)}), bf16[8,2,64,512]{3,2,1,0:T(8,128)(2,1)S(1)}, u32[]{:S(2)}, u32[]{:S(2)}) %all-to-all-start.2) | async-done | bytes 1048608 | tf_op jit(solution)/shard_map/all_to_all | solution.py:15
  142.1 11.2 %collective-permute-start.30 = (f32[64,512]{1,0:T(8,128)S(1)}, f32[64,512]{1,0:T(8,128)S(1)}, u32[]{:S(2)}, u32[]{:S(2)}) collective-permute-start(f32[64,512]{1,0:T(8,128)S(1)} %get-tuple-element.33), channel_id=1, source_target_pairs={{0,1},{1,0},{2,3},{3,2},{4,5},{5,4},{6,7},{7,6},{8,9},{9,8},{10,11... | collective-permute-start | bytes 393224 | tf_op jit(solution)/shard_map/ppermute | solution.py:81
  (103 shorter events, 32.2 us)
Async XLA Ops:
  0.6 17.8 %collective-permute-start.1 = (bf16[1024,512]{1,0:T(8,128)(2,1)}, bf16[1024,512]{1,0:T(8,128)(2,1)}, u32[]{:S(2)}, u32[]{:S(2)}) collective-permute-start(bf16[1024,512]{1,0:T(8,128)(2,1)} %bitcast.146), channel_id=1, source_target_pairs={{0,1},{1,0},{2,3},{3,2},{4,5},{5,4},{6,7},{7,6},{8,9},{9,8},{10,11... | collective-permute-start | bytes 3145736 | tf_op jit(solution)/shard_map/ppermute | solution.py:81
  5.3 13.2 %collective-permute-start = (bf16[512,512]{1,0:T(8,128)(2,1)S(1)}, bf16[512,512]{1,0:T(8,128)(2,1)S(1)}, u32[]{:S(2)}, u32[]{:S(2)}) collective-permute-start(bf16[512,512]{1,0:T(8,128)(2,1)S(1)} %bitcast.173), channel_id=1, source_target_pairs={{0,1},{1,0},{2,3},{3,2},{4,5},{5,4},{6,7},{7,6},{8,9},{9,8},{10,11... | collective-permute-start | bytes 1572872 | tf_op jit(solution)/shard_map/ppermute | solution.py:81
  12.7 20.8 %all-to-all-start = ((f32[8,16,2048]{2,1,0:T(8,128)}), f32[8,16,2048]{2,1,0:T(8,128)}, u32[]{:S(2)}, u32[]{:S(2)}) async-start(f32[8,16,2048]{2,1,0:T(8,128)} %fusion.11), calls=%async_computation | async-start | bytes 2097152 | tf_op jit(solution)/shard_map/all_to_all | solution.py:15
  21.2 18.5 %collective-permute-start.6 = (f32[32,1024]{1,0:T(8,128)}, f32[32,1024]{1,0:T(8,128)}, u32[]{:S(2)}, u32[]{:S(2)}) collective-permute-start(f32[32,1024]{1,0:T(8,128)} %get-tuple-element.18), channel_id=1, source_target_pairs={{0,28},{4,0},{8,4},{12,8},{16,12},{20,16},{24,20},{28,24},{1,29},{... | collective-permute-start | bytes 393224 | tf_op jit(solution)/shard_map/ppermute | solution.py:42
  26.8 12.9 %collective-permute-start.2 = (f32[32,1024]{1,0:T(8,128)}, f32[32,1024]{1,0:T(8,128)}, u32[]{:S(2)}, u32[]{:S(2)}) collective-permute-start(f32[32,1024]{1,0:T(8,128)} %get-tuple-element.17), channel_id=1, source_target_pairs={{0,4},{4,8},{8,12},{12,16},{16,20},{20,24},{24,28},{28,0},{1,5},{5... | collective-permute-start | bytes 393224 | tf_op jit(solution)/shard_map/ppermute | solution.py:41
  35.6 14.1 %all-to-all-start.1 = ((bf16[8,16,2048]{2,1,0:T(8,128)(2,1)}), bf16[8,16,2048]{2,1,0:T(8,128)(2,1)S(1)}, u32[]{:S(2)}, u32[]{:S(2)}) async-start(bf16[8,16,2048]{2,1,0:T(8,128)(2,1)} %broadcast_in_dim.32), calls=%async_computation.1 | async-start | bytes 1048576 | tf_op jit(solution)/shard_map/all_to_all | solution.py:15
  41.4 19.4 %collective-permute-start.7 = (f32[64,1024]{1,0:T(8,128)}, f32[64,1024]{1,0:T(8,128)}, u32[]{:S(2)}, u32[]{:S(2)}) collective-permute-start(f32[64,1024]{1,0:T(8,128)} %pad_maximum_fusion.2), channel_id=1, source_target_pairs={{0,28},{4,0},{8,4},{12,8},{16,12},{20,16},{24,20},{28,24},{1,29},{... | collective-permute-start | bytes 786440 | tf_op jit(solution)/shard_map/ppermute | solution.py:53
  47.8 24.9 %collective-permute-start.3 = (f32[64,1024]{1,0:T(8,128)}, f32[64,1024]{1,0:T(8,128)S(1)}, u32[]{:S(2)}, u32[]{:S(2)}) collective-permute-start(f32[64,1024]{1,0:T(8,128)} %pad_maximum_fusion.1), channel_id=1, source_target_pairs={{0,4},{4,8},{8,12},{12,16},{16,20},{20,24},{24,28},{28,0},{1,5},{5... | collective-permute-start | bytes 786440 | tf_op jit(solution)/shard_map/ppermute | solution.py:52
  59.0 19.9 %collective-permute-start.11 = (f32[16,64,128]{2,1,0:T(8,128)S(1)}, f32[16,64,128]{2,1,0:T(8,128)}, u32[]{:S(2)}, u32[]{:S(2)}) collective-permute-start(f32[16,64,128]{2,1,0:T(8,128)S(1)} %dynamic-slice_bitcast_fusion), channel_id=1, source_target_pairs={{0,1},{1,0},{2,3},{3,2},{4,5},{5,4},{6,7},{7,6},{8,9},{9,8},{10,11... | collective-permute-start | bytes 1572872 | tf_op jit(solution)/shard_map/ppermute | solution.py:81
  62.5 11.6 %collective-permute-start.8 = (f32[64,1024]{1,0:T(8,128)}, f32[64,1024]{1,0:T(8,128)}, u32[]{:S(2)}, u32[]{:S(2)}) collective-permute-start(f32[64,1024]{1,0:T(8,128)} %bitcast_add_fusion.1), channel_id=1, source_target_pairs={{0,28},{4,0},{8,4},{12,8},{16,12},{20,16},{24,20},{28,24},{1,29},{... | collective-permute-start | bytes 786440 | tf_op jit(solution)/shard_map/ppermute | solution.py:53
  75.2 9.4 %collective-permute-start.4 = (f32[64,1024]{1,0:T(8,128)S(1)}, f32[64,1024]{1,0:T(8,128)S(1)}, u32[]{:S(2)}, u32[]{:S(2)}) collective-permute-start(f32[64,1024]{1,0:T(8,128)S(1)} %get-tuple-element.15), channel_id=1, source_target_pairs={{0,4},{4,8},{8,12},{12,16},{16,20},{20,24},{24,28},{28,0},{1,5},{5... | collective-permute-start | bytes 786440 | tf_op jit(solution)/shard_map/ppermute | solution.py:52
  75.3 10.3 %collective-permute-start.9 = (f32[64,1024]{1,0:T(8,128)S(1)}, f32[64,1024]{1,0:T(8,128)S(1)}, u32[]{:S(2)}, u32[]{:S(2)}) collective-permute-start(f32[64,1024]{1,0:T(8,128)S(1)} %get-tuple-element.14), channel_id=1, source_target_pairs={{0,28},{4,0},{8,4},{12,8},{16,12},{20,16},{24,20},{28,24},{1,29},{... | collective-permute-start | bytes 786440 | tf_op jit(solution)/shard_map/ppermute | solution.py:53
  80.2 4.9 %collective-permute-start.16 = (f32[64,128]{1,0:T(8,128)S(1)}, f32[64,128]{1,0:T(8,128)S(1)}, u32[]{:S(2)}, u32[]{:S(2)}) collective-permute-start(f32[64,128]{1,0:T(8,128)S(1)} %get-tuple-element.28), channel_id=1, source_target_pairs={{0,28},{4,0},{8,4},{12,8},{16,12},{20,16},{24,20},{28,24},{1,29},{... | collective-permute-start | bytes 98312 | tf_op jit(solution)/shard_map/ppermute | solution.py:42
  81.5 4.1 %collective-permute-start.12 = (f32[64,128]{1,0:T(8,128)S(1)}, f32[64,128]{1,0:T(8,128)S(1)}, u32[]{:S(2)}, u32[]{:S(2)}) collective-permute-start(f32[64,128]{1,0:T(8,128)S(1)} %get-tuple-element.27), channel_id=1, source_target_pairs={{0,4},{4,8},{8,12},{12,16},{16,20},{20,24},{24,28},{28,0},{1,5},{5... | collective-permute-start | bytes 98312 | tf_op jit(solution)/shard_map/ppermute | solution.py:41
  84.6 7.7 %collective-permute-start.5 = (f32[64,1024]{1,0:T(8,128)S(1)}, f32[64,1024]{1,0:T(8,128)S(1)}, u32[]{:S(2)}, u32[]{:S(2)}) collective-permute-start(f32[64,1024]{1,0:T(8,128)S(1)} %bitcast_add_fusion.4), channel_id=1, source_target_pairs={{0,4},{4,8},{8,12},{12,16},{16,20},{20,24},{24,28},{28,0},{1,5},{5... | collective-permute-start | bytes 786440 | tf_op jit(solution)/shard_map/ppermute | solution.py:52
  92.3 3.9 %collective-permute-start.10 = (f32[1,32,1024]{2,1,0:T(8,128)S(1)}, f32[1,32,1024]{2,1,0:T(8,128)S(1)}, u32[]{:S(2)}, u32[]{:S(2)}) collective-permute-start(f32[1,32,1024]{2,1,0:T(8,128)S(1)} %dynamic-slice_bitcast_fusion.7), channel_id=1, source_target_pairs={{0,2},{2,0},{1,3},{3,1},{4,6},{6,4},{5,7},{7,5},{8,10},{10,8},{9,1... | collective-permute-start | bytes 393224 | tf_op jit(solution)/shard_map/ppermute | solution.py:81
  92.8 3.9 %collective-permute-start.17 = (f32[128,128]{1,0:T(8,128)S(1)}, f32[128,128]{1,0:T(8,128)S(1)}, u32[]{:S(2)}, u32[]{:S(2)}) collective-permute-start(f32[128,128]{1,0:T(8,128)S(1)} %pad_maximum_fusion.4), channel_id=1, source_target_pairs={{0,28},{4,0},{8,4},{12,8},{16,12},{20,16},{24,20},{28,24},{1,29},{... | collective-permute-start | bytes 196616 | tf_op jit(solution)/shard_map/ppermute | solution.py:53
  92.9 7.0 %collective-permute-start.13 = (f32[128,128]{1,0:T(8,128)S(1)}, f32[128,128]{1,0:T(8,128)S(1)}, u32[]{:S(2)}, u32[]{:S(2)}) collective-permute-start(f32[128,128]{1,0:T(8,128)S(1)} %pad_maximum_fusion.3), channel_id=1, source_target_pairs={{0,4},{4,8},{8,12},{12,16},{16,20},{20,24},{24,28},{28,0},{1,5},{5... | collective-permute-start | bytes 196616 | tf_op jit(solution)/shard_map/ppermute | solution.py:52
  96.8 3.5 %collective-permute-start.18 = (f32[128,128]{1,0:T(8,128)S(1)}, f32[128,128]{1,0:T(8,128)S(1)}, u32[]{:S(2)}, u32[]{:S(2)}) collective-permute-start(f32[128,128]{1,0:T(8,128)S(1)} %bitcast_add_fusion.7), channel_id=1, source_target_pairs={{0,28},{4,0},{8,4},{12,8},{16,12},{20,16},{24,20},{28,24},{1,29},{... | collective-permute-start | bytes 196616 | tf_op jit(solution)/shard_map/ppermute | solution.py:53
  99.8 5.1 %collective-permute-start.22 = (bf16[64,1024]{1,0:T(8,128)(2,1)S(1)}, bf16[64,1024]{1,0:T(8,128)(2,1)S(1)}, u32[]{:S(2)}, u32[]{:S(2)}) collective-permute-start(bf16[64,1024]{1,0:T(8,128)(2,1)S(1)} %bitcast.170), channel_id=1, source_target_pairs={{0,4},{4,8},{8,12},{12,16},{16,20},{20,24},{24,28},{28,0},{1,5},{5... | collective-permute-start | bytes 393224 | tf_op jit(solution)/shard_map/ppermute | solution.py:71
  100.3 30.7 %collective-permute-start.14 = (f32[128,128]{1,0:T(8,128)S(1)}, f32[128,128]{1,0:T(8,128)S(1)}, u32[]{:S(2)}, u32[]{:S(2)}) collective-permute-start(f32[128,128]{1,0:T(8,128)S(1)} %get-tuple-element.25), channel_id=1, source_target_pairs={{0,4},{4,8},{8,12},{12,16},{16,20},{20,24},{24,28},{28,0},{1,5},{5... | collective-permute-start | bytes 196616 | tf_op jit(solution)/shard_map/ppermute | solution.py:52
  100.4 30.7 %collective-permute-start.19 = (f32[128,128]{1,0:T(8,128)S(1)}, f32[128,128]{1,0:T(8,128)S(1)}, u32[]{:S(2)}, u32[]{:S(2)}) collective-permute-start(f32[128,128]{1,0:T(8,128)S(1)} %get-tuple-element.24), channel_id=1, source_target_pairs={{0,28},{4,0},{8,4},{12,8},{16,12},{20,16},{24,20},{28,24},{1,29},{... | collective-permute-start | bytes 196616 | tf_op jit(solution)/shard_map/ppermute | solution.py:53
  103.0 3.8 %collective-permute-start.23 = (bf16[64,1024]{1,0:T(8,128)(2,1)S(1)}, bf16[64,1024]{1,0:T(8,128)(2,1)S(1)}, u32[]{:S(2)}, u32[]{:S(2)}) collective-permute-start(bf16[64,1024]{1,0:T(8,128)(2,1)S(1)} %bitcast.171), channel_id=1, source_target_pairs={{0,28},{4,0},{8,4},{12,8},{16,12},{20,16},{24,20},{28,24},{1,29},{... | collective-permute-start | bytes 393224 | tf_op jit(solution)/shard_map/ppermute | solution.py:72
  104.9 6.7 %collective-permute-start.24 = (bf16[64,1024]{1,0:T(8,128)(2,1)S(1)}, bf16[64,1024]{1,0:T(8,128)(2,1)S(1)}, u32[]{:S(2)}, u32[]{:S(2)}) collective-permute-start(bf16[64,1024]{1,0:T(8,128)(2,1)S(1)} %collective-permute-done.22), channel_id=1, source_target_pairs={{0,4},{4,8},{8,12},{12,16},{16,20},{20,24},{24,28},{28,0},{1,5},{5... | collective-permute-start | bytes 393224 | tf_op jit(solution)/shard_map/ppermute | solution.py:71
  106.9 5.2 %collective-permute-start.25 = (bf16[64,1024]{1,0:T(8,128)(2,1)S(1)}, bf16[64,1024]{1,0:T(8,128)(2,1)S(1)}, u32[]{:S(2)}, u32[]{:S(2)}) collective-permute-start(bf16[64,1024]{1,0:T(8,128)(2,1)S(1)} %collective-permute-done.23), channel_id=1, source_target_pairs={{0,28},{4,0},{8,4},{12,8},{16,12},{20,16},{24,20},{28,24},{1,29},{... | collective-permute-start | bytes 393224 | tf_op jit(solution)/shard_map/ppermute | solution.py:72
  111.6 8.9 %collective-permute-start.26 = (bf16[64,1024]{1,0:T(8,128)(2,1)S(1)}, bf16[64,1024]{1,0:T(8,128)(2,1)S(1)}, u32[]{:S(2)}, u32[]{:S(2)}) collective-permute-start(bf16[64,1024]{1,0:T(8,128)(2,1)S(1)} %collective-permute-done.24), channel_id=1, source_target_pairs={{0,4},{4,8},{8,12},{12,16},{16,20},{20,24},{24,28},{28,0},{1,5},{5... | collective-permute-start | bytes 393224 | tf_op jit(solution)/shard_map/ppermute | solution.py:71
  112.0 5.4 %collective-permute-start.27 = (bf16[64,1024]{1,0:T(8,128)(2,1)S(1)}, bf16[64,1024]{1,0:T(8,128)(2,1)S(1)}, u32[]{:S(2)}, u32[]{:S(2)}) collective-permute-start(bf16[64,1024]{1,0:T(8,128)(2,1)S(1)} %collective-permute-done.25), channel_id=1, source_target_pairs={{0,28},{4,0},{8,4},{12,8},{16,12},{20,16},{24,20},{28,24},{1,29},{... | collective-permute-start | bytes 393224 | tf_op jit(solution)/shard_map/ppermute | solution.py:72
  117.4 4.4 %collective-permute-start.29 = (bf16[32,1024]{1,0:T(8,128)(2,1)S(1)}, bf16[32,1024]{1,0:T(8,128)(2,1)S(1)}, u32[]{:S(2)}, u32[]{:S(2)}) collective-permute-start(bf16[32,1024]{1,0:T(8,128)(2,1)S(1)} %slice.105), channel_id=1, source_target_pairs={{0,28},{4,0},{8,4},{12,8},{16,12},{20,16},{24,20},{28,24},{1,29},{... | collective-permute-start | bytes 196616 | tf_op jit(solution)/shard_map/ppermute | solution.py:76
  120.5 4.4 %collective-permute-start.28 = (bf16[32,1024]{1,0:T(8,128)(2,1)S(1)}, bf16[32,1024]{1,0:T(8,128)(2,1)S(1)}, u32[]{:S(2)}, u32[]{:S(2)}) collective-permute-start(bf16[32,1024]{1,0:T(8,128)(2,1)S(1)} %slice.104), channel_id=1, source_target_pairs={{0,4},{4,8},{8,12},{12,16},{16,20},{20,24},{24,28},{28,0},{1,5},{5... | collective-permute-start | bytes 196616 | tf_op jit(solution)/shard_map/ppermute | solution.py:75
  127.2 14.8 %all-to-all-start.2 = ((bf16[8,2,64,512]{3,2,1,0:T(8,128)(2,1)}), bf16[8,2,64,512]{3,2,1,0:T(8,128)(2,1)S(1)}, u32[]{:S(2)}, u32[]{:S(2)}) async-start(bf16[8,2,64,512]{3,2,1,0:T(8,128)(2,1)} %bitcast.63), calls=%async_computation.2 | async-start | bytes 2097152 | tf_op jit(solution)/shard_map/all_to_all | solution.py:15
  131.0 4.4 %collective-permute-start.15 = (f32[128,128]{1,0:T(8,128)S(1)}, f32[128,128]{1,0:T(8,128)S(1)}, u32[]{:S(2)}, u32[]{:S(2)}) collective-permute-start(f32[128,128]{1,0:T(8,128)S(1)} %bitcast_add_fusion.10), channel_id=1, source_target_pairs={{0,4},{4,8},{8,12},{12,16},{16,20},{20,24},{24,28},{28,0},{1,5},{5... | collective-permute-start | bytes 196616 | tf_op jit(solution)/shard_map/ppermute | solution.py:52
  142.1 12.1 %collective-permute-start.30 = (f32[64,512]{1,0:T(8,128)S(1)}, f32[64,512]{1,0:T(8,128)S(1)}, u32[]{:S(2)}, u32[]{:S(2)}) collective-permute-start(f32[64,512]{1,0:T(8,128)S(1)} %get-tuple-element.33), channel_id=1, source_target_pairs={{0,1},{1,0},{2,3},{3,2},{4,5},{5,4},{6,7},{7,6},{8,9},{9,8},{10,11... | collective-permute-start | bytes 393224 | tf_op jit(solution)/shard_map/ppermute | solution.py:81
  (6 other events, 40.2 us)

commit v4 on v2

v4 whole, which is shorter than its diff:
```python
import itertools
import math

import jax
import jax.numpy as jnp
from jax import lax
from jax.sharding import Mesh, PartitionSpec as P

AXES = ("x", "yh", "z", "yl", "c")
AA = ("x", "yh")
ZY = ("z", "yl")
F32 = jnp.float32
F16 = jnp.float16
BF16 = jnp.bfloat16
LANES = 128


def exchange(pieces, axes):
    return lax.all_to_all(pieces, axes, 0, 0, tiled=True)


def shifts(sizes):
    return list(itertools.product(*(range(size) for size in sizes)))[1:]


def flat(place, sizes):
    index = 0
    for part, size in zip(place, sizes):
        index = index * size + part
    return index


def moved(sizes, shift):
    places = itertools.product(*(range(size) for size in sizes))
    return [
        (flat(place, sizes), flat([(p + s) % n for p, s, n in zip(place, shift, sizes)], sizes))
        for place in places
    ]


def peer(axes, sizes, shift):
    return flat(
        [lax.rem(lax.axis_index(name) + s, n) for name, s, n in zip(axes, shift, sizes)], sizes
    )


def direct_sum(pieces, axes, sizes):
    own = (0,) * len(sizes)
    total = lax.dynamic_index_in_dim(pieces, peer(axes, sizes, own), 0, keepdims=False).astype(F32)
    for shift in shifts(sizes):
        piece = lax.dynamic_index_in_dim(pieces, peer(axes, sizes, shift), 0, keepdims=False)
        total = total + lax.ppermute(piece, axes, moved(sizes, shift)).astype(F32)
    return total


def direct_gather(block, axes, sizes):
    own = (0,) * len(sizes)
    out = jnp.zeros((math.prod(sizes),) + block.shape, block.dtype)
    out = lax.dynamic_update_index_in_dim(out, block, peer(axes, sizes, own), 0)
    for shift in shifts(sizes):
        got = lax.ppermute(block, axes, moved(sizes, shift))
        back = [n - s for s, n in zip(shift, sizes)]
        out = lax.dynamic_update_index_in_dim(out, got, peer(axes, sizes, back), 0)
    return out


def other(block, axis):
    return lax.ppermute(block, axis, [(0, 1), (1, 0)])


def pair_sum(pieces, axis):
    me = lax.axis_index(axis)
    keep = lax.dynamic_index_in_dim(pieces, me, 1, keepdims=False)
    send = lax.dynamic_index_in_dim(pieces, 1 - me, 1, keepdims=False)
    return keep + other(send, axis)


def after(array, done):
    return array + (0.0 * done[:1, :1].astype(F32)).astype(array.dtype)


def dot(left, right, contract):
    return lax.dot_general(left, right, (contract, ((), ())), preferred_element_type=F32)


def largest(array):
    return jnp.max(jnp.abs(array)).astype(F32)


def on_device(ligand_slab, protein_slab, protein_orbitals, ligand_orbitals, *, sizes):
    aa = (sizes["x"], sizes["yh"])
    n_aa = aa[0] * aa[1]
    n_z, n_yl = sizes["z"], sizes["yl"]
    n_zy = n_z * n_yl
    fit, lig, mus = ligand_slab.shape
    _, pro, nus = protein_slab.shape
    lig_total, pro_total = ligand_orbitals.shape[0], protein_orbitals.shape[0]
    core = lax.axis_index("c")
    wide = fit * lig

    x_own = ligand_slab.reshape(wide, mus)
    y = protein_slab.reshape(fit * pro, nus)
    x_other = other(x_own, "c")
    orb = protein_orbitals.reshape(n_zy, 2, pro, mus)
    orb_own = lax.dynamic_index_in_dim(orb, core, 1, keepdims=False).reshape(n_zy * pro, mus)
    orb_send = lax.dynamic_index_in_dim(orb, 1 - core, 1, keepdims=False).reshape(n_zy * pro, mus)
    orb_other = other(orb_send, "c")

    tops = jnp.broadcast_to(
        jnp.stack([largest(x_own), largest(protein_orbitals)])[:, None], (2, LANES)
    )
    tops = jnp.maximum(tops, other(tops, "c"))[:, 0]
    bound = (2.0 * mus) * tops[0] * tops[1]
    code = jnp.ceil(jnp.log2(jnp.maximum(bound, 1e-30))) + 1.0
    a_part = dot(orb_own, x_own, ((1,), (1,))) + dot(orb_other, x_other, ((1,), (1,)))
    a_sent = (a_part * jnp.exp2(15.0 - code)).astype(F16)
    a_sent = jnp.concatenate([a_sent, jnp.broadcast_to(code.astype(F16), (n_zy * pro, LANES))], axis=1)
    a_got = exchange(a_sent.reshape(n_zy, pro, wide + LANES), ZY)
    codes = a_got[:, :1, wide : wide + 1].astype(F32)
    a_own = jnp.sum(a_got[:, :, :wide].astype(F32) * jnp.exp2(codes - 15.0), axis=0)
    a_block = jnp.broadcast_to(a_own.astype(BF16)[None], (n_zy, pro, wide))
    a_all = exchange(a_block, ZY).reshape(n_zy * pro, wide)

    b_part = dot(after(ligand_orbitals, a_sent), y, ((1,), (1,))).astype(BF16)
    b_own = direct_sum(b_part.reshape(n_aa, lig, fit * pro), AA, aa)
    b_block = after(b_own, a_own).astype(BF16)
    b_all = direct_gather(b_block, AA, aa).reshape(n_aa * lig, fit * pro)

    pair = jnp.sum(
        jnp.transpose(a_own.reshape(pro, fit, lig), (1, 2, 0))
        * jnp.transpose(b_own.reshape(lig, fit, pro), (1, 0, 2)),
        axis=0,
    )
    pair_exchange = -pair / math.sqrt(fit)

    scale_ligand = 1.0 / math.sqrt(fit * pro_total)
    rows_b = nus // (2 * n_zy)
    back_b = dot(y, b_all, ((0,), (1,))) * scale_ligand
    back_b = pair_sum(back_b.reshape(n_zy, 2, rows_b, lig_total), "c")
    back_b = pair_sum(back_b.reshape(n_z, n_yl, rows_b, lig_total), "yl")
    back_b = after(back_b.reshape(n_z * rows_b, lig_total), a_all)
    ligand_back = direct_sum(back_b.reshape(n_z, rows_b, lig_total), ("z",), (n_z,))

    scale_protein = 1.0 / math.sqrt(fit * lig_total)
    half = n_zy * pro
    rows = mus // n_aa
    x_chip = jnp.stack(
        [x_own.T.reshape(n_aa, rows, wide), x_other.T.reshape(n_aa, rows, wide)], axis=1
    ).reshape(2 * mus, wide)
    back_a = (dot(x_chip, a_all, ((1,), (1,))) * scale_protein).astype(BF16)
    back_a = exchange(back_a.reshape(n_aa, 2, rows, half), AA)
    here, away = jnp.sum(back_a.astype(F32), axis=0)
    there = other(away, "c")
    here = here.reshape(rows, n_zy, 1, pro)
    there = there.reshape(rows, n_zy, 1, pro)
    protein_back = jnp.where(
        core == 0,
        jnp.concatenate([here, there], axis=2),
        jnp.concatenate([there, here], axis=2),
    ).reshape(rows, pro_total)
    return (pair_exchange, ligand_back, protein_back)


def solution(mesh):
    sizes = {"x": mesh.shape["aa"] // 2, "yh": 2, "z": mesh.shape["ba"] // 4, "yl": 2, "c": 2}
    fine = Mesh(mesh.devices.reshape([sizes[name] for name in AXES]), AXES)
    aa, ba = AA, ("z", "yl", "c")
    placed = (P(None, aa, ba), P(None, ba, aa), P(None, ba), P(None, aa))

    def body(*args):
        return on_device(*args, sizes=sizes)

    return jax.shard_map(
        body,
        mesh=fine,
        in_specs=placed,
        out_specs=(P(aa, ba), P(aa + ba, None), P(ba + aa, None)),
        check_vma=False,
    )
```

time: 161 us -> 151 us (0.938)
  the two profiles are of different devices: /device:TPU:1 before, /device:TPU:16 now
where the time goes in v4:
time: 151 us; the launch traced here: 150 us
  starting transfers between devices  65 us (43%)
  waiting for transfers between devices  36.4 us (24%)
  local copies, waits for them, and re-layouts  19.6 us (13%)
  matrix products  17.9 us (12%)
  other arithmetic  7.03 us (5%)
  between operations  4.44 us (3%)
    ppermute x14, starting transfers between devices, direct_sum(): total = total + lax.ppermute(piece, axes, moved(sizes, shift)).astype(F32)  28.1 us
    all_to_all x3, starting transfers between devices, exchange(): return lax.all_to_all(pieces, axes, 0, 0, tiled=True)  21.6 us
    dot_general x5, matrix products, dot(): lax.dot_general(left, right, (contract, ((), ())), preferred_element_type...  17.9 us
    all_to_all x3, waiting for transfers between devices, exchange(): return lax.all_to_all(pieces, axes, 0, 0, tiled=True)  16 us
    ppermute x7, starting transfers between devices, direct_gather(): got = lax.ppermute(block, axes, moved(sizes, shift))  14.3 us
    ppermute x6, waiting for transfers between devices, other(): return lax.ppermute(block, axis, [(0, 1), (1, 0)])  11.8 us
    ppermute x14, waiting for transfers between devices, direct_sum(): total = total + lax.ppermute(piece, axes, moved(sizes, shift)).astype(F32)  7.67 us
    dynamic_update_slice x7, local copies, waits for them, and re-layouts, direct_gather(): out = lax.dynamic_update_index_in_dim(out, got, peer(axes, sizes, back), 0)  4.43 us
  transfers between devices with their start and end apart: 30, of which 10 were waited for; matrix products, arithmetic and copies ran while one was open for 25% of the time, Pallas kernels for 0%

profile of v4, /device:TPU:16, one launch (start us, length us, event | category | flops | bytes accessed | tf_op | source)
XLA Modules:
  0.0 150.4 jit_solution(8484318525658674733)
XLA Ops:
  0.7 1.4 constant_dynamic-slice_fusion
  4.2 1.4 maximum_convert_fusion
  11.0 9.3 %all-to-all-start = ((f16[16,32,1152]{2,1,0:T(8,128)(2,1)}), f16[16,32,1152]{2,1,0:T(8,128)(2,1)S(1)}, u32[]{:S(2)}, u32[]{:S(2)}) async-start(f16[16,32,1152]{2,1,0:T(8,128)(2,1)} %bitcast.8), calls=%async_computation | async-start | bytes 2359296 | tf_op jit(solution)/shard_map/all_to_all | solution.py:19
  21.6 6.4 %convolution_convert_fusion = bf16[128,2048]{1,0:T(8,128)(2,1)S(1)} fusion(bf16[2048,2048]{1,0:T(8,128)(2,1)} %bitcast.122, bf16[128,2048]{1,0:T(8,128)(2,1)} %param.7, bf16[]{:T(256)} %bitcast.12), kind=kOutput, calls=%fused_computation.2 | convolution fusion | flops 1074266112 | bytes 9437186 | tf_op jit(solution)/shard_map/dot_general | solution.py:83
  28.7 2.8 %collective-permute-start.9 = (bf16[16,2048]{1,0:T(8,128)(2,1)S(1)}, bf16[16,2048]{1,0:T(8,128)(2,1)S(1)}, u32[]{:S(2)}, u32[]{:S(2)}) collective-permute-start(bf16[16,2048]{1,0:T(8,128)(2,1)S(1)} %get-tuple-element.24), channel_id=1, source_target_pairs={{0,224},{32,192},{64,32},{96,0},{128,96},{160,64},{192,160},{224,1... | collective-permute-start | bytes 196616 | tf_op jit(solution)/shard_map/ppermute | solution.py:52
  32.4 2.8 %collective-permute-start.7 = (bf16[16,2048]{1,0:T(8,128)(2,1)}, bf16[16,2048]{1,0:T(8,128)(2,1)S(1)}, u32[]{:S(2)}, u32[]{:S(2)}) collective-permute-start(bf16[16,2048]{1,0:T(8,128)(2,1)} %get-tuple-element.26), channel_id=1, source_target_pairs={{0,160},{32,128},{64,224},{96,192},{128,32},{160,0},{192,96},{224,... | collective-permute-start | bytes 196616 | tf_op jit(solution)/shard_map/ppermute | solution.py:52
  35.2 3.0 %collective-permute-start.6 = (bf16[16,2048]{1,0:T(8,128)(2,1)S(1)}, bf16[16,2048]{1,0:T(8,128)(2,1)S(1)}, u32[]{:S(2)}, u32[]{:S(2)}) collective-permute-start(bf16[16,2048]{1,0:T(8,128)(2,1)S(1)} %get-tuple-element.27), channel_id=1, source_target_pairs={{0,128},{32,160},{64,192},{96,224},{128,0},{160,32},{192,64},{224,... | collective-permute-start | bytes 196616 | tf_op jit(solution)/shard_map/ppermute | solution.py:52
  39.5 12.6 %all-to-all-done = f16[16,32,1152]{2,1,0:T(8,128)(2,1)S(1)} async-done(((f16[16,32,1152]{2,1,0:T(8,128)(2,1)}), f16[16,32,1152]{2,1,0:T(8,128)(2,1)S(1)}, u32[]{:S(2)}, u32[]{:S(2)}) %all-to-all-start) | async-done | bytes 1179680 | tf_op jit(solution)/shard_map/all_to_all | solution.py:19
  52.3 1.6 %collective-permute-start.4 = (bf16[16,2048]{1,0:T(8,128)(2,1)S(1)}, bf16[16,2048]{1,0:T(8,128)(2,1)S(1)}, u32[]{:S(2)}, u32[]{:S(2)}) collective-permute-start(bf16[16,2048]{1,0:T(8,128)(2,1)S(1)} %get-tuple-element.29), channel_id=1, source_target_pairs={{0,64},{32,96},{64,128},{96,160},{128,192},{160,224},{192,0},{224,... | collective-permute-start | bytes 196616 | tf_op jit(solution)/shard_map/ppermute | solution.py:52
  55.7 2.1 %collective-permute-done.4 = bf16[16,2048]{1,0:T(8,128)(2,1)S(1)} collective-permute-done((bf16[16,2048]{1,0:T(8,128)(2,1)S(1)}, bf16[16,2048]{1,0:T(8,128)(2,1)S(1)}, u32[]{:S(2)}, u32[]{:S(2)}) %collective-permute-start.4) | collective-permute-done | bytes 65568 | tf_op jit(solution)/shard_map/ppermute | solution.py:52
  57.8 1.8 %collective-permute-done.3 = bf16[16,2048]{1,0:T(8,128)(2,1)S(1)} collective-permute-done((bf16[16,2048]{1,0:T(8,128)(2,1)S(1)}, bf16[16,2048]{1,0:T(8,128)(2,1)S(1)}, u32[]{:S(2)}, u32[]{:S(2)}) %collective-permute-start.3) | collective-permute-done | bytes 65568 | tf_op jit(solution)/shard_map/ppermute | solution.py:52
  62.7 1.6 %collective-permute-start.11 = (bf16[16,2048]{1,0:T(8,128)(2,1)S(1)}, bf16[16,2048]{1,0:T(8,128)(2,1)S(1)}, u32[]{:S(2)}, u32[]{:S(2)}) collective-permute-start(bf16[16,2048]{1,0:T(8,128)(2,1)S(1)} %get-tuple-element.19), channel_id=1, source_target_pairs={{0,64},{32,96},{64,128},{96,160},{128,192},{160,224},{192,0},{224,... | collective-permute-start | bytes 196616 | tf_op jit(solution)/shard_map/ppermute | solution.py:61
  64.3 3.5 %collective-permute-start.12 = (bf16[16,2048]{1,0:T(8,128)(2,1)S(1)}, bf16[16,2048]{1,0:T(8,128)(2,1)S(1)}, u32[]{:S(2)}, u32[]{:S(2)}) collective-permute-start(bf16[16,2048]{1,0:T(8,128)(2,1)S(1)} %get-tuple-element.19), channel_id=1, source_target_pairs={{0,96},{32,64},{64,160},{96,128},{128,224},{160,192},{192,32},{224... | collective-permute-start | bytes 196616 | tf_op jit(solution)/shard_map/ppermute | solution.py:61
  67.8 2.3 %collective-permute-start.13 = (bf16[16,2048]{1,0:T(8,128)(2,1)S(1)}, bf16[16,2048]{1,0:T(8,128)(2,1)S(1)}, u32[]{:S(2)}, u32[]{:S(2)}) collective-permute-start(bf16[16,2048]{1,0:T(8,128)(2,1)S(1)} %get-tuple-element.19), channel_id=1, source_target_pairs={{0,128},{32,160},{64,192},{96,224},{128,0},{160,32},{192,64},{224,... | collective-permute-start | bytes 196616 | tf_op jit(solution)/shard_map/ppermute | solution.py:61
  70.1 1.5 %collective-permute-start.14 = (bf16[16,2048]{1,0:T(8,128)(2,1)S(1)}, bf16[16,2048]{1,0:T(8,128)(2,1)S(1)}, u32[]{:S(2)}, u32[]{:S(2)}) collective-permute-start(bf16[16,2048]{1,0:T(8,128)(2,1)S(1)} %get-tuple-element.19), channel_id=1, source_target_pairs={{0,160},{32,128},{64,224},{96,192},{128,32},{160,0},{192,96},{224,... | collective-permute-start | bytes 196616 | tf_op jit(solution)/shard_map/ppermute | solution.py:61
  72.7 4.8 %all-to-all-start.1 = ((bf16[16,32,1024]{2,1,0:T(8,128)(2,1)}), bf16[16,32,1024]{2,1,0:T(8,128)(2,1)}, u32[]{:S(2)}, u32[]{:S(2)}) async-start(bf16[16,32,1024]{2,1,0:T(8,128)(2,1)} %broadcast_in_dim.51), calls=%async_computation.1 | async-start | bytes 2097152 | tf_op jit(solution)/shard_map/all_to_all | solution.py:19
  77.5 2.0 %collective-permute-start.15 = (bf16[16,2048]{1,0:T(8,128)(2,1)S(1)}, bf16[16,2048]{1,0:T(8,128)(2,1)S(1)}, u32[]{:S(2)}, u32[]{:S(2)}) collective-permute-start(bf16[16,2048]{1,0:T(8,128)(2,1)S(1)} %get-tuple-element.19), channel_id=1, source_target_pairs={{0,192},{32,224},{64,0},{96,32},{128,64},{160,96},{192,128},{224,1... | collective-permute-start | bytes 196616 | tf_op jit(solution)/shard_map/ppermute | solution.py:61
  80.2 3.0 %collective-permute-start.16 = (bf16[16,2048]{1,0:T(8,128)(2,1)S(1)}, bf16[16,2048]{1,0:T(8,128)(2,1)S(1)}, u32[]{:S(2)}, u32[]{:S(2)}) collective-permute-start(bf16[16,2048]{1,0:T(8,128)(2,1)S(1)} %get-tuple-element.19), channel_id=1, source_target_pairs={{0,224},{32,192},{64,32},{96,0},{128,96},{160,64},{192,160},{224,1... | collective-permute-start | bytes 196616 | tf_op jit(solution)/shard_map/ppermute | solution.py:61
  88.0 5.8 %fusion = f32[2048,128]{0,1:T(8,128)} fusion(bf16[128,2048]{1,0:T(8,128)(2,1)} %bitcast.33, bf16[2048,2048]{1,0:T(8,128)(2,1)} %bitcast.123), kind=kOutput, calls=%fused_computation.1 | convolution fusion | flops 1074003968 | bytes 9961472 | tf_op jit(solution)/shard_map/dot_general | solution.py:83
  93.8 1.5 %copy.48 = f32[2048,128]{1,0:T(8,128)S(1)} copy(f32[2048,128]{0,1:T(8,128)} %fusion) | data formatting | bytes 2097152 | tf_op jit(solution)/shard_map/mul | solution.py:138
  96.4 1.5 %copy.51 = bf16[8,2,64,1024]{3,2,1,0:T(8,128)(2,1)} copy(bf16[8,2,64,1024]{3,2,0,1:T(8,128)(2,1)S(1)} %pad_maximum_fusion) | data formatting | bytes 4194304 | tf_op jit(solution)/shard_map/stack | solution.py:147
  98.3 3.3 %all-to-all-done.1 = bf16[16,32,1024]{2,1,0:T(8,128)(2,1)} async-done(((bf16[16,32,1024]{2,1,0:T(8,128)(2,1)}), bf16[16,32,1024]{2,1,0:T(8,128)(2,1)}, u32[]{:S(2)}, u32[]{:S(2)}) %all-to-all-start.1) | async-done | bytes 1048608 | tf_op jit(solution)/shard_map/all_to_all | solution.py:19
  101.6 4.1 %multiply_convert_fusion = bf16[1024,512]{1,0:T(8,128)(2,1)} fusion(bf16[1024,1024]{1,0:T(8,128)(2,1)} %bitcast.136, bf16[512,1024]{1,0:T(8,128)(2,1)} %bitcast.41), kind=kOutput, calls=%fused_computation.5 | convolution fusion | flops 1074790400 | bytes 4194304 | tf_op jit(solution)/shard_map/dot_general | solution.py:83
  105.7 7.5 %all-to-all-start.2 = ((bf16[8,2,64,512]{3,2,1,0:T(8,128)(2,1)}), bf16[8,2,64,512]{3,2,1,0:T(8,128)(2,1)S(1)}, u32[]{:S(2)}, u32[]{:S(2)}) async-start(bf16[8,2,64,512]{3,2,1,0:T(8,128)(2,1)} %bitcast.141), calls=%async_computation.2 | async-start | bytes 2097152 | tf_op jit(solution)/shard_map/all_to_all | solution.py:19
  117.5 11.5 %collective-permute-done.18 = f32[8,64,128]{2,1,0:T(8,128)S(1)} collective-permute-done((f32[8,64,128]{2,1,0:T(8,128)S(1)}, f32[8,64,128]{2,1,0:T(8,128)S(1)}, u32[]{:S(2)}, u32[]{:S(2)}) %collective-permute-start.18) | collective-permute-done | bytes 262176 | tf_op jit(solution)/shard_map/ppermute | solution.py:68
  129.0 2.4 %collective-permute-start.25 = (f32[64,128]{1,0:T(8,128)S(1)}, f32[64,128]{1,0:T(8,128)S(1)}, u32[]{:S(2)}, u32[]{:S(2)}) collective-permute-start(f32[64,128]{1,0:T(8,128)S(1)} %get-tuple-element.33), channel_id=1, source_target_pairs={{0,28},{4,0},{8,4},{12,8},{16,12},{20,16},{24,20},{28,24},{1,29},{... | collective-permute-start | bytes 98312 | tf_op jit(solution)/shard_map/ppermute | solution.py:52
  131.5 2.5 %collective-permute-start.24 = (f32[64,128]{1,0:T(8,128)S(1)}, f32[64,128]{1,0:T(8,128)S(1)}, u32[]{:S(2)}, u32[]{:S(2)}) collective-permute-start(f32[64,128]{1,0:T(8,128)S(1)} %get-tuple-element.34), channel_id=1, source_target_pairs={{0,24},{4,28},{8,0},{12,4},{16,8},{20,12},{24,16},{28,20},{1,25},{... | collective-permute-start | bytes 98312 | tf_op jit(solution)/shard_map/ppermute | solution.py:52
  133.9 1.5 %collective-permute-start.23 = (f32[64,128]{1,0:T(8,128)S(1)}, f32[64,128]{1,0:T(8,128)S(1)}, u32[]{:S(2)}, u32[]{:S(2)}) collective-permute-start(f32[64,128]{1,0:T(8,128)S(1)} %get-tuple-element.35), channel_id=1, source_target_pairs={{0,20},{4,24},{8,28},{12,0},{16,4},{20,8},{24,12},{28,16},{1,21},{... | collective-permute-start | bytes 98312 | tf_op jit(solution)/shard_map/ppermute | solution.py:52
  135.4 3.9 %collective-permute-start.22 = (f32[64,128]{1,0:T(8,128)S(1)}, f32[64,128]{1,0:T(8,128)S(1)}, u32[]{:S(2)}, u32[]{:S(2)}) collective-permute-start(f32[64,128]{1,0:T(8,128)S(1)} %get-tuple-element.36), channel_id=1, source_target_pairs={{0,16},{4,20},{8,24},{12,28},{16,0},{20,4},{24,8},{28,12},{1,17},{... | collective-permute-start | bytes 98312 | tf_op jit(solution)/shard_map/ppermute | solution.py:52
  139.6 3.7 %collective-permute-start.20 = (f32[64,128]{1,0:T(8,128)S(1)}, f32[64,128]{1,0:T(8,128)S(1)}, u32[]{:S(2)}, u32[]{:S(2)}) collective-permute-start(f32[64,128]{1,0:T(8,128)S(1)} %get-tuple-element.38), channel_id=1, source_target_pairs={{0,8},{4,12},{8,16},{12,20},{16,24},{20,28},{24,0},{28,4},{1,9},{5... | collective-permute-start | bytes 98312 | tf_op jit(solution)/shard_map/ppermute | solution.py:52
  144.7 1.6 %collective-permute-done.21 = f32[64,128]{1,0:T(8,128)S(1)} collective-permute-done((f32[64,128]{1,0:T(8,128)S(1)}, f32[64,128]{1,0:T(8,128)S(1)}, u32[]{:S(2)}, u32[]{:S(2)}) %collective-permute-start.21) | collective-permute-done | bytes 32800 | tf_op jit(solution)/shard_map/ppermute | solution.py:52
  146.7 1.8 %collective-permute-done.19 = f32[64,128]{1,0:T(8,128)S(1)} collective-permute-done((f32[64,128]{1,0:T(8,128)S(1)}, f32[64,128]{1,0:T(8,128)S(1)}, u32[]{:S(2)}, u32[]{:S(2)}) %collective-permute-start.19) | collective-permute-done | bytes 32800 | tf_op jit(solution)/shard_map/ppermute | solution.py:52
  (90 shorter events, 29.3 us)
Async XLA Ops:
  0.6 2.1 %copy-start.3 = (bf16[1024,512]{1,0:T(8,128)(2,1)S(1)}, bf16[1024,512]{1,0:T(8,128)(2,1)}, u32[]{:S(2)}) copy-start(bf16[1024,512]{1,0:T(8,128)(2,1)} %param.6) | copy-start | bytes 3145732
  2.1 6.7 %collective-permute-start = (bf16[512,512]{1,0:T(8,128)(2,1)S(1)}, bf16[512,512]{1,0:T(8,128)(2,1)S(1)}, u32[]{:S(2)}, u32[]{:S(2)}) collective-permute-start(bf16[512,512]{1,0:T(8,128)(2,1)S(1)} %bitcast.144), channel_id=1, source_target_pairs={{0,1},{1,0},{2,3},{3,2},{4,5},{5,4},{6,7},{7,6},{8,9},{9,8},{10,11... | collective-permute-start | bytes 1572872 | tf_op jit(solution)/shard_map/ppermute | solution.py:68
  2.3 6.5 %collective-permute-start.1 = (bf16[1024,512]{1,0:T(8,128)(2,1)S(1)}, bf16[1024,512]{1,0:T(8,128)(2,1)S(1)}, u32[]{:S(2)}, u32[]{:S(2)}) collective-permute-start(bf16[1024,512]{1,0:T(8,128)(2,1)S(1)} %bitcast.124), channel_id=1, source_target_pairs={{0,1},{1,0},{2,3},{3,2},{4,5},{5,4},{6,7},{7,6},{8,9},{9,8},{10,11... | collective-permute-start | bytes 3145736 | tf_op jit(solution)/shard_map/ppermute | solution.py:68
  5.6 1.1 collective-permute-start.2
  11.0 41.1 %all-to-all-start = ((f16[16,32,1152]{2,1,0:T(8,128)(2,1)}), f16[16,32,1152]{2,1,0:T(8,128)(2,1)S(1)}, u32[]{:S(2)}, u32[]{:S(2)}) async-start(f16[16,32,1152]{2,1,0:T(8,128)(2,1)} %bitcast.8), calls=%async_computation | async-start | bytes 2359296 | tf_op jit(solution)/shard_map/all_to_all | solution.py:19
  28.7 23.6 %collective-permute-start.9 = (bf16[16,2048]{1,0:T(8,128)(2,1)S(1)}, bf16[16,2048]{1,0:T(8,128)(2,1)S(1)}, u32[]{:S(2)}, u32[]{:S(2)}) collective-permute-start(bf16[16,2048]{1,0:T(8,128)(2,1)S(1)} %get-tuple-element.24), channel_id=1, source_target_pairs={{0,224},{32,192},{64,32},{96,0},{128,96},{160,64},{192,160},{224,1... | collective-permute-start | bytes 196616 | tf_op jit(solution)/shard_map/ppermute | solution.py:52
  31.5 22.3 %collective-permute-start.8 = (bf16[16,2048]{1,0:T(8,128)(2,1)S(1)}, bf16[16,2048]{1,0:T(8,128)(2,1)S(1)}, u32[]{:S(2)}, u32[]{:S(2)}) collective-permute-start(bf16[16,2048]{1,0:T(8,128)(2,1)S(1)} %get-tuple-element.25), channel_id=1, source_target_pairs={{0,192},{32,224},{64,0},{96,32},{128,64},{160,96},{192,128},{224,1... | collective-permute-start | bytes 196616 | tf_op jit(solution)/shard_map/ppermute | solution.py:52
  32.4 23.3 %collective-permute-start.7 = (bf16[16,2048]{1,0:T(8,128)(2,1)}, bf16[16,2048]{1,0:T(8,128)(2,1)S(1)}, u32[]{:S(2)}, u32[]{:S(2)}) collective-permute-start(bf16[16,2048]{1,0:T(8,128)(2,1)} %get-tuple-element.26), channel_id=1, source_target_pairs={{0,160},{32,128},{64,224},{96,192},{128,32},{160,0},{192,96},{224,... | collective-permute-start | bytes 196616 | tf_op jit(solution)/shard_map/ppermute | solution.py:52
  35.2 20.5 %collective-permute-start.6 = (bf16[16,2048]{1,0:T(8,128)(2,1)S(1)}, bf16[16,2048]{1,0:T(8,128)(2,1)S(1)}, u32[]{:S(2)}, u32[]{:S(2)}) collective-permute-start(bf16[16,2048]{1,0:T(8,128)(2,1)S(1)} %get-tuple-element.27), channel_id=1, source_target_pairs={{0,128},{32,160},{64,192},{96,224},{128,0},{160,32},{192,64},{224,... | collective-permute-start | bytes 196616 | tf_op jit(solution)/shard_map/ppermute | solution.py:52
  38.2 17.5 %collective-permute-start.5 = (bf16[16,2048]{1,0:T(8,128)(2,1)S(1)}, bf16[16,2048]{1,0:T(8,128)(2,1)S(1)}, u32[]{:S(2)}, u32[]{:S(2)}) collective-permute-start(bf16[16,2048]{1,0:T(8,128)(2,1)S(1)} %get-tuple-element.28), channel_id=1, source_target_pairs={{0,96},{32,64},{64,160},{96,128},{128,224},{160,192},{192,32},{224... | collective-permute-start | bytes 196616 | tf_op jit(solution)/shard_map/ppermute | solution.py:52
  52.3 5.6 %collective-permute-start.4 = (bf16[16,2048]{1,0:T(8,128)(2,1)S(1)}, bf16[16,2048]{1,0:T(8,128)(2,1)S(1)}, u32[]{:S(2)}, u32[]{:S(2)}) collective-permute-start(bf16[16,2048]{1,0:T(8,128)(2,1)S(1)} %get-tuple-element.29), channel_id=1, source_target_pairs={{0,64},{32,96},{64,128},{96,160},{128,192},{160,224},{192,0},{224,... | collective-permute-start | bytes 196616 | tf_op jit(solution)/shard_map/ppermute | solution.py:52
  53.8 5.8 %collective-permute-start.3 = (bf16[16,2048]{1,0:T(8,128)(2,1)S(1)}, bf16[16,2048]{1,0:T(8,128)(2,1)S(1)}, u32[]{:S(2)}, u32[]{:S(2)}) collective-permute-start(bf16[16,2048]{1,0:T(8,128)(2,1)S(1)} %get-tuple-element.23), channel_id=1, source_target_pairs={{0,32},{32,0},{64,96},{96,64},{128,160},{160,128},{192,224},{224,1... | collective-permute-start | bytes 196616 | tf_op jit(solution)/shard_map/ppermute | solution.py:52
  54.5 7.7 %copy-start.2 = (bf16[1024,512]{1,0:T(8,128)(2,1)S(1)}, bf16[1024,512]{1,0:T(8,128)(2,1)}, u32[]{:S(2)}) copy-start(bf16[1024,512]{1,0:T(8,128)(2,1)} %copy-done.1) | copy-start | bytes 3145732
  61.2 16.3 %collective-permute-start.10 = (bf16[16,2048]{1,0:T(8,128)(2,1)S(1)}, bf16[16,2048]{1,0:T(8,128)(2,1)S(1)}, u32[]{:S(2)}, u32[]{:S(2)}) collective-permute-start(bf16[16,2048]{1,0:T(8,128)(2,1)S(1)} %get-tuple-element.19), channel_id=1, source_target_pairs={{0,32},{32,0},{64,96},{96,64},{128,160},{160,128},{192,224},{224,1... | collective-permute-start | bytes 196616 | tf_op jit(solution)/shard_map/ppermute | solution.py:61
  62.7 17.5 %collective-permute-start.11 = (bf16[16,2048]{1,0:T(8,128)(2,1)S(1)}, bf16[16,2048]{1,0:T(8,128)(2,1)S(1)}, u32[]{:S(2)}, u32[]{:S(2)}) collective-permute-start(bf16[16,2048]{1,0:T(8,128)(2,1)S(1)} %get-tuple-element.19), channel_id=1, source_target_pairs={{0,64},{32,96},{64,128},{96,160},{128,192},{160,224},{192,0},{224,... | collective-permute-start | bytes 196616 | tf_op jit(solution)/shard_map/ppermute | solution.py:61
  64.3 19.5 %collective-permute-start.12 = (bf16[16,2048]{1,0:T(8,128)(2,1)S(1)}, bf16[16,2048]{1,0:T(8,128)(2,1)S(1)}, u32[]{:S(2)}, u32[]{:S(2)}) collective-permute-start(bf16[16,2048]{1,0:T(8,128)(2,1)S(1)} %get-tuple-element.19), channel_id=1, source_target_pairs={{0,96},{32,64},{64,160},{96,128},{128,224},{160,192},{192,32},{224... | collective-permute-start | bytes 196616 | tf_op jit(solution)/shard_map/ppermute | solution.py:61
  67.8 16.7 %collective-permute-start.13 = (bf16[16,2048]{1,0:T(8,128)(2,1)S(1)}, bf16[16,2048]{1,0:T(8,128)(2,1)S(1)}, u32[]{:S(2)}, u32[]{:S(2)}) collective-permute-start(bf16[16,2048]{1,0:T(8,128)(2,1)S(1)} %get-tuple-element.19), channel_id=1, source_target_pairs={{0,128},{32,160},{64,192},{96,224},{128,0},{160,32},{192,64},{224,... | collective-permute-start | bytes 196616 | tf_op jit(solution)/shard_map/ppermute | solution.py:61
  70.1 15.0 %collective-permute-start.14 = (bf16[16,2048]{1,0:T(8,128)(2,1)S(1)}, bf16[16,2048]{1,0:T(8,128)(2,1)S(1)}, u32[]{:S(2)}, u32[]{:S(2)}) collective-permute-start(bf16[16,2048]{1,0:T(8,128)(2,1)S(1)} %get-tuple-element.19), channel_id=1, source_target_pairs={{0,160},{32,128},{64,224},{96,192},{128,32},{160,0},{192,96},{224,... | collective-permute-start | bytes 196616 | tf_op jit(solution)/shard_map/ppermute | solution.py:61
  72.7 28.9 %all-to-all-start.1 = ((bf16[16,32,1024]{2,1,0:T(8,128)(2,1)}), bf16[16,32,1024]{2,1,0:T(8,128)(2,1)}, u32[]{:S(2)}, u32[]{:S(2)}) async-start(bf16[16,32,1024]{2,1,0:T(8,128)(2,1)} %broadcast_in_dim.51), calls=%async_computation.1 | async-start | bytes 2097152 | tf_op jit(solution)/shard_map/all_to_all | solution.py:19
  77.5 8.2 %collective-permute-start.15 = (bf16[16,2048]{1,0:T(8,128)(2,1)S(1)}, bf16[16,2048]{1,0:T(8,128)(2,1)S(1)}, u32[]{:S(2)}, u32[]{:S(2)}) collective-permute-start(bf16[16,2048]{1,0:T(8,128)(2,1)S(1)} %get-tuple-element.19), channel_id=1, source_target_pairs={{0,192},{32,224},{64,0},{96,32},{128,64},{160,96},{192,128},{224,1... | collective-permute-start | bytes 196616 | tf_op jit(solution)/shard_map/ppermute | solution.py:61
  80.2 7.1 %collective-permute-start.16 = (bf16[16,2048]{1,0:T(8,128)(2,1)S(1)}, bf16[16,2048]{1,0:T(8,128)(2,1)S(1)}, u32[]{:S(2)}, u32[]{:S(2)}) collective-permute-start(bf16[16,2048]{1,0:T(8,128)(2,1)S(1)} %get-tuple-element.19), channel_id=1, source_target_pairs={{0,224},{32,192},{64,32},{96,0},{128,96},{160,64},{192,160},{224,1... | collective-permute-start | bytes 196616 | tf_op jit(solution)/shard_map/ppermute | solution.py:61
  96.2 17.0 %collective-permute-start.17 = (f32[16,64,128]{2,1,0:T(8,128)}, f32[16,64,128]{2,1,0:T(8,128)}, u32[]{:S(2)}, u32[]{:S(2)}) collective-permute-start(f32[16,64,128]{2,1,0:T(8,128)} %dynamic-slice_bitcast_fusion), channel_id=1, source_target_pairs={{0,1},{1,0},{2,3},{3,2},{4,5},{5,4},{6,7},{7,6},{8,9},{9,8},{10,11... | collective-permute-start | bytes 1572872 | tf_op jit(solution)/shard_map/ppermute | solution.py:68
  105.7 33.8 %all-to-all-start.2 = ((bf16[8,2,64,512]{3,2,1,0:T(8,128)(2,1)}), bf16[8,2,64,512]{3,2,1,0:T(8,128)(2,1)S(1)}, u32[]{:S(2)}, u32[]{:S(2)}) async-start(bf16[8,2,64,512]{3,2,1,0:T(8,128)(2,1)} %bitcast.141), calls=%async_computation.2 | async-start | bytes 2097152 | tf_op jit(solution)/shard_map/all_to_all | solution.py:19
  114.3 14.6 %collective-permute-start.18 = (f32[8,64,128]{2,1,0:T(8,128)S(1)}, f32[8,64,128]{2,1,0:T(8,128)S(1)}, u32[]{:S(2)}, u32[]{:S(2)}) collective-permute-start(f32[8,64,128]{2,1,0:T(8,128)S(1)} %dynamic-slice_bitcast_fusion.1), channel_id=1, source_target_pairs={{0,2},{2,0},{1,3},{3,1},{4,6},{6,4},{5,7},{7,5},{8,10},{10,8},{9,1... | collective-permute-start | bytes 786440 | tf_op jit(solution)/shard_map/ppermute | solution.py:68
  129.0 10.6 %collective-permute-start.25 = (f32[64,128]{1,0:T(8,128)S(1)}, f32[64,128]{1,0:T(8,128)S(1)}, u32[]{:S(2)}, u32[]{:S(2)}) collective-permute-start(f32[64,128]{1,0:T(8,128)S(1)} %get-tuple-element.33), channel_id=1, source_target_pairs={{0,28},{4,0},{8,4},{12,8},{16,12},{20,16},{24,20},{28,24},{1,29},{... | collective-permute-start | bytes 98312 | tf_op jit(solution)/shard_map/ppermute | solution.py:52
  131.5 11.9 %collective-permute-start.24 = (f32[64,128]{1,0:T(8,128)S(1)}, f32[64,128]{1,0:T(8,128)S(1)}, u32[]{:S(2)}, u32[]{:S(2)}) collective-permute-start(f32[64,128]{1,0:T(8,128)S(1)} %get-tuple-element.34), channel_id=1, source_target_pairs={{0,24},{4,28},{8,0},{12,4},{16,8},{20,12},{24,16},{28,20},{1,25},{... | collective-permute-start | bytes 98312 | tf_op jit(solution)/shard_map/ppermute | solution.py:52
  133.9 10.7 %collective-permute-start.23 = (f32[64,128]{1,0:T(8,128)S(1)}, f32[64,128]{1,0:T(8,128)S(1)}, u32[]{:S(2)}, u32[]{:S(2)}) collective-permute-start(f32[64,128]{1,0:T(8,128)S(1)} %get-tuple-element.35), channel_id=1, source_target_pairs={{0,20},{4,24},{8,28},{12,0},{16,4},{20,8},{24,12},{28,16},{1,21},{... | collective-permute-start | bytes 98312 | tf_op jit(solution)/shard_map/ppermute | solution.py:52
  135.4 9.3 %collective-permute-start.22 = (f32[64,128]{1,0:T(8,128)S(1)}, f32[64,128]{1,0:T(8,128)S(1)}, u32[]{:S(2)}, u32[]{:S(2)}) collective-permute-start(f32[64,128]{1,0:T(8,128)S(1)} %get-tuple-element.36), channel_id=1, source_target_pairs={{0,16},{4,20},{8,24},{12,28},{16,0},{20,4},{24,8},{28,12},{1,17},{... | collective-permute-start | bytes 98312 | tf_op jit(solution)/shard_map/ppermute | solution.py:52
  139.3 6.9 %collective-permute-start.21 = (f32[64,128]{1,0:T(8,128)S(1)}, f32[64,128]{1,0:T(8,128)S(1)}, u32[]{:S(2)}, u32[]{:S(2)}) collective-permute-start(f32[64,128]{1,0:T(8,128)S(1)} %get-tuple-element.37), channel_id=1, source_target_pairs={{0,12},{4,16},{8,20},{12,24},{16,28},{20,0},{24,4},{28,8},{1,13},{... | collective-permute-start | bytes 98312 | tf_op jit(solution)/shard_map/ppermute | solution.py:52
  139.6 7.0 %collective-permute-start.20 = (f32[64,128]{1,0:T(8,128)S(1)}, f32[64,128]{1,0:T(8,128)S(1)}, u32[]{:S(2)}, u32[]{:S(2)}) collective-permute-start(f32[64,128]{1,0:T(8,128)S(1)} %get-tuple-element.38), channel_id=1, source_target_pairs={{0,8},{4,12},{8,16},{12,20},{16,24},{20,28},{24,0},{28,4},{1,9},{5... | collective-permute-start | bytes 98312 | tf_op jit(solution)/shard_map/ppermute | solution.py:52
  143.4 5.1 %collective-permute-start.19 = (f32[64,128]{1,0:T(8,128)S(1)}, f32[64,128]{1,0:T(8,128)S(1)}, u32[]{:S(2)}, u32[]{:S(2)}) collective-permute-start(f32[64,128]{1,0:T(8,128)S(1)} %get-tuple-element.32), channel_id=1, source_target_pairs={{0,4},{4,8},{8,12},{12,16},{16,20},{20,24},{24,28},{28,0},{1,5},{5... | collective-permute-start | bytes 98312 | tf_op jit(solution)/shard_map/ppermute | solution.py:52
  144.6 4.6 %collective-permute-start.26 = (f32[64,512]{1,0:T(8,128)S(1)}, f32[64,512]{1,0:T(8,128)S(1)}, u32[]{:S(2)}, u32[]{:S(2)}) collective-permute-start(f32[64,512]{1,0:T(8,128)S(1)} %get-tuple-element.31), channel_id=1, source_target_pairs={{0,1},{1,0},{2,3},{3,2},{4,5},{5,4},{6,7},{7,6},{8,9},{9,8},{10,11... | collective-permute-start | bytes 393224 | tf_op jit(solution)/shard_map/ppermute | solution.py:68
  (2 other events, 2.6 us)

commit v5 on v4

--- a/solution.py
+++ b/solution.py
@@ -4,6 +4,8 @@
 import jax
 import jax.numpy as jnp
 from jax import lax
+from jax.experimental import pallas as pl
+from jax.experimental.pallas import tpu as pltpu
 from jax.sharding import Mesh, PartitionSpec as P
 
 AXES = ("x", "yh", "z", "yl", "c")
@@ -13,6 +15,7 @@
 F16 = jnp.float16
 BF16 = jnp.bfloat16
 LANES = 128
+VMEM = 54 * 2**20
 
 
 def exchange(pieces, axes):
@@ -54,14 +57,11 @@
 
 
 def direct_gather(block, axes, sizes):
-    own = (0,) * len(sizes)
-    out = jnp.zeros((math.prod(sizes),) + block.shape, block.dtype)
-    out = lax.dynamic_update_index_in_dim(out, block, peer(axes, sizes, own), 0)
+    blocks, places = [block], [peer(axes, sizes, (0,) * len(sizes))]
     for shift in shifts(sizes):
-        got = lax.ppermute(block, axes, moved(sizes, shift))
-        back = [n - s for s, n in zip(shift, sizes)]
-        out = lax.dynamic_update_index_in_dim(out, got, peer(axes, sizes, back), 0)
-    return out
+        blocks.append(lax.ppermute(block, axes, moved(sizes, shift)))
+        places.append(peer(axes, sizes, [n - s for s, n in zip(shift, sizes)]))
+    return blocks, places
 
 
 def other(block, axis):
@@ -75,16 +75,121 @@
     return keep + other(send, axis)
 
 
-def after(array, done):
-    return array + (0.0 * done[:1, :1].astype(F32)).astype(array.dtype)
-
-
 def dot(left, right, contract):
     return lax.dot_general(left, right, (contract, ((), ())), preferred_element_type=F32)
 
 
 def largest(array):
     return jnp.max(jnp.abs(array)).astype(F32)
+
+
+def cross_kernel(token_ref, left_ref, right_ref, out_ref):
+    del token_ref
+    out_ref[...] = dot(left_ref[...], right_ref[...], ((1,), (1,))).astype(out_ref.dtype)
+
+
+def cross_part(token, orbitals, slab):
+    rows, depth = slab.shape
+    step = min(rows, 256)
+    return pl.pallas_call(
+        cross_kernel,
+        grid=(rows // step,),
+        in_specs=[
+            pl.BlockSpec(token.shape, lambda i: (0, 0)),
+            pl.BlockSpec(orbitals.shape, lambda i: (0, 0)),
+            pl.BlockSpec((step, depth), lambda i: (i, 0)),
+        ],
+        out_specs=pl.BlockSpec((orbitals.shape[0], step), lambda i: (0, i)),
+        out_shape=jax.ShapeDtypeStruct((orbitals.shape[0], rows), BF16),
+        compiler_params=pltpu.CompilerParams(vmem_limit_bytes=VMEM),
+        cost_estimate=pl.CostEstimate(flops=0, bytes_accessed=0, transcendentals=0),
+        name="cross_part",
+    )(token, orbitals, slab)
+
+
+def back_kernel(place_ref, slab_ref, *refs, count, scale, fine):
+    blocks, (keep_ref, send_ref, all_ref) = refs[:count], refs[count:]
+
+    @pl.when(pl.program_id(0) == 0)
+    def _():
+        for k, block_ref in enumerate(blocks):
+            rows = block_ref.shape[0]
+            all_ref[pl.ds(pl.multiple_of(place_ref[k] * rows, rows), rows), :] = block_ref[...]
+
+    part = dot(all_ref[...], slab_ref[...], ((1,), (0,))) * scale
+    part = part.T.reshape(-1, 2, fine, all_ref.shape[0])
+    first, second = part[:, 0], part[:, 1]
+    low = place_ref[count] == 0
+    keep_ref[...] = jnp.where(low, first, second)
+    send_ref[...] = jnp.where(low, second, first)
+
+
+def back_part(slab, blocks, places, core, scale, fine):
+    count = len(blocks)
+    depth, total = slab.shape
+    rows = blocks[0].shape[0]
+    step = min(total, 256)
+    out = pl.BlockSpec((step // (2 * fine), fine, count * rows), lambda i, _: (i, 0, 0))
+    shape = jax.ShapeDtypeStruct((total // (2 * fine), fine, count * rows), F32)
+    return pl.pallas_call(
+        lambda *refs: back_kernel(*refs, count=count, scale=scale, fine=fine),
+        grid_spec=pltpu.PrefetchScalarGridSpec(
+            num_scalar_prefetch=1,
+            grid=(total // step,),
+            in_specs=[pl.BlockSpec((depth, step), lambda i, _: (0, i))]
+            + [pl.BlockSpec((rows, depth), lambda i, _: (0, 0))] * count,
+            out_specs=[out, out],
+            scratch_shapes=[pltpu.VMEM((count * rows, depth), BF16)],
+        ),
+        out_shape=[shape, shape],
+        compiler_params=pltpu.CompilerParams(vmem_limit_bytes=VMEM),
+        cost_estimate=pl.CostEstimate(flops=0, bytes_accessed=0, transcendentals=0),
+        name="back_part",
+    )(jnp.stack(places + [core]).astype(jnp.int32), slab, *blocks)
+
+
+def spread_kernel(token_ref, block_ref, out_ref):
+    del token_ref
+    out_ref[...] = jnp.broadcast_to(block_ref[...].astype(out_ref.dtype)[None], out_ref.shape)
+
+
+def spread(token, block, count):
+    return pl.pallas_call(
+        spread_kernel,
+        grid=(1,),
+        in_specs=[
+            pl.BlockSpec((8, LANES), lambda i: (0, 0)),
+            pl.BlockSpec(block.shape, lambda i: (0, 0)),
+        ],
+        out_specs=pl.BlockSpec((count,) + block.shape, lambda i: (0, 0, 0)),
+        out_shape=jax.ShapeDtypeStruct((count,) + block.shape, BF16),
+        cost_estimate=pl.CostEstimate(flops=0, bytes_accessed=0, transcendentals=0),
+        name="spread",
+    )(token, block)
+
+
+def product_kernel(token_ref, left_ref, right_ref, out_ref, *, scale):
+    del token_ref
+    part = dot(left_ref[...], right_ref[...], ((1,), (1,))) * scale
+    out_ref[...] = part.astype(out_ref.dtype)
+
+
+def product(token, left, right, scale):
+    rows, depth = left.shape
+    step = min(rows, 256)
+    return pl.pallas_call(
+        lambda *refs: product_kernel(*refs, scale=scale),
+        grid=(rows // step,),
+        in_specs=[
+            pl.BlockSpec((8, LANES), lambda i: (0, 0)),
+            pl.BlockSpec((step, depth), lambda i: (i, 0)),
+            pl.BlockSpec(right.shape, lambda i: (0, 0)),
+        ],
+        out_specs=pl.BlockSpec((step, right.shape[0]), lambda i: (i, 0)),
+        out_shape=jax.ShapeDtypeStruct((rows, right.shape[0]), BF16),
+        cost_estimate=pl.CostEstimate(flops=0, bytes_accessed=0, transcendentals=0),
+        name="product",
+    )(token, left, right)
 
 
 def on_device(ligand_slab, protein_slab, protein_orbitals, ligand_orbitals, *, sizes):
@@ -118,13 +223,11 @@
     a_got = exchange(a_sent.reshape(n_zy, pro, wide + LANES), ZY)
     codes = a_got[:, :1, wide : wide + 1].astype(F32)
     a_own = jnp.sum(a_got[:, :, :wide].astype(F32) * jnp.exp2(codes - 15.0), axis=0)
-    a_block = jnp.broadcast_to(a_own.astype(BF16)[None], (n_zy, pro, wide))
-    a_all = exchange(a_block, ZY).reshape(n_zy * pro, wide)
-
-    b_part = dot(after(ligand_orbitals, a_sent), y, ((1,), (1,))).astype(BF16)
+
+    b_part = cross_part(a_sent[:8, :LANES].astype(F32), ligand_orbitals, y)
     b_own = direct_sum(b_part.reshape(n_aa, lig, fit * pro), AA, aa)
-    b_block = after(b_own, a_own).astype(BF16)
-    b_all = direct_gather(b_block, AA, aa).reshape(n_aa * lig, fit * pro)
+    a_all = exchange(spread(b_own, a_own, n_zy), ZY).reshape(n_zy * pro, wide)
+    b_blocks, b_places = direct_gather(b_own.astype(BF16), AA, aa)
 
     pair = jnp.sum(
         jnp.transpose(a_own.reshape(pro, fit, lig), (1, 2, 0))
@@ -135,11 +238,10 @@
 
     scale_ligand = 1.0 / math.sqrt(fit * pro_total)
     rows_b = nus // (2 * n_zy)
-    back_b = dot(y, b_all, ((0,), (1,))) * scale_ligand
-    back_b = pair_sum(back_b.reshape(n_zy, 2, rows_b, lig_total), "c")
-    back_b = pair_sum(back_b.reshape(n_z, n_yl, rows_b, lig_total), "yl")
-    back_b = after(back_b.reshape(n_z * rows_b, lig_total), a_all)
-    ligand_back = direct_sum(back_b.reshape(n_z, rows_b, lig_total), ("z",), (n_z,))
+    keep, send = back_part(y, b_blocks, b_places, core, scale_ligand, rows_b)
+    back_b = keep + other(send, "c")
+    ligand_back = direct_sum(back_b.reshape(n_z, n_yl * rows_b, lig_total), ("z",), (n_z,))
+    ligand_back = pair_sum(ligand_back.reshape(1, n_yl, rows_b, lig_total), "yl").reshape(rows_b, lig_total)
 
     scale_protein = 1.0 / math.sqrt(fit * lig_total)
     half = n_zy * pro
@@ -147,7 +249,7 @@
     x_chip = jnp.stack(
         [x_own.T.reshape(n_aa, rows, wide), x_other.T.reshape(n_aa, rows, wide)], axis=1
     ).reshape(2 * mus, wide)
-    back_a = (dot(x_chip, a_all, ((1,), (1,))) * scale_protein).astype(BF16)
+    back_a = product(back_b.reshape(n_zy * rows_b, lig_total), x_chip, a_all, scale_protein)
     back_a = exchange(back_a.reshape(n_aa, 2, rows, half), AA)
     here, away = jnp.sum(back_a.astype(F32), axis=0)
     there = other(away, "c")

time: 151 us -> 147 us (0.974)
  the two profiles are of different devices: /device:TPU:16 before, /device:TPU:1 now
where the time goes in v5:
time: 147 us
  starting transfers between devices  67.5 us (46%)
  waiting for transfers between devices  27.1 us (18%)
  Pallas kernels  24.3 us (17%)
  other arithmetic  12.6 us (9%)
  local copies, waits for them, and re-layouts  11.2 us (8%)
  between operations  2.36 us (2%)
  matrix products  1.48 us (1%)
    ppermute x14, starting transfers between devices, direct_sum(): total = total + lax.ppermute(piece, axes, moved(sizes, shift)).astype(F32)  26.2 us
    ppermute x14, waiting for transfers between devices, direct_sum(): total = total + lax.ppermute(piece, axes, moved(sizes, shift)).astype(F32)  20.9 us
    all_to_all x3, starting transfers between devices, exchange(): return lax.all_to_all(pieces, axes, 0, 0, tiled=True)  18.2 us
    ppermute x7, starting transfers between devices, direct_gather(): blocks.append(lax.ppermute(block, axes, moved(sizes, shift)))  12.4 us
    ppermute x6, starting transfers between devices, other(): return lax.ppermute(block, axis, [(0, 1), (1, 0)])  10.7 us
    pallas_call x1, Pallas kernels, back_part(): pl.pallas_call(lambda *refs: back_kernel(*refs, count=count, scale=scale,...  8.9 us
    pallas_call x1, Pallas kernels, cross_part(): pl.pallas_call(cross_kernel, grid=(rows // step,), in_specs=[pl.BlockSpec...  8.56 us
    pallas_call x1, Pallas kernels, product(): pl.pallas_call(lambda *refs: product_kernel(*refs, scale=scale), grid=(ro...  4.84 us
  transfers between devices with their start and end apart: 30, of which 12 were waited for; matrix products, arithmetic and copies ran while one was open for 12% of the time, Pallas kernels for 12%

profile of v5, /device:TPU:1, one launch (start us, length us, event | category | flops | bytes accessed | tf_op | source)
XLA Modules:
  0.0 146.5 jit_solution(9628699518364632519)
XLA Ops:
  2.1 3.3 %collective-permute-start = (bf16[512,512]{1,0:T(8,128)(2,1)S(1)}, bf16[512,512]{1,0:T(8,128)(2,1)S(1)}, u32[]{:S(2)}, u32[]{:S(2)}) collective-permute-start(bf16[512,512]{1,0:T(8,128)(2,1)S(1)} %bitcast.125), channel_id=1, source_target_pairs={{0,1},{1,0},{2,3},{3,2},{4,5},{5,4},{6,7},{7,6},{8,9},{9,8},{10,11... | collective-permute-start | bytes 1572872 | tf_op jit(solution)/shard_map/ppermute | solution.py:68
  14.0 7.6 %all-to-all-start = ((f16[16,32,1152]{2,1,0:T(8,128)(2,1)}), f16[16,32,1152]{2,1,0:T(8,128)(2,1)S(1)}, u32[]{:S(2)}, u32[]{:S(2)}) async-start(f16[16,32,1152]{2,1,0:T(8,128)(2,1)} %bitcast.8), calls=%async_computation | async-start | bytes 2359296 | tf_op jit(solution)/shard_map/all_to_all | solution.py:22
  22.2 8.6 %cross_part.1 = bf16[128,2048]{1,0:T(8,128)(2,1)} custom-call(f32[8,128]{1,0:T(8,128)} %slice_convert_fusion.token_ref, bf16[128,2048]{1,0:T(8,128)(2,1)} %left_ref.1, bf16[2048,2048]{1,0:T(8,128)(2,1)} %bitcast.103), custom_call_target="tpu_custom_call" | custom-call | tf_op jit(solution)/shard_map/cross_part/pallas_call | solution.py:94
  31.8 4.9 %collective-permute-start.9 = (bf16[16,2048]{1,0:T(8,128)(2,1)S(1)}, bf16[16,2048]{1,0:T(8,128)(2,1)S(1)}, u32[]{:S(2)}, u32[]{:S(2)}) collective-permute-start(bf16[16,2048]{1,0:T(8,128)(2,1)S(1)} %get-tuple-element.31), channel_id=1, source_target_pairs={{0,224},{32,192},{64,32},{96,0},{128,96},{160,64},{192,160},{224,1... | collective-permute-start | bytes 196616 | tf_op jit(solution)/shard_map/ppermute | solution.py:55
  37.6 2.7 %collective-permute-start.6 = (bf16[16,2048]{1,0:T(8,128)(2,1)S(1)}, bf16[16,2048]{1,0:T(8,128)(2,1)S(1)}, u32[]{:S(2)}, u32[]{:S(2)}) collective-permute-start(bf16[16,2048]{1,0:T(8,128)(2,1)S(1)} %get-tuple-element.34), channel_id=1, source_target_pairs={{0,128},{32,160},{64,192},{96,224},{128,0},{160,32},{192,64},{224,... | collective-permute-start | bytes 196616 | tf_op jit(solution)/shard_map/ppermute | solution.py:55
  40.3 3.2 %collective-permute-start.5 = (bf16[16,2048]{1,0:T(8,128)(2,1)S(1)}, bf16[16,2048]{1,0:T(8,128)(2,1)S(1)}, u32[]{:S(2)}, u32[]{:S(2)}) collective-permute-start(bf16[16,2048]{1,0:T(8,128)(2,1)S(1)} %get-tuple-element.35), channel_id=1, source_target_pairs={{0,96},{32,64},{64,160},{96,128},{128,224},{160,192},{192,32},{224... | collective-permute-start | bytes 196616 | tf_op jit(solution)/shard_map/ppermute | solution.py:55
  44.8 3.6 %collective-permute-done.5 = bf16[16,2048]{1,0:T(8,128)(2,1)S(1)} collective-permute-done((bf16[16,2048]{1,0:T(8,128)(2,1)S(1)}, bf16[16,2048]{1,0:T(8,128)(2,1)S(1)}, u32[]{:S(2)}, u32[]{:S(2)}) %collective-permute-start.5) | collective-permute-done | bytes 65568 | tf_op jit(solution)/shard_map/ppermute | solution.py:55
  48.5 7.0 %collective-permute-done.3 = bf16[16,2048]{1,0:T(8,128)(2,1)S(1)} collective-permute-done((bf16[16,2048]{1,0:T(8,128)(2,1)S(1)}, bf16[16,2048]{1,0:T(8,128)(2,1)S(1)}, u32[]{:S(2)}, u32[]{:S(2)}) %collective-permute-start.3) | collective-permute-done | bytes 65568 | tf_op jit(solution)/shard_map/ppermute | solution.py:55
  55.5 1.6 %fusion.14 = (bf16[16,2048]{1,0:T(8,128)(2,1)S(1)}, f32[16,2048]{1,0:T(8,128)}) fusion(bf16[16,2048]{1,0:T(8,128)(2,1)S(1)} %collective-permute-done.9, bf16[16,2048]{1,0:T(8,128)(2,1)S(1)} %collective-permute-done.8, bf16[16,2048]{1,0:T(8,128)(2,1)S(1)} %collective-permute-done.7, bf16[16,2048]{1,0:T(8,128)(2,1)S(1)} %collective-permute-done.6, ...), kind=kLoop, calls=%fused_computation.48 | loop fusion | flops 524288 | bytes 720900 | tf_op jit(solution)/shard_map/convert_element_type | solution.py:230
  58.1 2.0 %spread.1 = bf16[16,32,1024]{2,1,0:T(8,128)(2,1)} custom-call(f32[16,2048]{1,0:T(8,128)} %get-tuple-element.20.token_ref, f32[32,1024]{1,0:T(8,128)} %multiply_reduce_fusion.block_ref), custom_call_target="tpu_custom_call" | custom-call | tf_op jit(solution)/shard_map/spread/pallas_call | solution.py:157
  60.1 6.6 %all-to-all-start.1 = ((bf16[16,32,1024]{2,1,0:T(8,128)(2,1)}), bf16[16,32,1024]{2,1,0:T(8,128)(2,1)S(1)}, u32[]{:S(2)}, u32[]{:S(2)}) async-start(bf16[16,32,1024]{2,1,0:T(8,128)(2,1)} %spread.1), calls=%async_computation.1 | async-start | bytes 2097152 | tf_op jit(solution)/shard_map/all_to_all | solution.py:22
  66.6 1.5 %collective-permute-start.10 = (bf16[16,2048]{1,0:T(8,128)(2,1)S(1)}, bf16[16,2048]{1,0:T(8,128)(2,1)S(1)}, u32[]{:S(2)}, u32[]{:S(2)}) collective-permute-start(bf16[16,2048]{1,0:T(8,128)(2,1)S(1)} %get-tuple-element.19.refs_2_), channel_id=1, source_target_pairs={{0,32},{32,0},{64,96},{96,64},{128,160},{160,128},{192,224},{224,1... | collective-permute-start | bytes 196616 | tf_op jit(solution)/shard_map/ppermute | solution.py:62
  70.7 2.5 %collective-permute-start.13 = (bf16[16,2048]{1,0:T(8,128)(2,1)S(1)}, bf16[16,2048]{1,0:T(8,128)(2,1)S(1)}, u32[]{:S(2)}, u32[]{:S(2)}) collective-permute-start(bf16[16,2048]{1,0:T(8,128)(2,1)S(1)} %get-tuple-element.19.refs_2_), channel_id=1, source_target_pairs={{0,128},{32,160},{64,192},{96,224},{128,0},{160,32},{192,64},{224,... | collective-permute-start | bytes 196616 | tf_op jit(solution)/shard_map/ppermute | solution.py:62
  73.3 1.9 %collective-permute-start.14 = (bf16[16,2048]{1,0:T(8,128)(2,1)S(1)}, bf16[16,2048]{1,0:T(8,128)(2,1)S(1)}, u32[]{:S(2)}, u32[]{:S(2)}) collective-permute-start(bf16[16,2048]{1,0:T(8,128)(2,1)S(1)} %get-tuple-element.19.refs_2_), channel_id=1, source_target_pairs={{0,160},{32,128},{64,224},{96,192},{128,32},{160,0},{192,96},{224,... | collective-permute-start | bytes 196616 | tf_op jit(solution)/shard_map/ppermute | solution.py:62
  75.1 2.3 %collective-permute-start.15 = (bf16[16,2048]{1,0:T(8,128)(2,1)S(1)}, bf16[16,2048]{1,0:T(8,128)(2,1)S(1)}, u32[]{:S(2)}, u32[]{:S(2)}) collective-permute-start(bf16[16,2048]{1,0:T(8,128)(2,1)S(1)} %get-tuple-element.19.refs_2_), channel_id=1, source_target_pairs={{0,192},{32,224},{64,0},{96,32},{128,64},{160,96},{192,128},{224,1... | collective-permute-start | bytes 196616 | tf_op jit(solution)/shard_map/ppermute | solution.py:62
  77.4 1.6 %collective-permute-start.16 = (bf16[16,2048]{1,0:T(8,128)(2,1)S(1)}, bf16[16,2048]{1,0:T(8,128)(2,1)S(1)}, u32[]{:S(2)}, u32[]{:S(2)}) collective-permute-start(bf16[16,2048]{1,0:T(8,128)(2,1)S(1)} %get-tuple-element.19.refs_2_), channel_id=1, source_target_pairs={{0,224},{32,192},{64,32},{96,0},{128,96},{160,64},{192,160},{224,1... | collective-permute-start | bytes 196616 | tf_op jit(solution)/shard_map/ppermute | solution.py:62
  80.3 3.4 %collective-permute-done.16.refs_9_ = bf16[16,2048]{1,0:T(8,128)(2,1)S(1)} collective-permute-done((bf16[16,2048]{1,0:T(8,128)(2,1)S(1)}, bf16[16,2048]{1,0:T(8,128)(2,1)S(1)}, u32[]{:S(2)}, u32[]{:S(2)}) %collective-permute-start.16) | collective-permute-done | bytes 65568 | tf_op jit(solution)/shard_map/ppermute | solution.py:62
  84.3 8.9 %back_part.1 = (f32[16,64,128]{2,1,0:T(8,128)}, f32[16,64,128]{2,1,0:T(8,128)}) custom-call(s32[9]{0:T(128)} %stack.60.refs_0_, bf16[2048,2048]{1,0:T(8,128)(2,1)} %bitcast.104, bf16[16,2048]{1,0:T(8,128)(2,1)} %copy-done.10, bf16[16,2048]{1,0:T(8,128)(2,1)} %copy-done.11, bf16[16,2048]{1,0:T(8,128)(2,1)} %copy-done.12, bf16[16,2048]{1,0:T(8,128)(2,1)} %copy-done.13, ...), custom_call_target="tpu_custom_call" | custom-call | tf_op jit(solution)/shard_map/back_part/pallas_call | solution.py:134
  93.2 3.7 %collective-permute-start.17 = (f32[16,64,128]{2,1,0:T(8,128)}, f32[16,64,128]{2,1,0:T(8,128)}, u32[]{:S(2)}, u32[]{:S(2)}) collective-permute-start(f32[16,64,128]{2,1,0:T(8,128)} %get-tuple-element.6), channel_id=1, source_target_pairs={{0,1},{1,0},{2,3},{3,2},{4,5},{5,4},{6,7},{7,6},{8,9},{9,8},{10,11... | collective-permute-start | bytes 1572872 | tf_op jit(solution)/shard_map/ppermute | solution.py:68
  99.6 2.8 %pad_maximum_fusion = bf16[8,2,64,1024]{3,2,1,0:T(8,128)(2,1)} fusion(bf16[8,1,64,1024]{3,2,1,0:T(8,128)(2,1)} %bitcast.117, bf16[8,1,64,1024]{3,2,1,0:T(8,128)(2,1)S(1)} %bitcast.116), kind=kLoop, calls=%fused_computation | loop fusion | flops 1048576 | bytes 4194304 | tf_op jit(solution)/shard_map/stack | solution.py:249
  102.4 1.9 %add.257 = f32[16,64,128]{2,1,0:T(8,128)} add(f32[16,64,128]{2,1,0:T(8,128)S(1)} %copy-done.9, f32[16,64,128]{2,1,0:T(8,128)} %collective-permute-done.17) | non-fusion elementwise | flops 131072 | bytes 1572864 | tf_op jit(solution)/shard_map/add | solution.py:242
  105.3 4.8 %product.1 = bf16[1024,512]{1,0:T(8,128)(2,1)} custom-call(f32[1024,128]{1,0:T(8,128)} %bitcast.109, bf16[1024,1024]{1,0:T(8,128)(2,1)} %bitcast.108, bf16[512,1024]{1,0:T(8,128)(2,1)} %bitcast.114), custom_call_target="tpu_custom_call" | custom-call | tf_op jit(solution)/shard_map/product/pallas_call | solution.py:180
  110.2 4.1 %all-to-all-start.2 = ((bf16[8,2,64,512]{3,2,1,0:T(8,128)(2,1)}), bf16[8,2,64,512]{3,2,1,0:T(8,128)(2,1)S(1)}, u32[]{:S(2)}, u32[]{:S(2)}) async-start(bf16[8,2,64,512]{3,2,1,0:T(8,128)(2,1)} %bitcast.115), calls=%async_computation.2 | async-start | bytes 2097152 | tf_op jit(solution)/shard_map/all_to_all | solution.py:22
  114.3 3.2 %collective-permute-start.24 = (f32[128,128]{1,0:T(8,128)S(1)}, f32[128,128]{1,0:T(8,128)S(1)}, u32[]{:S(2)}, u32[]{:S(2)}) collective-permute-start(f32[128,128]{1,0:T(8,128)S(1)} %get-tuple-element.24), channel_id=1, source_target_pairs={{0,28},{4,0},{8,4},{12,8},{16,12},{20,16},{24,20},{28,24},{1,29},{... | collective-permute-start | bytes 196616 | tf_op jit(solution)/shard_map/ppermute | solution.py:55
  117.5 2.1 %collective-permute-start.23 = (f32[128,128]{1,0:T(8,128)S(1)}, f32[128,128]{1,0:T(8,128)S(1)}, u32[]{:S(2)}, u32[]{:S(2)}) collective-permute-start(f32[128,128]{1,0:T(8,128)S(1)} %get-tuple-element.25), channel_id=1, source_target_pairs={{0,24},{4,28},{8,0},{12,4},{16,8},{20,12},{24,16},{28,20},{1,25},{... | collective-permute-start | bytes 196616 | tf_op jit(solution)/shard_map/ppermute | solution.py:55
  119.6 1.9 %collective-permute-start.22 = (f32[128,128]{1,0:T(8,128)S(1)}, f32[128,128]{1,0:T(8,128)S(1)}, u32[]{:S(2)}, u32[]{:S(2)}) collective-permute-start(f32[128,128]{1,0:T(8,128)S(1)} %get-tuple-element.26), channel_id=1, source_target_pairs={{0,20},{4,24},{8,28},{12,0},{16,4},{20,8},{24,12},{28,16},{1,21},{... | collective-permute-start | bytes 196616 | tf_op jit(solution)/shard_map/ppermute | solution.py:55
  121.5 2.8 %collective-permute-start.21 = (f32[128,128]{1,0:T(8,128)S(1)}, f32[128,128]{1,0:T(8,128)S(1)}, u32[]{:S(2)}, u32[]{:S(2)}) collective-permute-start(f32[128,128]{1,0:T(8,128)S(1)} %get-tuple-element.27), channel_id=1, source_target_pairs={{0,16},{4,20},{8,24},{12,28},{16,0},{20,4},{24,8},{28,12},{1,17},{... | collective-permute-start | bytes 196616 | tf_op jit(solution)/shard_map/ppermute | solution.py:55
  124.6 3.6 %collective-permute-start.19 = (f32[128,128]{1,0:T(8,128)S(1)}, f32[128,128]{1,0:T(8,128)S(1)}, u32[]{:S(2)}, u32[]{:S(2)}) collective-permute-start(f32[128,128]{1,0:T(8,128)S(1)} %get-tuple-element.29), channel_id=1, source_target_pairs={{0,8},{4,12},{8,16},{12,20},{16,24},{20,28},{24,0},{28,4},{1,9},{5... | collective-permute-start | bytes 196616 | tf_op jit(solution)/shard_map/ppermute | solution.py:55
  129.4 5.9 %collective-permute-done.20 = f32[128,128]{1,0:T(8,128)S(1)} collective-permute-done((f32[128,128]{1,0:T(8,128)S(1)}, f32[128,128]{1,0:T(8,128)S(1)}, u32[]{:S(2)}, u32[]{:S(2)}) %collective-permute-start.20) | collective-permute-done | bytes 65568 | tf_op jit(solution)/shard_map/ppermute | solution.py:55
  135.9 1.9 %collective-permute-done.18 = f32[128,128]{1,0:T(8,128)S(1)} collective-permute-done((f32[128,128]{1,0:T(8,128)S(1)}, f32[128,128]{1,0:T(8,128)S(1)}, u32[]{:S(2)}, u32[]{:S(2)}) %collective-permute-start.18) | collective-permute-done | bytes 65568 | tf_op jit(solution)/shard_map/ppermute | solution.py:55
  138.8 1.9 %collective-permute-done.25 = f32[1,64,128]{2,1,0:T(8,128)S(1)} collective-permute-done((f32[1,64,128]{2,1,0:T(8,128)S(1)}, f32[1,64,128]{2,1,0:T(8,128)S(1)}, u32[]{:S(2)}, u32[]{:S(2)}) %collective-permute-start.25) | collective-permute-done | bytes 32800 | tf_op jit(solution)/shard_map/ppermute | solution.py:68
  142.0 2.4 %collective-permute-start.26 = (f32[64,512]{1,0:T(8,128)S(1)}, f32[64,512]{1,0:T(8,128)S(1)}, u32[]{:S(2)}, u32[]{:S(2)}) collective-permute-start(f32[64,512]{1,0:T(8,128)S(1)} %get-tuple-element.38), channel_id=1, source_target_pairs={{0,1},{1,0},{2,3},{3,2},{4,5},{5,4},{6,7},{7,6},{8,9},{9,8},{10,11... | collective-permute-start | bytes 393224 | tf_op jit(solution)/shard_map/ppermute | solution.py:68
  (105 shorter events, 28.1 us)
Async XLA Ops:
  2.1 9.6 %collective-permute-start = (bf16[512,512]{1,0:T(8,128)(2,1)S(1)}, bf16[512,512]{1,0:T(8,128)(2,1)S(1)}, u32[]{:S(2)}, u32[]{:S(2)}) collective-permute-start(bf16[512,512]{1,0:T(8,128)(2,1)S(1)} %bitcast.125), channel_id=1, source_target_pairs={{0,1},{1,0},{2,3},{3,2},{4,5},{5,4},{6,7},{7,6},{8,9},{9,8},{10,11... | collective-permute-start | bytes 1572872 | tf_op jit(solution)/shard_map/ppermute | solution.py:68
  5.4 6.3 %collective-permute-start.1 = (bf16[1024,512]{1,0:T(8,128)(2,1)S(1)}, bf16[1024,512]{1,0:T(8,128)(2,1)S(1)}, u32[]{:S(2)}, u32[]{:S(2)}) collective-permute-start(bf16[1024,512]{1,0:T(8,128)(2,1)S(1)} %bitcast.105), channel_id=1, source_target_pairs={{0,1},{1,0},{2,3},{3,2},{4,5},{5,4},{6,7},{7,6},{8,9},{9,8},{10,11... | collective-permute-start | bytes 3145736 | tf_op jit(solution)/shard_map/ppermute | solution.py:68
  8.5 1.2 collective-permute-start.2
  14.0 43.1 %all-to-all-start = ((f16[16,32,1152]{2,1,0:T(8,128)(2,1)}), f16[16,32,1152]{2,1,0:T(8,128)(2,1)S(1)}, u32[]{:S(2)}, u32[]{:S(2)}) async-start(f16[16,32,1152]{2,1,0:T(8,128)(2,1)} %bitcast.8), calls=%async_computation | async-start | bytes 2359296 | tf_op jit(solution)/shard_map/all_to_all | solution.py:22
  31.8 11.7 %collective-permute-start.9 = (bf16[16,2048]{1,0:T(8,128)(2,1)S(1)}, bf16[16,2048]{1,0:T(8,128)(2,1)S(1)}, u32[]{:S(2)}, u32[]{:S(2)}) collective-permute-start(bf16[16,2048]{1,0:T(8,128)(2,1)S(1)} %get-tuple-element.31), channel_id=1, source_target_pairs={{0,224},{32,192},{64,32},{96,0},{128,96},{160,64},{192,160},{224,1... | collective-permute-start | bytes 196616 | tf_op jit(solution)/shard_map/ppermute | solution.py:55
  36.7 6.8 %collective-permute-start.8 = (bf16[16,2048]{1,0:T(8,128)(2,1)S(1)}, bf16[16,2048]{1,0:T(8,128)(2,1)S(1)}, u32[]{:S(2)}, u32[]{:S(2)}) collective-permute-start(bf16[16,2048]{1,0:T(8,128)(2,1)S(1)} %get-tuple-element.32), channel_id=1, source_target_pairs={{0,192},{32,224},{64,0},{96,32},{128,64},{160,96},{192,128},{224,1... | collective-permute-start | bytes 196616 | tf_op jit(solution)/shard_map/ppermute | solution.py:55
  37.3 7.6 %collective-permute-start.7 = (bf16[16,2048]{1,0:T(8,128)(2,1)S(1)}, bf16[16,2048]{1,0:T(8,128)(2,1)S(1)}, u32[]{:S(2)}, u32[]{:S(2)}) collective-permute-start(bf16[16,2048]{1,0:T(8,128)(2,1)S(1)} %get-tuple-element.33), channel_id=1, source_target_pairs={{0,160},{32,128},{64,224},{96,192},{128,32},{160,0},{192,96},{224,... | collective-permute-start | bytes 196616 | tf_op jit(solution)/shard_map/ppermute | solution.py:55
  37.6 7.3 %collective-permute-start.6 = (bf16[16,2048]{1,0:T(8,128)(2,1)S(1)}, bf16[16,2048]{1,0:T(8,128)(2,1)S(1)}, u32[]{:S(2)}, u32[]{:S(2)}) collective-permute-start(bf16[16,2048]{1,0:T(8,128)(2,1)S(1)} %get-tuple-element.34), channel_id=1, source_target_pairs={{0,128},{32,160},{64,192},{96,224},{128,0},{160,32},{192,64},{224,... | collective-permute-start | bytes 196616 | tf_op jit(solution)/shard_map/ppermute | solution.py:55
  40.3 8.2 %collective-permute-start.5 = (bf16[16,2048]{1,0:T(8,128)(2,1)S(1)}, bf16[16,2048]{1,0:T(8,128)(2,1)S(1)}, u32[]{:S(2)}, u32[]{:S(2)}) collective-permute-start(bf16[16,2048]{1,0:T(8,128)(2,1)S(1)} %get-tuple-element.35), channel_id=1, source_target_pairs={{0,96},{32,64},{64,160},{96,128},{128,224},{160,192},{192,32},{224... | collective-permute-start | bytes 196616 | tf_op jit(solution)/shard_map/ppermute | solution.py:55
  43.6 4.9 %collective-permute-start.4 = (bf16[16,2048]{1,0:T(8,128)(2,1)S(1)}, bf16[16,2048]{1,0:T(8,128)(2,1)S(1)}, u32[]{:S(2)}, u32[]{:S(2)}) collective-permute-start(bf16[16,2048]{1,0:T(8,128)(2,1)S(1)} %get-tuple-element.36), channel_id=1, source_target_pairs={{0,64},{32,96},{64,128},{96,160},{128,192},{160,224},{192,0},{224,... | collective-permute-start | bytes 196616 | tf_op jit(solution)/shard_map/ppermute | solution.py:55
  43.6 11.9 %collective-permute-start.3 = (bf16[16,2048]{1,0:T(8,128)(2,1)S(1)}, bf16[16,2048]{1,0:T(8,128)(2,1)S(1)}, u32[]{:S(2)}, u32[]{:S(2)}) collective-permute-start(bf16[16,2048]{1,0:T(8,128)(2,1)S(1)} %get-tuple-element.30), channel_id=1, source_target_pairs={{0,32},{32,0},{64,96},{96,64},{128,160},{160,128},{192,224},{224,1... | collective-permute-start | bytes 196616 | tf_op jit(solution)/shard_map/ppermute | solution.py:55
  60.1 44.2 %all-to-all-start.1 = ((bf16[16,32,1024]{2,1,0:T(8,128)(2,1)}), bf16[16,32,1024]{2,1,0:T(8,128)(2,1)S(1)}, u32[]{:S(2)}, u32[]{:S(2)}) async-start(bf16[16,32,1024]{2,1,0:T(8,128)(2,1)} %spread.1), calls=%async_computation.1 | async-start | bytes 2097152 | tf_op jit(solution)/shard_map/all_to_all | solution.py:22
  66.6 8.5 %collective-permute-start.10 = (bf16[16,2048]{1,0:T(8,128)(2,1)S(1)}, bf16[16,2048]{1,0:T(8,128)(2,1)S(1)}, u32[]{:S(2)}, u32[]{:S(2)}) collective-permute-start(bf16[16,2048]{1,0:T(8,128)(2,1)S(1)} %get-tuple-element.19.refs_2_), channel_id=1, source_target_pairs={{0,32},{32,0},{64,96},{96,64},{128,160},{160,128},{192,224},{224,1... | collective-permute-start | bytes 196616 | tf_op jit(solution)/shard_map/ppermute | solution.py:62
  68.2 9.2 %collective-permute-start.11 = (bf16[16,2048]{1,0:T(8,128)(2,1)S(1)}, bf16[16,2048]{1,0:T(8,128)(2,1)S(1)}, u32[]{:S(2)}, u32[]{:S(2)}) collective-permute-start(bf16[16,2048]{1,0:T(8,128)(2,1)S(1)} %get-tuple-element.19.refs_2_), channel_id=1, source_target_pairs={{0,64},{32,96},{64,128},{96,160},{128,192},{160,224},{192,0},{224,... | collective-permute-start | bytes 196616 | tf_op jit(solution)/shard_map/ppermute | solution.py:62
  69.3 10.3 %collective-permute-start.12 = (bf16[16,2048]{1,0:T(8,128)(2,1)S(1)}, bf16[16,2048]{1,0:T(8,128)(2,1)S(1)}, u32[]{:S(2)}, u32[]{:S(2)}) collective-permute-start(bf16[16,2048]{1,0:T(8,128)(2,1)S(1)} %get-tuple-element.19.refs_2_), channel_id=1, source_target_pairs={{0,96},{32,64},{64,160},{96,128},{128,224},{160,192},{192,32},{224... | collective-permute-start | bytes 196616 | tf_op jit(solution)/shard_map/ppermute | solution.py:62
  70.7 8.9 %collective-permute-start.13 = (bf16[16,2048]{1,0:T(8,128)(2,1)S(1)}, bf16[16,2048]{1,0:T(8,128)(2,1)S(1)}, u32[]{:S(2)}, u32[]{:S(2)}) collective-permute-start(bf16[16,2048]{1,0:T(8,128)(2,1)S(1)} %get-tuple-element.19.refs_2_), channel_id=1, source_target_pairs={{0,128},{32,160},{64,192},{96,224},{128,0},{160,32},{192,64},{224,... | collective-permute-start | bytes 196616 | tf_op jit(solution)/shard_map/ppermute | solution.py:62
  73.3 7.0 %collective-permute-start.14 = (bf16[16,2048]{1,0:T(8,128)(2,1)S(1)}, bf16[16,2048]{1,0:T(8,128)(2,1)S(1)}, u32[]{:S(2)}, u32[]{:S(2)}) collective-permute-start(bf16[16,2048]{1,0:T(8,128)(2,1)S(1)} %get-tuple-element.19.refs_2_), channel_id=1, source_target_pairs={{0,160},{32,128},{64,224},{96,192},{128,32},{160,0},{192,96},{224,... | collective-permute-start | bytes 196616 | tf_op jit(solution)/shard_map/ppermute | solution.py:62
  75.1 5.2 %collective-permute-start.15 = (bf16[16,2048]{1,0:T(8,128)(2,1)S(1)}, bf16[16,2048]{1,0:T(8,128)(2,1)S(1)}, u32[]{:S(2)}, u32[]{:S(2)}) collective-permute-start(bf16[16,2048]{1,0:T(8,128)(2,1)S(1)} %get-tuple-element.19.refs_2_), channel_id=1, source_target_pairs={{0,192},{32,224},{64,0},{96,32},{128,64},{160,96},{192,128},{224,1... | collective-permute-start | bytes 196616 | tf_op jit(solution)/shard_map/ppermute | solution.py:62
  77.4 6.2 %collective-permute-start.16 = (bf16[16,2048]{1,0:T(8,128)(2,1)S(1)}, bf16[16,2048]{1,0:T(8,128)(2,1)S(1)}, u32[]{:S(2)}, u32[]{:S(2)}) collective-permute-start(bf16[16,2048]{1,0:T(8,128)(2,1)S(1)} %get-tuple-element.19.refs_2_), channel_id=1, source_target_pairs={{0,224},{32,192},{64,32},{96,0},{128,96},{160,64},{192,160},{224,1... | collective-permute-start | bytes 196616 | tf_op jit(solution)/shard_map/ppermute | solution.py:62
  93.2 9.2 %collective-permute-start.17 = (f32[16,64,128]{2,1,0:T(8,128)}, f32[16,64,128]{2,1,0:T(8,128)}, u32[]{:S(2)}, u32[]{:S(2)}) collective-permute-start(f32[16,64,128]{2,1,0:T(8,128)} %get-tuple-element.6), channel_id=1, source_target_pairs={{0,1},{1,0},{2,3},{3,2},{4,5},{5,4},{6,7},{7,6},{8,9},{9,8},{10,11... | collective-permute-start | bytes 1572872 | tf_op jit(solution)/shard_map/ppermute | solution.py:68
  110.2 28.5 %copy-start.7 = (f32[16,2048]{1,0:T(8,128)S(1)}, f32[16,2048]{1,0:T(8,128)}, u32[]{:S(2)}) copy-start(f32[16,2048]{1,0:T(8,128)} %get-tuple-element.20.token_ref) | copy-start | bytes 393220
  110.2 31.1 %copy-start.8 = (f32[32,1024]{1,0:T(8,128)S(1)}, f32[32,1024]{1,0:T(8,128)}, u32[]{:S(2)}) copy-start(f32[32,1024]{1,0:T(8,128)} %multiply_reduce_fusion.block_ref) | copy-start | bytes 393220
  110.2 31.6 %all-to-all-start.2 = ((bf16[8,2,64,512]{3,2,1,0:T(8,128)(2,1)}), bf16[8,2,64,512]{3,2,1,0:T(8,128)(2,1)S(1)}, u32[]{:S(2)}, u32[]{:S(2)}) async-start(bf16[8,2,64,512]{3,2,1,0:T(8,128)(2,1)} %bitcast.115), calls=%async_computation.2 | async-start | bytes 2097152 | tf_op jit(solution)/shard_map/all_to_all | solution.py:22
  114.3 10.4 %collective-permute-start.24 = (f32[128,128]{1,0:T(8,128)S(1)}, f32[128,128]{1,0:T(8,128)S(1)}, u32[]{:S(2)}, u32[]{:S(2)}) collective-permute-start(f32[128,128]{1,0:T(8,128)S(1)} %get-tuple-element.24), channel_id=1, source_target_pairs={{0,28},{4,0},{8,4},{12,8},{16,12},{20,16},{24,20},{28,24},{1,29},{... | collective-permute-start | bytes 196616 | tf_op jit(solution)/shard_map/ppermute | solution.py:55
  117.5 10.7 %collective-permute-start.23 = (f32[128,128]{1,0:T(8,128)S(1)}, f32[128,128]{1,0:T(8,128)S(1)}, u32[]{:S(2)}, u32[]{:S(2)}) collective-permute-start(f32[128,128]{1,0:T(8,128)S(1)} %get-tuple-element.25), channel_id=1, source_target_pairs={{0,24},{4,28},{8,0},{12,4},{16,8},{20,12},{24,16},{28,20},{1,25},{... | collective-permute-start | bytes 196616 | tf_op jit(solution)/shard_map/ppermute | solution.py:55
  119.6 8.8 %collective-permute-start.22 = (f32[128,128]{1,0:T(8,128)S(1)}, f32[128,128]{1,0:T(8,128)S(1)}, u32[]{:S(2)}, u32[]{:S(2)}) collective-permute-start(f32[128,128]{1,0:T(8,128)S(1)} %get-tuple-element.26), channel_id=1, source_target_pairs={{0,20},{4,24},{8,28},{12,0},{16,4},{20,8},{24,12},{28,16},{1,21},{... | collective-permute-start | bytes 196616 | tf_op jit(solution)/shard_map/ppermute | solution.py:55
  121.5 7.9 %collective-permute-start.21 = (f32[128,128]{1,0:T(8,128)S(1)}, f32[128,128]{1,0:T(8,128)S(1)}, u32[]{:S(2)}, u32[]{:S(2)}) collective-permute-start(f32[128,128]{1,0:T(8,128)S(1)} %get-tuple-element.27), channel_id=1, source_target_pairs={{0,16},{4,20},{8,24},{12,28},{16,0},{20,4},{24,8},{28,12},{1,17},{... | collective-permute-start | bytes 196616 | tf_op jit(solution)/shard_map/ppermute | solution.py:55
  124.3 11.0 %collective-permute-start.20 = (f32[128,128]{1,0:T(8,128)S(1)}, f32[128,128]{1,0:T(8,128)S(1)}, u32[]{:S(2)}, u32[]{:S(2)}) collective-permute-start(f32[128,128]{1,0:T(8,128)S(1)} %get-tuple-element.28), channel_id=1, source_target_pairs={{0,12},{4,16},{8,20},{12,24},{16,28},{20,0},{24,4},{28,8},{1,13},{... | collective-permute-start | bytes 196616 | tf_op jit(solution)/shard_map/ppermute | solution.py:55
  124.6 11.2 %collective-permute-start.19 = (f32[128,128]{1,0:T(8,128)S(1)}, f32[128,128]{1,0:T(8,128)S(1)}, u32[]{:S(2)}, u32[]{:S(2)}) collective-permute-start(f32[128,128]{1,0:T(8,128)S(1)} %get-tuple-element.29), channel_id=1, source_target_pairs={{0,8},{4,12},{8,16},{12,20},{16,24},{20,28},{24,0},{28,4},{1,9},{5... | collective-permute-start | bytes 196616 | tf_op jit(solution)/shard_map/ppermute | solution.py:55
  128.2 9.5 %collective-permute-start.18 = (f32[128,128]{1,0:T(8,128)S(1)}, f32[128,128]{1,0:T(8,128)S(1)}, u32[]{:S(2)}, u32[]{:S(2)}) collective-permute-start(f32[128,128]{1,0:T(8,128)S(1)} %get-tuple-element.23), channel_id=1, source_target_pairs={{0,4},{4,8},{8,12},{12,16},{16,20},{20,24},{24,28},{28,0},{1,5},{5... | collective-permute-start | bytes 196616 | tf_op jit(solution)/shard_map/ppermute | solution.py:55
  137.8 2.9 %collective-permute-start.25 = (f32[1,64,128]{2,1,0:T(8,128)S(1)}, f32[1,64,128]{2,1,0:T(8,128)S(1)}, u32[]{:S(2)}, u32[]{:S(2)}) collective-permute-start(f32[1,64,128]{2,1,0:T(8,128)S(1)} %dynamic-slice_bitcast_fusion.14), channel_id=1, source_target_pairs={{0,2},{2,0},{1,3},{3,1},{4,6},{6,4},{5,7},{7,5},{8,10},{10,8},{9,1... | collective-permute-start | bytes 98312 | tf_op jit(solution)/shard_map/ppermute | solution.py:68
  142.0 3.4 %collective-permute-start.26 = (f32[64,512]{1,0:T(8,128)S(1)}, f32[64,512]{1,0:T(8,128)S(1)}, u32[]{:S(2)}, u32[]{:S(2)}) collective-permute-start(f32[64,512]{1,0:T(8,128)S(1)} %get-tuple-element.38), channel_id=1, source_target_pairs={{0,1},{1,0},{2,3},{3,2},{4,5},{5,4},{6,7},{7,6},{8,9},{9,8},{10,11... | collective-permute-start | bytes 393224 | tf_op jit(solution)/shard_map/ppermute | solution.py:68
  (16 other events, 75.5 us)

commit v6 on v5

--- a/solution.py
+++ b/solution.py
@@ -15,7 +15,7 @@
 F16 = jnp.float16
 BF16 = jnp.bfloat16
 LANES = 128
-VMEM = 54 * 2**20
+VMEM = 24 * 2**20
 
 
 def exchange(pieces, axes):
@@ -47,12 +47,12 @@
     )
 
 
-def direct_sum(pieces, axes, sizes):
+def direct_sum(pieces, axes, sizes, sent):
     own = (0,) * len(sizes)
     total = lax.dynamic_index_in_dim(pieces, peer(axes, sizes, own), 0, keepdims=False).astype(F32)
     for shift in shifts(sizes):
         piece = lax.dynamic_index_in_dim(pieces, peer(axes, sizes, shift), 0, keepdims=False)
-        total = total + lax.ppermute(piece, axes, moved(sizes, shift)).astype(F32)
+        total = total + lax.ppermute(piece.astype(sent), axes, moved(sizes, shift)).astype(F32)
     return total
 
 
@@ -83,45 +83,58 @@
     return jnp.max(jnp.abs(array)).astype(F32)
 
 
-def cross_kernel(token_ref, left_ref, right_ref, out_ref):
+def cross_kernel(token_ref, left_ref, slab_ref, out_ref, held_ref, sems, *, step):
     del token_ref
-    out_ref[...] = dot(left_ref[...], right_ref[...], ((1,), (1,))).astype(out_ref.dtype)
+    copies = []
+    for i in range(held_ref.shape[0] // step):
+        rows = pl.ds(i * step, step)
+        copies.append(pltpu.make_async_copy(slab_ref.at[rows], held_ref.at[rows], sems.at[i]))
+        copies[i].start()
+    for i, copy in enumerate(copies):
+        rows = pl.ds(i * step, step)
+        copy.wait()
+        part = dot(left_ref[...], held_ref[rows, :], ((1,), (1,)))
+        out_ref[:, rows] = part.astype(out_ref.dtype)
 
 
 def cross_part(token, orbitals, slab):
-    rows, depth = slab.shape
+    rows = slab.shape[0]
     step = min(rows, 256)
     return pl.pallas_call(
-        cross_kernel,
-        grid=(rows // step,),
+        lambda *refs: cross_kernel(*refs, step=step),
         in_specs=[
-            pl.BlockSpec(token.shape, lambda i: (0, 0)),
-            pl.BlockSpec(orbitals.shape, lambda i: (0, 0)),
-            pl.BlockSpec((step, depth), lambda i: (i, 0)),
+            pl.BlockSpec(memory_space=pltpu.VMEM),
+            pl.BlockSpec(memory_space=pltpu.VMEM),
+            pl.BlockSpec(memory_space=pltpu.HBM),
         ],
-        out_specs=pl.BlockSpec((orbitals.shape[0], step), lambda i: (0, i)),
+        out_specs=pl.BlockSpec(memory_space=pltpu.VMEM),
         out_shape=jax.ShapeDtypeStruct((orbitals.shape[0], rows), BF16),
+        scratch_shapes=[pltpu.VMEM(slab.shape, BF16), pltpu.SemaphoreType.DMA((rows // step,))],
         compiler_params=pltpu.CompilerParams(vmem_limit_bytes=VMEM),
         cost_estimate=pl.CostEstimate(flops=0, bytes_accessed=0, transcendentals=0),
         name="cross_part",
     )(token, orbitals, slab)
 
 
-def back_kernel(place_ref, slab_ref, *refs, count, scale, fine):
-    blocks, (keep_ref, send_ref, all_ref) = refs[:count], refs[count:]
-
-    @pl.when(pl.program_id(0) == 0)
-    def _():
-        for k, block_ref in enumerate(blocks):
-            rows = block_ref.shape[0]
-            all_ref[pl.ds(pl.multiple_of(place_ref[k] * rows, rows), rows), :] = block_ref[...]
-
-    part = dot(all_ref[...], slab_ref[...], ((1,), (0,))) * scale
-    part = part.T.reshape(-1, 2, fine, all_ref.shape[0])
-    first, second = part[:, 0], part[:, 1]
+def back_kernel(place_ref, slab_ref, *refs, count, scale, fine, step):
+    blocks, (keep_ref, send_ref, all_ref, held_ref, sems) = refs[:count], refs[count:]
+    copies = []
+    for i in range(held_ref.shape[0]):
+        columns = pl.ds(i * step, step)
+        copies.append(pltpu.make_async_copy(slab_ref.at[:, columns], held_ref.at[i], sems.at[i]))
+        copies[i].start()
+    for k, block_ref in enumerate(blocks):
+        rows = block_ref.shape[0]
+        all_ref[pl.ds(pl.multiple_of(place_ref[k] * rows, rows), rows), :] = block_ref[...]
     low = place_ref[count] == 0
-    keep_ref[...] = jnp.where(low, first, second)
-    send_ref[...] = jnp.where(low, second, first)
+    runs = step // (2 * fine)
+    for i, copy in enumerate(copies):
+        copy.wait()
+        part = dot(all_ref[...], held_ref[i], ((1,), (0,))) * scale
+        part = part.T.reshape(runs, 2, fine, all_ref.shape[0])
+        first, second = part[:, 0], part[:, 1]
+        keep_ref[pl.ds(i * runs, runs)] = jnp.where(low, first, second)
+        send_ref[pl.ds(i * runs, runs)] = jnp.where(low, second, first)
 
 
 def back_part(slab, blocks, places, core, scale, fine):
@@ -129,19 +142,19 @@
     depth, total = slab.shape
     rows = blocks[0].shape[0]
     step = min(total, 256)
-    out = pl.BlockSpec((step // (2 * fine), fine, count * rows), lambda i, _: (i, 0, 0))
     shape = jax.ShapeDtypeStruct((total // (2 * fine), fine, count * rows), F32)
-    return pl.pallas_call(
-        lambda *refs: back_kernel(*refs, count=count, scale=scale, fine=fine),
-        grid_spec=pltpu.PrefetchScalarGridSpec(
-            num_scalar_prefetch=1,
-            grid=(total // step,),
-            in_specs=[pl.BlockSpec((depth, step), lambda i, _: (0, i))]
-            + [pl.BlockSpec((rows, depth), lambda i, _: (0, 0))] * count,
-            out_specs=[out, out],
-            scratch_shapes=[pltpu.VMEM((count * rows, depth), BF16)],
-        ),
+    whole = pl.BlockSpec(memory_space=pltpu.VMEM)
+    return pl.pallas_call(
+        lambda *refs: back_kernel(*refs, count=count, scale=scale, fine=fine, step=step),
+        in_specs=[pl.BlockSpec(memory_space=pltpu.SMEM), pl.BlockSpec(memory_space=pltpu.HBM)]
+        + [whole] * count,
+        out_specs=[whole, whole],
         out_shape=[shape, shape],
+        scratch_shapes=[
+            pltpu.VMEM((count * rows, depth), BF16),
+            pltpu.VMEM((total // step, depth, step), BF16),
+            pltpu.SemaphoreType.DMA((total // step,)),
+        ],
         compiler_params=pltpu.CompilerParams(vmem_limit_bytes=VMEM),
         cost_estimate=pl.CostEstimate(flops=0, bytes_accessed=0, transcendentals=0),
         name="back_part",
@@ -168,28 +181,31 @@
     )(token, block)
 
 
-def product_kernel(token_ref, left_ref, right_ref, out_ref, *, scale):
+def product_kernel(token_ref, own_ref, other_ref, right_ref, out_ref, *, scale, step):
     del token_ref
-    part = dot(left_ref[...], right_ref[...], ((1,), (1,))) * scale
-    out_ref[...] = part.astype(out_ref.dtype)
-
-
-def product(token, left, right, scale):
-    rows, depth = left.shape
-    step = min(rows, 256)
-    return pl.pallas_call(
-        lambda *refs: product_kernel(*refs, scale=scale),
-        grid=(rows // step,),
-        in_specs=[
-            pl.BlockSpec((8, LANES), lambda i: (0, 0)),
-            pl.BlockSpec((step, depth), lambda i: (i, 0)),
-            pl.BlockSpec(right.shape, lambda i: (0, 0)),
-        ],
-        out_specs=pl.BlockSpec((step, right.shape[0]), lambda i: (i, 0)),
-        out_shape=jax.ShapeDtypeStruct((rows, right.shape[0]), BF16),
+    runs = step // out_ref.shape[2]
+    for i in range(own_ref.shape[1] // step):
+        columns = pl.ds(i * step, step)
+        for k, left_ref in enumerate((own_ref, other_ref)):
+            part = dot(right_ref[...], left_ref[:, columns], ((1,), (0,))) * scale
+            part = part.T.reshape(runs, out_ref.shape[2], right_ref.shape[0])
+            out_ref[pl.ds(i * runs, runs), k] = part.astype(out_ref.dtype)
+
+
+def product(token, own, other_core, right, scale, fine):
+    total = own.shape[1]
+    step = min(total, 256)
+    whole = pl.BlockSpec(memory_space=pltpu.VMEM)
+    return pl.pallas_call(
+        lambda *refs: product_kernel(*refs, scale=scale, step=step),
+        grid=(1,),
+        in_specs=[pl.BlockSpec((8, LANES), lambda i: (0, 0)), whole, whole, whole],
+        out_specs=whole,
+        out_shape=jax.ShapeDtypeStruct((total // fine, 2, fine, right.shape[0]), BF16),
+        compiler_params=pltpu.CompilerParams(vmem_limit_bytes=VMEM),
         cost_estimate=pl.CostEstimate(flops=0, bytes_accessed=0, transcendentals=0),
         name="product",
-    )(token, left, right)
+    )(token, own, other_core, right)
 
 
 def on_device(ligand_slab, protein_slab, protein_orbitals, ligand_orbitals, *, sizes):
@@ -211,21 +227,21 @@
     orb_send = lax.dynamic_index_in_dim(orb, 1 - core, 1, keepdims=False).reshape(n_zy * pro, mus)
     orb_other = other(orb_send, "c")
 
-    tops = jnp.broadcast_to(
-        jnp.stack([largest(x_own), largest(protein_orbitals)])[:, None], (2, LANES)
-    )
-    tops = jnp.maximum(tops, other(tops, "c"))[:, 0]
-    bound = (2.0 * mus) * tops[0] * tops[1]
+    tops = jnp.stack([largest(x_own), largest(protein_orbitals)])
+    tops = jnp.broadcast_to(tops[:, None], (2, wide + LANES))
+    tops = jnp.maximum(tops, other(tops, "c"))
+    bound = (2.0 * mus) * tops[:1] * tops[1:]
     code = jnp.ceil(jnp.log2(jnp.maximum(bound, 1e-30))) + 1.0
     a_part = dot(orb_own, x_own, ((1,), (1,))) + dot(orb_other, x_other, ((1,), (1,)))
-    a_sent = (a_part * jnp.exp2(15.0 - code)).astype(F16)
-    a_sent = jnp.concatenate([a_sent, jnp.broadcast_to(code.astype(F16), (n_zy * pro, LANES))], axis=1)
+    a_sent = (a_part * jnp.exp2(15.0 - code[:, :wide])).astype(F16)
+    code = jnp.broadcast_to(code[:, wide:].astype(F16), (n_zy * pro, LANES))
+    a_sent = jnp.concatenate([a_sent, code], axis=1)
     a_got = exchange(a_sent.reshape(n_zy, pro, wide + LANES), ZY)
     codes = a_got[:, :1, wide : wide + 1].astype(F32)
     a_own = jnp.sum(a_got[:, :, :wide].astype(F32) * jnp.exp2(codes - 15.0), axis=0)
 
     b_part = cross_part(a_sent[:8, :LANES].astype(F32), ligand_orbitals, y)
-    b_own = direct_sum(b_part.reshape(n_aa, lig, fit * pro), AA, aa)
+    b_own = direct_sum(b_part.reshape(n_aa, lig, fit * pro), AA, aa, BF16)
     a_all = exchange(spread(b_own, a_own, n_zy), ZY).reshape(n_zy * pro, wide)
     b_blocks, b_places = direct_gather(b_own.astype(BF16), AA, aa)
 
@@ -240,17 +256,14 @@
     rows_b = nus // (2 * n_zy)
     keep, send = back_part(y, b_blocks, b_places, core, scale_ligand, rows_b)
     back_b = keep + other(send, "c")
-    ligand_back = direct_sum(back_b.reshape(n_z, n_yl * rows_b, lig_total), ("z",), (n_z,))
+    ligand_back = direct_sum(back_b.reshape(n_z, n_yl * rows_b, lig_total), ("z",), (n_z,), BF16)
     ligand_back = pair_sum(ligand_back.reshape(1, n_yl, rows_b, lig_total), "yl").reshape(rows_b, lig_total)
 
     scale_protein = 1.0 / math.sqrt(fit * lig_total)
-    half = n_zy * pro
     rows = mus // n_aa
-    x_chip = jnp.stack(
-        [x_own.T.reshape(n_aa, rows, wide), x_other.T.reshape(n_aa, rows, wide)], axis=1
-    ).reshape(2 * mus, wide)
-    back_a = product(back_b.reshape(n_zy * rows_b, lig_total), x_chip, a_all, scale_protein)
-    back_a = exchange(back_a.reshape(n_aa, 2, rows, half), AA)
+    token = back_b.reshape(n_zy * rows_b, lig_total)
+    back_a = product(token, x_own, x_other, a_all, scale_protein, rows)
+    back_a = exchange(back_a, AA)
     here, away = jnp.sum(back_a.astype(F32), axis=0)
     there = other(away, "c")
     here = here.reshape(rows, n_zy, 1, pro)

time: 147 us -> 140 us (0.952)
  Pallas kernels: 24.3 us -> 17.5 us
  waiting for transfers between devices: 27.1 us -> 24.1 us
  local copies, waits for them, and re-layouts: 11.2 us -> 13.7 us
  starting transfers between devices: 67.5 us -> 69.5 us
    unnamed x38 -> x24, local copies, waits for them, and re-layouts: 2.87 us -> 10.6 us
    ppermute x14, waiting for transfers between devices: 20.9 us -> 15.5 us  [direct_sum(): lax.ppermute(piece.astype(sent), axes, moved(sizes, shift)).astype(F32)]
    pallas_call x2, Pallas kernels: 13.4 us -> 8.63 us  [the longest x1 6.29 us: cross_part(): pl.pallas_call(lambda *refs: cross_kernel(*refs, step=step), in_specs=[pl...]
    another operation x2 -> x1, other arithmetic: 4.2 us -> 1.37 us  [on_device(): tops = jnp.stack([largest(x_own), largest(protein_orbitals)])]
    transpose x2 -> x0, local copies, waits for them, and re-layouts: 2.63 us -> none  [the longest x1 1.33 us: on_device(): x_own.T.reshape(n_aa, rows, wide)]
    ppermute x6, starting transfers between devices: 10.7 us -> 12.8 us  [other(): return lax.ppermute(block, axis, [(0, 1), (1, 0)])]
    pallas_call x1, Pallas kernels: 8.9 us -> 6.9 us  [back_part(): pl.pallas_call(lambda *refs: back_kernel(*refs, count=count, scale=scale,...]
    ppermute x6, waiting for transfers between devices: 2.22 us -> 3.86 us  [other(): return lax.ppermute(block, axis, [(0, 1), (1, 0)])]
  transfers between devices with their start and end apart: 30 -> 30, of which waited for: 12 -> 13; matrix products, arithmetic and copies ran while one was open for 12% -> 7% of each run, Pallas kernels for 12% -> 9%
where the time goes in v6:
time: 140 us; the launch traced here: 139 us
  starting transfers between devices  69.5 us (50%)
  waiting for transfers between devices  24.1 us (17%)
  Pallas kernels  17.5 us (12%)
  local copies, waits for them, and re-layouts  13.7 us (10%)
  other arithmetic  11.7 us (8%)
  matrix products  1.49 us (1%)
    ppermute x14, starting transfers between devices, direct_sum(): lax.ppermute(piece.astype(sent), axes, moved(sizes, shift)).astype(F32)  26.1 us
    all_to_all x3, starting transfers between devices, exchange(): return lax.all_to_all(pieces, axes, 0, 0, tiled=True)  18.2 us
    ppermute x14, waiting for transfers between devices, direct_sum(): lax.ppermute(piece.astype(sent), axes, moved(sizes, shift)).astype(F32)  15.5 us
    ppermute x6, starting transfers between devices, other(): return lax.ppermute(block, axis, [(0, 1), (1, 0)])  12.8 us
    ppermute x7, starting transfers between devices, direct_gather(): blocks.append(lax.ppermute(block, axes, moved(sizes, shift)))  12.5 us
    unnamed x24, local copies, waits for them, and re-layouts  10.6 us
    pallas_call x1, Pallas kernels, back_part(): pl.pallas_call(lambda *refs: back_kernel(*refs, count=count, scale=scale,...  6.9 us
    pallas_call x1, Pallas kernels, cross_part(): pl.pallas_call(lambda *refs: cross_kernel(*refs, step=step), in_specs=[pl...  6.29 us
  transfers between devices with their start and end apart: 30, of which 13 were waited for; matrix products, arithmetic and copies ran while one was open for 7% of the time, Pallas kernels for 9%

profile of v6, /device:TPU:1, one launch (start us, length us, event | category | flops | bytes accessed | tf_op | source)
XLA Modules:
  0.0 139.0 jit_solution(1826312781984894808)
XLA Ops:
  2.1 3.3 %collective-permute-start = (bf16[512,512]{1,0:T(8,128)(2,1)S(1)}, bf16[512,512]{1,0:T(8,128)(2,1)S(1)}, u32[]{:S(2)}, u32[]{:S(2)}) collective-permute-start(bf16[512,512]{1,0:T(8,128)(2,1)S(1)} %bitcast.115), channel_id=1, source_target_pairs={{0,1},{1,0},{2,3},{3,2},{4,5},{5,4},{6,7},{7,6},{8,9},{9,8},{10,11... | collective-permute-start | bytes 1572872 | tf_op jit(solution)/shard_map/ppermute | solution.py:68
  12.9 7.6 %all-to-all-start = ((f16[16,32,1152]{2,1,0:T(8,128)(2,1)}), f16[16,32,1152]{2,1,0:T(8,128)(2,1)}, u32[]{:S(2)}, u32[]{:S(2)}) async-start(f16[16,32,1152]{2,1,0:T(8,128)(2,1)} %bitcast.108), calls=%async_computation | async-start | bytes 2359296 | tf_op jit(solution)/shard_map/all_to_all | solution.py:22
  21.2 3.4 %copy-done = bf16[64,32,2048]{2,1,0:T(8,128)(2,1)S(1)} copy-done((bf16[64,32,2048]{2,1,0:T(8,128)(2,1)S(1)}, bf16[64,32,2048]{2,1,0:T(8,128)(2,1)}, u32[]{:S(2)}) %copy-start) | copy-done | bytes 8388632
  24.6 6.3 %cross_part.1 = bf16[128,2048]{1,0:T(8,128)(2,1)S(1)} custom-call(f32[8,128]{1,0:T(8,128)S(1)} %slice_convert_fusion.refs_0_, bf16[128,2048]{1,0:T(8,128)(2,1)S(1)} %copy-done.5, bf16[2048,2048]{1,0:T(8,128)(2,1)S(1)} %bitcast.97), custom_call_target="tpu_custom_call" | custom-call | tf_op jit(solution)/shard_map/cross_part/pallas_call | solution.py:103
  31.0 4.9 %collective-permute-start.9 = (bf16[16,2048]{1,0:T(8,128)(2,1)S(1)}, bf16[16,2048]{1,0:T(8,128)(2,1)S(1)}, u32[]{:S(2)}, u32[]{:S(2)}) collective-permute-start(bf16[16,2048]{1,0:T(8,128)(2,1)S(1)} %get-tuple-element.31), channel_id=1, source_target_pairs={{0,224},{32,192},{64,32},{96,0},{128,96},{160,64},{192,160},{224,1... | collective-permute-start | bytes 196616 | tf_op jit(solution)/shard_map/ppermute | solution.py:55
  36.7 2.7 %collective-permute-start.6 = (bf16[16,2048]{1,0:T(8,128)(2,1)S(1)}, bf16[16,2048]{1,0:T(8,128)(2,1)S(1)}, u32[]{:S(2)}, u32[]{:S(2)}) collective-permute-start(bf16[16,2048]{1,0:T(8,128)(2,1)S(1)} %get-tuple-element.34), channel_id=1, source_target_pairs={{0,128},{32,160},{64,192},{96,224},{128,0},{160,32},{192,64},{224,... | collective-permute-start | bytes 196616 | tf_op jit(solution)/shard_map/ppermute | solution.py:55
  39.5 3.3 %collective-permute-start.5 = (bf16[16,2048]{1,0:T(8,128)(2,1)S(1)}, bf16[16,2048]{1,0:T(8,128)(2,1)S(1)}, u32[]{:S(2)}, u32[]{:S(2)}) collective-permute-start(bf16[16,2048]{1,0:T(8,128)(2,1)S(1)} %get-tuple-element.35), channel_id=1, source_target_pairs={{0,96},{32,64},{64,160},{96,128},{128,224},{160,192},{192,32},{224... | collective-permute-start | bytes 196616 | tf_op jit(solution)/shard_map/ppermute | solution.py:55
  43.9 3.6 %collective-permute-done.5 = bf16[16,2048]{1,0:T(8,128)(2,1)S(1)} collective-permute-done((bf16[16,2048]{1,0:T(8,128)(2,1)S(1)}, bf16[16,2048]{1,0:T(8,128)(2,1)S(1)}, u32[]{:S(2)}, u32[]{:S(2)}) %collective-permute-start.5) | collective-permute-done | bytes 65568 | tf_op jit(solution)/shard_map/ppermute | solution.py:55
  47.5 6.9 %collective-permute-done.3 = bf16[16,2048]{1,0:T(8,128)(2,1)S(1)} collective-permute-done((bf16[16,2048]{1,0:T(8,128)(2,1)S(1)}, bf16[16,2048]{1,0:T(8,128)(2,1)S(1)}, u32[]{:S(2)}, u32[]{:S(2)}) %collective-permute-start.3) | collective-permute-done | bytes 65568 | tf_op jit(solution)/shard_map/ppermute | solution.py:55
  56.0 2.2 %multiply_reduce_fusion.block_ref = f32[32,1024]{1,0:T(8,128)} fusion(f16[16,32,1152]{2,1,0:T(8,128)(2,1)} %all-to-all-done, f32[16]{0:T(128)S(1)} %exponential_bitcast_fusion), kind=kLoop, calls=%fused_computation.1 | loop fusion | flops 1540096 | bytes 1179712 | tf_op jit(solution)/shard_map/reduce_sum | solution.py:241
  58.2 2.0 %spread.1 = bf16[16,32,1024]{2,1,0:T(8,128)(2,1)} custom-call(f32[16,2048]{1,0:T(8,128)} %get-tuple-element.20.token_ref, f32[32,1024]{1,0:T(8,128)} %multiply_reduce_fusion.block_ref), custom_call_target="tpu_custom_call" | custom-call | tf_op jit(solution)/shard_map/spread/pallas_call | solution.py:170
  60.2 6.6 %all-to-all-start.1 = ((bf16[16,32,1024]{2,1,0:T(8,128)(2,1)}), bf16[16,32,1024]{2,1,0:T(8,128)(2,1)S(1)}, u32[]{:S(2)}, u32[]{:S(2)}) async-start(bf16[16,32,1024]{2,1,0:T(8,128)(2,1)} %spread.1), calls=%async_computation.1 | async-start | bytes 2097152 | tf_op jit(solution)/shard_map/all_to_all | solution.py:22
  66.8 1.8 %collective-permute-start.10 = (bf16[16,2048]{1,0:T(8,128)(2,1)S(1)}, bf16[16,2048]{1,0:T(8,128)(2,1)S(1)}, u32[]{:S(2)}, u32[]{:S(2)}) collective-permute-start(bf16[16,2048]{1,0:T(8,128)(2,1)S(1)} %get-tuple-element.19.refs_2_), channel_id=1, source_target_pairs={{0,32},{32,0},{64,96},{96,64},{128,160},{160,128},{192,224},{224,1... | collective-permute-start | bytes 196616 | tf_op jit(solution)/shard_map/ppermute | solution.py:62
  71.1 2.5 %collective-permute-start.13 = (bf16[16,2048]{1,0:T(8,128)(2,1)S(1)}, bf16[16,2048]{1,0:T(8,128)(2,1)S(1)}, u32[]{:S(2)}, u32[]{:S(2)}) collective-permute-start(bf16[16,2048]{1,0:T(8,128)(2,1)S(1)} %get-tuple-element.19.refs_2_), channel_id=1, source_target_pairs={{0,128},{32,160},{64,192},{96,224},{128,0},{160,32},{192,64},{224,... | collective-permute-start | bytes 196616 | tf_op jit(solution)/shard_map/ppermute | solution.py:62
  73.6 1.9 %collective-permute-start.14 = (bf16[16,2048]{1,0:T(8,128)(2,1)S(1)}, bf16[16,2048]{1,0:T(8,128)(2,1)S(1)}, u32[]{:S(2)}, u32[]{:S(2)}) collective-permute-start(bf16[16,2048]{1,0:T(8,128)(2,1)S(1)} %get-tuple-element.19.refs_2_), channel_id=1, source_target_pairs={{0,160},{32,128},{64,224},{96,192},{128,32},{160,0},{192,96},{224,... | collective-permute-start | bytes 196616 | tf_op jit(solution)/shard_map/ppermute | solution.py:62
  75.5 2.2 %collective-permute-start.15 = (bf16[16,2048]{1,0:T(8,128)(2,1)S(1)}, bf16[16,2048]{1,0:T(8,128)(2,1)}, u32[]{:S(2)}, u32[]{:S(2)}) collective-permute-start(bf16[16,2048]{1,0:T(8,128)(2,1)S(1)} %get-tuple-element.19.refs_2_), channel_id=1, source_target_pairs={{0,192},{32,224},{64,0},{96,32},{128,64},{160,96},{192,128},{224,1... | collective-permute-start | bytes 196616 | tf_op jit(solution)/shard_map/ppermute | solution.py:62
  80.7 3.4 %collective-permute-done.16.refs_9_ = bf16[16,2048]{1,0:T(8,128)(2,1)} collective-permute-done((bf16[16,2048]{1,0:T(8,128)(2,1)S(1)}, bf16[16,2048]{1,0:T(8,128)(2,1)}, u32[]{:S(2)}, u32[]{:S(2)}) %collective-permute-start.16) | collective-permute-done | bytes 65568 | tf_op jit(solution)/shard_map/ppermute | solution.py:62
  84.1 3.4 %copy-done.1 = bf16[64,32,2048]{2,1,0:T(8,128)(2,1)S(1)} copy-done((bf16[64,32,2048]{2,1,0:T(8,128)(2,1)S(1)}, bf16[64,32,2048]{2,1,0:T(8,128)(2,1)}, u32[]{:S(2)}) %copy-start.1) | copy-done | bytes 8388632
  87.5 6.9 %back_part.1 = (f32[16,64,128]{2,1,0:T(8,128)S(1)}, f32[16,64,128]{2,1,0:T(8,128)}) custom-call(s32[9]{0:T(128)S(1)} %stack.57.refs_0_, bf16[2048,2048]{1,0:T(8,128)(2,1)S(1)} %bitcast.98, bf16[16,2048]{1,0:T(8,128)(2,1)S(1)} %get-tuple-element.19.refs_2_, bf16[16,2048]{1,0:T(8,128)(2,1)S(1)} %collective-permute-done.10.refs_3_, ...), custom_call_target="tpu_custom_call" | custom-call | tf_op jit(solution)/shard_map/back_part/pallas_call | solution.py:147
  95.2 3.6 %collective-permute-start.17 = (f32[16,64,128]{2,1,0:T(8,128)}, f32[16,64,128]{2,1,0:T(8,128)}, u32[]{:S(2)}, u32[]{:S(2)}) collective-permute-start(f32[16,64,128]{2,1,0:T(8,128)} %get-tuple-element.6), channel_id=1, source_target_pairs={{0,1},{1,0},{2,3},{3,2},{4,5},{5,4},{6,7},{7,6},{8,9},{9,8},{10,11... | collective-permute-start | bytes 1572872 | tf_op jit(solution)/shard_map/ppermute | solution.py:68
  98.8 1.9 %collective-permute-done.17 = f32[16,64,128]{2,1,0:T(8,128)} collective-permute-done((f32[16,64,128]{2,1,0:T(8,128)}, f32[16,64,128]{2,1,0:T(8,128)}, u32[]{:S(2)}, u32[]{:S(2)}) %collective-permute-start.17) | collective-permute-done | bytes 524320 | tf_op jit(solution)/shard_map/ppermute | solution.py:68
  100.7 2.0 %add.259 = f32[16,64,128]{2,1,0:T(8,128)} add(f32[16,64,128]{2,1,0:T(8,128)} %copy-done.6, f32[16,64,128]{2,1,0:T(8,128)} %collective-permute-done.17) | non-fusion elementwise | flops 131072 | bytes 1572864 | tf_op jit(solution)/shard_map/add | solution.py:258
  103.8 2.3 %product.1 = bf16[8,2,64,512]{3,2,1,0:T(8,128)(2,1)} custom-call(f32[1024,128]{1,0:T(8,128)S(1)} %bitcast.103, bf16[1024,512]{1,0:T(8,128)(2,1)S(1)} %bitcast.101, bf16[1024,512]{1,0:T(8,128)(2,1)S(1)} %collective-permute-done.1.refs_2_, bf16[512,1024]{1,0:T(8,128)(2,1)S(1)} %bitcast.102), custom_call_target="tpu_custom_call" | custom-call | tf_op jit(solution)/shard_map/product/pallas_call | solution.py:199
  106.1 4.1 %all-to-all-start.2 = ((bf16[8,2,64,512]{3,2,1,0:T(8,128)(2,1)}), bf16[8,2,64,512]{3,2,1,0:T(8,128)(2,1)S(1)}, u32[]{:S(2)}, u32[]{:S(2)}) async-start(bf16[8,2,64,512]{3,2,1,0:T(8,128)(2,1)} %product.1), calls=%async_computation.2 | async-start | bytes 2097152 | tf_op jit(solution)/shard_map/all_to_all | solution.py:22
  110.3 3.0 %collective-permute-start.24 = (bf16[128,128]{1,0:T(8,128)(2,1)S(1)}, bf16[128,128]{1,0:T(8,128)(2,1)S(1)}, u32[]{:S(2)}, u32[]{:S(2)}) collective-permute-start(bf16[128,128]{1,0:T(8,128)(2,1)S(1)} %get-tuple-element.24), channel_id=1, source_target_pairs={{0,28},{4,0},{8,4},{12,8},{16,12},{20,16},{24,20},{28,24},{1,29},{... | collective-permute-start | bytes 98312 | tf_op jit(solution)/shard_map/ppermute | solution.py:55
  113.3 2.1 %collective-permute-start.23 = (bf16[128,128]{1,0:T(8,128)(2,1)S(1)}, bf16[128,128]{1,0:T(8,128)(2,1)S(1)}, u32[]{:S(2)}, u32[]{:S(2)}) collective-permute-start(bf16[128,128]{1,0:T(8,128)(2,1)S(1)} %get-tuple-element.25), channel_id=1, source_target_pairs={{0,24},{4,28},{8,0},{12,4},{16,8},{20,12},{24,16},{28,20},{1,25},{... | collective-permute-start | bytes 98312 | tf_op jit(solution)/shard_map/ppermute | solution.py:55
  115.4 1.8 %collective-permute-start.22 = (bf16[128,128]{1,0:T(8,128)(2,1)S(1)}, bf16[128,128]{1,0:T(8,128)(2,1)S(1)}, u32[]{:S(2)}, u32[]{:S(2)}) collective-permute-start(bf16[128,128]{1,0:T(8,128)(2,1)S(1)} %get-tuple-element.26), channel_id=1, source_target_pairs={{0,20},{4,24},{8,28},{12,0},{16,4},{20,8},{24,12},{28,16},{1,21},{... | collective-permute-start | bytes 98312 | tf_op jit(solution)/shard_map/ppermute | solution.py:55
  117.2 2.9 %collective-permute-start.21 = (bf16[128,128]{1,0:T(8,128)(2,1)S(1)}, bf16[128,128]{1,0:T(8,128)(2,1)S(1)}, u32[]{:S(2)}, u32[]{:S(2)}) collective-permute-start(bf16[128,128]{1,0:T(8,128)(2,1)S(1)} %get-tuple-element.27), channel_id=1, source_target_pairs={{0,16},{4,20},{8,24},{12,28},{16,0},{20,4},{24,8},{28,12},{1,17},{... | collective-permute-start | bytes 98312 | tf_op jit(solution)/shard_map/ppermute | solution.py:55
  120.4 3.6 %collective-permute-start.19 = (bf16[128,128]{1,0:T(8,128)(2,1)S(1)}, bf16[128,128]{1,0:T(8,128)(2,1)S(1)}, u32[]{:S(2)}, u32[]{:S(2)}) collective-permute-start(bf16[128,128]{1,0:T(8,128)(2,1)S(1)} %get-tuple-element.29), channel_id=1, source_target_pairs={{0,8},{4,12},{8,16},{12,20},{16,24},{20,28},{24,0},{28,4},{1,9},{5... | collective-permute-start | bytes 98312 | tf_op jit(solution)/shard_map/ppermute | solution.py:55
  124.4 2.0 %collective-permute-done.20 = bf16[128,128]{1,0:T(8,128)(2,1)S(1)} collective-permute-done((bf16[128,128]{1,0:T(8,128)(2,1)S(1)}, bf16[128,128]{1,0:T(8,128)(2,1)S(1)}, u32[]{:S(2)}, u32[]{:S(2)}) %collective-permute-start.20) | collective-permute-done | bytes 32800 | tf_op jit(solution)/shard_map/ppermute | solution.py:55
  129.7 1.6 %collective-permute-done.25 = f32[1,64,128]{2,1,0:T(8,128)S(1)} collective-permute-done((f32[1,64,128]{2,1,0:T(8,128)S(1)}, f32[1,64,128]{2,1,0:T(8,128)S(1)}, u32[]{:S(2)}, u32[]{:S(2)}) %collective-permute-start.25) | collective-permute-done | bytes 32800 | tf_op jit(solution)/shard_map/ppermute | solution.py:68
  132.6 4.2 %collective-permute-start.26 = (f32[64,512]{1,0:T(8,128)S(1)}, f32[64,512]{1,0:T(8,128)S(1)}, u32[]{:S(2)}, u32[]{:S(2)}) collective-permute-start(f32[64,512]{1,0:T(8,128)S(1)} %get-tuple-element.38), channel_id=1, source_target_pairs={{0,1},{1,0},{2,3},{3,2},{4,5},{5,4},{6,7},{7,6},{8,9},{9,8},{10,11... | collective-permute-start | bytes 393224 | tf_op jit(solution)/shard_map/ppermute | solution.py:68
  (91 shorter events, 28.0 us)
Async XLA Ops:
  2.1 7.8 %collective-permute-start = (bf16[512,512]{1,0:T(8,128)(2,1)S(1)}, bf16[512,512]{1,0:T(8,128)(2,1)S(1)}, u32[]{:S(2)}, u32[]{:S(2)}) collective-permute-start(bf16[512,512]{1,0:T(8,128)(2,1)S(1)} %bitcast.115), channel_id=1, source_target_pairs={{0,1},{1,0},{2,3},{3,2},{4,5},{5,4},{6,7},{7,6},{8,9},{9,8},{10,11... | collective-permute-start | bytes 1572872 | tf_op jit(solution)/shard_map/ppermute | solution.py:68
  5.4 4.4 %collective-permute-start.1 = (bf16[1024,512]{1,0:T(8,128)(2,1)S(1)}, bf16[1024,512]{1,0:T(8,128)(2,1)S(1)}, u32[]{:S(2)}, u32[]{:S(2)}) collective-permute-start(bf16[1024,512]{1,0:T(8,128)(2,1)S(1)} %bitcast.99), channel_id=1, source_target_pairs={{0,1},{1,0},{2,3},{3,2},{4,5},{5,4},{6,7},{7,6},{8,9},{9,8},{10,11... | collective-permute-start | bytes 3145736 | tf_op jit(solution)/shard_map/ppermute | solution.py:68
  8.5 1.2 collective-permute-start.2
  12.9 42.2 %all-to-all-start = ((f16[16,32,1152]{2,1,0:T(8,128)(2,1)}), f16[16,32,1152]{2,1,0:T(8,128)(2,1)}, u32[]{:S(2)}, u32[]{:S(2)}) async-start(f16[16,32,1152]{2,1,0:T(8,128)(2,1)} %bitcast.108), calls=%async_computation | async-start | bytes 2359296 | tf_op jit(solution)/shard_map/all_to_all | solution.py:22
  31.0 11.7 %collective-permute-start.9 = (bf16[16,2048]{1,0:T(8,128)(2,1)S(1)}, bf16[16,2048]{1,0:T(8,128)(2,1)S(1)}, u32[]{:S(2)}, u32[]{:S(2)}) collective-permute-start(bf16[16,2048]{1,0:T(8,128)(2,1)S(1)} %get-tuple-element.31), channel_id=1, source_target_pairs={{0,224},{32,192},{64,32},{96,0},{128,96},{160,64},{192,160},{224,1... | collective-permute-start | bytes 196616 | tf_op jit(solution)/shard_map/ppermute | solution.py:55
  35.9 6.8 %collective-permute-start.8 = (bf16[16,2048]{1,0:T(8,128)(2,1)S(1)}, bf16[16,2048]{1,0:T(8,128)(2,1)S(1)}, u32[]{:S(2)}, u32[]{:S(2)}) collective-permute-start(bf16[16,2048]{1,0:T(8,128)(2,1)S(1)} %get-tuple-element.32), channel_id=1, source_target_pairs={{0,192},{32,224},{64,0},{96,32},{128,64},{160,96},{192,128},{224,1... | collective-permute-start | bytes 196616 | tf_op jit(solution)/shard_map/ppermute | solution.py:55
  36.4 7.5 %collective-permute-start.7 = (bf16[16,2048]{1,0:T(8,128)(2,1)S(1)}, bf16[16,2048]{1,0:T(8,128)(2,1)S(1)}, u32[]{:S(2)}, u32[]{:S(2)}) collective-permute-start(bf16[16,2048]{1,0:T(8,128)(2,1)S(1)} %get-tuple-element.33), channel_id=1, source_target_pairs={{0,160},{32,128},{64,224},{96,192},{128,32},{160,0},{192,96},{224,... | collective-permute-start | bytes 196616 | tf_op jit(solution)/shard_map/ppermute | solution.py:55
  36.7 7.2 %collective-permute-start.6 = (bf16[16,2048]{1,0:T(8,128)(2,1)S(1)}, bf16[16,2048]{1,0:T(8,128)(2,1)S(1)}, u32[]{:S(2)}, u32[]{:S(2)}) collective-permute-start(bf16[16,2048]{1,0:T(8,128)(2,1)S(1)} %get-tuple-element.34), channel_id=1, source_target_pairs={{0,128},{32,160},{64,192},{96,224},{128,0},{160,32},{192,64},{224,... | collective-permute-start | bytes 196616 | tf_op jit(solution)/shard_map/ppermute | solution.py:55
  39.5 8.1 %collective-permute-start.5 = (bf16[16,2048]{1,0:T(8,128)(2,1)S(1)}, bf16[16,2048]{1,0:T(8,128)(2,1)S(1)}, u32[]{:S(2)}, u32[]{:S(2)}) collective-permute-start(bf16[16,2048]{1,0:T(8,128)(2,1)S(1)} %get-tuple-element.35), channel_id=1, source_target_pairs={{0,96},{32,64},{64,160},{96,128},{128,224},{160,192},{192,32},{224... | collective-permute-start | bytes 196616 | tf_op jit(solution)/shard_map/ppermute | solution.py:55
  42.7 4.8 %collective-permute-start.4 = (bf16[16,2048]{1,0:T(8,128)(2,1)S(1)}, bf16[16,2048]{1,0:T(8,128)(2,1)S(1)}, u32[]{:S(2)}, u32[]{:S(2)}) collective-permute-start(bf16[16,2048]{1,0:T(8,128)(2,1)S(1)} %get-tuple-element.36), channel_id=1, source_target_pairs={{0,64},{32,96},{64,128},{96,160},{128,192},{160,224},{192,0},{224,... | collective-permute-start | bytes 196616 | tf_op jit(solution)/shard_map/ppermute | solution.py:55
  42.7 11.7 %collective-permute-start.3 = (bf16[16,2048]{1,0:T(8,128)(2,1)S(1)}, bf16[16,2048]{1,0:T(8,128)(2,1)S(1)}, u32[]{:S(2)}, u32[]{:S(2)}) collective-permute-start(bf16[16,2048]{1,0:T(8,128)(2,1)S(1)} %get-tuple-element.30), channel_id=1, source_target_pairs={{0,32},{32,0},{64,96},{96,64},{128,160},{160,128},{192,224},{224,1... | collective-permute-start | bytes 196616 | tf_op jit(solution)/shard_map/ppermute | solution.py:55
  60.2 42.5 %all-to-all-start.1 = ((bf16[16,32,1024]{2,1,0:T(8,128)(2,1)}), bf16[16,32,1024]{2,1,0:T(8,128)(2,1)S(1)}, u32[]{:S(2)}, u32[]{:S(2)}) async-start(bf16[16,32,1024]{2,1,0:T(8,128)(2,1)} %spread.1), calls=%async_computation.1 | async-start | bytes 2097152 | tf_op jit(solution)/shard_map/all_to_all | solution.py:22
  66.8 8.7 %collective-permute-start.10 = (bf16[16,2048]{1,0:T(8,128)(2,1)S(1)}, bf16[16,2048]{1,0:T(8,128)(2,1)S(1)}, u32[]{:S(2)}, u32[]{:S(2)}) collective-permute-start(bf16[16,2048]{1,0:T(8,128)(2,1)S(1)} %get-tuple-element.19.refs_2_), channel_id=1, source_target_pairs={{0,32},{32,0},{64,96},{96,64},{128,160},{160,128},{192,224},{224,1... | collective-permute-start | bytes 196616 | tf_op jit(solution)/shard_map/ppermute | solution.py:62
  68.6 9.2 %collective-permute-start.11 = (bf16[16,2048]{1,0:T(8,128)(2,1)S(1)}, bf16[16,2048]{1,0:T(8,128)(2,1)S(1)}, u32[]{:S(2)}, u32[]{:S(2)}) collective-permute-start(bf16[16,2048]{1,0:T(8,128)(2,1)S(1)} %get-tuple-element.19.refs_2_), channel_id=1, source_target_pairs={{0,64},{32,96},{64,128},{96,160},{128,192},{160,224},{192,0},{224,... | collective-permute-start | bytes 196616 | tf_op jit(solution)/shard_map/ppermute | solution.py:62
  69.7 9.7 %collective-permute-start.12 = (bf16[16,2048]{1,0:T(8,128)(2,1)S(1)}, bf16[16,2048]{1,0:T(8,128)(2,1)S(1)}, u32[]{:S(2)}, u32[]{:S(2)}) collective-permute-start(bf16[16,2048]{1,0:T(8,128)(2,1)S(1)} %get-tuple-element.19.refs_2_), channel_id=1, source_target_pairs={{0,96},{32,64},{64,160},{96,128},{128,224},{160,192},{192,32},{224... | collective-permute-start | bytes 196616 | tf_op jit(solution)/shard_map/ppermute | solution.py:62
  71.1 8.2 %collective-permute-start.13 = (bf16[16,2048]{1,0:T(8,128)(2,1)S(1)}, bf16[16,2048]{1,0:T(8,128)(2,1)S(1)}, u32[]{:S(2)}, u32[]{:S(2)}) collective-permute-start(bf16[16,2048]{1,0:T(8,128)(2,1)S(1)} %get-tuple-element.19.refs_2_), channel_id=1, source_target_pairs={{0,128},{32,160},{64,192},{96,224},{128,0},{160,32},{192,64},{224,... | collective-permute-start | bytes 196616 | tf_op jit(solution)/shard_map/ppermute | solution.py:62
  73.6 7.1 %collective-permute-start.14 = (bf16[16,2048]{1,0:T(8,128)(2,1)S(1)}, bf16[16,2048]{1,0:T(8,128)(2,1)S(1)}, u32[]{:S(2)}, u32[]{:S(2)}) collective-permute-start(bf16[16,2048]{1,0:T(8,128)(2,1)S(1)} %get-tuple-element.19.refs_2_), channel_id=1, source_target_pairs={{0,160},{32,128},{64,224},{96,192},{128,32},{160,0},{192,96},{224,... | collective-permute-start | bytes 196616 | tf_op jit(solution)/shard_map/ppermute | solution.py:62
  75.5 5.2 %collective-permute-start.15 = (bf16[16,2048]{1,0:T(8,128)(2,1)S(1)}, bf16[16,2048]{1,0:T(8,128)(2,1)}, u32[]{:S(2)}, u32[]{:S(2)}) collective-permute-start(bf16[16,2048]{1,0:T(8,128)(2,1)S(1)} %get-tuple-element.19.refs_2_), channel_id=1, source_target_pairs={{0,192},{32,224},{64,0},{96,32},{128,64},{160,96},{192,128},{224,1... | collective-permute-start | bytes 196616 | tf_op jit(solution)/shard_map/ppermute | solution.py:62
  77.8 6.3 %collective-permute-start.16 = (bf16[16,2048]{1,0:T(8,128)(2,1)S(1)}, bf16[16,2048]{1,0:T(8,128)(2,1)}, u32[]{:S(2)}, u32[]{:S(2)}) collective-permute-start(bf16[16,2048]{1,0:T(8,128)(2,1)S(1)} %get-tuple-element.19.refs_2_), channel_id=1, source_target_pairs={{0,224},{32,192},{64,32},{96,0},{128,96},{160,64},{192,160},{224,1... | collective-permute-start | bytes 196616 | tf_op jit(solution)/shard_map/ppermute | solution.py:62
  95.2 5.5 %collective-permute-start.17 = (f32[16,64,128]{2,1,0:T(8,128)}, f32[16,64,128]{2,1,0:T(8,128)}, u32[]{:S(2)}, u32[]{:S(2)}) collective-permute-start(f32[16,64,128]{2,1,0:T(8,128)} %get-tuple-element.6), channel_id=1, source_target_pairs={{0,1},{1,0},{2,3},{3,2},{4,5},{5,4},{6,7},{7,6},{8,9},{9,8},{10,11... | collective-permute-start | bytes 1572872 | tf_op jit(solution)/shard_map/ppermute | solution.py:68
  106.1 23.4 %copy-start.9 = (f32[16,2048]{1,0:T(8,128)S(1)}, f32[16,2048]{1,0:T(8,128)}, u32[]{:S(2)}) copy-start(f32[16,2048]{1,0:T(8,128)} %get-tuple-element.20.token_ref) | copy-start | bytes 393220
  106.1 25.8 %copy-start.10 = (f32[32,1024]{1,0:T(8,128)S(1)}, f32[32,1024]{1,0:T(8,128)}, u32[]{:S(2)}) copy-start(f32[32,1024]{1,0:T(8,128)} %multiply_reduce_fusion.block_ref) | copy-start | bytes 393220
  106.1 26.3 %all-to-all-start.2 = ((bf16[8,2,64,512]{3,2,1,0:T(8,128)(2,1)}), bf16[8,2,64,512]{3,2,1,0:T(8,128)(2,1)S(1)}, u32[]{:S(2)}, u32[]{:S(2)}) async-start(bf16[8,2,64,512]{3,2,1,0:T(8,128)(2,1)} %product.1), calls=%async_computation.2 | async-start | bytes 2097152 | tf_op jit(solution)/shard_map/all_to_all | solution.py:22
  110.3 10.1 %collective-permute-start.24 = (bf16[128,128]{1,0:T(8,128)(2,1)S(1)}, bf16[128,128]{1,0:T(8,128)(2,1)S(1)}, u32[]{:S(2)}, u32[]{:S(2)}) collective-permute-start(bf16[128,128]{1,0:T(8,128)(2,1)S(1)} %get-tuple-element.24), channel_id=1, source_target_pairs={{0,28},{4,0},{8,4},{12,8},{16,12},{20,16},{24,20},{28,24},{1,29},{... | collective-permute-start | bytes 98312 | tf_op jit(solution)/shard_map/ppermute | solution.py:55
  113.3 10.7 %collective-permute-start.23 = (bf16[128,128]{1,0:T(8,128)(2,1)S(1)}, bf16[128,128]{1,0:T(8,128)(2,1)S(1)}, u32[]{:S(2)}, u32[]{:S(2)}) collective-permute-start(bf16[128,128]{1,0:T(8,128)(2,1)S(1)} %get-tuple-element.25), channel_id=1, source_target_pairs={{0,24},{4,28},{8,0},{12,4},{16,8},{20,12},{24,16},{28,20},{1,25},{... | collective-permute-start | bytes 98312 | tf_op jit(solution)/shard_map/ppermute | solution.py:55
  115.4 8.8 %collective-permute-start.22 = (bf16[128,128]{1,0:T(8,128)(2,1)S(1)}, bf16[128,128]{1,0:T(8,128)(2,1)S(1)}, u32[]{:S(2)}, u32[]{:S(2)}) collective-permute-start(bf16[128,128]{1,0:T(8,128)(2,1)S(1)} %get-tuple-element.26), channel_id=1, source_target_pairs={{0,20},{4,24},{8,28},{12,0},{16,4},{20,8},{24,12},{28,16},{1,21},{... | collective-permute-start | bytes 98312 | tf_op jit(solution)/shard_map/ppermute | solution.py:55
  117.2 7.2 %collective-permute-start.21 = (bf16[128,128]{1,0:T(8,128)(2,1)S(1)}, bf16[128,128]{1,0:T(8,128)(2,1)S(1)}, u32[]{:S(2)}, u32[]{:S(2)}) collective-permute-start(bf16[128,128]{1,0:T(8,128)(2,1)S(1)} %get-tuple-element.27), channel_id=1, source_target_pairs={{0,16},{4,20},{8,24},{12,28},{16,0},{20,4},{24,8},{28,12},{1,17},{... | collective-permute-start | bytes 98312 | tf_op jit(solution)/shard_map/ppermute | solution.py:55
  120.0 6.3 %collective-permute-start.20 = (bf16[128,128]{1,0:T(8,128)(2,1)S(1)}, bf16[128,128]{1,0:T(8,128)(2,1)S(1)}, u32[]{:S(2)}, u32[]{:S(2)}) collective-permute-start(bf16[128,128]{1,0:T(8,128)(2,1)S(1)} %get-tuple-element.28), channel_id=1, source_target_pairs={{0,12},{4,16},{8,20},{12,24},{16,28},{20,0},{24,4},{28,8},{1,13},{... | collective-permute-start | bytes 98312 | tf_op jit(solution)/shard_map/ppermute | solution.py:55
  120.4 6.5 %collective-permute-start.19 = (bf16[128,128]{1,0:T(8,128)(2,1)S(1)}, bf16[128,128]{1,0:T(8,128)(2,1)S(1)}, u32[]{:S(2)}, u32[]{:S(2)}) collective-permute-start(bf16[128,128]{1,0:T(8,128)(2,1)S(1)} %get-tuple-element.29), channel_id=1, source_target_pairs={{0,8},{4,12},{8,16},{12,20},{16,24},{20,28},{24,0},{28,4},{1,9},{5... | collective-permute-start | bytes 98312 | tf_op jit(solution)/shard_map/ppermute | solution.py:55
  124.0 4.4 %collective-permute-start.18 = (bf16[128,128]{1,0:T(8,128)(2,1)S(1)}, bf16[128,128]{1,0:T(8,128)(2,1)S(1)}, u32[]{:S(2)}, u32[]{:S(2)}) collective-permute-start(bf16[128,128]{1,0:T(8,128)(2,1)S(1)} %get-tuple-element.23), channel_id=1, source_target_pairs={{0,4},{4,8},{8,12},{12,16},{16,20},{20,24},{24,28},{28,0},{1,5},{5... | collective-permute-start | bytes 98312 | tf_op jit(solution)/shard_map/ppermute | solution.py:55
  128.5 2.9 %collective-permute-start.25 = (f32[1,64,128]{2,1,0:T(8,128)S(1)}, f32[1,64,128]{2,1,0:T(8,128)S(1)}, u32[]{:S(2)}, u32[]{:S(2)}) collective-permute-start(f32[1,64,128]{2,1,0:T(8,128)S(1)} %dynamic-slice_bitcast_fusion.7), channel_id=1, source_target_pairs={{0,2},{2,0},{1,3},{3,1},{4,6},{6,4},{5,7},{7,5},{8,10},{10,8},{9,1... | collective-permute-start | bytes 98312 | tf_op jit(solution)/shard_map/ppermute | solution.py:68
  132.6 5.2 %collective-permute-start.26 = (f32[64,512]{1,0:T(8,128)S(1)}, f32[64,512]{1,0:T(8,128)S(1)}, u32[]{:S(2)}, u32[]{:S(2)}) collective-permute-start(f32[64,512]{1,0:T(8,128)S(1)} %get-tuple-element.38), channel_id=1, source_target_pairs={{0,1},{1,0},{2,3},{3,2},{4,5},{5,4},{6,7},{7,6},{8,9},{9,8},{10,11... | collective-permute-start | bytes 393224 | tf_op jit(solution)/shard_map/ppermute | solution.py:68
  (9 other events, 33.0 us)

commit v7 on v6

--- a/solution.py
+++ b/solution.py
@@ -16,6 +16,8 @@
 BF16 = jnp.bfloat16
 LANES = 128
 VMEM = 24 * 2**20
+LARGE = 54 * 2**20
+DEEP = 3
 
 
 def exchange(pieces, axes):
@@ -83,53 +85,54 @@
     return jnp.max(jnp.abs(array)).astype(F32)
 
 
-def cross_kernel(token_ref, left_ref, slab_ref, out_ref, held_ref, sems, *, step):
-    del token_ref
-    copies = []
-    for i in range(held_ref.shape[0] // step):
-        rows = pl.ds(i * step, step)
-        copies.append(pltpu.make_async_copy(slab_ref.at[rows], held_ref.at[rows], sems.at[i]))
-        copies[i].start()
+def arriving(copies):
+    for copy in copies[:DEEP]:
+        copy.start()
     for i, copy in enumerate(copies):
-        rows = pl.ds(i * step, step)
         copy.wait()
-        part = dot(left_ref[...], held_ref[rows, :], ((1,), (1,)))
-        out_ref[:, rows] = part.astype(out_ref.dtype)
-
-
-def cross_part(token, orbitals, slab):
+        if i + DEEP < len(copies):
+            copies[i + DEEP].start()
+        yield i
+
+
+def cross_kernel(left_ref, slab_ref, out_ref, held_ref, sems, *, step):
+    runs = [pl.ds(i * step, step) for i in range(held_ref.shape[0] // step)]
+    copies = [
+        pltpu.make_async_copy(slab_ref.at[rows], held_ref.at[rows], sems.at[i])
+        for i, rows in enumerate(runs)
+    ]
+    for i in arriving(copies):
+        part = dot(left_ref[...], held_ref[runs[i], :], ((1,), (1,)))
+        out_ref[:, runs[i]] = part.astype(out_ref.dtype)
+
+
+def cross_part(orbitals, slab):
     rows = slab.shape[0]
     step = min(rows, 256)
     return pl.pallas_call(
         lambda *refs: cross_kernel(*refs, step=step),
-        in_specs=[
-            pl.BlockSpec(memory_space=pltpu.VMEM),
-            pl.BlockSpec(memory_space=pltpu.VMEM),
-            pl.BlockSpec(memory_space=pltpu.HBM),
-        ],
+        in_specs=[pl.BlockSpec(memory_space=pltpu.VMEM), pl.BlockSpec(memory_space=pltpu.HBM)],
         out_specs=pl.BlockSpec(memory_space=pltpu.VMEM),
         out_shape=jax.ShapeDtypeStruct((orbitals.shape[0], rows), BF16),
         scratch_shapes=[pltpu.VMEM(slab.shape, BF16), pltpu.SemaphoreType.DMA((rows // step,))],
-        compiler_params=pltpu.CompilerParams(vmem_limit_bytes=VMEM),
+        compiler_params=pltpu.CompilerParams(vmem_limit_bytes=LARGE),
         cost_estimate=pl.CostEstimate(flops=0, bytes_accessed=0, transcendentals=0),
         name="cross_part",
-    )(token, orbitals, slab)
+    )(orbitals, slab)
 
 
 def back_kernel(place_ref, slab_ref, *refs, count, scale, fine, step):
     blocks, (keep_ref, send_ref, all_ref, held_ref, sems) = refs[:count], refs[count:]
-    copies = []
-    for i in range(held_ref.shape[0]):
-        columns = pl.ds(i * step, step)
-        copies.append(pltpu.make_async_copy(slab_ref.at[:, columns], held_ref.at[i], sems.at[i]))
-        copies[i].start()
+    copies = [
+        pltpu.make_async_copy(slab_ref.at[:, pl.ds(i * step, step)], held_ref.at[i], sems.at[i])
+        for i in range(held_ref.shape[0])
+    ]
     for k, block_ref in enumerate(blocks):
         rows = block_ref.shape[0]
         all_ref[pl.ds(pl.multiple_of(place_ref[k] * rows, rows), rows), :] = block_ref[...]
     low = place_ref[count] == 0
     runs = step // (2 * fine)
-    for i, copy in enumerate(copies):
-        copy.wait()
+    for i in arriving(copies):
         part = dot(all_ref[...], held_ref[i], ((1,), (0,))) * scale
         part = part.T.reshape(runs, 2, fine, all_ref.shape[0])
         first, second = part[:, 0], part[:, 1]
@@ -155,7 +158,7 @@
             pltpu.VMEM((total // step, depth, step), BF16),
             pltpu.SemaphoreType.DMA((total // step,)),
         ],
-        compiler_params=pltpu.CompilerParams(vmem_limit_bytes=VMEM),
+        compiler_params=pltpu.CompilerParams(vmem_limit_bytes=LARGE),
         cost_estimate=pl.CostEstimate(flops=0, bytes_accessed=0, transcendentals=0),
         name="back_part",
     )(jnp.stack(places + [core]).astype(jnp.int32), slab, *blocks)
@@ -226,6 +229,9 @@
     orb_own = lax.dynamic_index_in_dim(orb, core, 1, keepdims=False).reshape(n_zy * pro, mus)
     orb_send = lax.dynamic_index_in_dim(orb, 1 - core, 1, keepdims=False).reshape(n_zy * pro, mus)
     orb_other = other(orb_send, "c")
+
+    b_part = cross_part(ligand_orbitals, y)
+    b_own = jnp.sum(exchange(b_part.reshape(n_aa, lig, fit * pro), AA).astype(F32), axis=0)
 
     tops = jnp.stack([largest(x_own), largest(protein_orbitals)])
     tops = jnp.broadcast_to(tops[:, None], (2, wide + LANES))
@@ -240,10 +246,13 @@
     codes = a_got[:, :1, wide : wide + 1].astype(F32)
     a_own = jnp.sum(a_got[:, :, :wide].astype(F32) * jnp.exp2(codes - 15.0), axis=0)
 
-    b_part = cross_part(a_sent[:8, :LANES].astype(F32), ligand_orbitals, y)
-    b_own = direct_sum(b_part.reshape(n_aa, lig, fit * pro), AA, aa, BF16)
-    a_all = exchange(spread(b_own, a_own, n_zy), ZY).reshape(n_zy * pro, wide)
     b_blocks, b_places = direct_gather(b_own.astype(BF16), AA, aa)
+    scale_ligand = 1.0 / math.sqrt(fit * pro_total)
+    rows_b = nus // (2 * n_zy)
+    keep, send = back_part(y, b_blocks, b_places, core, scale_ligand, rows_b)
+    back_b = keep + other(send, "c")
+    a_all = exchange(spread(back_b.reshape(-1, lig_total), a_own, n_zy), ZY).reshape(n_zy * pro, wide)
+    back_b = pair_sum(back_b.reshape(n_z, n_yl, rows_b, lig_total), "yl")
 
     pair = jnp.sum(
         jnp.transpose(a_own.reshape(pro, fit, lig), (1, 2, 0))
@@ -252,17 +261,11 @@
     )
     pair_exchange = -pair / math.sqrt(fit)
 
-    scale_ligand = 1.0 / math.sqrt(fit * pro_total)
-    rows_b = nus // (2 * n_zy)
-    keep, send = back_part(y, b_blocks, b_places, core, scale_ligand, rows_b)
-    back_b = keep + other(send, "c")
-    ligand_back = direct_sum(back_b.reshape(n_z, n_yl * rows_b, lig_total), ("z",), (n_z,), BF16)
-    ligand_back = pair_sum(ligand_back.reshape(1, n_yl, rows_b, lig_total), "yl").reshape(rows_b, lig_total)
-
     scale_protein = 1.0 / math.sqrt(fit * lig_total)
     rows = mus // n_aa
-    token = back_b.reshape(n_zy * rows_b, lig_total)
+    token = back_b.reshape(-1, lig_total)
     back_a = product(token, x_own, x_other, a_all, scale_protein, rows)
+    ligand_back = direct_sum(back_b, ("z",), (n_z,), F32)
     back_a = exchange(back_a, AA)
     here, away = jnp.sum(back_a.astype(F32), axis=0)
     there = other(away, "c")

time: 140 us -> 147 us (1.050)
  waiting for transfers between devices: 24.1 us -> 39.1 us
  local copies, waits for them, and re-layouts: 13.7 us -> 7.35 us
  starting transfers between devices: 69.5 us -> 64.5 us
  Pallas kernels: 17.5 us -> 20.5 us
    all_to_all x3 -> x4, waiting for transfers between devices: 0.01 us -> 21.5 us  [exchange(): return lax.all_to_all(pieces, axes, 0, 0, tiled=True)]
    ppermute x14 -> x7, starting transfers between devices: 26.1 us -> 13.9 us  [direct_sum(): lax.ppermute(piece.astype(sent), axes, moved(sizes, shift)).astype(F32)]
    ppermute x14 -> x7, waiting for transfers between devices: 15.5 us -> 4.53 us  [direct_sum(): lax.ppermute(piece.astype(sent), axes, moved(sizes, shift)).astype(F32)]
    unnamed x24 -> x18, local copies, waits for them, and re-layouts: 10.6 us -> 2.46 us
    all_to_all x3 -> x4, starting transfers between devices: 18.2 us -> 26.1 us  [exchange(): return lax.all_to_all(pieces, axes, 0, 0, tiled=True)]
    ppermute x6, waiting for transfers between devices: 3.86 us -> 9.07 us  [other(): return lax.ppermute(block, axis, [(0, 1), (1, 0)])]
    pallas_call x1, Pallas kernels: 6.29 us -> 8.87 us  [cross_part(): pl.pallas_call(lambda *refs: cross_kernel(*refs, step=step), in_specs=[pl...]
  transfers between devices with their start and end apart: 30 -> 24, of which waited for: 13 -> 11; matrix products, arithmetic and copies ran while one was open for 7% -> 10% of each run, Pallas kernels for 9% -> 11%
where the time goes in v7:
time: 147 us; the launch traced here: 146 us
  starting transfers between devices  64.5 us (44%)
  waiting for transfers between devices  39.1 us (27%)
  Pallas kernels  20.5 us (14%)
  other arithmetic  11.1 us (8%)
  local copies, waits for them, and re-layouts  7.35 us (5%)
  matrix products  2.54 us (2%)
    all_to_all x4, starting transfers between devices, exchange(): return lax.all_to_all(pieces, axes, 0, 0, tiled=True)  26.1 us
    all_to_all x4, waiting for transfers between devices, exchange(): return lax.all_to_all(pieces, axes, 0, 0, tiled=True)  21.5 us
    ppermute x7, starting transfers between devices, direct_sum(): lax.ppermute(piece.astype(sent), axes, moved(sizes, shift)).astype(F32)  13.9 us
    ppermute x7, starting transfers between devices, direct_gather(): blocks.append(lax.ppermute(block, axes, moved(sizes, shift)))  12.3 us
    ppermute x6, starting transfers between devices, other(): return lax.ppermute(block, axis, [(0, 1), (1, 0)])  12.2 us
    ppermute x6, waiting for transfers between devices, other(): return lax.ppermute(block, axis, [(0, 1), (1, 0)])  9.07 us
    pallas_call x1, Pallas kernels, cross_part(): pl.pallas_call(lambda *refs: cross_kernel(*refs, step=step), in_specs=[pl...  8.87 us
    pallas_call x1, Pallas kernels, back_part(): pl.pallas_call(lambda *refs: back_kernel(*refs, count=count, scale=scale,...  7.28 us
  transfers between devices with their start and end apart: 24, of which 11 were waited for; matrix products, arithmetic and copies ran while one was open for 10% of the time, Pallas kernels for 11%

profile of v7, /device:TPU:1, one launch (start us, length us, event | category | flops | bytes accessed | tf_op | source)
XLA Modules:
  0.0 146.1 jit_solution(13564711987740256792)
XLA Ops:
  0.7 2.5 %constant_dynamic-slice_fusion = (bf16[16,1,32,512]{3,2,1,0:T(8,128)(2,1)}, bf16[16,1,32,512]{3,2,1,0:T(8,128)(2,1)}) fusion(bf16[16,2,32,512]{3,2,1,0:T(8,128)(2,1)} %bitcast.85, s32[]{:T(128)S(6)} %select_n.52, s32[]{:T(128)S(6)} %select_n.51), kind=kLoop, calls=%fused_computation.36 | loop fusion | bytes 2097160 | tf_op jit(solution)/shard_map/jit(dynamic_index_in_dim)/dynamic_slice | solution.py:230
  3.1 3.2 %collective-permute-start = (bf16[512,512]{1,0:T(8,128)(2,1)}, bf16[512,512]{1,0:T(8,128)(2,1)}, u32[]{:S(2)}, u32[]{:S(2)}) collective-permute-start(bf16[512,512]{1,0:T(8,128)(2,1)} %bitcast.3), channel_id=1, source_target_pairs={{0,1},{1,0},{2,3},{3,2},{4,5},{5,4},{6,7},{7,6},{8,9},{9,8},{10,11... | collective-permute-start | bytes 1572872 | tf_op jit(solution)/shard_map/ppermute | solution.py:70
  9.8 8.9 %cross_part.1 = bf16[128,2048]{1,0:T(8,128)(2,1)} custom-call(bf16[128,2048]{1,0:T(8,128)(2,1)} %refs_0_.1, bf16[2048,2048]{1,0:T(8,128)(2,1)} %bitcast.80), custom_call_target="tpu_custom_call" | custom-call | tf_op jit(solution)/shard_map/cross_part/pallas_call | solution.py:112
  18.7 4.9 %all-to-all-start.1 = ((bf16[8,16,2048]{2,1,0:T(8,128)(2,1)}), bf16[8,16,2048]{2,1,0:T(8,128)(2,1)S(1)}, u32[]{:S(2)}, u32[]{:S(2)}) async-start(bf16[8,16,2048]{2,1,0:T(8,128)(2,1)} %bitcast.86), calls=%async_computation.1 | async-start | bytes 1048576 | tf_op jit(solution)/shard_map/all_to_all | solution.py:24
  24.5 1.8 %multiply_convert_fusion = f16[512,1024]{1,0:T(8,128)(2,1)S(1)} fusion(f32[512,1024]{1,0:T(8,128)S(1)} %fusion.12, bf16[512,512]{1,0:T(8,128)(2,1)} %collective-permute-done, bf16[1024,512]{1,0:T(8,128)(2,1)S(1)} %collective-permute-done.1.refs_2_, f32[1024]{0:T(1024)S(1)} %bitcast.92), kind=kOutput, calls=%fused_computation.2 | convolution fusion | flops 538443776 | bytes 4722688 | tf_op jit(solution)/shard_map/dot_general | solution.py:81
  27.7 6.4 %all-to-all-done.1 = bf16[8,16,2048]{2,1,0:T(8,128)(2,1)S(1)} async-done(((bf16[8,16,2048]{2,1,0:T(8,128)(2,1)}), bf16[8,16,2048]{2,1,0:T(8,128)(2,1)S(1)}, u32[]{:S(2)}, u32[]{:S(2)}) %all-to-all-start.1) | async-done | bytes 524320 | tf_op jit(solution)/shard_map/all_to_all | solution.py:24
  34.9 8.4 %all-to-all-start = ((f16[16,32,1152]{2,1,0:T(8,128)(2,1)}), f16[16,32,1152]{2,1,0:T(8,128)(2,1)S(1)}, u32[]{:S(2)}, u32[]{:S(2)}) async-start(f16[16,32,1152]{2,1,0:T(8,128)(2,1)} %bitcast.8), calls=%async_computation | async-start | bytes 2359296 | tf_op jit(solution)/shard_map/all_to_all | solution.py:24
  44.5 2.2 %collective-permute-start.3 = (bf16[16,2048]{1,0:T(8,128)(2,1)S(1)}, bf16[16,2048]{1,0:T(8,128)(2,1)S(1)}, u32[]{:S(2)}, u32[]{:S(2)}) collective-permute-start(bf16[16,2048]{1,0:T(8,128)(2,1)S(1)} %convert_element_type.25.refs_2_), channel_id=1, source_target_pairs={{0,32},{32,0},{64,96},{96,64},{128,160},{160,128},{192,224},{224,1... | collective-permute-start | bytes 196616 | tf_op jit(solution)/shard_map/ppermute | solution.py:64
  47.0 1.5 collective-permute-start.5
  48.4 2.7 %collective-permute-start.6 = (bf16[16,2048]{1,0:T(8,128)(2,1)S(1)}, bf16[16,2048]{1,0:T(8,128)(2,1)}, u32[]{:S(2)}, u32[]{:S(2)}) collective-permute-start(bf16[16,2048]{1,0:T(8,128)(2,1)S(1)} %convert_element_type.25.refs_2_), channel_id=1, source_target_pairs={{0,128},{32,160},{64,192},{96,224},{128,0},{160,32},{192,64},{224,... | collective-permute-start | bytes 196616 | tf_op jit(solution)/shard_map/ppermute | solution.py:64
  51.1 1.8 %collective-permute-start.7 = (bf16[16,2048]{1,0:T(8,128)(2,1)S(1)}, bf16[16,2048]{1,0:T(8,128)(2,1)}, u32[]{:S(2)}, u32[]{:S(2)}) collective-permute-start(bf16[16,2048]{1,0:T(8,128)(2,1)S(1)} %convert_element_type.25.refs_2_), channel_id=1, source_target_pairs={{0,160},{32,128},{64,224},{96,192},{128,32},{160,0},{192,96},{224,... | collective-permute-start | bytes 196616 | tf_op jit(solution)/shard_map/ppermute | solution.py:64
  53.0 2.1 %collective-permute-start.8 = (bf16[16,2048]{1,0:T(8,128)(2,1)S(1)}, bf16[16,2048]{1,0:T(8,128)(2,1)}, u32[]{:S(2)}, u32[]{:S(2)}) collective-permute-start(bf16[16,2048]{1,0:T(8,128)(2,1)S(1)} %convert_element_type.25.refs_2_), channel_id=1, source_target_pairs={{0,192},{32,224},{64,0},{96,32},{128,64},{160,96},{192,128},{224,1... | collective-permute-start | bytes 196616 | tf_op jit(solution)/shard_map/ppermute | solution.py:64
  55.7 1.8 %collective-permute-start.9 = (bf16[16,2048]{1,0:T(8,128)(2,1)S(1)}, bf16[16,2048]{1,0:T(8,128)(2,1)}, u32[]{:S(2)}, u32[]{:S(2)}) collective-permute-start(bf16[16,2048]{1,0:T(8,128)(2,1)S(1)} %convert_element_type.25.refs_2_), channel_id=1, source_target_pairs={{0,224},{32,192},{64,32},{96,0},{128,96},{160,64},{192,160},{224,1... | collective-permute-start | bytes 196616 | tf_op jit(solution)/shard_map/ppermute | solution.py:64
  58.6 3.6 %collective-permute-done.9.refs_9_ = bf16[16,2048]{1,0:T(8,128)(2,1)} collective-permute-done((bf16[16,2048]{1,0:T(8,128)(2,1)S(1)}, bf16[16,2048]{1,0:T(8,128)(2,1)}, u32[]{:S(2)}, u32[]{:S(2)}) %collective-permute-start.9) | collective-permute-done | bytes 65568 | tf_op jit(solution)/shard_map/ppermute | solution.py:64
  62.1 7.3 %back_part.1 = (f32[16,64,128]{2,1,0:T(8,128)}, f32[16,64,128]{2,1,0:T(8,128)}) custom-call(s32[9]{0:T(128)} %stack.57.refs_0_, bf16[2048,2048]{1,0:T(8,128)(2,1)} %bitcast.81, bf16[16,2048]{1,0:T(8,128)(2,1)} %copy-done.5, bf16[16,2048]{1,0:T(8,128)(2,1)} %copy-done.6, bf16[16,2048]{1,0:T(8,128)(2,1)} %copy-done.7, ...), custom_call_target="tpu_custom_call" | custom-call | tf_op jit(solution)/shard_map/back_part/pallas_call | solution.py:150
  69.4 4.0 %collective-permute-start.10 = (f32[16,64,128]{2,1,0:T(8,128)}, f32[16,64,128]{2,1,0:T(8,128)S(1)}, u32[]{:S(2)}, u32[]{:S(2)}) collective-permute-start(f32[16,64,128]{2,1,0:T(8,128)} %get-tuple-element.6), channel_id=1, source_target_pairs={{0,1},{1,0},{2,3},{3,2},{4,5},{5,4},{6,7},{7,6},{8,9},{9,8},{10,11... | collective-permute-start | bytes 1572872 | tf_op jit(solution)/shard_map/ppermute | solution.py:70
  73.4 1.7 %collective-permute-done.10 = f32[16,64,128]{2,1,0:T(8,128)S(1)} collective-permute-done((f32[16,64,128]{2,1,0:T(8,128)}, f32[16,64,128]{2,1,0:T(8,128)S(1)}, u32[]{:S(2)}, u32[]{:S(2)}) %collective-permute-start.10) | collective-permute-done | bytes 524320 | tf_op jit(solution)/shard_map/ppermute | solution.py:70
  75.2 1.9 %add.168 = f32[16,64,128]{2,1,0:T(8,128)} add(f32[16,64,128]{2,1,0:T(8,128)} %get-tuple-element.5, f32[16,64,128]{2,1,0:T(8,128)S(1)} %collective-permute-done.10) | non-fusion elementwise | flops 131072 | bytes 1572864 | tf_op jit(solution)/shard_map/add | solution.py:253
  78.2 2.0 %spread.1 = bf16[16,32,1024]{2,1,0:T(8,128)(2,1)} custom-call(f32[1024,128]{1,0:T(8,128)} %bitcast.82, f32[32,1024]{1,0:T(8,128)} %multiply_reduce_fusion.block_ref), custom_call_target="tpu_custom_call" | custom-call | tf_op jit(solution)/shard_map/spread/pallas_call | solution.py:173
  80.2 7.4 %all-to-all-start.2 = ((bf16[16,32,1024]{2,1,0:T(8,128)(2,1)}), bf16[16,32,1024]{2,1,0:T(8,128)(2,1)S(1)}, u32[]{:S(2)}, u32[]{:S(2)}) async-start(bf16[16,32,1024]{2,1,0:T(8,128)(2,1)} %spread.1), calls=%async_computation.2 | async-start | bytes 2097152 | tf_op jit(solution)/shard_map/all_to_all | solution.py:24
  88.5 1.4 collective-permute-start.11
  90.0 7.1 %collective-permute-done.11 = f32[8,64,128]{2,1,0:T(8,128)} collective-permute-done((f32[8,64,128]{2,1,0:T(8,128)S(1)}, f32[8,64,128]{2,1,0:T(8,128)}, u32[]{:S(2)}, u32[]{:S(2)}) %collective-permute-start.11) | collective-permute-done | bytes 262176 | tf_op jit(solution)/shard_map/ppermute | solution.py:70
  98.1 15.1 %all-to-all-done.2 = bf16[16,32,1024]{2,1,0:T(8,128)(2,1)S(1)} async-done(((bf16[16,32,1024]{2,1,0:T(8,128)(2,1)}), bf16[16,32,1024]{2,1,0:T(8,128)(2,1)S(1)}, u32[]{:S(2)}, u32[]{:S(2)}) %all-to-all-start.2) | async-done | bytes 1048608 | tf_op jit(solution)/shard_map/all_to_all | solution.py:24
  113.2 2.4 %product.1 = bf16[8,2,64,512]{3,2,1,0:T(8,128)(2,1)} custom-call(f32[512,128]{1,0:T(8,128)S(1)} %bitcast.79, bf16[1024,512]{1,0:T(8,128)(2,1)S(1)} %bitcast.77, bf16[1024,512]{1,0:T(8,128)(2,1)S(1)} %collective-permute-done.1.refs_2_, bf16[512,1024]{1,0:T(8,128)(2,1)S(1)} %bitcast.78), custom_call_target="tpu_custom_call" | custom-call | tf_op jit(solution)/shard_map/product/pallas_call | solution.py:202
  115.6 5.4 %all-to-all-start.3 = ((bf16[8,2,64,512]{3,2,1,0:T(8,128)(2,1)}), bf16[8,2,64,512]{3,2,1,0:T(8,128)(2,1)S(1)}, u32[]{:S(2)}, u32[]{:S(2)}) async-start(bf16[8,2,64,512]{3,2,1,0:T(8,128)(2,1)} %product.1), calls=%async_computation.3 | async-start | bytes 2097152 | tf_op jit(solution)/shard_map/all_to_all | solution.py:24
  121.9 3.1 %collective-permute-start.17 = (f32[64,128]{1,0:T(8,128)S(1)}, f32[64,128]{1,0:T(8,128)S(1)}, u32[]{:S(2)}, u32[]{:S(2)}) collective-permute-start(f32[64,128]{1,0:T(8,128)S(1)} %get-tuple-element.25), channel_id=1, source_target_pairs={{0,24},{4,28},{8,0},{12,4},{16,8},{20,12},{24,16},{28,20},{1,25},{... | collective-permute-start | bytes 98312 | tf_op jit(solution)/shard_map/ppermute | solution.py:57
  125.0 3.2 %collective-permute-start.16 = (f32[64,128]{1,0:T(8,128)S(1)}, f32[64,128]{1,0:T(8,128)S(1)}, u32[]{:S(2)}, u32[]{:S(2)}) collective-permute-start(f32[64,128]{1,0:T(8,128)S(1)} %get-tuple-element.26), channel_id=1, source_target_pairs={{0,20},{4,24},{8,28},{12,0},{16,4},{20,8},{24,12},{28,16},{1,21},{... | collective-permute-start | bytes 98312 | tf_op jit(solution)/shard_map/ppermute | solution.py:57
  128.2 1.6 %collective-permute-start.15 = (f32[64,128]{1,0:T(8,128)S(1)}, f32[64,128]{1,0:T(8,128)S(1)}, u32[]{:S(2)}, u32[]{:S(2)}) collective-permute-start(f32[64,128]{1,0:T(8,128)S(1)} %get-tuple-element.27), channel_id=1, source_target_pairs={{0,16},{4,20},{8,24},{12,28},{16,0},{20,4},{24,8},{28,12},{1,17},{... | collective-permute-start | bytes 98312 | tf_op jit(solution)/shard_map/ppermute | solution.py:57
  129.8 1.6 %collective-permute-start.14 = (f32[64,128]{1,0:T(8,128)S(1)}, f32[64,128]{1,0:T(8,128)S(1)}, u32[]{:S(2)}, u32[]{:S(2)}) collective-permute-start(f32[64,128]{1,0:T(8,128)S(1)} %get-tuple-element.28), channel_id=1, source_target_pairs={{0,12},{4,16},{8,20},{12,24},{16,28},{20,0},{24,4},{28,8},{1,13},{... | collective-permute-start | bytes 98312 | tf_op jit(solution)/shard_map/ppermute | solution.py:57
  131.4 3.6 %collective-permute-start.13 = (f32[64,128]{1,0:T(8,128)S(1)}, f32[64,128]{1,0:T(8,128)S(1)}, u32[]{:S(2)}, u32[]{:S(2)}) collective-permute-start(f32[64,128]{1,0:T(8,128)S(1)} %get-tuple-element.29), channel_id=1, source_target_pairs={{0,8},{4,12},{8,16},{12,20},{16,24},{20,28},{24,0},{28,4},{1,9},{5... | collective-permute-start | bytes 98312 | tf_op jit(solution)/shard_map/ppermute | solution.py:57
  136.7 2.9 %collective-permute-done.12 = f32[64,128]{1,0:T(8,128)S(1)} collective-permute-done((f32[64,128]{1,0:T(8,128)S(1)}, f32[64,128]{1,0:T(8,128)S(1)}, u32[]{:S(2)}, u32[]{:S(2)}) %collective-permute-start.12) | collective-permute-done | bytes 32800 | tf_op jit(solution)/shard_map/ppermute | solution.py:57
  141.0 3.0 %collective-permute-start.19 = (f32[64,512]{1,0:T(8,128)S(1)}, f32[64,512]{1,0:T(8,128)S(1)}, u32[]{:S(2)}, u32[]{:S(2)}) collective-permute-start(f32[64,512]{1,0:T(8,128)S(1)} %get-tuple-element.22), channel_id=1, source_target_pairs={{0,1},{1,0},{2,3},{3,2},{4,5},{5,4},{6,7},{7,6},{8,9},{9,8},{10,11... | collective-permute-start | bytes 393224 | tf_op jit(solution)/shard_map/ppermute | solution.py:70
  (72 shorter events, 18.8 us)
Async XLA Ops:
  0.6 5.8 %copy-start.1 = (bf16[1024,512]{1,0:T(8,128)(2,1)S(1)}, bf16[1024,512]{1,0:T(8,128)(2,1)}, u32[]{:S(2)}) copy-start(bf16[1024,512]{1,0:T(8,128)(2,1)} %param.6) | copy-start | bytes 3145732
  0.6 5.7 %copy-start = (bf16[64,16,512]{2,1,0:T(8,128)(2,1)S(1)}, bf16[64,16,512]{2,1,0:T(8,128)(2,1)}, u32[]{:S(2)}) copy-start(bf16[64,16,512]{2,1,0:T(8,128)(2,1)} %param.4) | copy-start | bytes 3145732
  3.1 21.4 %collective-permute-start = (bf16[512,512]{1,0:T(8,128)(2,1)}, bf16[512,512]{1,0:T(8,128)(2,1)}, u32[]{:S(2)}, u32[]{:S(2)}) collective-permute-start(bf16[512,512]{1,0:T(8,128)(2,1)} %bitcast.3), channel_id=1, source_target_pairs={{0,1},{1,0},{2,3},{3,2},{4,5},{5,4},{6,7},{7,6},{8,9},{9,8},{10,11... | collective-permute-start | bytes 1572872 | tf_op jit(solution)/shard_map/ppermute | solution.py:70
  6.4 18.2 %collective-permute-start.1 = (bf16[1024,512]{1,0:T(8,128)(2,1)S(1)}, bf16[1024,512]{1,0:T(8,128)(2,1)S(1)}, u32[]{:S(2)}, u32[]{:S(2)}) collective-permute-start(bf16[1024,512]{1,0:T(8,128)(2,1)S(1)} %bitcast.75), channel_id=1, source_target_pairs={{0,1},{1,0},{2,3},{3,2},{4,5},{5,4},{6,7},{7,6},{8,9},{9,8},{10,11... | collective-permute-start | bytes 3145736 | tf_op jit(solution)/shard_map/ppermute | solution.py:70
  9.3 15.0 %collective-permute-start.2 = (f32[2,1152]{1,0:T(2,128)S(1)}, f32[2,1152]{1,0:T(2,128)S(1)}, u32[]{:S(2)}, u32[]{:S(2)}) collective-permute-start(f32[2,1152]{1,0:T(2,128)S(1)} %broadcast_in_dim.6), channel_id=1, source_target_pairs={{0,1},{1,0},{2,3},{3,2},{4,5},{5,4},{6,7},{7,6},{8,9},{9,8},{10,11... | collective-permute-start | bytes 27656 | tf_op jit(solution)/shard_map/ppermute | solution.py:70
  9.8 13.8 %copy-start.3 = (bf16[16,1,32,512]{3,2,1,0:T(8,128)(2,1)S(1)}, bf16[16,1,32,512]{3,2,1,0:T(8,128)(2,1)}, u32[]{:S(2)}) copy-start(bf16[16,1,32,512]{3,2,1,0:T(8,128)(2,1)} %get-tuple-element.20) | copy-start | bytes 1572868
  18.7 15.4 %all-to-all-start.1 = ((bf16[8,16,2048]{2,1,0:T(8,128)(2,1)}), bf16[8,16,2048]{2,1,0:T(8,128)(2,1)S(1)}, u32[]{:S(2)}, u32[]{:S(2)}) async-start(bf16[8,16,2048]{2,1,0:T(8,128)(2,1)} %bitcast.86), calls=%async_computation.1 | async-start | bytes 1048576 | tf_op jit(solution)/shard_map/all_to_all | solution.py:24
  34.1 0.8 copy-start.2
  34.9 42.2 %all-to-all-start = ((f16[16,32,1152]{2,1,0:T(8,128)(2,1)}), f16[16,32,1152]{2,1,0:T(8,128)(2,1)S(1)}, u32[]{:S(2)}, u32[]{:S(2)}) async-start(f16[16,32,1152]{2,1,0:T(8,128)(2,1)} %bitcast.8), calls=%async_computation | async-start | bytes 2359296 | tf_op jit(solution)/shard_map/all_to_all | solution.py:24
  44.5 17.6 %copy-start.5 = (bf16[16,2048]{1,0:T(8,128)(2,1)}, bf16[16,2048]{1,0:T(8,128)(2,1)S(1)}, u32[]{:S(2)}) copy-start(bf16[16,2048]{1,0:T(8,128)(2,1)S(1)} %convert_element_type.25.refs_2_) | copy-start | bytes 196612
  44.5 8.5 %collective-permute-start.3 = (bf16[16,2048]{1,0:T(8,128)(2,1)S(1)}, bf16[16,2048]{1,0:T(8,128)(2,1)S(1)}, u32[]{:S(2)}, u32[]{:S(2)}) collective-permute-start(bf16[16,2048]{1,0:T(8,128)(2,1)S(1)} %convert_element_type.25.refs_2_), channel_id=1, source_target_pairs={{0,32},{32,0},{64,96},{96,64},{128,160},{160,128},{192,224},{224,1... | collective-permute-start | bytes 196616 | tf_op jit(solution)/shard_map/ppermute | solution.py:64
  46.7 8.3 %collective-permute-start.4 = (bf16[16,2048]{1,0:T(8,128)(2,1)S(1)}, bf16[16,2048]{1,0:T(8,128)(2,1)S(1)}, u32[]{:S(2)}, u32[]{:S(2)}) collective-permute-start(bf16[16,2048]{1,0:T(8,128)(2,1)S(1)} %convert_element_type.25.refs_2_), channel_id=1, source_target_pairs={{0,64},{32,96},{64,128},{96,160},{128,192},{160,224},{192,0},{224,... | collective-permute-start | bytes 196616 | tf_op jit(solution)/shard_map/ppermute | solution.py:64
  47.0 11.1 %collective-permute-start.5 = (bf16[16,2048]{1,0:T(8,128)(2,1)S(1)}, bf16[16,2048]{1,0:T(8,128)(2,1)}, u32[]{:S(2)}, u32[]{:S(2)}) collective-permute-start(bf16[16,2048]{1,0:T(8,128)(2,1)S(1)} %convert_element_type.25.refs_2_), channel_id=1, source_target_pairs={{0,96},{32,64},{64,160},{96,128},{128,224},{160,192},{192,32},{224... | collective-permute-start | bytes 196616 | tf_op jit(solution)/shard_map/ppermute | solution.py:64
  48.4 9.7 %collective-permute-start.6 = (bf16[16,2048]{1,0:T(8,128)(2,1)S(1)}, bf16[16,2048]{1,0:T(8,128)(2,1)}, u32[]{:S(2)}, u32[]{:S(2)}) collective-permute-start(bf16[16,2048]{1,0:T(8,128)(2,1)S(1)} %convert_element_type.25.refs_2_), channel_id=1, source_target_pairs={{0,128},{32,160},{64,192},{96,224},{128,0},{160,32},{192,64},{224,... | collective-permute-start | bytes 196616 | tf_op jit(solution)/shard_map/ppermute | solution.py:64
  51.1 7.4 %collective-permute-start.7 = (bf16[16,2048]{1,0:T(8,128)(2,1)S(1)}, bf16[16,2048]{1,0:T(8,128)(2,1)}, u32[]{:S(2)}, u32[]{:S(2)}) collective-permute-start(bf16[16,2048]{1,0:T(8,128)(2,1)S(1)} %convert_element_type.25.refs_2_), channel_id=1, source_target_pairs={{0,160},{32,128},{64,224},{96,192},{128,32},{160,0},{192,96},{224,... | collective-permute-start | bytes 196616 | tf_op jit(solution)/shard_map/ppermute | solution.py:64
  53.0 9.2 %copy-start.6 = (bf16[16,2048]{1,0:T(8,128)(2,1)}, bf16[16,2048]{1,0:T(8,128)(2,1)S(1)}, u32[]{:S(2)}) copy-start(bf16[16,2048]{1,0:T(8,128)(2,1)S(1)} %collective-permute-done.3.refs_3_) | copy-start | bytes 196612
  53.0 5.6 %collective-permute-start.8 = (bf16[16,2048]{1,0:T(8,128)(2,1)S(1)}, bf16[16,2048]{1,0:T(8,128)(2,1)}, u32[]{:S(2)}, u32[]{:S(2)}) collective-permute-start(bf16[16,2048]{1,0:T(8,128)(2,1)S(1)} %convert_element_type.25.refs_2_), channel_id=1, source_target_pairs={{0,192},{32,224},{64,0},{96,32},{128,64},{160,96},{192,128},{224,1... | collective-permute-start | bytes 196616 | tf_op jit(solution)/shard_map/ppermute | solution.py:64
  55.0 0.6 copy-start.7
  55.7 6.4 %collective-permute-start.9 = (bf16[16,2048]{1,0:T(8,128)(2,1)S(1)}, bf16[16,2048]{1,0:T(8,128)(2,1)}, u32[]{:S(2)}, u32[]{:S(2)}) collective-permute-start(bf16[16,2048]{1,0:T(8,128)(2,1)S(1)} %convert_element_type.25.refs_2_), channel_id=1, source_target_pairs={{0,224},{32,192},{64,32},{96,0},{128,96},{160,64},{192,160},{224,1... | collective-permute-start | bytes 196616 | tf_op jit(solution)/shard_map/ppermute | solution.py:64
  69.4 5.8 %collective-permute-start.10 = (f32[16,64,128]{2,1,0:T(8,128)}, f32[16,64,128]{2,1,0:T(8,128)S(1)}, u32[]{:S(2)}, u32[]{:S(2)}) collective-permute-start(f32[16,64,128]{2,1,0:T(8,128)} %get-tuple-element.6), channel_id=1, source_target_pairs={{0,1},{1,0},{2,3},{3,2},{4,5},{5,4},{6,7},{7,6},{8,9},{9,8},{10,11... | collective-permute-start | bytes 1572872 | tf_op jit(solution)/shard_map/ppermute | solution.py:70
  80.2 33.0 %all-to-all-start.2 = ((bf16[16,32,1024]{2,1,0:T(8,128)(2,1)}), bf16[16,32,1024]{2,1,0:T(8,128)(2,1)S(1)}, u32[]{:S(2)}, u32[]{:S(2)}) async-start(bf16[16,32,1024]{2,1,0:T(8,128)(2,1)} %spread.1), calls=%async_computation.2 | async-start | bytes 2097152 | tf_op jit(solution)/shard_map/all_to_all | solution.py:24
  88.5 8.5 %collective-permute-start.11 = (f32[8,64,128]{2,1,0:T(8,128)S(1)}, f32[8,64,128]{2,1,0:T(8,128)}, u32[]{:S(2)}, u32[]{:S(2)}) collective-permute-start(f32[8,64,128]{2,1,0:T(8,128)S(1)} %dynamic-slice_bitcast_fusion), channel_id=1, source_target_pairs={{0,2},{2,0},{1,3},{3,1},{4,6},{6,4},{5,7},{7,5},{8,10},{10,8},{9,1... | collective-permute-start | bytes 786440 | tf_op jit(solution)/shard_map/ppermute | solution.py:70
  115.6 24.7 %copy-start.4 = (f32[32,1024]{1,0:T(8,128)S(1)}, f32[32,1024]{1,0:T(8,128)}, u32[]{:S(2)}) copy-start(f32[32,1024]{1,0:T(8,128)} %multiply_reduce_fusion.block_ref) | copy-start | bytes 393220
  115.6 25.3 %all-to-all-start.3 = ((bf16[8,2,64,512]{3,2,1,0:T(8,128)(2,1)}), bf16[8,2,64,512]{3,2,1,0:T(8,128)(2,1)S(1)}, u32[]{:S(2)}, u32[]{:S(2)}) async-start(bf16[8,2,64,512]{3,2,1,0:T(8,128)(2,1)} %product.1), calls=%async_computation.3 | async-start | bytes 2097152 | tf_op jit(solution)/shard_map/all_to_all | solution.py:24
  121.0 10.4 %collective-permute-start.18 = (f32[64,128]{1,0:T(8,128)S(1)}, f32[64,128]{1,0:T(8,128)S(1)}, u32[]{:S(2)}, u32[]{:S(2)}) collective-permute-start(f32[64,128]{1,0:T(8,128)S(1)} %get-tuple-element.24), channel_id=1, source_target_pairs={{0,28},{4,0},{8,4},{12,8},{16,12},{20,16},{24,20},{28,24},{1,29},{... | collective-permute-start | bytes 98312 | tf_op jit(solution)/shard_map/ppermute | solution.py:57
  121.9 13.1 %collective-permute-start.17 = (f32[64,128]{1,0:T(8,128)S(1)}, f32[64,128]{1,0:T(8,128)S(1)}, u32[]{:S(2)}, u32[]{:S(2)}) collective-permute-start(f32[64,128]{1,0:T(8,128)S(1)} %get-tuple-element.25), channel_id=1, source_target_pairs={{0,24},{4,28},{8,0},{12,4},{16,8},{20,12},{24,16},{28,20},{1,25},{... | collective-permute-start | bytes 98312 | tf_op jit(solution)/shard_map/ppermute | solution.py:57
  125.0 10.2 %collective-permute-start.16 = (f32[64,128]{1,0:T(8,128)S(1)}, f32[64,128]{1,0:T(8,128)S(1)}, u32[]{:S(2)}, u32[]{:S(2)}) collective-permute-start(f32[64,128]{1,0:T(8,128)S(1)} %get-tuple-element.26), channel_id=1, source_target_pairs={{0,20},{4,24},{8,28},{12,0},{16,4},{20,8},{24,12},{28,16},{1,21},{... | collective-permute-start | bytes 98312 | tf_op jit(solution)/shard_map/ppermute | solution.py:57
  128.2 7.1 %collective-permute-start.15 = (f32[64,128]{1,0:T(8,128)S(1)}, f32[64,128]{1,0:T(8,128)S(1)}, u32[]{:S(2)}, u32[]{:S(2)}) collective-permute-start(f32[64,128]{1,0:T(8,128)S(1)} %get-tuple-element.27), channel_id=1, source_target_pairs={{0,16},{4,20},{8,24},{12,28},{16,0},{20,4},{24,8},{28,12},{1,17},{... | collective-permute-start | bytes 98312 | tf_op jit(solution)/shard_map/ppermute | solution.py:57
  129.8 6.4 %collective-permute-start.14 = (f32[64,128]{1,0:T(8,128)S(1)}, f32[64,128]{1,0:T(8,128)S(1)}, u32[]{:S(2)}, u32[]{:S(2)}) collective-permute-start(f32[64,128]{1,0:T(8,128)S(1)} %get-tuple-element.28), channel_id=1, source_target_pairs={{0,12},{4,16},{8,20},{12,24},{16,28},{20,0},{24,4},{28,8},{1,13},{... | collective-permute-start | bytes 98312 | tf_op jit(solution)/shard_map/ppermute | solution.py:57
  131.4 5.3 %collective-permute-start.13 = (f32[64,128]{1,0:T(8,128)S(1)}, f32[64,128]{1,0:T(8,128)S(1)}, u32[]{:S(2)}, u32[]{:S(2)}) collective-permute-start(f32[64,128]{1,0:T(8,128)S(1)} %get-tuple-element.29), channel_id=1, source_target_pairs={{0,8},{4,12},{8,16},{12,20},{16,24},{20,28},{24,0},{28,4},{1,9},{5... | collective-permute-start | bytes 98312 | tf_op jit(solution)/shard_map/ppermute | solution.py:57
  135.0 4.7 %collective-permute-start.12 = (f32[64,128]{1,0:T(8,128)S(1)}, f32[64,128]{1,0:T(8,128)S(1)}, u32[]{:S(2)}, u32[]{:S(2)}) collective-permute-start(f32[64,128]{1,0:T(8,128)S(1)} %get-tuple-element.23), channel_id=1, source_target_pairs={{0,4},{4,8},{8,12},{12,16},{16,20},{20,24},{24,28},{28,0},{1,5},{5... | collective-permute-start | bytes 98312 | tf_op jit(solution)/shard_map/ppermute | solution.py:57
  141.0 3.9 %collective-permute-start.19 = (f32[64,512]{1,0:T(8,128)S(1)}, f32[64,512]{1,0:T(8,128)S(1)}, u32[]{:S(2)}, u32[]{:S(2)}) collective-permute-start(f32[64,512]{1,0:T(8,128)S(1)} %get-tuple-element.22), channel_id=1, source_target_pairs={{0,1},{1,0},{2,3},{3,2},{4,5},{5,4},{6,7},{7,6},{8,9},{9,8},{10,11... | collective-permute-start | bytes 393224 | tf_op jit(solution)/shard_map/ppermute | solution.py:70

commit v8 on v5

--- a/solution.py
+++ b/solution.py
@@ -15,7 +15,7 @@
 F16 = jnp.float16
 BF16 = jnp.bfloat16
 LANES = 128
-VMEM = 54 * 2**20
+VMEM = 16 * 2**20
 
 
 def exchange(pieces, axes):
@@ -47,12 +47,12 @@
     )
 
 
-def direct_sum(pieces, axes, sizes):
+def direct_sum(pieces, axes, sizes, sent):
     own = (0,) * len(sizes)
     total = lax.dynamic_index_in_dim(pieces, peer(axes, sizes, own), 0, keepdims=False).astype(F32)
     for shift in shifts(sizes):
         piece = lax.dynamic_index_in_dim(pieces, peer(axes, sizes, shift), 0, keepdims=False)
-        total = total + lax.ppermute(piece, axes, moved(sizes, shift)).astype(F32)
+        total = total + lax.ppermute(piece.astype(sent), axes, moved(sizes, shift)).astype(F32)
     return total
 
 
@@ -73,6 +73,11 @@
     keep = lax.dynamic_index_in_dim(pieces, me, 1, keepdims=False)
     send = lax.dynamic_index_in_dim(pieces, 1 - me, 1, keepdims=False)
     return keep + other(send, axis)
+
+
+def in_order(mine, others, axis):
+    first = lax.axis_index(axis) == 0
+    return jnp.stack([jnp.where(first, mine, others), jnp.where(first, others, mine)])
 
 
 def dot(left, right, contract):
@@ -148,48 +153,49 @@
     )(jnp.stack(places + [core]).astype(jnp.int32), slab, *blocks)
 
 
-def spread_kernel(token_ref, block_ref, out_ref):
-    del token_ref
+def spread_kernel(*refs):
+    block_ref, out_ref = refs[-2:]
     out_ref[...] = jnp.broadcast_to(block_ref[...].astype(out_ref.dtype)[None], out_ref.shape)
 
 
-def spread(token, block, count):
+def spread(tokens, block, count):
     return pl.pallas_call(
         spread_kernel,
         grid=(1,),
-        in_specs=[
-            pl.BlockSpec((8, LANES), lambda i: (0, 0)),
-            pl.BlockSpec(block.shape, lambda i: (0, 0)),
-        ],
+        in_specs=[pl.BlockSpec((16, LANES), lambda i: (0, 0))] * len(tokens)
+        + [pl.BlockSpec(block.shape, lambda i: (0, 0))],
         out_specs=pl.BlockSpec((count,) + block.shape, lambda i: (0, 0, 0)),
         out_shape=jax.ShapeDtypeStruct((count,) + block.shape, BF16),
         cost_estimate=pl.CostEstimate(flops=0, bytes_accessed=0, transcendentals=0),
         name="spread",
-    )(token, block)
-
-
-def product_kernel(token_ref, left_ref, right_ref, out_ref, *, scale):
+    )(*tokens, block)
+
+
+def product_kernel(token_ref, own_ref, other_ref, right_ref, out_ref, *, scale, step):
     del token_ref
-    part = dot(left_ref[...], right_ref[...], ((1,), (1,))) * scale
-    out_ref[...] = part.astype(out_ref.dtype)
-
-
-def product(token, left, right, scale):
-    rows, depth = left.shape
-    step = min(rows, 256)
-    return pl.pallas_call(
-        lambda *refs: product_kernel(*refs, scale=scale),
-        grid=(rows // step,),
-        in_specs=[
-            pl.BlockSpec((8, LANES), lambda i: (0, 0)),
-            pl.BlockSpec((step, depth), lambda i: (i, 0)),
-            pl.BlockSpec(right.shape, lambda i: (0, 0)),
-        ],
-        out_specs=pl.BlockSpec((step, right.shape[0]), lambda i: (i, 0)),
-        out_shape=jax.ShapeDtypeStruct((rows, right.shape[0]), BF16),
+    runs = step // out_ref.shape[2]
+    for i in range(own_ref.shape[1] // step):
+        columns = pl.ds(i * step, step)
+        for k, left_ref in enumerate((own_ref, other_ref)):
+            part = dot(right_ref[...], left_ref[:, columns], ((1,), (0,))) * scale
+            part = part.T.reshape(runs, out_ref.shape[2], right_ref.shape[0])
+            out_ref[pl.ds(i * runs, runs), k] = part.astype(out_ref.dtype)
+
+
+def product(token, own, other_core, right, scale, fine):
+    total = own.shape[1]
+    step = min(total, 256)
+    whole = pl.BlockSpec(memory_space=pltpu.VMEM)
+    return pl.pallas_call(
+        lambda *refs: product_kernel(*refs, scale=scale, step=step),
+        grid=(1,),
+        in_specs=[pl.BlockSpec((8, LANES), lambda i: (0, 0)), whole, whole, whole],
+        out_specs=whole,
+        out_shape=jax.ShapeDtypeStruct((total // fine, 2, fine, right.shape[0]), BF16),
+        compiler_params=pltpu.CompilerParams(vmem_limit_bytes=VMEM),
         cost_estimate=pl.CostEstimate(flops=0, bytes_accessed=0, transcendentals=0),
         name="product",
-    )(token, left, right)
+    )(token, own, other_core, right)
 
 
 def on_device(ligand_slab, protein_slab, protein_orbitals, ligand_orbitals, *, sizes):
@@ -211,23 +217,27 @@
     orb_send = lax.dynamic_index_in_dim(orb, 1 - core, 1, keepdims=False).reshape(n_zy * pro, mus)
     orb_other = other(orb_send, "c")
 
-    tops = jnp.broadcast_to(
-        jnp.stack([largest(x_own), largest(protein_orbitals)])[:, None], (2, LANES)
-    )
-    tops = jnp.maximum(tops, other(tops, "c"))[:, 0]
-    bound = (2.0 * mus) * tops[0] * tops[1]
+    tops = jnp.stack([largest(x_own), largest(protein_orbitals)])
+    tops = jnp.broadcast_to(tops[:, None], (2, wide + LANES))
+    tops = jnp.maximum(tops, other(tops, "c"))
+    bound = (2.0 * mus) * tops[:1] * tops[1:]
     code = jnp.ceil(jnp.log2(jnp.maximum(bound, 1e-30))) + 1.0
     a_part = dot(orb_own, x_own, ((1,), (1,))) + dot(orb_other, x_other, ((1,), (1,)))
-    a_sent = (a_part * jnp.exp2(15.0 - code)).astype(F16)
-    a_sent = jnp.concatenate([a_sent, jnp.broadcast_to(code.astype(F16), (n_zy * pro, LANES))], axis=1)
+    a_sent = (a_part * jnp.exp2(15.0 - code[:, :wide])).astype(F16)
+    code = jnp.broadcast_to(code[:, wide:].astype(F16), (n_zy * pro, LANES))
+    a_sent = jnp.concatenate([a_sent, code], axis=1)
     a_got = exchange(a_sent.reshape(n_zy, pro, wide + LANES), ZY)
     codes = a_got[:, :1, wide : wide + 1].astype(F32)
     a_own = jnp.sum(a_got[:, :, :wide].astype(F32) * jnp.exp2(codes - 15.0), axis=0)
 
     b_part = cross_part(a_sent[:8, :LANES].astype(F32), ligand_orbitals, y)
-    b_own = direct_sum(b_part.reshape(n_aa, lig, fit * pro), AA, aa)
-    a_all = exchange(spread(b_own, a_own, n_zy), ZY).reshape(n_zy * pro, wide)
-    b_blocks, b_places = direct_gather(b_own.astype(BF16), AA, aa)
+    n_x, n_yh = aa
+    b_own = direct_sum(b_part.reshape(n_x, n_yh * lig, fit * pro), ("x",), (n_x,), BF16)
+    b_own = pair_sum(b_own.reshape(1, n_yh, lig, fit * pro), "yh").reshape(lig, fit * pro)
+    b_pair = b_own.astype(BF16)
+    b_pair = in_order(b_pair, other(b_pair, "yh"), "yh").reshape(n_yh * lig, fit * pro)
+    b_blocks, b_places = direct_gather(b_pair, ("x",), (n_x,))
+    a_all = exchange(spread(b_blocks[1:], a_own, n_zy), ZY).reshape(n_zy * pro, wide)
 
     pair = jnp.sum(
         jnp.transpose(a_own.reshape(pro, fit, lig), (1, 2, 0))
@@ -240,17 +250,14 @@
     rows_b = nus // (2 * n_zy)
     keep, send = back_part(y, b_blocks, b_places, core, scale_ligand, rows_b)
     back_b = keep + other(send, "c")
-    ligand_back = direct_sum(back_b.reshape(n_z, n_yl * rows_b, lig_total), ("z",), (n_z,))
-    ligand_back = pair_sum(ligand_back.reshape(1, n_yl, rows_b, lig_total), "yl").reshape(rows_b, lig_total)
+    back_b = pair_sum(back_b.reshape(n_z, n_yl, rows_b, lig_total), "yl")
+    ligand_back = direct_sum(back_b, ("z",), (n_z,), F32)
 
     scale_protein = 1.0 / math.sqrt(fit * lig_total)
-    half = n_zy * pro
     rows = mus // n_aa
-    x_chip = jnp.stack(
-        [x_own.T.reshape(n_aa, rows, wide), x_other.T.reshape(n_aa, rows, wide)], axis=1
-    ).reshape(2 * mus, wide)
-    back_a = product(back_b.reshape(n_zy * rows_b, lig_total), x_chip, a_all, scale_protein)
-    back_a = exchange(back_a.reshape(n_aa, 2, rows, half), AA)
+    token = back_b.reshape(n_z * rows_b, lig_total)
+    back_a = product(token, x_own, x_other, a_all, scale_protein, rows)
+    back_a = exchange(back_a, AA)
     here, away = jnp.sum(back_a.astype(F32), axis=0)
     there = other(away, "c")
     here = here.reshape(rows, n_zy, 1, pro)

time: 147 us -> 142 us (0.966)
  waiting for transfers between devices: 27.1 us -> 41.3 us
  starting transfers between devices: 67.5 us -> 53.6 us
  Pallas kernels: 24.3 us -> 14.2 us
  local copies, waits for them, and re-layouts: 11.2 us -> 15.2 us
  matrix products: 1.48 us -> 4.59 us
    ppermute x6 -> x8, waiting for transfers between devices: 2.22 us -> 28.1 us  [other(): return lax.ppermute(block, axis, [(0, 1), (1, 0)])]
    ppermute x14 -> x10, starting transfers between devices: 26.2 us -> 16.2 us  [direct_sum(): lax.ppermute(piece.astype(sent), axes, moved(sizes, shift)).astype(F32)]
    ppermute x7 -> x3, starting transfers between devices: 12.4 us -> 3.74 us  [direct_gather(): blocks.append(lax.ppermute(block, axes, moved(sizes, shift)))]
    ppermute x14 -> x10, waiting for transfers between devices: 20.9 us -> 12.4 us  [direct_sum(): lax.ppermute(piece.astype(sent), axes, moved(sizes, shift)).astype(F32)]
    unnamed x38 -> x36, local copies, waits for them, and re-layouts: 2.87 us -> 11.3 us
    pallas_call x1, Pallas kernels: 8.56 us -> 4.03 us  [cross_part(): pl.pallas_call(cross_kernel, grid=(rows // step,), in_specs=[pl.BlockSpec...]
    ppermute x6 -> x8, starting transfers between devices: 10.7 us -> 14.9 us  [other(): return lax.ppermute(block, axis, [(0, 1), (1, 0)])]
    ppermute x7 -> x3, waiting for transfers between devices: 4.02 us -> 0.85 us  [direct_gather(): blocks.append(lax.ppermute(block, axes, moved(sizes, shift)))]
  transfers between devices with their start and end apart: 30 -> 24, of which waited for: 12 -> 12; matrix products, arithmetic and copies ran while one was open for 12% -> 10% of each run, Pallas kernels for 12% -> 7%
where the time goes in v8:
time: 142 us; the launch traced here: 141 us
  starting transfers between devices  53.6 us (38%)
  waiting for transfers between devices  41.3 us (29%)
  local copies, waits for them, and re-layouts  15.2 us (11%)
  Pallas kernels  14.2 us (10%)
  other arithmetic  11.4 us (8%)
  matrix products  4.59 us (3%)
    ppermute x8, waiting for transfers between devices, other(): return lax.ppermute(block, axis, [(0, 1), (1, 0)])  28.1 us
    all_to_all x3, starting transfers between devices, exchange(): return lax.all_to_all(pieces, axes, 0, 0, tiled=True)  18.8 us
    ppermute x10, starting transfers between devices, direct_sum(): lax.ppermute(piece.astype(sent), axes, moved(sizes, shift)).astype(F32)  16.2 us
    ppermute x8, starting transfers between devices, other(): return lax.ppermute(block, axis, [(0, 1), (1, 0)])  14.9 us
    ppermute x10, waiting for transfers between devices, direct_sum(): lax.ppermute(piece.astype(sent), axes, moved(sizes, shift)).astype(F32)  12.4 us
    unnamed x36, local copies, waits for them, and re-layouts  11.3 us
    pallas_call x1, Pallas kernels, back_part(): pl.pallas_call(lambda *refs: back_kernel(*refs, count=count, scale=scale,...  5.79 us
    dot_general x2, matrix products, dot(): lax.dot_general(left, right, (contract, ((), ())), preferred_element_type...  4.59 us
  transfers between devices with their start and end apart: 24, of which 12 were waited for; matrix products, arithmetic and copies ran while one was open for 10% of the time, Pallas kernels for 7%

profile of v8, /device:TPU:1, one launch (start us, length us, event | category | flops | bytes accessed | tf_op | source)
XLA Modules:
  0.0 141.3 jit_solution(7451555446054329825)
XLA Ops:
  0.7 2.3 %constant_dynamic-slice_fusion = (bf16[16,1,32,512]{3,2,1,0:T(8,128)(2,1)}, bf16[16,1,32,512]{3,2,1,0:T(8,128)(2,1)S(1)}) fusion(bf16[16,2,32,512]{3,2,1,0:T(8,128)(2,1)} %bitcast.106, s32[]{:T(128)S(6)} %select_n.84, s32[]{:T(128)S(6)} %select_n.83), kind=kLoop, calls=%fused_computation.44 | loop fusion | bytes 2097160 | tf_op jit(solution)/shard_map/jit(dynamic_index_in_dim)/dynamic_slice | solution.py:217
  2.9 3.2 %collective-permute-start = (bf16[512,512]{1,0:T(8,128)(2,1)}, bf16[512,512]{1,0:T(8,128)(2,1)}, u32[]{:S(2)}, u32[]{:S(2)}) collective-permute-start(bf16[512,512]{1,0:T(8,128)(2,1)} %bitcast.3), channel_id=1, source_target_pairs={{0,1},{1,0},{2,3},{3,2},{4,5},{5,4},{6,7},{7,6},{8,9},{9,8},{10,11... | collective-permute-start | bytes 1572872 | tf_op jit(solution)/shard_map/ppermute | solution.py:68
  9.6 2.1 %fusion.14 = f32[512,1024]{1,0:T(8,128)} fusion(bf16[512,512]{1,0:T(8,128)(2,1)S(1)} %bitcast.110, bf16[1024,512]{1,0:T(8,128)(2,1)S(1)} %bitcast.95), kind=kOutput, calls=%fused_computation.55 | convolution fusion | flops 536870912 | bytes 3670016 | tf_op jit(solution)/shard_map/dot_general | solution.py:84
  11.9 2.5 %multiply_convert_fusion = f16[512,1024]{1,0:T(8,128)(2,1)S(1)} fusion(f32[512,1024]{1,0:T(8,128)} %fusion.14, bf16[512,512]{1,0:T(8,128)(2,1)} %collective-permute-done, bf16[1024,512]{1,0:T(8,128)(2,1)S(1)} %collective-permute-done.1.refs_2_, f32[1024]{0:T(1024)S(1)} %bitcast.116), kind=kOutput, calls=%fused_computation.2 | convolution fusion | flops 538443776 | bytes 4722688 | tf_op jit(solution)/shard_map/dot_general | solution.py:84
  15.7 7.6 %all-to-all-start = ((f16[16,32,1152]{2,1,0:T(8,128)(2,1)}), f16[16,32,1152]{2,1,0:T(8,128)(2,1)}, u32[]{:S(2)}, u32[]{:S(2)}) async-start(f16[16,32,1152]{2,1,0:T(8,128)(2,1)} %bitcast.105), calls=%async_computation | async-start | bytes 2359296 | tf_op jit(solution)/shard_map/all_to_all | solution.py:22
  23.4 3.4 %copy-done = bf16[64,32,2048]{2,1,0:T(8,128)(2,1)S(1)} copy-done((bf16[64,32,2048]{2,1,0:T(8,128)(2,1)S(1)}, bf16[64,32,2048]{2,1,0:T(8,128)(2,1)}, u32[]{:S(2)}) %copy-start) | copy-done | bytes 8388632
  26.7 4.0 %cross_part.1 = bf16[128,2048]{1,0:T(8,128)(2,1)S(1)} custom-call(f32[8,128]{1,0:T(8,128)S(1)} %slice_convert_fusion.token_ref, bf16[128,2048]{1,0:T(8,128)(2,1)S(1)} %copy-done.11, bf16[2048,2048]{1,0:T(8,128)(2,1)S(1)} %bitcast.92), custom_call_target="tpu_custom_call" | custom-call | tf_op jit(solution)/shard_map/cross_part/pallas_call | solution.py:99
  30.8 2.5 %collective-permute-start.5 = (bf16[32,2048]{1,0:T(8,128)(2,1)S(1)}, bf16[32,2048]{1,0:T(8,128)(2,1)S(1)}, u32[]{:S(2)}, u32[]{:S(2)}) collective-permute-start(bf16[32,2048]{1,0:T(8,128)(2,1)S(1)} %get-tuple-element.24), channel_id=1, source_target_pairs={{0,192},{64,0},{128,64},{192,128},{1,193},{65,1},{129,65},{193,129... | collective-permute-start | bytes 393224 | tf_op jit(solution)/shard_map/ppermute | solution.py:55
  34.5 4.1 %collective-permute-done.5 = bf16[32,2048]{1,0:T(8,128)(2,1)S(1)} collective-permute-done((bf16[32,2048]{1,0:T(8,128)(2,1)S(1)}, bf16[32,2048]{1,0:T(8,128)(2,1)S(1)}, u32[]{:S(2)}, u32[]{:S(2)}) %collective-permute-start.5) | collective-permute-done | bytes 131104 | tf_op jit(solution)/shard_map/ppermute | solution.py:55
  39.5 3.7 %collective-permute-done.3 = bf16[32,2048]{1,0:T(8,128)(2,1)S(1)} collective-permute-done((bf16[32,2048]{1,0:T(8,128)(2,1)S(1)}, bf16[32,2048]{1,0:T(8,128)(2,1)S(1)}, u32[]{:S(2)}, u32[]{:S(2)}) %collective-permute-start.3) | collective-permute-done | bytes 131104 | tf_op jit(solution)/shard_map/ppermute | solution.py:55
  43.3 2.7 %collective-permute-start.6 = (f32[1,16,2048]{2,1,0:T(8,128)S(1)}, f32[1,16,2048]{2,1,0:T(8,128)S(1)}, u32[]{:S(2)}, u32[]{:S(2)}) collective-permute-start(f32[1,16,2048]{2,1,0:T(8,128)S(1)} %dynamic-slice_bitcast_fusion.1), channel_id=1, source_target_pairs={{0,32},{32,0},{1,33},{33,1},{2,34},{34,2},{3,35},{35,3},{4,36},{36... | collective-permute-start | bytes 393224 | tf_op jit(solution)/shard_map/ppermute | solution.py:68
  46.0 10.4 %collective-permute-done.6 = f32[1,16,2048]{2,1,0:T(8,128)S(1)} collective-permute-done((f32[1,16,2048]{2,1,0:T(8,128)S(1)}, f32[1,16,2048]{2,1,0:T(8,128)S(1)}, u32[]{:S(2)}, u32[]{:S(2)}) %collective-permute-start.6) | collective-permute-done | bytes 131104 | tf_op jit(solution)/shard_map/ppermute | solution.py:68
  58.3 3.3 %collective-permute-done.7 = bf16[16,2048]{1,0:T(8,128)(2,1)S(1)} collective-permute-done((bf16[16,2048]{1,0:T(8,128)(2,1)S(1)}, bf16[16,2048]{1,0:T(8,128)(2,1)S(1)}, u32[]{:S(2)}, u32[]{:S(2)}) %collective-permute-start.7) | collective-permute-done | bytes 65568 | tf_op jit(solution)/shard_map/ppermute | solution.py:68
  61.8 1.7 %collective-permute-start.9 = (bf16[32,2048]{1,0:T(8,128)(2,1)S(1)}, bf16[32,2048]{1,0:T(8,128)(2,1)S(1)}, u32[]{:S(2)}, u32[]{:S(2)}) collective-permute-start(bf16[32,2048]{1,0:T(8,128)(2,1)S(1)} %bitcast.102), channel_id=1, source_target_pairs={{0,128},{64,192},{128,0},{192,64},{1,129},{65,193},{129,1},{193,65... | collective-permute-start | bytes 393224 | tf_op jit(solution)/shard_map/ppermute | solution.py:62
  63.5 2.0 %collective-permute-start.10 = (bf16[32,2048]{1,0:T(8,128)(2,1)S(1)}, bf16[32,2048]{1,0:T(8,128)(2,1)S(1)}, u32[]{:S(2)}, u32[]{:S(2)}) collective-permute-start(bf16[32,2048]{1,0:T(8,128)(2,1)S(1)} %bitcast.103), channel_id=1, source_target_pairs={{0,192},{64,0},{128,64},{192,128},{1,193},{65,1},{129,65},{193,129... | collective-permute-start | bytes 393224 | tf_op jit(solution)/shard_map/ppermute | solution.py:62
  66.3 2.2 %multiply_reduce_fusion.refs_3_ = f32[32,1024]{1,0:T(8,128)} fusion(f16[16,32,1152]{2,1,0:T(8,128)(2,1)} %all-to-all-done, f32[16]{0:T(128)S(1)} %exponential_bitcast_fusion), kind=kLoop, calls=%fused_computation.1 | loop fusion | flops 1540096 | bytes 1179712 | tf_op jit(solution)/shard_map/reduce_sum | solution.py:231
  70.5 2.0 %spread.1 = bf16[16,32,1024]{2,1,0:T(8,128)(2,1)} custom-call(bf16[32,2048]{1,0:T(8,128)(2,1)} %copy-done.3, bf16[32,2048]{1,0:T(8,128)(2,1)} %copy-done.5, bf16[32,2048]{1,0:T(8,128)(2,1)} %copy-done.7, f32[32,1024]{1,0:T(8,128)} %multiply_reduce_fusion.refs_3_), custom_call_target="tpu_custom_call" | custom-call | tf_op jit(solution)/shard_map/spread/pallas_call | solution.py:162
  72.5 6.0 %all-to-all-start.1 = ((bf16[16,32,1024]{2,1,0:T(8,128)(2,1)}), bf16[16,32,1024]{2,1,0:T(8,128)(2,1)S(1)}, u32[]{:S(2)}, u32[]{:S(2)}) async-start(bf16[16,32,1024]{2,1,0:T(8,128)(2,1)} %spread.1), calls=%async_computation.1 | async-start | bytes 2097152 | tf_op jit(solution)/shard_map/all_to_all | solution.py:22
  78.6 3.4 %copy-done.1 = bf16[64,32,2048]{2,1,0:T(8,128)(2,1)S(1)} copy-done((bf16[64,32,2048]{2,1,0:T(8,128)(2,1)S(1)}, bf16[64,32,2048]{2,1,0:T(8,128)(2,1)}, u32[]{:S(2)}) %copy-start.1) | copy-done | bytes 8388632
  82.8 5.8 %back_part.1 = (f32[16,64,128]{2,1,0:T(8,128)S(1)}, f32[16,64,128]{2,1,0:T(8,128)}) custom-call(s32[5]{0:T(128)S(1)} %stack.50.refs_0_, bf16[2048,2048]{1,0:T(8,128)(2,1)S(1)} %bitcast.93, bf16[32,2048]{1,0:T(8,128)(2,1)S(1)} %bitcast.104, bf16[32,2048]{1,0:T(8,128)(2,1)S(1)} %copy-done.4, bf16[32,2048]{1,0:T(8,128)(2,1)S(1)} %copy-done.6, ...), custom_call_target="tpu_custom_call" | custom-call | tf_op jit(solution)/shard_map/back_part/pallas_call | solution.py:139
  89.4 2.9 %collective-permute-start.11 = (f32[16,64,128]{2,1,0:T(8,128)}, f32[16,64,128]{2,1,0:T(8,128)}, u32[]{:S(2)}, u32[]{:S(2)}) collective-permute-start(f32[16,64,128]{2,1,0:T(8,128)} %get-tuple-element.6), channel_id=1, source_target_pairs={{0,1},{1,0},{2,3},{3,2},{4,5},{5,4},{6,7},{7,6},{8,9},{9,8},{10,11... | collective-permute-start | bytes 1572872 | tf_op jit(solution)/shard_map/ppermute | solution.py:68
  92.3 1.9 %collective-permute-done.11 = f32[16,64,128]{2,1,0:T(8,128)} collective-permute-done((f32[16,64,128]{2,1,0:T(8,128)}, f32[16,64,128]{2,1,0:T(8,128)}, u32[]{:S(2)}, u32[]{:S(2)}) %collective-permute-start.11) | collective-permute-done | bytes 524320 | tf_op jit(solution)/shard_map/ppermute | solution.py:68
  96.3 1.9 %collective-permute-start.12 = (f32[8,64,128]{2,1,0:T(8,128)S(1)}, f32[8,64,128]{2,1,0:T(8,128)}, u32[]{:S(2)}, u32[]{:S(2)}) collective-permute-start(f32[8,64,128]{2,1,0:T(8,128)S(1)} %dynamic-slice_bitcast_fusion), channel_id=1, source_target_pairs={{0,2},{2,0},{1,3},{3,1},{4,6},{6,4},{5,7},{7,5},{8,10},{10,8},{9,1... | collective-permute-start | bytes 786440 | tf_op jit(solution)/shard_map/ppermute | solution.py:68
  98.2 12.3 %collective-permute-done.12 = f32[8,64,128]{2,1,0:T(8,128)} collective-permute-done((f32[8,64,128]{2,1,0:T(8,128)S(1)}, f32[8,64,128]{2,1,0:T(8,128)}, u32[]{:S(2)}, u32[]{:S(2)}) %collective-permute-start.12) | collective-permute-done | bytes 262176 | tf_op jit(solution)/shard_map/ppermute | solution.py:68
  111.5 2.3 %product.1 = bf16[8,2,64,512]{3,2,1,0:T(8,128)(2,1)} custom-call(f32[512,128]{1,0:T(8,128)S(1)} %bitcast.98, bf16[1024,512]{1,0:T(8,128)(2,1)S(1)} %bitcast.96, bf16[1024,512]{1,0:T(8,128)(2,1)S(1)} %collective-permute-done.1.refs_2_, bf16[512,1024]{1,0:T(8,128)(2,1)S(1)} %bitcast.97), custom_call_target="tpu_custom_call" | custom-call | tf_op jit(solution)/shard_map/product/pallas_call | solution.py:189
  113.9 5.3 %all-to-all-start.2 = ((bf16[8,2,64,512]{3,2,1,0:T(8,128)(2,1)}), bf16[8,2,64,512]{3,2,1,0:T(8,128)(2,1)S(1)}, u32[]{:S(2)}, u32[]{:S(2)}) async-start(bf16[8,2,64,512]{3,2,1,0:T(8,128)(2,1)} %product.1), calls=%async_computation.2 | async-start | bytes 2097152 | tf_op jit(solution)/shard_map/all_to_all | solution.py:22
  119.2 1.7 %collective-permute-start.19 = (f32[64,128]{1,0:T(8,128)S(1)}, f32[64,128]{1,0:T(8,128)S(1)}, u32[]{:S(2)}, u32[]{:S(2)}) collective-permute-start(f32[64,128]{1,0:T(8,128)S(1)} %get-tuple-element.29), channel_id=1, source_target_pairs={{0,28},{4,0},{8,4},{12,8},{16,12},{20,16},{24,20},{28,24},{1,29},{... | collective-permute-start | bytes 98312 | tf_op jit(solution)/shard_map/ppermute | solution.py:55
  122.3 1.6 %collective-permute-start.17 = (f32[64,128]{1,0:T(8,128)S(1)}, f32[64,128]{1,0:T(8,128)S(1)}, u32[]{:S(2)}, u32[]{:S(2)}) collective-permute-start(f32[64,128]{1,0:T(8,128)S(1)} %get-tuple-element.31), channel_id=1, source_target_pairs={{0,20},{4,24},{8,28},{12,0},{16,4},{20,8},{24,12},{28,16},{1,21},{... | collective-permute-start | bytes 98312 | tf_op jit(solution)/shard_map/ppermute | solution.py:55
  123.9 3.9 %collective-permute-start.16 = (f32[64,128]{1,0:T(8,128)S(1)}, f32[64,128]{1,0:T(8,128)S(1)}, u32[]{:S(2)}, u32[]{:S(2)}) collective-permute-start(f32[64,128]{1,0:T(8,128)S(1)} %get-tuple-element.32), channel_id=1, source_target_pairs={{0,16},{4,20},{8,24},{12,28},{16,0},{20,4},{24,8},{28,12},{1,17},{... | collective-permute-start | bytes 98312 | tf_op jit(solution)/shard_map/ppermute | solution.py:55
  127.9 2.4 %collective-permute-start.14 = (f32[64,128]{1,0:T(8,128)S(1)}, f32[64,128]{1,0:T(8,128)S(1)}, u32[]{:S(2)}, u32[]{:S(2)}) collective-permute-start(f32[64,128]{1,0:T(8,128)S(1)} %get-tuple-element.34), channel_id=1, source_target_pairs={{0,8},{4,12},{8,16},{12,20},{16,24},{20,28},{24,0},{28,4},{1,9},{5... | collective-permute-start | bytes 98312 | tf_op jit(solution)/shard_map/ppermute | solution.py:55
  131.8 2.4 %collective-permute-done.15 = f32[64,128]{1,0:T(8,128)S(1)} collective-permute-done((f32[64,128]{1,0:T(8,128)S(1)}, f32[64,128]{1,0:T(8,128)S(1)}, u32[]{:S(2)}, u32[]{:S(2)}) %collective-permute-start.15) | collective-permute-done | bytes 32800 | tf_op jit(solution)/shard_map/ppermute | solution.py:55
  136.8 2.3 %collective-permute-start.20 = (f32[64,512]{1,0:T(8,128)S(1)}, f32[64,512]{1,0:T(8,128)S(1)}, u32[]{:S(2)}, u32[]{:S(2)}) collective-permute-start(f32[64,512]{1,0:T(8,128)S(1)} %get-tuple-element.27), channel_id=1, source_target_pairs={{0,1},{1,0},{2,3},{3,2},{4,5},{5,4},{6,7},{7,6},{8,9},{9,8},{10,11... | collective-permute-start | bytes 393224 | tf_op jit(solution)/shard_map/ppermute | solution.py:68
  (95 shorter events, 24.4 us)
Async XLA Ops:
  0.6 5.5 %copy-start.13 = (bf16[1024,512]{1,0:T(8,128)(2,1)S(1)}, bf16[1024,512]{1,0:T(8,128)(2,1)}, u32[]{:S(2)}) copy-start(bf16[1024,512]{1,0:T(8,128)(2,1)} %param.6) | copy-start | bytes 3145732
  2.9 8.9 %collective-permute-start = (bf16[512,512]{1,0:T(8,128)(2,1)}, bf16[512,512]{1,0:T(8,128)(2,1)}, u32[]{:S(2)}, u32[]{:S(2)}) collective-permute-start(bf16[512,512]{1,0:T(8,128)(2,1)} %bitcast.3), channel_id=1, source_target_pairs={{0,1},{1,0},{2,3},{3,2},{4,5},{5,4},{6,7},{7,6},{8,9},{9,8},{10,11... | collective-permute-start | bytes 1572872 | tf_op jit(solution)/shard_map/ppermute | solution.py:68
  6.2 5.7 %collective-permute-start.1 = (bf16[1024,512]{1,0:T(8,128)(2,1)S(1)}, bf16[1024,512]{1,0:T(8,128)(2,1)S(1)}, u32[]{:S(2)}, u32[]{:S(2)}) collective-permute-start(bf16[1024,512]{1,0:T(8,128)(2,1)S(1)} %bitcast.94), channel_id=1, source_target_pairs={{0,1},{1,0},{2,3},{3,2},{4,5},{5,4},{6,7},{7,6},{8,9},{9,8},{10,11... | collective-permute-start | bytes 3145736 | tf_op jit(solution)/shard_map/ppermute | solution.py:68
  9.1 2.6 %collective-permute-start.2 = (f32[2,1152]{1,0:T(2,128)S(1)}, f32[2,1152]{1,0:T(2,128)S(1)}, u32[]{:S(2)}, u32[]{:S(2)}) collective-permute-start(f32[2,1152]{1,0:T(2,128)S(1)} %broadcast_in_dim.6), channel_id=1, source_target_pairs={{0,1},{1,0},{2,3},{3,2},{4,5},{5,4},{6,7},{7,6},{8,9},{9,8},{10,11... | collective-permute-start | bytes 27656 | tf_op jit(solution)/shard_map/ppermute | solution.py:68
  14.4 9.0 %copy-start.11 = (bf16[128,2048]{1,0:T(8,128)(2,1)S(1)}, bf16[128,2048]{1,0:T(8,128)(2,1)}, u32[]{:S(2)}) copy-start(bf16[128,2048]{1,0:T(8,128)(2,1)} %left_ref.1) | copy-start | bytes 1572868
  15.7 49.8 %all-to-all-start = ((f16[16,32,1152]{2,1,0:T(8,128)(2,1)}), f16[16,32,1152]{2,1,0:T(8,128)(2,1)}, u32[]{:S(2)}, u32[]{:S(2)}) async-start(f16[16,32,1152]{2,1,0:T(8,128)(2,1)} %bitcast.105), calls=%async_computation | async-start | bytes 2359296 | tf_op jit(solution)/shard_map/all_to_all | solution.py:22
  30.8 7.8 %collective-permute-start.5 = (bf16[32,2048]{1,0:T(8,128)(2,1)S(1)}, bf16[32,2048]{1,0:T(8,128)(2,1)S(1)}, u32[]{:S(2)}, u32[]{:S(2)}) collective-permute-start(bf16[32,2048]{1,0:T(8,128)(2,1)S(1)} %get-tuple-element.24), channel_id=1, source_target_pairs={{0,192},{64,0},{128,64},{192,128},{1,193},{65,1},{129,65},{193,129... | collective-permute-start | bytes 393224 | tf_op jit(solution)/shard_map/ppermute | solution.py:55
  33.4 6.1 %collective-permute-start.4 = (bf16[32,2048]{1,0:T(8,128)(2,1)S(1)}, bf16[32,2048]{1,0:T(8,128)(2,1)S(1)}, u32[]{:S(2)}, u32[]{:S(2)}) collective-permute-start(bf16[32,2048]{1,0:T(8,128)(2,1)S(1)} %get-tuple-element.25), channel_id=1, source_target_pairs={{0,128},{64,192},{128,0},{192,64},{1,129},{65,193},{129,1},{193,65... | collective-permute-start | bytes 393224 | tf_op jit(solution)/shard_map/ppermute | solution.py:55
  33.9 9.3 %collective-permute-start.3 = (bf16[32,2048]{1,0:T(8,128)(2,1)S(1)}, bf16[32,2048]{1,0:T(8,128)(2,1)S(1)}, u32[]{:S(2)}, u32[]{:S(2)}) collective-permute-start(bf16[32,2048]{1,0:T(8,128)(2,1)S(1)} %get-tuple-element.23), channel_id=1, source_target_pairs={{0,64},{64,128},{128,192},{192,0},{1,65},{65,129},{129,193},{193,1... | collective-permute-start | bytes 393224 | tf_op jit(solution)/shard_map/ppermute | solution.py:55
  43.3 13.1 %collective-permute-start.6 = (f32[1,16,2048]{2,1,0:T(8,128)S(1)}, f32[1,16,2048]{2,1,0:T(8,128)S(1)}, u32[]{:S(2)}, u32[]{:S(2)}) collective-permute-start(f32[1,16,2048]{2,1,0:T(8,128)S(1)} %dynamic-slice_bitcast_fusion.1), channel_id=1, source_target_pairs={{0,32},{32,0},{1,33},{33,1},{2,34},{34,2},{3,35},{35,3},{4,36},{36... | collective-permute-start | bytes 393224 | tf_op jit(solution)/shard_map/ppermute | solution.py:68
  57.0 4.6 %collective-permute-start.7 = (bf16[16,2048]{1,0:T(8,128)(2,1)S(1)}, bf16[16,2048]{1,0:T(8,128)(2,1)S(1)}, u32[]{:S(2)}, u32[]{:S(2)}) collective-permute-start(bf16[16,2048]{1,0:T(8,128)(2,1)S(1)} %get-tuple-element.19), channel_id=1, source_target_pairs={{0,32},{32,0},{1,33},{33,1},{2,34},{34,2},{3,35},{35,3},{4,36},{36... | collective-permute-start | bytes 196616 | tf_op jit(solution)/shard_map/ppermute | solution.py:68
  61.7 10.8 %copy-start.9 = (bf16[2,16,2048]{2,1,0:T(8,128)(2,1)}, bf16[2,16,2048]{2,1,0:T(8,128)(2,1)S(1)}, u32[]{:S(2)}) copy-start(bf16[2,16,2048]{2,1,0:T(8,128)(2,1)S(1)} %pad_maximum_fusion.1) | copy-start | bytes 393220
  61.7 7.4 %collective-permute-start.8 = (bf16[32,2048]{1,0:T(8,128)(2,1)S(1)}, bf16[32,2048]{1,0:T(8,128)(2,1)S(1)}, u32[]{:S(2)}, u32[]{:S(2)}) collective-permute-start(bf16[32,2048]{1,0:T(8,128)(2,1)S(1)} %bitcast.101), channel_id=1, source_target_pairs={{0,64},{64,128},{128,192},{192,0},{1,65},{65,129},{129,193},{193,1... | collective-permute-start | bytes 393224 | tf_op jit(solution)/shard_map/ppermute | solution.py:62
  61.8 7.3 %collective-permute-start.9 = (bf16[32,2048]{1,0:T(8,128)(2,1)S(1)}, bf16[32,2048]{1,0:T(8,128)(2,1)S(1)}, u32[]{:S(2)}, u32[]{:S(2)}) collective-permute-start(bf16[32,2048]{1,0:T(8,128)(2,1)S(1)} %bitcast.102), channel_id=1, source_target_pairs={{0,128},{64,192},{128,0},{192,64},{1,129},{65,193},{129,1},{193,65... | collective-permute-start | bytes 393224 | tf_op jit(solution)/shard_map/ppermute | solution.py:62
  63.5 5.9 %collective-permute-start.10 = (bf16[32,2048]{1,0:T(8,128)(2,1)S(1)}, bf16[32,2048]{1,0:T(8,128)(2,1)S(1)}, u32[]{:S(2)}, u32[]{:S(2)}) collective-permute-start(bf16[32,2048]{1,0:T(8,128)(2,1)S(1)} %bitcast.103), channel_id=1, source_target_pairs={{0,192},{64,0},{128,64},{192,128},{1,193},{65,1},{129,65},{193,129... | collective-permute-start | bytes 393224 | tf_op jit(solution)/shard_map/ppermute | solution.py:62
  72.5 6.1 %copy-start.4 = (bf16[32,2048]{1,0:T(8,128)(2,1)S(1)}, bf16[32,2048]{1,0:T(8,128)(2,1)}, u32[]{:S(2)}) copy-start(bf16[32,2048]{1,0:T(8,128)(2,1)} %copy-done.3) | copy-start | bytes 393220
  72.5 6.1 %copy-start.6 = (bf16[32,2048]{1,0:T(8,128)(2,1)S(1)}, bf16[32,2048]{1,0:T(8,128)(2,1)}, u32[]{:S(2)}) copy-start(bf16[32,2048]{1,0:T(8,128)(2,1)} %copy-done.5) | copy-start | bytes 393220
  72.5 6.1 %copy-start.8 = (bf16[32,2048]{1,0:T(8,128)(2,1)S(1)}, bf16[32,2048]{1,0:T(8,128)(2,1)}, u32[]{:S(2)}) copy-start(bf16[32,2048]{1,0:T(8,128)(2,1)} %copy-done.7) | copy-start | bytes 393220
  72.5 39.0 %all-to-all-start.1 = ((bf16[16,32,1024]{2,1,0:T(8,128)(2,1)}), bf16[16,32,1024]{2,1,0:T(8,128)(2,1)S(1)}, u32[]{:S(2)}, u32[]{:S(2)}) async-start(bf16[16,32,1024]{2,1,0:T(8,128)(2,1)} %spread.1), calls=%async_computation.1 | async-start | bytes 2097152 | tf_op jit(solution)/shard_map/all_to_all | solution.py:22
  89.4 4.8 %collective-permute-start.11 = (f32[16,64,128]{2,1,0:T(8,128)}, f32[16,64,128]{2,1,0:T(8,128)}, u32[]{:S(2)}, u32[]{:S(2)}) collective-permute-start(f32[16,64,128]{2,1,0:T(8,128)} %get-tuple-element.6), channel_id=1, source_target_pairs={{0,1},{1,0},{2,3},{3,2},{4,5},{5,4},{6,7},{7,6},{8,9},{9,8},{10,11... | collective-permute-start | bytes 1572872 | tf_op jit(solution)/shard_map/ppermute | solution.py:68
  96.3 14.2 %collective-permute-start.12 = (f32[8,64,128]{2,1,0:T(8,128)S(1)}, f32[8,64,128]{2,1,0:T(8,128)}, u32[]{:S(2)}, u32[]{:S(2)}) collective-permute-start(f32[8,64,128]{2,1,0:T(8,128)S(1)} %dynamic-slice_bitcast_fusion), channel_id=1, source_target_pairs={{0,2},{2,0},{1,3},{3,1},{4,6},{6,4},{5,7},{7,5},{8,10},{10,8},{9,1... | collective-permute-start | bytes 786440 | tf_op jit(solution)/shard_map/ppermute | solution.py:68
  113.9 17.8 %copy-start.16 = (f32[1,16,2048]{2,1,0:T(8,128)S(1)}, f32[1,16,2048]{2,1,0:T(8,128)}, u32[]{:S(2)}) copy-start(f32[1,16,2048]{2,1,0:T(8,128)} %get-tuple-element.20) | copy-start | bytes 393220
  113.9 22.3 %copy-start.15 = (f32[32,1024]{1,0:T(8,128)S(1)}, f32[32,1024]{1,0:T(8,128)}, u32[]{:S(2)}) copy-start(f32[32,1024]{1,0:T(8,128)} %multiply_reduce_fusion.refs_3_) | copy-start | bytes 393220
  113.9 22.8 %all-to-all-start.2 = ((bf16[8,2,64,512]{3,2,1,0:T(8,128)(2,1)}), bf16[8,2,64,512]{3,2,1,0:T(8,128)(2,1)S(1)}, u32[]{:S(2)}, u32[]{:S(2)}) async-start(bf16[8,2,64,512]{3,2,1,0:T(8,128)(2,1)} %product.1), calls=%async_computation.2 | async-start | bytes 2097152 | tf_op jit(solution)/shard_map/all_to_all | solution.py:22
  119.2 8.7 %collective-permute-start.19 = (f32[64,128]{1,0:T(8,128)S(1)}, f32[64,128]{1,0:T(8,128)S(1)}, u32[]{:S(2)}, u32[]{:S(2)}) collective-permute-start(f32[64,128]{1,0:T(8,128)S(1)} %get-tuple-element.29), channel_id=1, source_target_pairs={{0,28},{4,0},{8,4},{12,8},{16,12},{20,16},{24,20},{28,24},{1,29},{... | collective-permute-start | bytes 98312 | tf_op jit(solution)/shard_map/ppermute | solution.py:55
  120.8 9.4 %collective-permute-start.18 = (f32[64,128]{1,0:T(8,128)S(1)}, f32[64,128]{1,0:T(8,128)S(1)}, u32[]{:S(2)}, u32[]{:S(2)}) collective-permute-start(f32[64,128]{1,0:T(8,128)S(1)} %get-tuple-element.30), channel_id=1, source_target_pairs={{0,24},{4,28},{8,0},{12,4},{16,8},{20,12},{24,16},{28,20},{1,25},{... | collective-permute-start | bytes 98312 | tf_op jit(solution)/shard_map/ppermute | solution.py:55
  122.3 9.5 %collective-permute-start.17 = (f32[64,128]{1,0:T(8,128)S(1)}, f32[64,128]{1,0:T(8,128)S(1)}, u32[]{:S(2)}, u32[]{:S(2)}) collective-permute-start(f32[64,128]{1,0:T(8,128)S(1)} %get-tuple-element.31), channel_id=1, source_target_pairs={{0,20},{4,24},{8,28},{12,0},{16,4},{20,8},{24,12},{28,16},{1,21},{... | collective-permute-start | bytes 98312 | tf_op jit(solution)/shard_map/ppermute | solution.py:55
  123.9 7.9 %collective-permute-start.16 = (f32[64,128]{1,0:T(8,128)S(1)}, f32[64,128]{1,0:T(8,128)S(1)}, u32[]{:S(2)}, u32[]{:S(2)}) collective-permute-start(f32[64,128]{1,0:T(8,128)S(1)} %get-tuple-element.32), channel_id=1, source_target_pairs={{0,16},{4,20},{8,24},{12,28},{16,0},{20,4},{24,8},{28,12},{1,17},{... | collective-permute-start | bytes 98312 | tf_op jit(solution)/shard_map/ppermute | solution.py:55
  127.9 6.4 %collective-permute-start.15 = (f32[64,128]{1,0:T(8,128)S(1)}, f32[64,128]{1,0:T(8,128)S(1)}, u32[]{:S(2)}, u32[]{:S(2)}) collective-permute-start(f32[64,128]{1,0:T(8,128)S(1)} %get-tuple-element.33), channel_id=1, source_target_pairs={{0,12},{4,16},{8,20},{12,24},{16,28},{20,0},{24,4},{28,8},{1,13},{... | collective-permute-start | bytes 98312 | tf_op jit(solution)/shard_map/ppermute | solution.py:55
  127.9 6.4 %collective-permute-start.14 = (f32[64,128]{1,0:T(8,128)S(1)}, f32[64,128]{1,0:T(8,128)S(1)}, u32[]{:S(2)}, u32[]{:S(2)}) collective-permute-start(f32[64,128]{1,0:T(8,128)S(1)} %get-tuple-element.34), channel_id=1, source_target_pairs={{0,8},{4,12},{8,16},{12,20},{16,24},{20,28},{24,0},{28,4},{1,9},{5... | collective-permute-start | bytes 98312 | tf_op jit(solution)/shard_map/ppermute | solution.py:55
  130.3 5.2 %collective-permute-start.13 = (f32[64,128]{1,0:T(8,128)S(1)}, f32[64,128]{1,0:T(8,128)S(1)}, u32[]{:S(2)}, u32[]{:S(2)}) collective-permute-start(f32[64,128]{1,0:T(8,128)S(1)} %get-tuple-element.28), channel_id=1, source_target_pairs={{0,4},{4,8},{8,12},{12,16},{16,20},{20,24},{24,28},{28,0},{1,5},{5... | collective-permute-start | bytes 98312 | tf_op jit(solution)/shard_map/ppermute | solution.py:55
  136.8 3.3 %collective-permute-start.20 = (f32[64,512]{1,0:T(8,128)S(1)}, f32[64,512]{1,0:T(8,128)S(1)}, u32[]{:S(2)}, u32[]{:S(2)}) collective-permute-start(f32[64,512]{1,0:T(8,128)S(1)} %get-tuple-element.27), channel_id=1, source_target_pairs={{0,1},{1,0},{2,3},{3,2},{4,5},{5,4},{6,7},{7,6},{8,9},{9,8},{10,11... | collective-permute-start | bytes 393224 | tf_op jit(solution)/shard_map/ppermute | solution.py:68
  (9 other events, 16.8 us)

commit v9 on v8

--- a/solution.py
+++ b/solution.py
@@ -47,23 +47,6 @@
     )
 
 
-def direct_sum(pieces, axes, sizes, sent):
-    own = (0,) * len(sizes)
-    total = lax.dynamic_index_in_dim(pieces, peer(axes, sizes, own), 0, keepdims=False).astype(F32)
-    for shift in shifts(sizes):
-        piece = lax.dynamic_index_in_dim(pieces, peer(axes, sizes, shift), 0, keepdims=False)
-        total = total + lax.ppermute(piece.astype(sent), axes, moved(sizes, shift)).astype(F32)
-    return total
-
-
-def direct_gather(block, axes, sizes):
-    blocks, places = [block], [peer(axes, sizes, (0,) * len(sizes))]
-    for shift in shifts(sizes):
-        blocks.append(lax.ppermute(block, axes, moved(sizes, shift)))
-        places.append(peer(axes, sizes, [n - s for s, n in zip(shift, sizes)]))
-    return blocks, places
-
-
 def other(block, axis):
     return lax.ppermute(block, axis, [(0, 1), (1, 0)])
 
@@ -78,6 +61,60 @@
 def in_order(mine, others, axis):
     first = lax.axis_index(axis) == 0
     return jnp.stack([jnp.where(first, mine, others), jnp.where(first, others, mine)])
+
+
+def halves(sizes):
+    every = [(0,) * len(sizes)] + shifts(sizes)
+    half = len(every) // 2
+    return every[1:half] + every[:1], every[half:]
+
+
+def joint(block, axes, sizes, first, second):
+    pairs = []
+    for core, shift in enumerate((first, second)):
+        if any(shift):
+            pairs += [(2 * i + core, 2 * j + core) for i, j in moved(sizes, shift)]
+    return lax.ppermute(block, axes + ("c",), pairs)
+
+
+def shared(pieces, axes, sizes):
+    first, second = (
+        jnp.stack(
+            [lax.dynamic_index_in_dim(pieces, peer(axes, sizes, shift), 0, keepdims=False) for shift in part]
+        )
+        for part in halves(sizes)
+    )
+    low = lax.axis_index("c") == 0
+    return jnp.where(low, first, second), jnp.where(low, second, first)
+
+
+def joint_sum(pieces, axes, sizes):
+    keep, send = shared(pieces, axes, sizes)
+    got = other(send, "c")
+    total = 0.0
+    for j, (first, second) in enumerate(zip(*halves(sizes))):
+        block = in_order(keep[j], got[j], "c")
+        total = total + joint(block, axes, sizes, first, second).astype(F32)
+    own = lax.dynamic_index_in_dim(pieces, peer(axes, sizes, (0,) * len(sizes)), 0, keepdims=False)
+    low = lax.axis_index("c") == 0
+    mine, away = jnp.where(low, total[0], total[1]), jnp.where(low, total[1], total[0])
+    return own.astype(F32) + (mine + other(away, "c"))
+
+
+def joint_gather(block, axes, sizes):
+    both = in_order(block, other(block, "c"), "c")
+    low = lax.axis_index("c") == 0
+    mine, away, mine_places, away_places = [], [], [], []
+    for first, second in zip(*halves(sizes)):
+        got = joint(both, axes, sizes, first, second)
+        mine.append(jnp.where(low, got[0], got[1]))
+        away.append(jnp.where(low, got[1], got[0]))
+        one, two = (peer(axes, sizes, [n - p for p, n in zip(shift, sizes)]) for shift in (first, second))
+        mine_places.append(jnp.where(low, one, two))
+        away_places.append(jnp.where(low, two, one))
+    theirs = other(jnp.stack(away), "c")
+    blocks = mine + [theirs[j] for j in range(len(mine))] + [block]
+    return blocks, mine_places + away_places + [peer(axes, sizes, (0,) * len(sizes))]
 
 
 def dot(left, right, contract):
@@ -112,8 +149,8 @@
     )(token, orbitals, slab)
 
 
-def back_kernel(place_ref, slab_ref, *refs, count, scale, fine):
-    blocks, (keep_ref, send_ref, all_ref) = refs[:count], refs[count:]
+def back_kernel(place_ref, slab_ref, *refs, count, scale):
+    blocks, (out_ref, all_ref) = refs[:count], refs[count:]
 
     @pl.when(pl.program_id(0) == 0)
     def _():
@@ -121,36 +158,28 @@
             rows = block_ref.shape[0]
             all_ref[pl.ds(pl.multiple_of(place_ref[k] * rows, rows), rows), :] = block_ref[...]
 
-    part = dot(all_ref[...], slab_ref[...], ((1,), (0,))) * scale
-    part = part.T.reshape(-1, 2, fine, all_ref.shape[0])
-    first, second = part[:, 0], part[:, 1]
-    low = place_ref[count] == 0
-    keep_ref[...] = jnp.where(low, first, second)
-    send_ref[...] = jnp.where(low, second, first)
-
-
-def back_part(slab, blocks, places, core, scale, fine):
+    out_ref[...] = (dot(all_ref[...], slab_ref[...], ((1,), (0,))) * scale).T
+
+
+def back_part(slab, blocks, places, scale, wide):
     count = len(blocks)
     depth, total = slab.shape
-    rows = blocks[0].shape[0]
     step = min(total, 256)
-    out = pl.BlockSpec((step // (2 * fine), fine, count * rows), lambda i, _: (i, 0, 0))
-    shape = jax.ShapeDtypeStruct((total // (2 * fine), fine, count * rows), F32)
     return pl.pallas_call(
-        lambda *refs: back_kernel(*refs, count=count, scale=scale, fine=fine),
+        lambda *refs: back_kernel(*refs, count=count, scale=scale),
         grid_spec=pltpu.PrefetchScalarGridSpec(
             num_scalar_prefetch=1,
             grid=(total // step,),
             in_specs=[pl.BlockSpec((depth, step), lambda i, _: (0, i))]
-            + [pl.BlockSpec((rows, depth), lambda i, _: (0, 0))] * count,
-            out_specs=[out, out],
-            scratch_shapes=[pltpu.VMEM((count * rows, depth), BF16)],
+            + [pl.BlockSpec(block.shape, lambda i, _: (0, 0)) for block in blocks],
+            out_specs=pl.BlockSpec((step, wide), lambda i, _: (i, 0)),
+            scratch_shapes=[pltpu.VMEM((wide, depth), BF16)],
         ),
-        out_shape=[shape, shape],
+        out_shape=jax.ShapeDtypeStruct((total, wide), F32),
         compiler_params=pltpu.CompilerParams(vmem_limit_bytes=VMEM),
         cost_estimate=pl.CostEstimate(flops=0, bytes_accessed=0, transcendentals=0),
         name="back_part",
-    )(jnp.stack(places + [core]).astype(jnp.int32), slab, *blocks)
+    )(jnp.stack(places).astype(jnp.int32), slab, *blocks)
 
 
 def spread_kernel(*refs):
@@ -231,13 +260,9 @@
     a_own = jnp.sum(a_got[:, :, :wide].astype(F32) * jnp.exp2(codes - 15.0), axis=0)
 
     b_part = cross_part(a_sent[:8, :LANES].astype(F32), ligand_orbitals, y)
-    n_x, n_yh = aa
-    b_own = direct_sum(b_part.reshape(n_x, n_yh * lig, fit * pro), ("x",), (n_x,), BF16)
-    b_own = pair_sum(b_own.reshape(1, n_yh, lig, fit * pro), "yh").reshape(lig, fit * pro)
-    b_pair = b_own.astype(BF16)
-    b_pair = in_order(b_pair, other(b_pair, "yh"), "yh").reshape(n_yh * lig, fit * pro)
-    b_blocks, b_places = direct_gather(b_pair, ("x",), (n_x,))
-    a_all = exchange(spread(b_blocks[1:], a_own, n_zy), ZY).reshape(n_zy * pro, wide)
+    b_own = joint_sum(b_part.reshape(n_aa, lig, fit * pro), AA, aa)
+    a_all = exchange(spread([b_own], a_own, n_zy), ZY).reshape(n_zy * pro, wide)
+    b_blocks, b_places = joint_gather(b_own.astype(BF16), AA, aa)
 
     pair = jnp.sum(
         jnp.transpose(a_own.reshape(pro, fit, lig), (1, 2, 0))
@@ -248,14 +273,18 @@
 
     scale_ligand = 1.0 / math.sqrt(fit * pro_total)
     rows_b = nus // (2 * n_zy)
-    keep, send = back_part(y, b_blocks, b_places, core, scale_ligand, rows_b)
+    back_b = back_part(y, b_blocks, b_places, scale_ligand, lig_total)
+    keep, send = shared(back_b.reshape(n_z, nus // n_z, lig_total), ("z",), (n_z,))
     back_b = keep + other(send, "c")
-    back_b = pair_sum(back_b.reshape(n_z, n_yl, rows_b, lig_total), "yl")
-    ligand_back = direct_sum(back_b, ("z",), (n_z,), F32)
+    total = jnp.where(core == 0, back_b[-1], 0.0)
+    for j, (first, second) in enumerate(zip(*halves((n_z,)))):
+        total = total + joint(back_b[j].astype(BF16), ("z",), (n_z,), first, second).astype(F32)
+    total = pair_sum(total.reshape(n_yl, 2, rows_b, lig_total), "c")
+    ligand_back = pair_sum(total.reshape(1, n_yl, rows_b, lig_total), "yl").reshape(rows_b, lig_total)
 
     scale_protein = 1.0 / math.sqrt(fit * lig_total)
     rows = mus // n_aa
-    token = back_b.reshape(n_z * rows_b, lig_total)
+    token = back_b.reshape(-1, lig_total)
     back_a = product(token, x_own, x_other, a_all, scale_protein, rows)
     back_a = exchange(back_a, AA)
     here, away = jnp.sum(back_a.astype(F32), axis=0)

time: 142 us -> 149 us (1.049)
  starting transfers between devices: 53.6 us -> 61.3 us
  waiting for transfers between devices: 41.3 us -> 43.9 us
    ppermute x8 -> x11, waiting for transfers between devices: 28.1 us -> 12.6 us  [other(): return lax.ppermute(block, axis, [(0, 1), (1, 0)])]
    all_to_all x3, waiting for transfers between devices: 0.01 us -> 13.7 us  [exchange(): return lax.all_to_all(pieces, axes, 0, 0, tiled=True)]
    ppermute x13 -> x12, starting transfers between devices: 19.9 us -> 29 us  [joint(): return lax.ppermute(block, axes + ('c',), pairs)]
    ppermute x13 -> x12, waiting for transfers between devices: 13.2 us -> 17.5 us  [joint(): return lax.ppermute(block, axes + ('c',), pairs)]
    unnamed x36 -> x20, local copies, waits for them, and re-layouts: 11.3 us -> 8.8 us
    ppermute x8 -> x11, starting transfers between devices: 14.9 us -> 12.6 us  [other(): return lax.ppermute(block, axis, [(0, 1), (1, 0)])]
    add x3 -> x2, other arithmetic: 1.95 us -> 0.11 us  [the longest x1 0.06 us: joint_sum(): total = total + joint(block, axes, sizes, first, second).astype(F32)]
  transfers between devices with their start and end apart: 24 -> 26, of which waited for: 12 -> 16; matrix products, arithmetic and copies ran while one was open for 10% -> 9% of each run, Pallas kernels for 7% -> 5%
where the time goes in v9:
time: 149 us; the launch traced here: 148 us
  starting transfers between devices  61.3 us (41%)
  waiting for transfers between devices  43.9 us (29%)
  local copies, waits for them, and re-layouts  13.8 us (9%)
  Pallas kernels  13.2 us (9%)
  other arithmetic  10.2 us (7%)
  matrix products  4.66 us (3%)
    ppermute x12, starting transfers between devices, joint(): return lax.ppermute(block, axes + ('c',), pairs)  29 us
    all_to_all x3, starting transfers between devices, exchange(): return lax.all_to_all(pieces, axes, 0, 0, tiled=True)  19.7 us
    ppermute x12, waiting for transfers between devices, joint(): return lax.ppermute(block, axes + ('c',), pairs)  17.5 us
    all_to_all x3, waiting for transfers between devices, exchange(): return lax.all_to_all(pieces, axes, 0, 0, tiled=True)  13.7 us
    ppermute x11, waiting for transfers between devices, other(): return lax.ppermute(block, axis, [(0, 1), (1, 0)])  12.6 us
    ppermute x11, starting transfers between devices, other(): return lax.ppermute(block, axis, [(0, 1), (1, 0)])  12.6 us
    unnamed x20, local copies, waits for them, and re-layouts  8.8 us
    pallas_call x1, Pallas kernels, back_part(): pl.pallas_call(lambda *refs: back_kernel(*refs, count=count, scale=scale)...  4.93 us
  transfers between devices with their start and end apart: 26, of which 16 were waited for; matrix products, arithmetic and copies ran while one was open for 9% of the time, Pallas kernels for 5%

profile of v9, /device:TPU:1, one launch (start us, length us, event | category | flops | bytes accessed | tf_op | source)
XLA Modules:
  0.0 148.2 jit_solution(14914267334564197957)
XLA Ops:
  0.7 2.3 %constant_dynamic-slice_fusion.17 = (bf16[16,1,32,512]{3,2,1,0:T(8,128)(2,1)}, bf16[16,1,32,512]{3,2,1,0:T(8,128)(2,1)S(1)}) fusion(bf16[16,2,32,512]{3,2,1,0:T(8,128)(2,1)} %bitcast.109, s32[]{:T(128)S(6)} %select_n.255, s32[]{:T(128)S(6)} %select_n.254), kind=kLoop, calls=%fused_computation.80 | loop fusion | bytes 2097160 | tf_op jit(solution)/shard_map/jit(dynamic_index_in_dim)/dynamic_slice | solution.py:246
  2.9 3.2 %collective-permute-start = (bf16[512,512]{1,0:T(8,128)(2,1)}, bf16[512,512]{1,0:T(8,128)(2,1)}, u32[]{:S(2)}, u32[]{:S(2)}) collective-permute-start(bf16[512,512]{1,0:T(8,128)(2,1)} %bitcast.3), channel_id=1, source_target_pairs={{0,1},{1,0},{2,3},{3,2},{4,5},{5,4},{6,7},{7,6},{8,9},{9,8},{10,11... | collective-permute-start | bytes 1572872 | tf_op jit(solution)/shard_map/ppermute | solution.py:51
  9.6 2.1 %fusion.13 = f32[512,1024]{1,0:T(8,128)} fusion(bf16[512,512]{1,0:T(8,128)(2,1)S(1)} %bitcast.111, bf16[1024,512]{1,0:T(8,128)(2,1)S(1)} %bitcast.103), kind=kOutput, calls=%fused_computation.98 | convolution fusion | flops 536870912 | bytes 3670016 | tf_op jit(solution)/shard_map/dot_general | solution.py:121
  11.9 2.6 %multiply_convert_fusion = f16[512,1024]{1,0:T(8,128)(2,1)S(1)} fusion(f32[512,1024]{1,0:T(8,128)} %fusion.13, bf16[512,512]{1,0:T(8,128)(2,1)} %collective-permute-done, bf16[1024,512]{1,0:T(8,128)(2,1)S(1)} %collective-permute-done.1.refs_2_, f32[1024]{0:T(1024)S(1)} %bitcast.117), kind=kOutput, calls=%fused_computation.2 | convolution fusion | flops 538443776 | bytes 4722688 | tf_op jit(solution)/shard_map/dot_general | solution.py:121
  14.5 3.4 %copy-done = bf16[64,32,2048]{2,1,0:T(8,128)(2,1)S(1)} copy-done((bf16[64,32,2048]{2,1,0:T(8,128)(2,1)S(1)}, bf16[64,32,2048]{2,1,0:T(8,128)(2,1)}, u32[]{:S(2)}) %copy-start) | copy-done | bytes 8388632
  17.8 4.0 %cross_part.1 = bf16[128,2048]{1,0:T(8,128)(2,1)S(1)} custom-call(f32[8,128]{1,0:T(8,128)S(1)} %slice_convert_fusion.1.token_ref, bf16[128,2048]{1,0:T(8,128)(2,1)S(1)} %copy-done.5, bf16[2048,2048]{1,0:T(8,128)(2,1)S(1)} %bitcast.100), custom_call_target="tpu_custom_call" | custom-call | tf_op jit(solution)/shard_map/cross_part/pallas_call | solution.py:136
  23.7 5.3 %collective-permute-start.7 = (bf16[2,16,2048]{2,1,0:T(8,128)(2,1)S(1)}, bf16[2,16,2048]{2,1,0:T(8,128)(2,1)S(1)}, u32[]{:S(2)}, u32[]{:S(2)}) collective-permute-start(bf16[2,16,2048]{2,1,0:T(8,128)(2,1)S(1)} %pad_maximum_fusion.9), channel_id=1, source_target_pairs={{1,225},{33,193},{65,33},{97,1},{129,97},{161,65},{193,161},{225,1... | collective-permute-start | bytes 393224 | tf_op jit(solution)/shard_map/ppermute | solution.py:77
  29.6 1.8 %collective-permute-start.5 = (bf16[2,16,2048]{2,1,0:T(8,128)(2,1)S(1)}, bf16[2,16,2048]{2,1,0:T(8,128)(2,1)S(1)}, u32[]{:S(2)}, u32[]{:S(2)}) collective-permute-start(bf16[2,16,2048]{2,1,0:T(8,128)(2,1)S(1)} %pad_maximum_fusion.7), channel_id=1, source_target_pairs={{0,64},{32,96},{64,128},{96,160},{128,192},{160,224},{192,0},{224,... | collective-permute-start | bytes 393224 | tf_op jit(solution)/shard_map/ppermute | solution.py:77
  32.9 4.6 %collective-permute-done.5 = bf16[2,16,2048]{2,1,0:T(8,128)(2,1)S(1)} collective-permute-done((bf16[2,16,2048]{2,1,0:T(8,128)(2,1)S(1)}, bf16[2,16,2048]{2,1,0:T(8,128)(2,1)S(1)}, u32[]{:S(2)}, u32[]{:S(2)}) %collective-permute-start.5) | collective-permute-done | bytes 131104 | tf_op jit(solution)/shard_map/ppermute | solution.py:77
  41.1 8.4 %all-to-all-start = ((f16[16,32,1152]{2,1,0:T(8,128)(2,1)}), f16[16,32,1152]{2,1,0:T(8,128)(2,1)}, u32[]{:S(2)}, u32[]{:S(2)}) async-start(f16[16,32,1152]{2,1,0:T(8,128)(2,1)} %bitcast.8), calls=%async_computation | async-start | bytes 2359296 | tf_op jit(solution)/shard_map/all_to_all | solution.py:22
  51.1 3.6 %collective-permute-start.11 = (bf16[2,16,2048]{2,1,0:T(8,128)(2,1)S(1)}, bf16[2,16,2048]{2,1,0:T(8,128)(2,1)S(1)}, u32[]{:S(2)}, u32[]{:S(2)}) collective-permute-start(bf16[2,16,2048]{2,1,0:T(8,128)(2,1)S(1)} %pad_maximum_fusion.10), channel_id=1, source_target_pairs={{0,64},{32,96},{64,128},{96,160},{128,192},{160,224},{192,0},{224,... | collective-permute-start | bytes 393224 | tf_op jit(solution)/shard_map/ppermute | solution.py:77
  54.8 2.0 %collective-permute-start.12 = (bf16[2,16,2048]{2,1,0:T(8,128)(2,1)S(1)}, bf16[2,16,2048]{2,1,0:T(8,128)(2,1)S(1)}, u32[]{:S(2)}, u32[]{:S(2)}) collective-permute-start(bf16[2,16,2048]{2,1,0:T(8,128)(2,1)S(1)} %pad_maximum_fusion.10), channel_id=1, source_target_pairs={{0,96},{32,64},{64,160},{96,128},{128,224},{160,192},{192,32},{224... | collective-permute-start | bytes 393224 | tf_op jit(solution)/shard_map/ppermute | solution.py:77
  56.8 2.0 %collective-permute-start.13 = (bf16[2,16,2048]{2,1,0:T(8,128)(2,1)S(1)}, bf16[2,16,2048]{2,1,0:T(8,128)(2,1)S(1)}, u32[]{:S(2)}, u32[]{:S(2)}) collective-permute-start(bf16[2,16,2048]{2,1,0:T(8,128)(2,1)S(1)} %pad_maximum_fusion.10), channel_id=1, source_target_pairs={{1,225},{33,193},{65,33},{97,1},{129,97},{161,65},{193,161},{225,1... | collective-permute-start | bytes 393224 | tf_op jit(solution)/shard_map/ppermute | solution.py:77
  60.1 5.3 %collective-permute-done.13 = bf16[2,16,2048]{2,1,0:T(8,128)(2,1)S(1)} collective-permute-done((bf16[2,16,2048]{2,1,0:T(8,128)(2,1)S(1)}, bf16[2,16,2048]{2,1,0:T(8,128)(2,1)S(1)}, u32[]{:S(2)}, u32[]{:S(2)}) %collective-permute-start.13) | collective-permute-done | bytes 131104 | tf_op jit(solution)/shard_map/ppermute | solution.py:77
  66.2 12.1 %all-to-all-done = f16[16,32,1152]{2,1,0:T(8,128)(2,1)} async-done(((f16[16,32,1152]{2,1,0:T(8,128)(2,1)}), f16[16,32,1152]{2,1,0:T(8,128)(2,1)}, u32[]{:S(2)}, u32[]{:S(2)}) %all-to-all-start) | async-done | bytes 1179680 | tf_op jit(solution)/shard_map/all_to_all | solution.py:22
  79.2 2.2 %multiply_reduce_fusion.refs_1_ = f32[32,1024]{1,0:T(8,128)} fusion(f16[16,32,1152]{2,1,0:T(8,128)(2,1)} %all-to-all-done, f32[16]{0:T(128)S(1)} %exponential_bitcast_fusion), kind=kLoop, calls=%fused_computation.1 | loop fusion | flops 1540096 | bytes 1179712 | tf_op jit(solution)/shard_map/reduce_sum | solution.py:260
  81.4 2.0 %spread.1 = bf16[16,32,1024]{2,1,0:T(8,128)(2,1)} custom-call(f32[16,2048]{1,0:T(8,128)} %get-tuple-element.18.refs_0_, f32[32,1024]{1,0:T(8,128)} %multiply_reduce_fusion.refs_1_), custom_call_target="tpu_custom_call" | custom-call | tf_op jit(solution)/shard_map/spread/pallas_call | solution.py:191
  83.4 5.8 %all-to-all-start.1 = ((bf16[16,32,1024]{2,1,0:T(8,128)(2,1)}), bf16[16,32,1024]{2,1,0:T(8,128)(2,1)S(1)}, u32[]{:S(2)}, u32[]{:S(2)}) async-start(bf16[16,32,1024]{2,1,0:T(8,128)(2,1)} %spread.1), calls=%async_computation.1 | async-start | bytes 2097152 | tf_op jit(solution)/shard_map/all_to_all | solution.py:22
  90.2 3.4 %copy-done.1 = bf16[64,32,2048]{2,1,0:T(8,128)(2,1)S(1)} copy-done((bf16[64,32,2048]{2,1,0:T(8,128)(2,1)S(1)}, bf16[64,32,2048]{2,1,0:T(8,128)(2,1)}, u32[]{:S(2)}) %copy-start.1) | copy-done | bytes 8388632
  93.5 4.9 %back_part.1 = f32[2048,128]{1,0:T(8,128)S(1)} custom-call(s32[9]{0:T(128)S(1)} %stack.127.refs_0_, bf16[2048,2048]{1,0:T(8,128)(2,1)S(1)} %bitcast.101, bf16[16,2048]{1,0:T(8,128)(2,1)S(1)} %get-tuple-element.57.refs_2_, bf16[16,2048]{1,0:T(8,128)(2,1)S(1)} %get-tuple-element.59.refs_3_, bf16[16,2048]{1,0:T(8,128)(2,1)S(1)} %get-tuple-element.61.refs_4_, ...), custom_call_target="tpu_custom_call" | custom-call | tf_op jit(solution)/shard_map/back_part/pallas_call | solution.py:168
  98.6 1.8 %collective-permute-start.15 = (f32[4,256,128]{2,1,0:T(8,128)S(1)}, f32[4,256,128]{2,1,0:T(8,128)S(1)}, u32[]{:S(2)}, u32[]{:S(2)}) collective-permute-start(f32[4,256,128]{2,1,0:T(8,128)S(1)} %fusion.1), channel_id=1, source_target_pairs={{0,1},{1,0},{2,3},{3,2},{4,5},{5,4},{6,7},{7,6},{8,9},{9,8},{10,11... | collective-permute-start | bytes 1572872 | tf_op jit(solution)/shard_map/ppermute | solution.py:51
  100.5 1.5 %collective-permute-done.15 = f32[4,256,128]{2,1,0:T(8,128)S(1)} collective-permute-done((f32[4,256,128]{2,1,0:T(8,128)S(1)}, f32[4,256,128]{2,1,0:T(8,128)S(1)}, u32[]{:S(2)}, u32[]{:S(2)}) %collective-permute-start.15) | collective-permute-done | bytes 524320 | tf_op jit(solution)/shard_map/ppermute | solution.py:51
  102.1 4.5 %collective-permute-start.19 = (bf16[256,128]{1,0:T(8,128)(2,1)S(1)}, bf16[256,128]{1,0:T(8,128)(2,1)S(1)}, u32[]{:S(2)}, u32[]{:S(2)}) collective-permute-start(bf16[256,128]{1,0:T(8,128)(2,1)S(1)} %fusion.5), channel_id=1, source_target_pairs={{1,29},{5,1},{9,5},{13,9},{17,13},{21,17},{25,21},{29,25},{3,31},{... | collective-permute-start | bytes 196616 | tf_op jit(solution)/shard_map/ppermute | solution.py:77
  106.7 2.1 %collective-permute-start.18 = (bf16[256,128]{1,0:T(8,128)(2,1)S(1)}, bf16[256,128]{1,0:T(8,128)(2,1)S(1)}, u32[]{:S(2)}, u32[]{:S(2)}) collective-permute-start(bf16[256,128]{1,0:T(8,128)(2,1)S(1)} %get-tuple-element.50), channel_id=1, source_target_pairs={{0,12},{4,16},{8,20},{12,24},{16,28},{20,0},{24,4},{28,8},{1,25},{... | collective-permute-start | bytes 196616 | tf_op jit(solution)/shard_map/ppermute | solution.py:77
  110.0 3.3 %collective-permute-start.16 = (bf16[256,128]{1,0:T(8,128)(2,1)S(1)}, bf16[256,128]{1,0:T(8,128)(2,1)S(1)}, u32[]{:S(2)}, u32[]{:S(2)}) collective-permute-start(bf16[256,128]{1,0:T(8,128)(2,1)S(1)} %get-tuple-element.49), channel_id=1, source_target_pairs={{0,4},{4,8},{8,12},{12,16},{16,20},{20,24},{24,28},{28,0},{1,17},{... | collective-permute-start | bytes 196616 | tf_op jit(solution)/shard_map/ppermute | solution.py:77
  114.8 3.0 %collective-permute-done.18 = bf16[256,128]{1,0:T(8,128)(2,1)S(1)} collective-permute-done((bf16[256,128]{1,0:T(8,128)(2,1)S(1)}, bf16[256,128]{1,0:T(8,128)(2,1)S(1)}, u32[]{:S(2)}, u32[]{:S(2)}) %collective-permute-start.18) | collective-permute-done | bytes 65568 | tf_op jit(solution)/shard_map/ppermute | solution.py:77
  120.6 2.3 %product.1 = bf16[8,2,64,512]{3,2,1,0:T(8,128)(2,1)} custom-call(f32[1024,128]{1,0:T(8,128)S(1)} %bitcast.107, bf16[1024,512]{1,0:T(8,128)(2,1)S(1)} %bitcast.104, bf16[1024,512]{1,0:T(8,128)(2,1)S(1)} %collective-permute-done.1.refs_2_, bf16[512,1024]{1,0:T(8,128)(2,1)S(1)} %bitcast.106), custom_call_target="tpu_custom_call" | custom-call | tf_op jit(solution)/shard_map/product/pallas_call | solution.py:218
  122.9 5.4 %all-to-all-start.2 = ((bf16[8,2,64,512]{3,2,1,0:T(8,128)(2,1)}), bf16[8,2,64,512]{3,2,1,0:T(8,128)(2,1)S(1)}, u32[]{:S(2)}, u32[]{:S(2)}) async-start(bf16[8,2,64,512]{3,2,1,0:T(8,128)(2,1)} %product.1), calls=%async_computation.2 | async-start | bytes 2097152 | tf_op jit(solution)/shard_map/all_to_all | solution.py:22
  128.3 2.6 %collective-permute-start.20 = (f32[2,64,128]{2,1,0:T(8,128)S(1)}, f32[2,64,128]{2,1,0:T(8,128)S(1)}, u32[]{:S(2)}, u32[]{:S(2)}) collective-permute-start(f32[2,64,128]{2,1,0:T(8,128)S(1)} %dynamic-slice_bitcast_fusion), channel_id=1, source_target_pairs={{0,1},{1,0},{2,3},{3,2},{4,5},{5,4},{6,7},{7,6},{8,9},{9,8},{10,11... | collective-permute-start | bytes 196616 | tf_op jit(solution)/shard_map/ppermute | solution.py:51
  132.7 7.1 %collective-permute-done.21 = f32[1,64,128]{2,1,0:T(8,128)S(1)} collective-permute-done((f32[1,64,128]{2,1,0:T(8,128)S(1)}, f32[1,64,128]{2,1,0:T(8,128)S(1)}, u32[]{:S(2)}, u32[]{:S(2)}) %collective-permute-start.21) | collective-permute-done | bytes 32800 | tf_op jit(solution)/shard_map/ppermute | solution.py:51
  140.9 1.6 %all-to-all-done.2 = bf16[8,2,64,512]{3,2,1,0:T(8,128)(2,1)S(1)} async-done(((bf16[8,2,64,512]{3,2,1,0:T(8,128)(2,1)}), bf16[8,2,64,512]{3,2,1,0:T(8,128)(2,1)S(1)}, u32[]{:S(2)}, u32[]{:S(2)}) %all-to-all-start.2) | async-done | bytes 1048608 | tf_op jit(solution)/shard_map/all_to_all | solution.py:22
  142.7 3.4 %collective-permute-start.22 = (f32[64,512]{1,0:T(8,128)S(1)}, f32[64,512]{1,0:T(8,128)S(1)}, u32[]{:S(2)}, u32[]{:S(2)}) collective-permute-start(f32[64,512]{1,0:T(8,128)S(1)} %get-tuple-element.48), channel_id=1, source_target_pairs={{0,1},{1,0},{2,3},{3,2},{4,5},{5,4},{6,7},{7,6},{8,9},{9,8},{10,11... | collective-permute-start | bytes 393224 | tf_op jit(solution)/shard_map/ppermute | solution.py:51
  (100 shorter events, 27.4 us)
Async XLA Ops:
  0.6 5.5 %copy-start.6 = (bf16[1024,512]{1,0:T(8,128)(2,1)S(1)}, bf16[1024,512]{1,0:T(8,128)(2,1)}, u32[]{:S(2)}) copy-start(bf16[1024,512]{1,0:T(8,128)(2,1)} %param.6) | copy-start | bytes 3145732
  0.6 5.5 %copy-start.2 = (bf16[64,16,512]{2,1,0:T(8,128)(2,1)S(1)}, bf16[64,16,512]{2,1,0:T(8,128)(2,1)}, u32[]{:S(2)}) copy-start(bf16[64,16,512]{2,1,0:T(8,128)(2,1)} %param.4) | copy-start | bytes 3145732
  2.9 8.9 %collective-permute-start = (bf16[512,512]{1,0:T(8,128)(2,1)}, bf16[512,512]{1,0:T(8,128)(2,1)}, u32[]{:S(2)}, u32[]{:S(2)}) collective-permute-start(bf16[512,512]{1,0:T(8,128)(2,1)} %bitcast.3), channel_id=1, source_target_pairs={{0,1},{1,0},{2,3},{3,2},{4,5},{5,4},{6,7},{7,6},{8,9},{9,8},{10,11... | collective-permute-start | bytes 1572872 | tf_op jit(solution)/shard_map/ppermute | solution.py:51
  6.2 5.7 %collective-permute-start.1 = (bf16[1024,512]{1,0:T(8,128)(2,1)S(1)}, bf16[1024,512]{1,0:T(8,128)(2,1)S(1)}, u32[]{:S(2)}, u32[]{:S(2)}) collective-permute-start(bf16[1024,512]{1,0:T(8,128)(2,1)S(1)} %bitcast.102), channel_id=1, source_target_pairs={{0,1},{1,0},{2,3},{3,2},{4,5},{5,4},{6,7},{7,6},{8,9},{9,8},{10,11... | collective-permute-start | bytes 3145736 | tf_op jit(solution)/shard_map/ppermute | solution.py:51
  9.1 2.6 %collective-permute-start.2 = (f32[2,1152]{1,0:T(2,128)S(1)}, f32[2,1152]{1,0:T(2,128)S(1)}, u32[]{:S(2)}, u32[]{:S(2)}) collective-permute-start(f32[2,1152]{1,0:T(2,128)S(1)} %broadcast_in_dim.17), channel_id=1, source_target_pairs={{0,1},{1,0},{2,3},{3,2},{4,5},{5,4},{6,7},{7,6},{8,9},{9,8},{10,11... | collective-permute-start | bytes 27656 | tf_op jit(solution)/shard_map/ppermute | solution.py:51
  14.5 3.4 %copy-start = (bf16[64,32,2048]{2,1,0:T(8,128)(2,1)S(1)}, bf16[64,32,2048]{2,1,0:T(8,128)(2,1)}, u32[]{:S(2)}) copy-start(bf16[64,32,2048]{2,1,0:T(8,128)(2,1)} %param.5) | copy-start | bytes 25165828
  22.0 1.6 %collective-permute-start.3 = (bf16[4,16,2048]{2,1,0:T(8,128)(2,1)S(1)}, bf16[4,16,2048]{2,1,0:T(8,128)(2,1)S(1)}, u32[]{:S(2)}, u32[]{:S(2)}) collective-permute-start(bf16[4,16,2048]{2,1,0:T(8,128)(2,1)S(1)} %get-tuple-element.38), channel_id=1, source_target_pairs={{0,1},{1,0},{2,3},{3,2},{4,5},{5,4},{6,7},{7,6},{8,9},{9,8},{10,11... | collective-permute-start | bytes 786440 | tf_op jit(solution)/shard_map/ppermute | solution.py:51
  23.7 8.9 %collective-permute-start.7 = (bf16[2,16,2048]{2,1,0:T(8,128)(2,1)S(1)}, bf16[2,16,2048]{2,1,0:T(8,128)(2,1)S(1)}, u32[]{:S(2)}, u32[]{:S(2)}) collective-permute-start(bf16[2,16,2048]{2,1,0:T(8,128)(2,1)S(1)} %pad_maximum_fusion.9), channel_id=1, source_target_pairs={{1,225},{33,193},{65,33},{97,1},{129,97},{161,65},{193,161},{225,1... | collective-permute-start | bytes 393224 | tf_op jit(solution)/shard_map/ppermute | solution.py:77
  29.0 3.9 %collective-permute-start.6 = (bf16[2,16,2048]{2,1,0:T(8,128)(2,1)S(1)}, bf16[2,16,2048]{2,1,0:T(8,128)(2,1)S(1)}, u32[]{:S(2)}, u32[]{:S(2)}) collective-permute-start(bf16[2,16,2048]{2,1,0:T(8,128)(2,1)S(1)} %pad_maximum_fusion.8), channel_id=1, source_target_pairs={{0,96},{32,64},{64,160},{96,128},{128,224},{160,192},{192,32},{224... | collective-permute-start | bytes 393224 | tf_op jit(solution)/shard_map/ppermute | solution.py:77
  29.6 7.8 %collective-permute-start.5 = (bf16[2,16,2048]{2,1,0:T(8,128)(2,1)S(1)}, bf16[2,16,2048]{2,1,0:T(8,128)(2,1)S(1)}, u32[]{:S(2)}, u32[]{:S(2)}) collective-permute-start(bf16[2,16,2048]{2,1,0:T(8,128)(2,1)S(1)} %pad_maximum_fusion.7), channel_id=1, source_target_pairs={{0,64},{32,96},{64,128},{96,160},{128,192},{160,224},{192,0},{224,... | collective-permute-start | bytes 393224 | tf_op jit(solution)/shard_map/ppermute | solution.py:77
  31.5 6.0 %collective-permute-start.4 = (bf16[2,16,2048]{2,1,0:T(8,128)(2,1)S(1)}, bf16[2,16,2048]{2,1,0:T(8,128)(2,1)S(1)}, u32[]{:S(2)}, u32[]{:S(2)}) collective-permute-start(bf16[2,16,2048]{2,1,0:T(8,128)(2,1)S(1)} %pad_maximum_fusion.6), channel_id=1, source_target_pairs={{0,32},{32,0},{64,96},{96,64},{128,160},{160,128},{192,224},{224,1... | collective-permute-start | bytes 393224 | tf_op jit(solution)/shard_map/ppermute | solution.py:77
  37.5 1.4 collective-permute-start.8
  39.6 9.9 %collective-permute-start.9 = (bf16[16,2048]{1,0:T(8,128)(2,1)S(1)}, bf16[16,2048]{1,0:T(8,128)(2,1)S(1)}, u32[]{:S(2)}, u32[]{:S(2)}) collective-permute-start(bf16[16,2048]{1,0:T(8,128)(2,1)S(1)} %get-tuple-element.17.refs_10_), channel_id=1, source_target_pairs={{0,1},{1,0},{2,3},{3,2},{4,5},{5,4},{6,7},{7,6},{8,9},{9,8},{10,11... | collective-permute-start | bytes 196616 | tf_op jit(solution)/shard_map/ppermute | solution.py:51
  41.1 37.2 %all-to-all-start = ((f16[16,32,1152]{2,1,0:T(8,128)(2,1)}), f16[16,32,1152]{2,1,0:T(8,128)(2,1)}, u32[]{:S(2)}, u32[]{:S(2)}) async-start(f16[16,32,1152]{2,1,0:T(8,128)(2,1)} %bitcast.8), calls=%async_computation | async-start | bytes 2359296 | tf_op jit(solution)/shard_map/all_to_all | solution.py:22
  49.6 9.2 %collective-permute-start.10 = (bf16[2,16,2048]{2,1,0:T(8,128)(2,1)S(1)}, bf16[2,16,2048]{2,1,0:T(8,128)(2,1)S(1)}, u32[]{:S(2)}, u32[]{:S(2)}) collective-permute-start(bf16[2,16,2048]{2,1,0:T(8,128)(2,1)S(1)} %pad_maximum_fusion.10), channel_id=1, source_target_pairs={{0,32},{32,0},{64,96},{96,64},{128,160},{160,128},{192,224},{224,1... | collective-permute-start | bytes 393224 | tf_op jit(solution)/shard_map/ppermute | solution.py:77
  51.1 8.9 %collective-permute-start.11 = (bf16[2,16,2048]{2,1,0:T(8,128)(2,1)S(1)}, bf16[2,16,2048]{2,1,0:T(8,128)(2,1)S(1)}, u32[]{:S(2)}, u32[]{:S(2)}) collective-permute-start(bf16[2,16,2048]{2,1,0:T(8,128)(2,1)S(1)} %pad_maximum_fusion.10), channel_id=1, source_target_pairs={{0,64},{32,96},{64,128},{96,160},{128,192},{160,224},{192,0},{224,... | collective-permute-start | bytes 393224 | tf_op jit(solution)/shard_map/ppermute | solution.py:77
  54.8 5.3 %collective-permute-start.12 = (bf16[2,16,2048]{2,1,0:T(8,128)(2,1)S(1)}, bf16[2,16,2048]{2,1,0:T(8,128)(2,1)S(1)}, u32[]{:S(2)}, u32[]{:S(2)}) collective-permute-start(bf16[2,16,2048]{2,1,0:T(8,128)(2,1)S(1)} %pad_maximum_fusion.10), channel_id=1, source_target_pairs={{0,96},{32,64},{64,160},{96,128},{128,224},{160,192},{192,32},{224... | collective-permute-start | bytes 393224 | tf_op jit(solution)/shard_map/ppermute | solution.py:77
  56.8 8.6 %collective-permute-start.13 = (bf16[2,16,2048]{2,1,0:T(8,128)(2,1)S(1)}, bf16[2,16,2048]{2,1,0:T(8,128)(2,1)S(1)}, u32[]{:S(2)}, u32[]{:S(2)}) collective-permute-start(bf16[2,16,2048]{2,1,0:T(8,128)(2,1)S(1)} %pad_maximum_fusion.10), channel_id=1, source_target_pairs={{1,225},{33,193},{65,33},{97,1},{129,97},{161,65},{193,161},{225,1... | collective-permute-start | bytes 393224 | tf_op jit(solution)/shard_map/ppermute | solution.py:77
  66.1 23.0 %collective-permute-start.14 = (bf16[4,16,2048]{2,1,0:T(8,128)(2,1)}, bf16[4,16,2048]{2,1,0:T(8,128)(2,1)}, u32[]{:S(2)}, u32[]{:S(2)}) collective-permute-start(bf16[4,16,2048]{2,1,0:T(8,128)(2,1)} %pad_maximum_fusion.5), channel_id=1, source_target_pairs={{0,1},{1,0},{2,3},{3,2},{4,5},{5,4},{6,7},{7,6},{8,9},{9,8},{10,11... | collective-permute-start | bytes 786440 | tf_op jit(solution)/shard_map/ppermute | solution.py:51
  83.4 36.1 %all-to-all-start.1 = ((bf16[16,32,1024]{2,1,0:T(8,128)(2,1)}), bf16[16,32,1024]{2,1,0:T(8,128)(2,1)S(1)}, u32[]{:S(2)}, u32[]{:S(2)}) async-start(bf16[16,32,1024]{2,1,0:T(8,128)(2,1)} %spread.1), calls=%async_computation.1 | async-start | bytes 2097152 | tf_op jit(solution)/shard_map/all_to_all | solution.py:22
  98.6 3.4 %collective-permute-start.15 = (f32[4,256,128]{2,1,0:T(8,128)S(1)}, f32[4,256,128]{2,1,0:T(8,128)S(1)}, u32[]{:S(2)}, u32[]{:S(2)}) collective-permute-start(f32[4,256,128]{2,1,0:T(8,128)S(1)} %fusion.1), channel_id=1, source_target_pairs={{0,1},{1,0},{2,3},{3,2},{4,5},{5,4},{6,7},{7,6},{8,9},{9,8},{10,11... | collective-permute-start | bytes 1572872 | tf_op jit(solution)/shard_map/ppermute | solution.py:51
  102.1 17.3 %copy-start.3 = (f32[4,256,128]{2,1,0:T(8,128)}, f32[4,256,128]{2,1,0:T(8,128)S(1)}, u32[]{:S(2)}) copy-start(f32[4,256,128]{2,1,0:T(8,128)S(1)} %get-tuple-element.16) | copy-start | bytes 1572868
  102.1 12.7 %collective-permute-start.19 = (bf16[256,128]{1,0:T(8,128)(2,1)S(1)}, bf16[256,128]{1,0:T(8,128)(2,1)S(1)}, u32[]{:S(2)}, u32[]{:S(2)}) collective-permute-start(bf16[256,128]{1,0:T(8,128)(2,1)S(1)} %fusion.5), channel_id=1, source_target_pairs={{1,29},{5,1},{9,5},{13,9},{17,13},{21,17},{25,21},{29,25},{3,31},{... | collective-permute-start | bytes 196616 | tf_op jit(solution)/shard_map/ppermute | solution.py:77
  106.7 11.1 %collective-permute-start.18 = (bf16[256,128]{1,0:T(8,128)(2,1)S(1)}, bf16[256,128]{1,0:T(8,128)(2,1)S(1)}, u32[]{:S(2)}, u32[]{:S(2)}) collective-permute-start(bf16[256,128]{1,0:T(8,128)(2,1)S(1)} %get-tuple-element.50), channel_id=1, source_target_pairs={{0,12},{4,16},{8,20},{12,24},{16,28},{20,0},{24,4},{28,8},{1,25},{... | collective-permute-start | bytes 196616 | tf_op jit(solution)/shard_map/ppermute | solution.py:77
  108.9 9.6 %collective-permute-start.17 = (bf16[256,128]{1,0:T(8,128)(2,1)S(1)}, bf16[256,128]{1,0:T(8,128)(2,1)S(1)}, u32[]{:S(2)}, u32[]{:S(2)}) collective-permute-start(bf16[256,128]{1,0:T(8,128)(2,1)S(1)} %get-tuple-element.51), channel_id=1, source_target_pairs={{0,8},{4,12},{8,16},{12,20},{16,24},{20,28},{24,0},{28,4},{1,21},{... | collective-permute-start | bytes 196616 | tf_op jit(solution)/shard_map/ppermute | solution.py:77
  110.0 9.5 %collective-permute-start.16 = (bf16[256,128]{1,0:T(8,128)(2,1)S(1)}, bf16[256,128]{1,0:T(8,128)(2,1)S(1)}, u32[]{:S(2)}, u32[]{:S(2)}) collective-permute-start(bf16[256,128]{1,0:T(8,128)(2,1)S(1)} %get-tuple-element.49), channel_id=1, source_target_pairs={{0,4},{4,8},{8,12},{12,16},{16,20},{20,24},{24,28},{28,0},{1,17},{... | collective-permute-start | bytes 196616 | tf_op jit(solution)/shard_map/ppermute | solution.py:77
  122.9 9.6 %copy-start.8 = (f32[16,2048]{1,0:T(8,128)S(1)}, f32[16,2048]{1,0:T(8,128)}, u32[]{:S(2)}) copy-start(f32[16,2048]{1,0:T(8,128)} %get-tuple-element.18.refs_0_) | copy-start | bytes 393220
  122.9 17.5 %copy-start.7 = (f32[32,1024]{1,0:T(8,128)S(1)}, f32[32,1024]{1,0:T(8,128)}, u32[]{:S(2)}) copy-start(f32[32,1024]{1,0:T(8,128)} %multiply_reduce_fusion.refs_1_) | copy-start | bytes 393220
  122.9 19.6 %all-to-all-start.2 = ((bf16[8,2,64,512]{3,2,1,0:T(8,128)(2,1)}), bf16[8,2,64,512]{3,2,1,0:T(8,128)(2,1)S(1)}, u32[]{:S(2)}, u32[]{:S(2)}) async-start(bf16[8,2,64,512]{3,2,1,0:T(8,128)(2,1)} %product.1), calls=%async_computation.2 | async-start | bytes 2097152 | tf_op jit(solution)/shard_map/all_to_all | solution.py:22
  128.3 3.5 %collective-permute-start.20 = (f32[2,64,128]{2,1,0:T(8,128)S(1)}, f32[2,64,128]{2,1,0:T(8,128)S(1)}, u32[]{:S(2)}, u32[]{:S(2)}) collective-permute-start(f32[2,64,128]{2,1,0:T(8,128)S(1)} %dynamic-slice_bitcast_fusion), channel_id=1, source_target_pairs={{0,1},{1,0},{2,3},{3,2},{4,5},{5,4},{6,7},{7,6},{8,9},{9,8},{10,11... | collective-permute-start | bytes 196616 | tf_op jit(solution)/shard_map/ppermute | solution.py:51
  131.9 7.9 %collective-permute-start.21 = (f32[1,64,128]{2,1,0:T(8,128)S(1)}, f32[1,64,128]{2,1,0:T(8,128)S(1)}, u32[]{:S(2)}, u32[]{:S(2)}) collective-permute-start(f32[1,64,128]{2,1,0:T(8,128)S(1)} %constant_dynamic-slice_fusion), channel_id=1, source_target_pairs={{0,2},{2,0},{1,3},{3,1},{4,6},{6,4},{5,7},{7,5},{8,10},{10,8},{9,1... | collective-permute-start | bytes 98312 | tf_op jit(solution)/shard_map/ppermute | solution.py:51
  142.7 4.4 %collective-permute-start.22 = (f32[64,512]{1,0:T(8,128)S(1)}, f32[64,512]{1,0:T(8,128)S(1)}, u32[]{:S(2)}, u32[]{:S(2)}) collective-permute-start(f32[64,512]{1,0:T(8,128)S(1)} %get-tuple-element.48), channel_id=1, source_target_pairs={{0,1},{1,0},{2,3},{3,2},{4,5},{5,4},{6,7},{7,6},{8,9},{9,8},{10,11... | collective-permute-start | bytes 393224 | tf_op jit(solution)/shard_map/ppermute | solution.py:51
  (3 other events, 7.0 us)

commit v10 on v9

--- a/solution.py
+++ b/solution.py
@@ -101,8 +101,7 @@
     return own.astype(F32) + (mine + other(away, "c"))
 
 
-def joint_gather(block, axes, sizes):
-    both = in_order(block, other(block, "c"), "c")
+def joint_gather(both, axes, sizes):
     low = lax.axis_index("c") == 0
     mine, away, mine_places, away_places = [], [], [], []
     for first, second in zip(*halves(sizes)):
@@ -113,7 +112,7 @@
         mine_places.append(jnp.where(low, one, two))
         away_places.append(jnp.where(low, two, one))
     theirs = other(jnp.stack(away), "c")
-    blocks = mine + [theirs[j] for j in range(len(mine))] + [block]
+    blocks = mine + [theirs[j] for j in range(len(mine))] + [jnp.where(low, both[0], both[1])]
     return blocks, mine_places + away_places + [peer(axes, sizes, (0,) * len(sizes))]
 
 
@@ -182,26 +181,28 @@
     )(jnp.stack(places).astype(jnp.int32), slab, *blocks)
 
 
-def spread_kernel(*refs):
-    block_ref, out_ref = refs[-2:]
+def spread_kernel(pair_ref, block_ref, out_ref, copy_ref):
     out_ref[...] = jnp.broadcast_to(block_ref[...].astype(out_ref.dtype)[None], out_ref.shape)
-
-
-def spread(tokens, block, count):
+    copy_ref[...] = pair_ref[...]
+
+
+def spread(pair, block, count):
+    whole = pl.BlockSpec(pair.shape, lambda i: (0, 0))
     return pl.pallas_call(
         spread_kernel,
         grid=(1,),
-        in_specs=[pl.BlockSpec((16, LANES), lambda i: (0, 0))] * len(tokens)
-        + [pl.BlockSpec(block.shape, lambda i: (0, 0))],
-        out_specs=pl.BlockSpec((count,) + block.shape, lambda i: (0, 0, 0)),
-        out_shape=jax.ShapeDtypeStruct((count,) + block.shape, BF16),
+        in_specs=[whole, pl.BlockSpec(block.shape, lambda i: (0, 0))],
+        out_specs=[pl.BlockSpec((count,) + block.shape, lambda i: (0, 0, 0)), whole],
+        out_shape=[
+            jax.ShapeDtypeStruct((count,) + block.shape, BF16),
+            jax.ShapeDtypeStruct(pair.shape, pair.dtype),
+        ],
         cost_estimate=pl.CostEstimate(flops=0, bytes_accessed=0, transcendentals=0),
         name="spread",
-    )(*tokens, block)
-
-
-def product_kernel(token_ref, own_ref, other_ref, right_ref, out_ref, *, scale, step):
-    del token_ref
+    )(pair, block)
+
+
+def product_kernel(parts_ref, own_ref, other_ref, right_ref, out_ref, sent_ref, *, scale, step):
     runs = step // out_ref.shape[2]
     for i in range(own_ref.shape[1] // step):
         columns = pl.ds(i * step, step)
@@ -209,22 +210,25 @@
             part = dot(right_ref[...], left_ref[:, columns], ((1,), (0,))) * scale
             part = part.T.reshape(runs, out_ref.shape[2], right_ref.shape[0])
             out_ref[pl.ds(i * runs, runs), k] = part.astype(out_ref.dtype)
-
-
-def product(token, own, other_core, right, scale, fine):
+    sent_ref[...] = parts_ref[...].astype(sent_ref.dtype)
+
+
+def product(parts, own, other_core, right, scale, fine):
     total = own.shape[1]
     step = min(total, 256)
     whole = pl.BlockSpec(memory_space=pltpu.VMEM)
     return pl.pallas_call(
         lambda *refs: product_kernel(*refs, scale=scale, step=step),
-        grid=(1,),
-        in_specs=[pl.BlockSpec((8, LANES), lambda i: (0, 0)), whole, whole, whole],
-        out_specs=whole,
-        out_shape=jax.ShapeDtypeStruct((total // fine, 2, fine, right.shape[0]), BF16),
+        in_specs=[whole] * 4,
+        out_specs=[whole] * 2,
+        out_shape=[
+            jax.ShapeDtypeStruct((total // fine, 2, fine, right.shape[0]), BF16),
+            jax.ShapeDtypeStruct(parts.shape, BF16),
+        ],
         compiler_params=pltpu.CompilerParams(vmem_limit_bytes=VMEM),
         cost_estimate=pl.CostEstimate(flops=0, bytes_accessed=0, transcendentals=0),
         name="product",
-    )(token, own, other_core, right)
+    )(parts, own, other_core, right)
 
 
 def on_device(ligand_slab, protein_slab, protein_orbitals, ligand_orbitals, *, sizes):
@@ -261,8 +265,11 @@
 
     b_part = cross_part(a_sent[:8, :LANES].astype(F32), ligand_orbitals, y)
     b_own = joint_sum(b_part.reshape(n_aa, lig, fit * pro), AA, aa)
-    a_all = exchange(spread([b_own], a_own, n_zy), ZY).reshape(n_zy * pro, wide)
-    b_blocks, b_places = joint_gather(b_own.astype(BF16), AA, aa)
+    b_pair = b_own.astype(BF16)
+    b_pair = in_order(b_pair, other(b_pair, "c"), "c").reshape(2 * lig, fit * pro)
+    a_block, b_pair = spread(b_pair, a_own, n_zy)
+    a_all = exchange(a_block, ZY).reshape(n_zy * pro, wide)
+    b_blocks, b_places = joint_gather(b_pair.reshape(2, lig, fit * pro), AA, aa)
 
     pair = jnp.sum(
         jnp.transpose(a_own.reshape(pro, fit, lig), (1, 2, 0))
@@ -276,16 +283,16 @@
     back_b = back_part(y, b_blocks, b_places, scale_ligand, lig_total)
     keep, send = shared(back_b.reshape(n_z, nus // n_z, lig_total), ("z",), (n_z,))
     back_b = keep + other(send, "c")
+    scale_protein = 1.0 / math.sqrt(fit * lig_total)
+    rows = mus // n_aa
+    back_a, sent = product(back_b, x_own, x_other, a_all, scale_protein, rows)
+
     total = jnp.where(core == 0, back_b[-1], 0.0)
     for j, (first, second) in enumerate(zip(*halves((n_z,)))):
-        total = total + joint(back_b[j].astype(BF16), ("z",), (n_z,), first, second).astype(F32)
+        total = total + joint(sent[j], ("z",), (n_z,), first, second).astype(F32)
     total = pair_sum(total.reshape(n_yl, 2, rows_b, lig_total), "c")
     ligand_back = pair_sum(total.reshape(1, n_yl, rows_b, lig_total), "yl").reshape(rows_b, lig_total)
 
-    scale_protein = 1.0 / math.sqrt(fit * lig_total)
-    rows = mus // n_aa
-    token = back_b.reshape(-1, lig_total)
-    back_a = product(token, x_own, x_other, a_all, scale_protein, rows)
     back_a = exchange(back_a, AA)
     here, away = jnp.sum(back_a.astype(F32), axis=0)
     there = other(away, "c")

time: 149 us -> 151 us (1.013)
  starting transfers between devices: 61.3 us -> 51.5 us
  other arithmetic: 10.2 us -> 17.5 us
  local copies, waits for them, and re-layouts: 13.8 us -> 17.1 us
  waiting for transfers between devices: 43.9 us -> 46.2 us
    all_to_all x3, waiting for transfers between devices: 13.7 us -> 38.9 us  [exchange(): return lax.all_to_all(pieces, axes, 0, 0, tiled=True)]
    ppermute x12, waiting for transfers between devices: 17.5 us -> 0.58 us  [joint(): return lax.ppermute(block, axes + ('c',), pairs)]
    ppermute x11, starting transfers between devices: 12.6 us -> 4.86 us  [other(): return lax.ppermute(block, axis, [(0, 1), (1, 0)])]
    ppermute x11, waiting for transfers between devices: 12.6 us -> 6.65 us  [other(): return lax.ppermute(block, axis, [(0, 1), (1, 0)])]
    add x1 -> x2, other arithmetic: 0.05 us -> 3.12 us  [the longest x1 2.17 us: on_device(): back_b = keep + other(send, 'c')]
    another operation x6, other arithmetic: 0.09 us -> 2.68 us  [in_order(): jnp.stack([jnp.where(first, mine, others), jnp.where(first, others, mine)])]
    ppermute x12, starting transfers between devices: 29 us -> 27 us  [joint(): return lax.ppermute(block, axes + ('c',), pairs)]
    select_n x4, other arithmetic: 0.06 us -> 1.8 us  [joint_gather(): away.append(jnp.where(low, got[1], got[0]))]
  transfers between devices with their start and end apart: 26 -> 26, of which waited for: 16 -> 10; matrix products, arithmetic and copies ran while one was open for 9% -> 15% of each run, Pallas kernels for 5% -> 3%
where the time goes in v10:
time: 151 us
  starting transfers between devices  51.5 us (34%)
  waiting for transfers between devices  46.2 us (31%)
  other arithmetic  17.5 us (12%)
  local copies, waits for them, and re-layouts  17.1 us (11%)
  Pallas kernels  12.4 us (8%)
  matrix products  4.65 us (3%)
    all_to_all x3, waiting for transfers between devices, exchange(): return lax.all_to_all(pieces, axes, 0, 0, tiled=True)  38.9 us
    ppermute x12, starting transfers between devices, joint(): return lax.ppermute(block, axes + ('c',), pairs)  27 us
    all_to_all x3, starting transfers between devices, exchange(): return lax.all_to_all(pieces, axes, 0, 0, tiled=True)  19.7 us
    unnamed x32, local copies, waits for them, and re-layouts  10.4 us
    ppermute x11, waiting for transfers between devices, other(): return lax.ppermute(block, axis, [(0, 1), (1, 0)])  6.65 us
    pallas_call x1, Pallas kernels, back_part(): pl.pallas_call(lambda *refs: back_kernel(*refs, count=count, scale=scale)...  4.92 us
    ppermute x11, starting transfers between devices, other(): return lax.ppermute(block, axis, [(0, 1), (1, 0)])  4.86 us
    dot_general x2, matrix products, dot(): lax.dot_general(left, right, (contract, ((), ())), preferred_element_type...  4.65 us
  transfers between devices with their start and end apart: 26, of which 10 were waited for; matrix products, arithmetic and copies ran while one was open for 15% of the time, Pallas kernels for 3%

profile of v10, /device:TPU:1, one launch (start us, length us, event | category | flops | bytes accessed | tf_op | source)
XLA Modules:
  0.0 150.6 jit_solution(6486433999793590989)
XLA Ops:
  0.7 2.3 %constant_dynamic-slice_fusion.17 = (bf16[16,1,32,512]{3,2,1,0:T(8,128)(2,1)}, bf16[16,1,32,512]{3,2,1,0:T(8,128)(2,1)S(1)}) fusion(bf16[16,2,32,512]{3,2,1,0:T(8,128)(2,1)} %bitcast.107, s32[]{:T(128)S(6)} %select_n.259, s32[]{:T(128)S(6)} %select_n.258), kind=kLoop, calls=%fused_computation.82 | loop fusion | bytes 2097160 | tf_op jit(solution)/shard_map/jit(dynamic_index_in_dim)/dynamic_slice | solution.py:250
  2.9 3.2 %collective-permute-start = (bf16[512,512]{1,0:T(8,128)(2,1)}, bf16[512,512]{1,0:T(8,128)(2,1)}, u32[]{:S(2)}, u32[]{:S(2)}) collective-permute-start(bf16[512,512]{1,0:T(8,128)(2,1)} %bitcast.3), channel_id=1, source_target_pairs={{0,1},{1,0},{2,3},{3,2},{4,5},{5,4},{6,7},{7,6},{8,9},{9,8},{10,11... | collective-permute-start | bytes 1572872 | tf_op jit(solution)/shard_map/ppermute | solution.py:51
  7.7 1.4 maximum_convert_fusion
  9.6 2.1 %fusion.13 = f32[512,1024]{1,0:T(8,128)} fusion(bf16[512,512]{1,0:T(8,128)(2,1)S(1)} %bitcast.109, bf16[1024,512]{1,0:T(8,128)(2,1)S(1)} %bitcast.102), kind=kOutput, calls=%fused_computation.99 | convolution fusion | flops 536870912 | bytes 3670016 | tf_op jit(solution)/shard_map/dot_general | solution.py:120
  11.9 2.6 %multiply_convert_fusion = f16[512,1024]{1,0:T(8,128)(2,1)S(1)} fusion(f32[512,1024]{1,0:T(8,128)} %fusion.13, bf16[512,512]{1,0:T(8,128)(2,1)} %collective-permute-done, bf16[1024,512]{1,0:T(8,128)(2,1)S(1)} %collective-permute-done.1.refs_2_, f32[1024]{0:T(1024)S(1)} %bitcast.120), kind=kOutput, calls=%fused_computation.2 | convolution fusion | flops 538443776 | bytes 4722688 | tf_op jit(solution)/shard_map/dot_general | solution.py:120
  14.5 3.4 %copy-done = bf16[64,32,2048]{2,1,0:T(8,128)(2,1)S(1)} copy-done((bf16[64,32,2048]{2,1,0:T(8,128)(2,1)S(1)}, bf16[64,32,2048]{2,1,0:T(8,128)(2,1)}, u32[]{:S(2)}) %copy-start) | copy-done | bytes 8388632
  17.8 4.0 %cross_part.1 = bf16[128,2048]{1,0:T(8,128)(2,1)S(1)} custom-call(f32[8,128]{1,0:T(8,128)S(1)} %slice_convert_fusion.token_ref, bf16[128,2048]{1,0:T(8,128)(2,1)S(1)} %copy-done.5, bf16[2048,2048]{1,0:T(8,128)(2,1)S(1)} %bitcast.99), custom_call_target="tpu_custom_call" | custom-call | tf_op jit(solution)/shard_map/cross_part/pallas_call | solution.py:135
  22.1 1.5 collective-permute-done.3
  23.7 5.3 %collective-permute-start.7 = (bf16[2,16,2048]{2,1,0:T(8,128)(2,1)S(1)}, bf16[2,16,2048]{2,1,0:T(8,128)(2,1)}, u32[]{:S(2)}, u32[]{:S(2)}) collective-permute-start(bf16[2,16,2048]{2,1,0:T(8,128)(2,1)S(1)} %pad_maximum_fusion.9), channel_id=1, source_target_pairs={{1,225},{33,193},{65,33},{97,1},{129,97},{161,65},{193,161},{225,1... | collective-permute-start | bytes 393224 | tf_op jit(solution)/shard_map/ppermute | solution.py:77
  30.8 1.7 %collective-permute-start.5 = (bf16[2,16,2048]{2,1,0:T(8,128)(2,1)}, bf16[2,16,2048]{2,1,0:T(8,128)(2,1)}, u32[]{:S(2)}, u32[]{:S(2)}) collective-permute-start(bf16[2,16,2048]{2,1,0:T(8,128)(2,1)} %pad_maximum_fusion.7), channel_id=1, source_target_pairs={{0,64},{32,96},{64,128},{96,160},{128,192},{160,224},{192,0},{224,... | collective-permute-start | bytes 393224 | tf_op jit(solution)/shard_map/ppermute | solution.py:77
  35.6 9.3 %all-to-all-start = ((f16[16,32,1152]{2,1,0:T(8,128)(2,1)}), f16[16,32,1152]{2,1,0:T(8,128)(2,1)S(1)}, u32[]{:S(2)}, u32[]{:S(2)}) async-start(f16[16,32,1152]{2,1,0:T(8,128)(2,1)} %bitcast.8), calls=%async_computation | async-start | bytes 2359296 | tf_op jit(solution)/shard_map/all_to_all | solution.py:22
  50.2 23.9 %all-to-all-done = f16[16,32,1152]{2,1,0:T(8,128)(2,1)S(1)} async-done(((f16[16,32,1152]{2,1,0:T(8,128)(2,1)}), f16[16,32,1152]{2,1,0:T(8,128)(2,1)S(1)}, u32[]{:S(2)}, u32[]{:S(2)}) %all-to-all-start) | async-done | bytes 1179680 | tf_op jit(solution)/shard_map/all_to_all | solution.py:22
  75.1 2.1 %spread.1 = (bf16[16,32,1024]{2,1,0:T(8,128)(2,1)}, bf16[32,2048]{1,0:T(8,128)(2,1)}) custom-call(bf16[32,2048]{1,0:T(8,128)(2,1)} %bitcast.115, f32[32,1024]{1,0:T(8,128)} %multiply_reduce_fusion.block_ref), custom_call_target="tpu_custom_call" | custom-call | tf_op jit(solution)/shard_map/spread/pallas_call | solution.py:191
  77.2 1.9 %collective-permute-start.10 = (bf16[2,16,2048]{2,1,0:T(8,128)(2,1)}, bf16[2,16,2048]{2,1,0:T(8,128)(2,1)S(1)}, u32[]{:S(2)}, u32[]{:S(2)}) collective-permute-start(bf16[2,16,2048]{2,1,0:T(8,128)(2,1)} %bitcast.116), channel_id=1, source_target_pairs={{0,32},{32,0},{64,96},{96,64},{128,160},{160,128},{192,224},{224,1... | collective-permute-start | bytes 393224 | tf_op jit(solution)/shard_map/ppermute | solution.py:77
  79.2 3.5 %collective-permute-start.11 = (bf16[2,16,2048]{2,1,0:T(8,128)(2,1)}, bf16[2,16,2048]{2,1,0:T(8,128)(2,1)}, u32[]{:S(2)}, u32[]{:S(2)}) collective-permute-start(bf16[2,16,2048]{2,1,0:T(8,128)(2,1)} %bitcast.117), channel_id=1, source_target_pairs={{0,64},{32,96},{64,128},{96,160},{128,192},{160,224},{192,0},{224,... | collective-permute-start | bytes 393224 | tf_op jit(solution)/shard_map/ppermute | solution.py:77
  82.6 1.9 %collective-permute-start.12 = (bf16[2,16,2048]{2,1,0:T(8,128)(2,1)}, bf16[2,16,2048]{2,1,0:T(8,128)(2,1)}, u32[]{:S(2)}, u32[]{:S(2)}) collective-permute-start(bf16[2,16,2048]{2,1,0:T(8,128)(2,1)} %bitcast.118), channel_id=1, source_target_pairs={{0,96},{32,64},{64,160},{96,128},{128,224},{160,192},{192,32},{224... | collective-permute-start | bytes 393224 | tf_op jit(solution)/shard_map/ppermute | solution.py:77
  84.5 2.2 %collective-permute-start.13 = (bf16[2,16,2048]{2,1,0:T(8,128)(2,1)}, bf16[2,16,2048]{2,1,0:T(8,128)(2,1)S(1)}, u32[]{:S(2)}, u32[]{:S(2)}) collective-permute-start(bf16[2,16,2048]{2,1,0:T(8,128)(2,1)} %bitcast.119), channel_id=1, source_target_pairs={{1,225},{33,193},{65,33},{97,1},{129,97},{161,65},{193,161},{225,1... | collective-permute-start | bytes 393224 | tf_op jit(solution)/shard_map/ppermute | solution.py:77
  86.7 3.7 %all-to-all-start.1 = ((bf16[16,32,1024]{2,1,0:T(8,128)(2,1)}), bf16[16,32,1024]{2,1,0:T(8,128)(2,1)S(1)}, u32[]{:S(2)}, u32[]{:S(2)}) async-start(bf16[16,32,1024]{2,1,0:T(8,128)(2,1)} %get-tuple-element.8), calls=%async_computation.1 | async-start | bytes 2097152 | tf_op jit(solution)/shard_map/all_to_all | solution.py:22
  93.2 1.5 collective-permute-done.14
  94.7 3.4 %copy-done.1 = bf16[64,32,2048]{2,1,0:T(8,128)(2,1)S(1)} copy-done((bf16[64,32,2048]{2,1,0:T(8,128)(2,1)S(1)}, bf16[64,32,2048]{2,1,0:T(8,128)(2,1)}, u32[]{:S(2)}) %copy-start.1) | copy-done | bytes 8388632
  98.1 4.9 %back_part.1 = f32[2048,128]{1,0:T(8,128)S(1)} custom-call(s32[9]{0:T(128)S(1)} %stack.127.refs_0_, bf16[2048,2048]{1,0:T(8,128)(2,1)S(1)} %bitcast.100, bf16[16,2048]{1,0:T(8,128)(2,1)S(1)} %get-tuple-element.64.refs_2_, bf16[16,2048]{1,0:T(8,128)(2,1)S(1)} %get-tuple-element.66.refs_3_, bf16[16,2048]{1,0:T(8,128)(2,1)S(1)} %get-tuple-element.68.refs_4_, ...), custom_call_target="tpu_custom_call" | custom-call | tf_op jit(solution)/shard_map/back_part/pallas_call | solution.py:167
  104.9 1.9 %reshape.96 = f32[16,64,32]{2,1,0:T(8,128)} reshape(f32[16,2048]{1,0:T(8,128)} %get-tuple-element.24) | data formatting | bytes 262144 | tf_op jit(solution)/shard_map/reshape | solution.py:276
  106.7 1.9 %copy.27 = f32[32,1024]{0,1:T(8,128)} copy(f32[32,1024]{1,0:T(8,128)} %multiply_reduce_fusion.block_ref) | data formatting | bytes 262144 | tf_op jit(solution)/shard_map/reduce_sum | solution.py:264
  108.6 2.2 %select_add_fusion.refs_0_ = f32[4,256,128]{2,1,0:T(8,128)} fusion(f32[4,256,128]{2,1,0:T(8,128)} %collective-permute-done.15, f32[1,256,128]{2,1,0:T(8,128)S(1)} %get-tuple-element.26, f32[1,256,128]{2,1,0:T(8,128)S(1)} %get-tuple-element.27, f32[1,256,128]{2,1,0:T(8,128)} %copy-done.9, f32[1,256,128]{2,1,0:T(8,128)} %copy-done.10, ...), kind=kLoop, calls=%fused_computation.11 | loop fusion | flops 1048576 | bytes 2097153 | tf_op jit(solution)/shard_map/add | solution.py:285
  110.8 4.4 %all-to-all-done.1 = bf16[16,32,1024]{2,1,0:T(8,128)(2,1)S(1)} async-done(((bf16[16,32,1024]{2,1,0:T(8,128)(2,1)}), bf16[16,32,1024]{2,1,0:T(8,128)(2,1)S(1)}, u32[]{:S(2)}, u32[]{:S(2)}) %all-to-all-start.1) | async-done | bytes 1048608 | tf_op jit(solution)/shard_map/all_to_all | solution.py:22
  116.2 1.4 product.1
  118.6 2.1 %collective-permute-start.19 = (bf16[256,128]{1,0:T(8,128)(2,1)S(1)}, bf16[256,128]{1,0:T(8,128)(2,1)S(1)}, u32[]{:S(2)}, u32[]{:S(2)}) collective-permute-start(bf16[256,128]{1,0:T(8,128)(2,1)S(1)} %get-tuple-element.56), channel_id=1, source_target_pairs={{1,29},{5,1},{9,5},{13,9},{17,13},{21,17},{25,21},{29,25},{3,31},{... | collective-permute-start | bytes 196616 | tf_op jit(solution)/shard_map/ppermute | solution.py:77
  120.7 1.4 collective-permute-start.18
  122.1 2.9 %collective-permute-start.17 = (bf16[256,128]{1,0:T(8,128)(2,1)S(1)}, bf16[256,128]{1,0:T(8,128)(2,1)S(1)}, u32[]{:S(2)}, u32[]{:S(2)}) collective-permute-start(bf16[256,128]{1,0:T(8,128)(2,1)S(1)} %get-tuple-element.58), channel_id=1, source_target_pairs={{0,8},{4,12},{8,16},{12,20},{16,24},{20,28},{24,0},{28,4},{1,21},{... | collective-permute-start | bytes 196616 | tf_op jit(solution)/shard_map/ppermute | solution.py:77
  125.0 2.7 %collective-permute-start.16 = (bf16[256,128]{1,0:T(8,128)(2,1)S(1)}, bf16[256,128]{1,0:T(8,128)(2,1)S(1)}, u32[]{:S(2)}, u32[]{:S(2)}) collective-permute-start(bf16[256,128]{1,0:T(8,128)(2,1)S(1)} %get-tuple-element.55), channel_id=1, source_target_pairs={{0,4},{4,8},{8,12},{12,16},{16,20},{20,24},{24,28},{28,0},{1,17},{... | collective-permute-start | bytes 196616 | tf_op jit(solution)/shard_map/ppermute | solution.py:77
  127.6 6.7 %all-to-all-start.2 = ((bf16[8,2,64,512]{3,2,1,0:T(8,128)(2,1)}), bf16[8,2,64,512]{3,2,1,0:T(8,128)(2,1)S(1)}, u32[]{:S(2)}, u32[]{:S(2)}) async-start(bf16[8,2,64,512]{3,2,1,0:T(8,128)(2,1)} %copy-done.4), calls=%async_computation.2 | async-start | bytes 2097152 | tf_op jit(solution)/shard_map/all_to_all | solution.py:22
  137.1 10.7 %all-to-all-done.2 = bf16[8,2,64,512]{3,2,1,0:T(8,128)(2,1)S(1)} async-done(((bf16[8,2,64,512]{3,2,1,0:T(8,128)(2,1)}), bf16[8,2,64,512]{3,2,1,0:T(8,128)(2,1)S(1)}, u32[]{:S(2)}, u32[]{:S(2)}) %all-to-all-start.2) | async-done | bytes 1048608 | tf_op jit(solution)/shard_map/all_to_all | solution.py:22
  (112 shorter events, 25.8 us)
Async XLA Ops:
  0.6 5.5 %copy-start.6 = (bf16[1024,512]{1,0:T(8,128)(2,1)S(1)}, bf16[1024,512]{1,0:T(8,128)(2,1)}, u32[]{:S(2)}) copy-start(bf16[1024,512]{1,0:T(8,128)(2,1)} %param.6) | copy-start | bytes 3145732
  0.6 5.5 %copy-start.2 = (bf16[64,16,512]{2,1,0:T(8,128)(2,1)S(1)}, bf16[64,16,512]{2,1,0:T(8,128)(2,1)}, u32[]{:S(2)}) copy-start(bf16[64,16,512]{2,1,0:T(8,128)(2,1)} %param.4) | copy-start | bytes 3145732
  2.9 8.9 %collective-permute-start = (bf16[512,512]{1,0:T(8,128)(2,1)}, bf16[512,512]{1,0:T(8,128)(2,1)}, u32[]{:S(2)}, u32[]{:S(2)}) collective-permute-start(bf16[512,512]{1,0:T(8,128)(2,1)} %bitcast.3), channel_id=1, source_target_pairs={{0,1},{1,0},{2,3},{3,2},{4,5},{5,4},{6,7},{7,6},{8,9},{9,8},{10,11... | collective-permute-start | bytes 1572872 | tf_op jit(solution)/shard_map/ppermute | solution.py:51
  6.2 5.7 %collective-permute-start.1 = (bf16[1024,512]{1,0:T(8,128)(2,1)S(1)}, bf16[1024,512]{1,0:T(8,128)(2,1)S(1)}, u32[]{:S(2)}, u32[]{:S(2)}) collective-permute-start(bf16[1024,512]{1,0:T(8,128)(2,1)S(1)} %bitcast.101), channel_id=1, source_target_pairs={{0,1},{1,0},{2,3},{3,2},{4,5},{5,4},{6,7},{7,6},{8,9},{9,8},{10,11... | collective-permute-start | bytes 3145736 | tf_op jit(solution)/shard_map/ppermute | solution.py:51
  9.1 2.6 %collective-permute-start.2 = (f32[2,1152]{1,0:T(2,128)S(1)}, f32[2,1152]{1,0:T(2,128)S(1)}, u32[]{:S(2)}, u32[]{:S(2)}) collective-permute-start(f32[2,1152]{1,0:T(2,128)S(1)} %broadcast_in_dim.17), channel_id=1, source_target_pairs={{0,1},{1,0},{2,3},{3,2},{4,5},{5,4},{6,7},{7,6},{8,9},{9,8},{10,11... | collective-permute-start | bytes 27656 | tf_op jit(solution)/shard_map/ppermute | solution.py:51
  14.4 3.4 %copy-start = (bf16[64,32,2048]{2,1,0:T(8,128)(2,1)S(1)}, bf16[64,32,2048]{2,1,0:T(8,128)(2,1)}, u32[]{:S(2)}) copy-start(bf16[64,32,2048]{2,1,0:T(8,128)(2,1)} %param.5) | copy-start | bytes 25165828
  22.0 1.6 %collective-permute-start.3 = (bf16[4,16,2048]{2,1,0:T(8,128)(2,1)S(1)}, bf16[4,16,2048]{2,1,0:T(8,128)(2,1)S(1)}, u32[]{:S(2)}, u32[]{:S(2)}) collective-permute-start(bf16[4,16,2048]{2,1,0:T(8,128)(2,1)S(1)} %get-tuple-element.44), channel_id=1, source_target_pairs={{0,1},{1,0},{2,3},{3,2},{4,5},{5,4},{6,7},{7,6},{8,9},{9,8},{10,11... | collective-permute-start | bytes 786440 | tf_op jit(solution)/shard_map/ppermute | solution.py:51
  23.7 21.2 %collective-permute-start.7 = (bf16[2,16,2048]{2,1,0:T(8,128)(2,1)S(1)}, bf16[2,16,2048]{2,1,0:T(8,128)(2,1)}, u32[]{:S(2)}, u32[]{:S(2)}) collective-permute-start(bf16[2,16,2048]{2,1,0:T(8,128)(2,1)S(1)} %pad_maximum_fusion.9), channel_id=1, source_target_pairs={{1,225},{33,193},{65,33},{97,1},{129,97},{161,65},{193,161},{225,1... | collective-permute-start | bytes 393224 | tf_op jit(solution)/shard_map/ppermute | solution.py:77
  29.6 15.3 %collective-permute-start.6 = (bf16[2,16,2048]{2,1,0:T(8,128)(2,1)}, bf16[2,16,2048]{2,1,0:T(8,128)(2,1)}, u32[]{:S(2)}, u32[]{:S(2)}) collective-permute-start(bf16[2,16,2048]{2,1,0:T(8,128)(2,1)} %pad_maximum_fusion.8), channel_id=1, source_target_pairs={{0,96},{32,64},{64,160},{96,128},{128,224},{160,192},{192,32},{224... | collective-permute-start | bytes 393224 | tf_op jit(solution)/shard_map/ppermute | solution.py:77
  30.8 14.1 %collective-permute-start.5 = (bf16[2,16,2048]{2,1,0:T(8,128)(2,1)}, bf16[2,16,2048]{2,1,0:T(8,128)(2,1)}, u32[]{:S(2)}, u32[]{:S(2)}) collective-permute-start(bf16[2,16,2048]{2,1,0:T(8,128)(2,1)} %pad_maximum_fusion.7), channel_id=1, source_target_pairs={{0,64},{32,96},{64,128},{96,160},{128,192},{160,224},{192,0},{224,... | collective-permute-start | bytes 393224 | tf_op jit(solution)/shard_map/ppermute | solution.py:77
  33.2 11.7 %collective-permute-start.4 = (bf16[2,16,2048]{2,1,0:T(8,128)(2,1)}, bf16[2,16,2048]{2,1,0:T(8,128)(2,1)}, u32[]{:S(2)}, u32[]{:S(2)}) collective-permute-start(bf16[2,16,2048]{2,1,0:T(8,128)(2,1)} %pad_maximum_fusion.6), channel_id=1, source_target_pairs={{0,32},{32,0},{64,96},{96,64},{128,160},{160,128},{192,224},{224,1... | collective-permute-start | bytes 393224 | tf_op jit(solution)/shard_map/ppermute | solution.py:77
  35.6 38.5 %all-to-all-start = ((f16[16,32,1152]{2,1,0:T(8,128)(2,1)}), f16[16,32,1152]{2,1,0:T(8,128)(2,1)S(1)}, u32[]{:S(2)}, u32[]{:S(2)}) async-start(f16[16,32,1152]{2,1,0:T(8,128)(2,1)} %bitcast.8), calls=%async_computation | async-start | bytes 2359296 | tf_op jit(solution)/shard_map/all_to_all | solution.py:22
  46.1 1.4 collective-permute-start.8
  48.2 1.3 collective-permute-start.9
  77.2 15.9 %copy-start.14 = (bf16[32,2048]{1,0:T(8,128)(2,1)S(1)}, bf16[32,2048]{1,0:T(8,128)(2,1)}, u32[]{:S(2)}) copy-start(bf16[32,2048]{1,0:T(8,128)(2,1)} %get-tuple-element.7) | copy-start | bytes 393220
  77.2 13.2 %collective-permute-start.10 = (bf16[2,16,2048]{2,1,0:T(8,128)(2,1)}, bf16[2,16,2048]{2,1,0:T(8,128)(2,1)S(1)}, u32[]{:S(2)}, u32[]{:S(2)}) collective-permute-start(bf16[2,16,2048]{2,1,0:T(8,128)(2,1)} %bitcast.116), channel_id=1, source_target_pairs={{0,32},{32,0},{64,96},{96,64},{128,160},{160,128},{192,224},{224,1... | collective-permute-start | bytes 393224 | tf_op jit(solution)/shard_map/ppermute | solution.py:77
  79.2 11.3 %collective-permute-start.11 = (bf16[2,16,2048]{2,1,0:T(8,128)(2,1)}, bf16[2,16,2048]{2,1,0:T(8,128)(2,1)}, u32[]{:S(2)}, u32[]{:S(2)}) collective-permute-start(bf16[2,16,2048]{2,1,0:T(8,128)(2,1)} %bitcast.117), channel_id=1, source_target_pairs={{0,64},{32,96},{64,128},{96,160},{128,192},{160,224},{192,0},{224,... | collective-permute-start | bytes 393224 | tf_op jit(solution)/shard_map/ppermute | solution.py:77
  82.6 8.7 %collective-permute-start.12 = (bf16[2,16,2048]{2,1,0:T(8,128)(2,1)}, bf16[2,16,2048]{2,1,0:T(8,128)(2,1)}, u32[]{:S(2)}, u32[]{:S(2)}) collective-permute-start(bf16[2,16,2048]{2,1,0:T(8,128)(2,1)} %bitcast.118), channel_id=1, source_target_pairs={{0,96},{32,64},{64,160},{96,128},{128,224},{160,192},{192,32},{224... | collective-permute-start | bytes 393224 | tf_op jit(solution)/shard_map/ppermute | solution.py:77
  84.5 8.3 %collective-permute-start.13 = (bf16[2,16,2048]{2,1,0:T(8,128)(2,1)}, bf16[2,16,2048]{2,1,0:T(8,128)(2,1)S(1)}, u32[]{:S(2)}, u32[]{:S(2)}) collective-permute-start(bf16[2,16,2048]{2,1,0:T(8,128)(2,1)} %bitcast.119), channel_id=1, source_target_pairs={{1,225},{33,193},{65,33},{97,1},{129,97},{161,65},{193,161},{225,1... | collective-permute-start | bytes 393224 | tf_op jit(solution)/shard_map/ppermute | solution.py:77
  86.7 28.4 %all-to-all-start.1 = ((bf16[16,32,1024]{2,1,0:T(8,128)(2,1)}), bf16[16,32,1024]{2,1,0:T(8,128)(2,1)S(1)}, u32[]{:S(2)}, u32[]{:S(2)}) async-start(bf16[16,32,1024]{2,1,0:T(8,128)(2,1)} %get-tuple-element.8), calls=%async_computation.1 | async-start | bytes 2097152 | tf_op jit(solution)/shard_map/all_to_all | solution.py:22
  92.9 1.8 %collective-permute-start.14 = (bf16[4,16,2048]{2,1,0:T(8,128)(2,1)S(1)}, bf16[4,16,2048]{2,1,0:T(8,128)(2,1)S(1)}, u32[]{:S(2)}, u32[]{:S(2)}) collective-permute-start(bf16[4,16,2048]{2,1,0:T(8,128)(2,1)S(1)} %pad_maximum_fusion.5), channel_id=1, source_target_pairs={{0,1},{1,0},{2,3},{3,2},{4,5},{5,4},{6,7},{7,6},{8,9},{9,8},{10,11... | collective-permute-start | bytes 786440 | tf_op jit(solution)/shard_map/ppermute | solution.py:51
  104.6 4.0 %collective-permute-start.15 = (f32[4,256,128]{2,1,0:T(8,128)}, f32[4,256,128]{2,1,0:T(8,128)}, u32[]{:S(2)}, u32[]{:S(2)}) collective-permute-start(f32[4,256,128]{2,1,0:T(8,128)} %fusion.1), channel_id=1, source_target_pairs={{0,1},{1,0},{2,3},{3,2},{4,5},{5,4},{6,7},{7,6},{8,9},{9,8},{10,11... | collective-permute-start | bytes 1572872 | tf_op jit(solution)/shard_map/ppermute | solution.py:51
  118.6 15.7 %copy-start.7 = (f32[16,64,32]{2,1,0:T(8,128)S(1)}, f32[16,64,32]{2,1,0:T(8,128)}, u32[]{:S(2)}) copy-start(f32[16,64,32]{2,1,0:T(8,128)} %reshape.96) | copy-start | bytes 393220
  118.6 15.7 %copy-start.8 = (f32[32,1024]{0,1:T(8,128)S(1)}, f32[32,1024]{0,1:T(8,128)}, u32[]{:S(2)}) copy-start(f32[32,1024]{0,1:T(8,128)} %copy.27) | copy-start | bytes 393220
  118.6 16.1 %collective-permute-start.19 = (bf16[256,128]{1,0:T(8,128)(2,1)S(1)}, bf16[256,128]{1,0:T(8,128)(2,1)S(1)}, u32[]{:S(2)}, u32[]{:S(2)}) collective-permute-start(bf16[256,128]{1,0:T(8,128)(2,1)S(1)} %get-tuple-element.56), channel_id=1, source_target_pairs={{1,29},{5,1},{9,5},{13,9},{17,13},{21,17},{25,21},{29,25},{3,31},{... | collective-permute-start | bytes 196616 | tf_op jit(solution)/shard_map/ppermute | solution.py:77
  120.7 14.0 %collective-permute-start.18 = (bf16[256,128]{1,0:T(8,128)(2,1)S(1)}, bf16[256,128]{1,0:T(8,128)(2,1)S(1)}, u32[]{:S(2)}, u32[]{:S(2)}) collective-permute-start(bf16[256,128]{1,0:T(8,128)(2,1)S(1)} %get-tuple-element.57), channel_id=1, source_target_pairs={{0,12},{4,16},{8,20},{12,24},{16,28},{20,0},{24,4},{28,8},{1,25},{... | collective-permute-start | bytes 196616 | tf_op jit(solution)/shard_map/ppermute | solution.py:77
  122.1 12.6 %collective-permute-start.17 = (bf16[256,128]{1,0:T(8,128)(2,1)S(1)}, bf16[256,128]{1,0:T(8,128)(2,1)S(1)}, u32[]{:S(2)}, u32[]{:S(2)}) collective-permute-start(bf16[256,128]{1,0:T(8,128)(2,1)S(1)} %get-tuple-element.58), channel_id=1, source_target_pairs={{0,8},{4,12},{8,16},{12,20},{16,24},{20,28},{24,0},{28,4},{1,21},{... | collective-permute-start | bytes 196616 | tf_op jit(solution)/shard_map/ppermute | solution.py:77
  125.0 9.7 %collective-permute-start.16 = (bf16[256,128]{1,0:T(8,128)(2,1)S(1)}, bf16[256,128]{1,0:T(8,128)(2,1)S(1)}, u32[]{:S(2)}, u32[]{:S(2)}) collective-permute-start(bf16[256,128]{1,0:T(8,128)(2,1)S(1)} %get-tuple-element.55), channel_id=1, source_target_pairs={{0,4},{4,8},{8,12},{12,16},{16,20},{20,24},{24,28},{28,0},{1,17},{... | collective-permute-start | bytes 196616 | tf_op jit(solution)/shard_map/ppermute | solution.py:77
  127.6 20.2 %all-to-all-start.2 = ((bf16[8,2,64,512]{3,2,1,0:T(8,128)(2,1)}), bf16[8,2,64,512]{3,2,1,0:T(8,128)(2,1)S(1)}, u32[]{:S(2)}, u32[]{:S(2)}) async-start(bf16[8,2,64,512]{3,2,1,0:T(8,128)(2,1)} %copy-done.4), calls=%async_computation.2 | async-start | bytes 2097152 | tf_op jit(solution)/shard_map/all_to_all | solution.py:22
  135.7 1.3 collective-permute-start.20
  137.0 11.1 %collective-permute-start.21 = (f32[1,64,128]{2,1,0:T(8,128)S(1)}, f32[1,64,128]{2,1,0:T(8,128)S(1)}, u32[]{:S(2)}, u32[]{:S(2)}) collective-permute-start(f32[1,64,128]{2,1,0:T(8,128)S(1)} %constant_dynamic-slice_fusion), channel_id=1, source_target_pairs={{0,2},{2,0},{1,3},{3,1},{4,6},{6,4},{5,7},{7,5},{8,10},{10,8},{9,1... | collective-permute-start | bytes 98312 | tf_op jit(solution)/shard_map/ppermute | solution.py:51
  148.0 1.4 collective-permute-start.22
  (9 other events, 14.6 us)

commit v11 on v10

--- a/solution.py
+++ b/solution.py
@@ -181,6 +181,15 @@
     )(jnp.stack(places).astype(jnp.int32), slab, *blocks)
 
 
+def together(work, core, *operands):
+    shapes = jax.eval_shape(work, *operands)
+
+    def none(*_):
+        return jax.tree.map(lambda shape: jnp.zeros(shape.shape, shape.dtype), shapes)
+
+    return lax.cond(core >= 0, work, none, *operands)
+
+
 def spread_kernel(pair_ref, block_ref, out_ref, copy_ref):
     out_ref[...] = jnp.broadcast_to(block_ref[...].astype(out_ref.dtype)[None], out_ref.shape)
     copy_ref[...] = pair_ref[...]
@@ -263,14 +272,15 @@
     codes = a_got[:, :1, wide : wide + 1].astype(F32)
     a_own = jnp.sum(a_got[:, :, :wide].astype(F32) * jnp.exp2(codes - 15.0), axis=0)
 
-    b_part = cross_part(a_sent[:8, :LANES].astype(F32), ligand_orbitals, y)
-    b_own = joint_sum(b_part.reshape(n_aa, lig, fit * pro), AA, aa)
-    b_pair = b_own.astype(BF16)
-    b_pair = in_order(b_pair, other(b_pair, "c"), "c").reshape(2 * lig, fit * pro)
+    def sum_b(token, orbitals, slab):
+        b_part = cross_part(token, orbitals, slab)
+        b_own = joint_sum(b_part.reshape(n_aa, lig, fit * pro), AA, aa)
+        b_pair = b_own.astype(BF16)
+        return b_own, in_order(b_pair, other(b_pair, "c"), "c").reshape(2 * lig, fit * pro)
+
+    b_own, b_pair = together(sum_b, core, a_sent[:8, :LANES].astype(F32), ligand_orbitals, y)
     a_block, b_pair = spread(b_pair, a_own, n_zy)
     a_all = exchange(a_block, ZY).reshape(n_zy * pro, wide)
-    b_blocks, b_places = joint_gather(b_pair.reshape(2, lig, fit * pro), AA, aa)
-
     pair = jnp.sum(
         jnp.transpose(a_own.reshape(pro, fit, lig), (1, 2, 0))
         * jnp.transpose(b_own.reshape(lig, fit, pro), (1, 0, 2)),
@@ -280,22 +290,30 @@
 
     scale_ligand = 1.0 / math.sqrt(fit * pro_total)
     rows_b = nus // (2 * n_zy)
-    back_b = back_part(y, b_blocks, b_places, scale_ligand, lig_total)
-    keep, send = shared(back_b.reshape(n_z, nus // n_z, lig_total), ("z",), (n_z,))
-    back_b = keep + other(send, "c")
+
+    def multiply_b(b_pair, slab):
+        blocks, places = joint_gather(b_pair.reshape(2, lig, fit * pro), AA, aa)
+        back_b = back_part(slab, blocks, places, scale_ligand, lig_total)
+        keep, send = shared(back_b.reshape(n_z, nus // n_z, lig_total), ("z",), (n_z,))
+        return keep + other(send, "c")
+
+    back_b = together(multiply_b, core, b_pair, y)
+
     scale_protein = 1.0 / math.sqrt(fit * lig_total)
     rows = mus // n_aa
     back_a, sent = product(back_b, x_own, x_other, a_all, scale_protein, rows)
 
-    total = jnp.where(core == 0, back_b[-1], 0.0)
-    for j, (first, second) in enumerate(zip(*halves((n_z,)))):
-        total = total + joint(sent[j], ("z",), (n_z,), first, second).astype(F32)
-    total = pair_sum(total.reshape(n_yl, 2, rows_b, lig_total), "c")
-    ligand_back = pair_sum(total.reshape(1, n_yl, rows_b, lig_total), "yl").reshape(rows_b, lig_total)
-
+    def sum_back(back_b, sent):
+        total = jnp.where(core == 0, back_b[-1], 0.0)
+        for j, (first, second) in enumerate(zip(*halves((n_z,)))):
+            total = total + joint(sent[j], ("z",), (n_z,), first, second).astype(F32)
+        total = pair_sum(total.reshape(n_yl, 2, rows_b, lig_total), "c")
+        return pair_sum(total.reshape(1, n_yl, rows_b, lig_total), "yl").reshape(rows_b, lig_total)
+
+    ligand_back = together(sum_back, core, back_b, sent)
     back_a = exchange(back_a, AA)
     here, away = jnp.sum(back_a.astype(F32), axis=0)
-    there = other(away, "c")
+    there = other(away + 0.0 * ligand_back[:1, :1], "c")
     here = here.reshape(rows, n_zy, 1, pro)
     there = there.reshape(rows, n_zy, 1, pro)
     protein_back = jnp.where(

time: 151 us -> 126 us (0.83)
  waiting for transfers between devices: 46.2 us -> 23 us
  local copies, waits for them, and re-layouts: 17.1 us -> 5.95 us
  starting transfers between devices: 51.5 us -> 59.8 us
  Pallas kernels: 12.4 us -> 20.5 us
  other arithmetic: 17.5 us -> 12.9 us
  matrix products: 4.65 us -> 1.49 us
    all_to_all x3, waiting for transfers between devices: 38.9 us -> 0.01 us  [exchange(): return lax.all_to_all(pieces, axes, 0, 0, tiled=True)]
    ppermute x12, waiting for transfers between devices: 0.58 us -> 13.7 us  [joint(): return lax.ppermute(block, axes + ('c',), pairs)]
    unnamed x32 -> x16, local copies, waits for them, and re-layouts: 10.4 us -> 2.98 us
    ppermute x12, starting transfers between devices: 27 us -> 30.9 us  [joint(): return lax.ppermute(block, axes + ('c',), pairs)]
    pallas_call x1, Pallas kernels: 3.99 us -> 7.78 us  [cross_part(): pl.pallas_call(cross_kernel, grid=(rows // step,), in_specs=[pl.BlockSpec...]
    ppermute x11, starting transfers between devices: 4.86 us -> 8.05 us  [other(): return lax.ppermute(block, axis, [(0, 1), (1, 0)])]
    dot_general x2, matrix products: 4.65 us -> 1.49 us  [dot(): lax.dot_general(left, right, (contract, ((), ())), preferred_element_type...]
    pallas_call x1, Pallas kernels: 4.92 us -> 7.68 us  [back_part(): pl.pallas_call(lambda *refs: back_kernel(*refs, count=count, scale=scale)...]
  transfers between devices with their start and end apart: 26 -> 26, of which waited for: 10 -> 16; matrix products, arithmetic and copies ran while one was open for 15% -> 10% of each run, Pallas kernels for 3% -> 12%
where the time goes in v11:
time: 126 us; the launch traced here: 125 us
  starting transfers between devices  59.8 us (47%)
  waiting for transfers between devices  23 us (18%)
  Pallas kernels  20.5 us (16%)
  other arithmetic  12.9 us (10%)
  local copies, waits for them, and re-layouts  5.95 us (5%)
  between operations  1.52 us (1%)
  matrix products  1.49 us (1%)
    ppermute x12, starting transfers between devices, joint(): return lax.ppermute(block, axes + ('c',), pairs)  30.9 us
    all_to_all x3, starting transfers between devices, exchange(): return lax.all_to_all(pieces, axes, 0, 0, tiled=True)  20.8 us
    ppermute x12, waiting for transfers between devices, joint(): return lax.ppermute(block, axes + ('c',), pairs)  13.7 us
    ppermute x11, waiting for transfers between devices, other(): return lax.ppermute(block, axis, [(0, 1), (1, 0)])  9.26 us
    ppermute x11, starting transfers between devices, other(): return lax.ppermute(block, axis, [(0, 1), (1, 0)])  8.05 us
    pallas_call x1, Pallas kernels, cross_part(): pl.pallas_call(cross_kernel, grid=(rows // step,), in_specs=[pl.BlockSpec...  7.78 us
    pallas_call x1, Pallas kernels, back_part(): pl.pallas_call(lambda *refs: back_kernel(*refs, count=count, scale=scale)...  7.68 us
    pallas_call x1, Pallas kernels, product(): pl.pallas_call(lambda *refs: product_kernel(*refs, scale=scale, step=step...  3.06 us
  transfers between devices with their start and end apart: 26, of which 16 were waited for; matrix products, arithmetic and copies ran while one was open for 10% of the time, Pallas kernels for 12%

profile of v11, /device:TPU:1, one launch (start us, length us, event | category | flops | bytes accessed | tf_op | source)
XLA Modules:
  0.0 125.5 jit_solution(13199762909694727790)
XLA Ops:
  0.7 1.4 %constant_dynamic-slice_fusion.17 = (bf16[16,1,32,512]{3,2,1,0:T(8,128)(2,1)S(1)}, bf16[16,1,32,512]{3,2,1,0:T(8,128)(2,1)S(1)}) fusion(bf16[16,2,32,512]{3,2,1,0:T(8,128)(2,1)} %bitcast.110, s32[]{:T(128)S(6)} %select_n.267, s32[]{:T(128)S(6)} %select_n.266), kind=kLoop, calls=%fused_computation.94 | loop fusion | bytes 2097160 | tf_op jit(solution)/shard_map/jit(dynamic_index_in_dim)/dynamic_slice | solution.py:259
  2.1 3.3 %collective-permute-start.19 = (bf16[512,512]{1,0:T(8,128)(2,1)S(1)}, bf16[512,512]{1,0:T(8,128)(2,1)S(1)}, u32[]{:S(2)}, u32[]{:S(2)}) collective-permute-start(bf16[512,512]{1,0:T(8,128)(2,1)S(1)} %bitcast.119), channel_id=1, source_target_pairs={{0,1},{1,0},{2,3},{3,2},{4,5},{5,4},{6,7},{7,6},{8,9},{9,8},{10,11... | collective-permute-start | bytes 1572872 | tf_op jit(solution)/shard_map/ppermute | solution.py:51
  7.0 1.4 %maximum_convert_fusion = f32[2]{0:T(128)S(1)} fusion(bf16[1]{0:T(256)(128)(2,1)} %bitcast.40, bf16[1]{0:T(256)(128)(2,1)} %bitcast.39), kind=kLoop, calls=%fused_computation.92 | loop fusion | flops 8 | bytes 12 | tf_op jit(solution)/shard_map/stack | solution.py:262
  11.6 1.3 %pad_maximum_fusion.10 = f16[512,1152]{1,0:T(8,128)(2,1)} fusion(f16[512,1024]{1,0:T(8,128)(2,1)S(1)} %multiply_convert_fusion, f16[1152]{0:T(1024)(128)(2,1)S(1)} %pad.35.clone), kind=kLoop, calls=%fused_computation.72 | loop fusion | flops 589824 | bytes 2230528 | tf_op jit(solution)/shard_map/concatenate | solution.py:270
  12.9 7.6 %all-to-all-start = ((f16[16,32,1152]{2,1,0:T(8,128)(2,1)}), f16[16,32,1152]{2,1,0:T(8,128)(2,1)S(1)}, u32[]{:S(2)}, u32[]{:S(2)}) async-start(f16[16,32,1152]{2,1,0:T(8,128)(2,1)} %bitcast.43), calls=%async_computation | async-start | bytes 2359296 | tf_op jit(solution)/shard_map/all_to_all | solution.py:22
  21.2 31.9 %conditional.3 = (f32[16,2048]{1,0:T(8,128)S(1)}, bf16[32,2048]{1,0:T(8,128)(2,1)S(1)}) conditional(s32[]{:T(128)} %convert_element_type.59, () %tuple.28, (f32[8,128]{1,0:T(8,128)S(1)}, bf16[128,2048]{1,0:T(8,128)(2,1)}, bf16[2048,2048]{1,0:T(8,128)(2,1)}) %tuple.81), branch_computations={%region_3.4_spmd, %region_4.5_spmd} | conditional | flops 2359381 | bytes 10487028 | solution.py:190
  21.2 7.8 %cross_part.1 = bf16[128,2048]{1,0:T(8,128)(2,1)S(1)} custom-call(f32[8,128]{1,0:T(8,128)S(1)} %get-tuple-element.18.token_ref, bf16[128,2048]{1,0:T(8,128)(2,1)} %get-tuple-element.46.left_ref, bf16[2048,2048]{1,0:T(8,128)(2,1)} %get-tuple-element.24.right_ref), custom_call_target="tpu_custom_call" | custom-call | tf_op jit(solution)/shard_map/cond/branch_1_fun/cross_part/pallas_call | solution.py:135
  31.1 2.8 %collective-permute-start.13 = (bf16[2,16,2048]{2,1,0:T(8,128)(2,1)S(1)}, bf16[2,16,2048]{2,1,0:T(8,128)(2,1)S(1)}, u32[]{:S(2)}, u32[]{:S(2)}) collective-permute-start(bf16[2,16,2048]{2,1,0:T(8,128)(2,1)S(1)} %pad_maximum_fusion.2), channel_id=1, source_target_pairs={{0,32},{32,0},{64,96},{96,64},{128,160},{160,128},{192,224},{224,1... | collective-permute-start | bytes 393224 | tf_op jit(solution)/shard_map/cond/branch_1_fun/ppermute | solution.py:77
  33.9 2.6 %collective-permute-start.14 = (bf16[2,16,2048]{2,1,0:T(8,128)(2,1)S(1)}, bf16[2,16,2048]{2,1,0:T(8,128)(2,1)S(1)}, u32[]{:S(2)}, u32[]{:S(2)}) collective-permute-start(bf16[2,16,2048]{2,1,0:T(8,128)(2,1)S(1)} %pad_maximum_fusion.3), channel_id=1, source_target_pairs={{0,64},{32,96},{64,128},{96,160},{128,192},{160,224},{192,0},{224,... | collective-permute-start | bytes 393224 | tf_op jit(solution)/shard_map/cond/branch_1_fun/ppermute | solution.py:77
  36.6 2.5 %collective-permute-start.15 = (bf16[2,16,2048]{2,1,0:T(8,128)(2,1)S(1)}, bf16[2,16,2048]{2,1,0:T(8,128)(2,1)S(1)}, u32[]{:S(2)}, u32[]{:S(2)}) collective-permute-start(bf16[2,16,2048]{2,1,0:T(8,128)(2,1)S(1)} %pad_maximum_fusion.4), channel_id=1, source_target_pairs={{0,96},{32,64},{64,160},{96,128},{128,224},{160,192},{192,32},{224... | collective-permute-start | bytes 393224 | tf_op jit(solution)/shard_map/cond/branch_1_fun/ppermute | solution.py:77
  39.2 2.5 %collective-permute-start.16 = (bf16[2,16,2048]{2,1,0:T(8,128)(2,1)S(1)}, bf16[2,16,2048]{2,1,0:T(8,128)(2,1)S(1)}, u32[]{:S(2)}, u32[]{:S(2)}) collective-permute-start(bf16[2,16,2048]{2,1,0:T(8,128)(2,1)S(1)} %pad_maximum_fusion.5), channel_id=1, source_target_pairs={{1,225},{33,193},{65,33},{97,1},{129,97},{161,65},{193,161},{225,1... | collective-permute-start | bytes 393224 | tf_op jit(solution)/shard_map/cond/branch_1_fun/ppermute | solution.py:77
  41.7 1.6 %collective-permute-done.14 = bf16[2,16,2048]{2,1,0:T(8,128)(2,1)S(1)} collective-permute-done((bf16[2,16,2048]{2,1,0:T(8,128)(2,1)S(1)}, bf16[2,16,2048]{2,1,0:T(8,128)(2,1)S(1)}, u32[]{:S(2)}, u32[]{:S(2)}) %collective-permute-start.14) | collective-permute-done | bytes 131104 | tf_op jit(solution)/shard_map/cond/branch_1_fun/ppermute | solution.py:77
  43.3 6.9 %collective-permute-done.16 = bf16[2,16,2048]{2,1,0:T(8,128)(2,1)S(1)} collective-permute-done((bf16[2,16,2048]{2,1,0:T(8,128)(2,1)S(1)}, bf16[2,16,2048]{2,1,0:T(8,128)(2,1)S(1)}, u32[]{:S(2)}, u32[]{:S(2)}) %collective-permute-start.16) | collective-permute-done | bytes 131104 | tf_op jit(solution)/shard_map/cond/branch_1_fun/ppermute | solution.py:77
  50.4 1.3 %collective-permute-done.17 = f32[16,2048]{1,0:T(8,128)S(1)} collective-permute-done((f32[16,2048]{1,0:T(8,128)S(1)}, f32[16,2048]{1,0:T(8,128)S(1)}, u32[]{:S(2)}, u32[]{:S(2)}) %collective-permute-start.17) | collective-permute-done | bytes 131104 | tf_op jit(solution)/shard_map/cond/branch_1_fun/ppermute | solution.py:51
  54.2 2.0 %spread.1 = (bf16[16,32,1024]{2,1,0:T(8,128)(2,1)}, bf16[32,2048]{1,0:T(8,128)(2,1)}) custom-call(bf16[32,2048]{1,0:T(8,128)(2,1)S(1)} %get-tuple-element.40.pair_ref, f32[32,1024]{1,0:T(8,128)} %multiply_reduce_fusion.block_ref), custom_call_target="tpu_custom_call" | custom-call | tf_op jit(solution)/shard_map/spread/pallas_call | solution.py:200
  56.3 9.4 %all-to-all-start.1 = ((bf16[16,32,1024]{2,1,0:T(8,128)(2,1)}), bf16[16,32,1024]{2,1,0:T(8,128)(2,1)S(1)}, u32[]{:S(2)}, u32[]{:S(2)}) async-start(bf16[16,32,1024]{2,1,0:T(8,128)(2,1)} %get-tuple-element.42), calls=%async_computation.1 | async-start | bytes 2097152 | tf_op jit(solution)/shard_map/all_to_all | solution.py:22
  65.6 27.4 %conditional.4 = (f32[4,256,128]{2,1,0:T(8,128)}) conditional(s32[]{:T(128)} %convert_element_type.59, () %tuple.31, (bf16[32,2048]{1,0:T(8,128)(2,1)}, bf16[2048,2048]{1,0:T(8,128)(2,1)}) %tuple.82), branch_computations={%region_6.7_spmd, %region_7.8_spmd} | conditional | flops 2654375 | bytes 13306000 | solution.py:190
  65.7 1.8 %collective-permute-start = (bf16[2,16,2048]{2,1,0:T(8,128)(2,1)}, bf16[2,16,2048]{2,1,0:T(8,128)(2,1)}, u32[]{:S(2)}, u32[]{:S(2)}) collective-permute-start(bf16[2,16,2048]{2,1,0:T(8,128)(2,1)} %bitcast.16), channel_id=1, source_target_pairs={{0,32},{32,0},{64,96},{96,64},{128,160},{160,128},{192,224},{224,1... | collective-permute-start | bytes 393224 | tf_op jit(solution)/shard_map/cond/branch_1_fun/ppermute | solution.py:77
  67.4 3.0 %collective-permute-start.1 = (bf16[2,16,2048]{2,1,0:T(8,128)(2,1)}, bf16[2,16,2048]{2,1,0:T(8,128)(2,1)}, u32[]{:S(2)}, u32[]{:S(2)}) collective-permute-start(bf16[2,16,2048]{2,1,0:T(8,128)(2,1)} %bitcast.16), channel_id=1, source_target_pairs={{0,64},{32,96},{64,128},{96,160},{128,192},{160,224},{192,0},{224,... | collective-permute-start | bytes 393224 | tf_op jit(solution)/shard_map/cond/branch_1_fun/ppermute | solution.py:77
  71.8 3.2 %collective-permute-start.3 = (bf16[2,16,2048]{2,1,0:T(8,128)(2,1)}, bf16[2,16,2048]{2,1,0:T(8,128)(2,1)S(1)}, u32[]{:S(2)}, u32[]{:S(2)}) collective-permute-start(bf16[2,16,2048]{2,1,0:T(8,128)(2,1)} %bitcast.16), channel_id=1, source_target_pairs={{1,225},{33,193},{65,33},{97,1},{129,97},{161,65},{193,161},{225,1... | collective-permute-start | bytes 393224 | tf_op jit(solution)/shard_map/cond/branch_1_fun/ppermute | solution.py:77
  78.7 1.8 %collective-permute-done.3 = bf16[2,16,2048]{2,1,0:T(8,128)(2,1)S(1)} collective-permute-done((bf16[2,16,2048]{2,1,0:T(8,128)(2,1)}, bf16[2,16,2048]{2,1,0:T(8,128)(2,1)S(1)}, u32[]{:S(2)}, u32[]{:S(2)}) %collective-permute-start.3) | collective-permute-done | bytes 131104 | tf_op jit(solution)/shard_map/cond/branch_1_fun/ppermute | solution.py:77
  82.3 7.7 %back_part.1 = f32[2048,128]{1,0:T(8,128)S(1)} custom-call(s32[9]{0:T(128)S(1)} %stack.72.refs_0_, bf16[2048,2048]{1,0:T(8,128)(2,1)} %get-tuple-element.25.refs_1_, bf16[16,2048]{1,0:T(8,128)(2,1)S(1)} %get-tuple-element.74.refs_2_, bf16[16,2048]{1,0:T(8,128)(2,1)S(1)} %get-tuple-element.76.refs_3_, bf16[16,2048]{1,0:T(8,128)(2,1)S(1)} %get-tuple-element.78.refs_4_, ...), custom_call_target="tpu_custom_call" | custom-call | tf_op jit(solution)/shard_map/cond/branch_1_fun/back_part/pallas_call | solution.py:167
  90.4 1.8 %collective-permute-done.5 = f32[4,256,128]{2,1,0:T(8,128)S(1)} collective-permute-done((f32[4,256,128]{2,1,0:T(8,128)S(1)}, f32[4,256,128]{2,1,0:T(8,128)S(1)}, u32[]{:S(2)}, u32[]{:S(2)}) %collective-permute-start.5) | collective-permute-done | bytes 524320 | tf_op jit(solution)/shard_map/cond/branch_1_fun/ppermute | solution.py:51
  93.1 3.1 %product.1 = (bf16[8,2,64,512]{3,2,1,0:T(8,128)(2,1)S(1)}, bf16[4,256,128]{2,1,0:T(8,128)(2,1)}) custom-call(f32[4,256,128]{2,1,0:T(8,128)} %get-tuple-element.113.refs_0_, bf16[1024,512]{1,0:T(8,128)(2,1)S(1)} %bitcast.104, bf16[1024,512]{1,0:T(8,128)(2,1)S(1)} %collective-permute-done.20.refs_2_, bf16[512,1024]{1,0:T(8,128)(2,1)S(1)} %bitcast.105), custom_call_target="tpu_custom_call" | custom-call | tf_op jit(solution)/shard_map/product/pallas_call | solution.py:229
  97.1 3.9 %all-to-all-start.2 = ((bf16[8,2,64,512]{3,2,1,0:T(8,128)(2,1)}), bf16[8,2,64,512]{3,2,1,0:T(8,128)(2,1)S(1)}, u32[]{:S(2)}, u32[]{:S(2)}) async-start(bf16[8,2,64,512]{3,2,1,0:T(8,128)(2,1)} %copy-done.1), calls=%async_computation.2 | async-start | bytes 2097152 | tf_op jit(solution)/shard_map/all_to_all | solution.py:22
  101.7 18.9 %conditional.5 = (f32[64,128]{1,0:T(8,128)S(1)}) conditional(s32[]{:T(128)} %convert_element_type.59, () %tuple.30, (s32[]{:T(128)}, f32[4,256,128]{2,1,0:T(8,128)}, bf16[4,256,128]{2,1,0:T(8,128)(2,1)S(1)}) %tuple.83), branch_computations={%region_8.9_spmd, %region_9.10_spmd} | conditional | flops 319508 | bytes 2982374 | solution.py:190
  101.7 5.9 %collective-permute-start.6 = (bf16[256,128]{1,0:T(8,128)(2,1)S(1)}, bf16[256,128]{1,0:T(8,128)(2,1)S(1)}, u32[]{:S(2)}, u32[]{:S(2)}) collective-permute-start(bf16[256,128]{1,0:T(8,128)(2,1)S(1)} %get-tuple-element.81), channel_id=1, source_target_pairs={{0,4},{4,8},{8,12},{12,16},{16,20},{20,24},{24,28},{28,0},{1,17},{... | collective-permute-start | bytes 196616 | tf_op jit(solution)/shard_map/cond/branch_1_fun/ppermute | solution.py:77
  107.8 2.3 %collective-permute-start.8 = (bf16[256,128]{1,0:T(8,128)(2,1)S(1)}, bf16[256,128]{1,0:T(8,128)(2,1)S(1)}, u32[]{:S(2)}, u32[]{:S(2)}) collective-permute-start(bf16[256,128]{1,0:T(8,128)(2,1)S(1)} %get-tuple-element.83), channel_id=1, source_target_pairs={{0,12},{4,16},{8,20},{12,24},{16,28},{20,0},{24,4},{28,8},{1,25},{... | collective-permute-start | bytes 196616 | tf_op jit(solution)/shard_map/cond/branch_1_fun/ppermute | solution.py:77
  110.1 2.6 %collective-permute-start.9 = (bf16[256,128]{1,0:T(8,128)(2,1)S(1)}, bf16[256,128]{1,0:T(8,128)(2,1)S(1)}, u32[]{:S(2)}, u32[]{:S(2)}) collective-permute-start(bf16[256,128]{1,0:T(8,128)(2,1)S(1)} %get-tuple-element.82), channel_id=1, source_target_pairs={{1,29},{5,1},{9,5},{13,9},{17,13},{21,17},{25,21},{29,25},{3,31},{... | collective-permute-start | bytes 196616 | tf_op jit(solution)/shard_map/cond/branch_1_fun/ppermute | solution.py:77
  112.9 1.4 %collective-permute-done.8 = bf16[256,128]{1,0:T(8,128)(2,1)S(1)} collective-permute-done((bf16[256,128]{1,0:T(8,128)(2,1)S(1)}, bf16[256,128]{1,0:T(8,128)(2,1)S(1)}, u32[]{:S(2)}, u32[]{:S(2)}) %collective-permute-start.8) | collective-permute-done | bytes 65568 | tf_op jit(solution)/shard_map/cond/branch_1_fun/ppermute | solution.py:77
  118.9 1.7 %collective-permute-done.11 = f32[1,64,128]{2,1,0:T(8,128)S(1)} collective-permute-done((f32[1,64,128]{2,1,0:T(8,128)S(1)}, f32[1,64,128]{2,1,0:T(8,128)S(1)}, u32[]{:S(2)}, u32[]{:S(2)}) %collective-permute-start.11) | collective-permute-done | bytes 32800 | tf_op jit(solution)/shard_map/cond/branch_1_fun/ppermute | solution.py:51
  122.0 1.4 %collective-permute-start.22 = (f32[64,512]{1,0:T(8,128)S(1)}, f32[64,512]{1,0:T(8,128)S(1)}, u32[]{:S(2)}, u32[]{:S(2)}) collective-permute-start(f32[64,512]{1,0:T(8,128)S(1)} %get-tuple-element.108), channel_id=1, source_target_pairs={{0,1},{1,0},{2,3},{3,2},{4,5},{5,4},{6,7},{7,6},{8,9},{9,8},{10,11... | collective-permute-start | bytes 393224 | tf_op jit(solution)/shard_map/ppermute | solution.py:51
  (100 shorter events, 27.5 us)
Async XLA Ops:
  0.6 5.7 %copy-start.3 = (bf16[1024,512]{1,0:T(8,128)(2,1)S(1)}, bf16[1024,512]{1,0:T(8,128)(2,1)}, u32[]{:S(2)}) copy-start(bf16[1024,512]{1,0:T(8,128)(2,1)} %param.12) | copy-start | bytes 3145732
  0.6 4.8 %copy-start = (bf16[64,16,512]{2,1,0:T(8,128)(2,1)S(1)}, bf16[64,16,512]{2,1,0:T(8,128)(2,1)}, u32[]{:S(2)}) copy-start(bf16[64,16,512]{2,1,0:T(8,128)(2,1)} %param.10) | copy-start | bytes 3145732
  2.1 7.8 %collective-permute-start.19 = (bf16[512,512]{1,0:T(8,128)(2,1)S(1)}, bf16[512,512]{1,0:T(8,128)(2,1)S(1)}, u32[]{:S(2)}, u32[]{:S(2)}) collective-permute-start(bf16[512,512]{1,0:T(8,128)(2,1)S(1)} %bitcast.119), channel_id=1, source_target_pairs={{0,1},{1,0},{2,3},{3,2},{4,5},{5,4},{6,7},{7,6},{8,9},{9,8},{10,11... | collective-permute-start | bytes 1572872 | tf_op jit(solution)/shard_map/ppermute | solution.py:51
  5.4 4.4 %collective-permute-start.20 = (bf16[1024,512]{1,0:T(8,128)(2,1)S(1)}, bf16[1024,512]{1,0:T(8,128)(2,1)S(1)}, u32[]{:S(2)}, u32[]{:S(2)}) collective-permute-start(bf16[1024,512]{1,0:T(8,128)(2,1)S(1)} %bitcast.102), channel_id=1, source_target_pairs={{0,1},{1,0},{2,3},{3,2},{4,5},{5,4},{6,7},{7,6},{8,9},{9,8},{10,11... | collective-permute-start | bytes 3145736 | tf_op jit(solution)/shard_map/ppermute | solution.py:51
  8.5 1.2 collective-permute-start.21
  12.9 40.2 %all-to-all-start = ((f16[16,32,1152]{2,1,0:T(8,128)(2,1)}), f16[16,32,1152]{2,1,0:T(8,128)(2,1)S(1)}, u32[]{:S(2)}, u32[]{:S(2)}) async-start(f16[16,32,1152]{2,1,0:T(8,128)(2,1)} %bitcast.43), calls=%async_computation | async-start | bytes 2359296 | tf_op jit(solution)/shard_map/all_to_all | solution.py:22
  29.1 1.9 %collective-permute-start.12 = (bf16[4,16,2048]{2,1,0:T(8,128)(2,1)S(1)}, bf16[4,16,2048]{2,1,0:T(8,128)(2,1)S(1)}, u32[]{:S(2)}, u32[]{:S(2)}) collective-permute-start(bf16[4,16,2048]{2,1,0:T(8,128)(2,1)S(1)} %get-tuple-element.94), channel_id=1, source_target_pairs={{0,1},{1,0},{2,3},{3,2},{4,5},{5,4},{6,7},{7,6},{8,9},{9,8},{10,11... | collective-permute-start | bytes 786440 | tf_op jit(solution)/shard_map/cond/branch_1_fun/ppermute | solution.py:51
  31.1 10.6 %collective-permute-start.13 = (bf16[2,16,2048]{2,1,0:T(8,128)(2,1)S(1)}, bf16[2,16,2048]{2,1,0:T(8,128)(2,1)S(1)}, u32[]{:S(2)}, u32[]{:S(2)}) collective-permute-start(bf16[2,16,2048]{2,1,0:T(8,128)(2,1)S(1)} %pad_maximum_fusion.2), channel_id=1, source_target_pairs={{0,32},{32,0},{64,96},{96,64},{128,160},{160,128},{192,224},{224,1... | collective-permute-start | bytes 393224 | tf_op jit(solution)/shard_map/cond/branch_1_fun/ppermute | solution.py:77
  33.9 9.4 %collective-permute-start.14 = (bf16[2,16,2048]{2,1,0:T(8,128)(2,1)S(1)}, bf16[2,16,2048]{2,1,0:T(8,128)(2,1)S(1)}, u32[]{:S(2)}, u32[]{:S(2)}) collective-permute-start(bf16[2,16,2048]{2,1,0:T(8,128)(2,1)S(1)} %pad_maximum_fusion.3), channel_id=1, source_target_pairs={{0,64},{32,96},{64,128},{96,160},{128,192},{160,224},{192,0},{224,... | collective-permute-start | bytes 393224 | tf_op jit(solution)/shard_map/cond/branch_1_fun/ppermute | solution.py:77
  36.6 6.7 %collective-permute-start.15 = (bf16[2,16,2048]{2,1,0:T(8,128)(2,1)S(1)}, bf16[2,16,2048]{2,1,0:T(8,128)(2,1)S(1)}, u32[]{:S(2)}, u32[]{:S(2)}) collective-permute-start(bf16[2,16,2048]{2,1,0:T(8,128)(2,1)S(1)} %pad_maximum_fusion.4), channel_id=1, source_target_pairs={{0,96},{32,64},{64,160},{96,128},{128,224},{160,192},{192,32},{224... | collective-permute-start | bytes 393224 | tf_op jit(solution)/shard_map/cond/branch_1_fun/ppermute | solution.py:77
  39.2 11.1 %collective-permute-start.16 = (bf16[2,16,2048]{2,1,0:T(8,128)(2,1)S(1)}, bf16[2,16,2048]{2,1,0:T(8,128)(2,1)S(1)}, u32[]{:S(2)}, u32[]{:S(2)}) collective-permute-start(bf16[2,16,2048]{2,1,0:T(8,128)(2,1)S(1)} %pad_maximum_fusion.5), channel_id=1, source_target_pairs={{1,225},{33,193},{65,33},{97,1},{129,97},{161,65},{193,161},{225,1... | collective-permute-start | bytes 393224 | tf_op jit(solution)/shard_map/cond/branch_1_fun/ppermute | solution.py:77
  50.3 1.4 %collective-permute-start.17 = (f32[16,2048]{1,0:T(8,128)S(1)}, f32[16,2048]{1,0:T(8,128)S(1)}, u32[]{:S(2)}, u32[]{:S(2)}) collective-permute-start(f32[16,2048]{1,0:T(8,128)S(1)} %select_bitcast_fusion), channel_id=1, source_target_pairs={{0,1},{1,0},{2,3},{3,2},{4,5},{5,4},{6,7},{7,6},{8,9},{9,8},{10,11... | collective-permute-start | bytes 393224 | tf_op jit(solution)/shard_map/cond/branch_1_fun/ppermute | solution.py:51
  51.8 1.3 %collective-permute-start.18 = (bf16[16,2048]{1,0:T(8,128)(2,1)S(1)}, bf16[16,2048]{1,0:T(8,128)(2,1)S(1)}, u32[]{:S(2)}, u32[]{:S(2)}) collective-permute-start(bf16[16,2048]{1,0:T(8,128)(2,1)S(1)} %get-tuple-element.59), channel_id=1, source_target_pairs={{0,1},{1,0},{2,3},{3,2},{4,5},{5,4},{6,7},{7,6},{8,9},{9,8},{10,11... | collective-permute-start | bytes 196616 | tf_op jit(solution)/shard_map/cond/branch_1_fun/ppermute | solution.py:51
  56.3 36.8 %all-to-all-start.1 = ((bf16[16,32,1024]{2,1,0:T(8,128)(2,1)}), bf16[16,32,1024]{2,1,0:T(8,128)(2,1)S(1)}, u32[]{:S(2)}, u32[]{:S(2)}) async-start(bf16[16,32,1024]{2,1,0:T(8,128)(2,1)} %get-tuple-element.42), calls=%async_computation.1 | async-start | bytes 2097152 | tf_op jit(solution)/shard_map/all_to_all | solution.py:22
  65.7 9.5 %collective-permute-start = (bf16[2,16,2048]{2,1,0:T(8,128)(2,1)}, bf16[2,16,2048]{2,1,0:T(8,128)(2,1)}, u32[]{:S(2)}, u32[]{:S(2)}) collective-permute-start(bf16[2,16,2048]{2,1,0:T(8,128)(2,1)} %bitcast.16), channel_id=1, source_target_pairs={{0,32},{32,0},{64,96},{96,64},{128,160},{160,128},{192,224},{224,1... | collective-permute-start | bytes 393224 | tf_op jit(solution)/shard_map/cond/branch_1_fun/ppermute | solution.py:77
  67.4 9.5 %collective-permute-start.1 = (bf16[2,16,2048]{2,1,0:T(8,128)(2,1)}, bf16[2,16,2048]{2,1,0:T(8,128)(2,1)}, u32[]{:S(2)}, u32[]{:S(2)}) collective-permute-start(bf16[2,16,2048]{2,1,0:T(8,128)(2,1)} %bitcast.16), channel_id=1, source_target_pairs={{0,64},{32,96},{64,128},{96,160},{128,192},{160,224},{192,0},{224,... | collective-permute-start | bytes 393224 | tf_op jit(solution)/shard_map/cond/branch_1_fun/ppermute | solution.py:77
  70.5 7.3 %collective-permute-start.2 = (bf16[2,16,2048]{2,1,0:T(8,128)(2,1)}, bf16[2,16,2048]{2,1,0:T(8,128)(2,1)}, u32[]{:S(2)}, u32[]{:S(2)}) collective-permute-start(bf16[2,16,2048]{2,1,0:T(8,128)(2,1)} %bitcast.16), channel_id=1, source_target_pairs={{0,96},{32,64},{64,160},{96,128},{128,224},{160,192},{192,32},{224... | collective-permute-start | bytes 393224 | tf_op jit(solution)/shard_map/cond/branch_1_fun/ppermute | solution.py:77
  71.8 8.7 %collective-permute-start.3 = (bf16[2,16,2048]{2,1,0:T(8,128)(2,1)}, bf16[2,16,2048]{2,1,0:T(8,128)(2,1)S(1)}, u32[]{:S(2)}, u32[]{:S(2)}) collective-permute-start(bf16[2,16,2048]{2,1,0:T(8,128)(2,1)} %bitcast.16), channel_id=1, source_target_pairs={{1,225},{33,193},{65,33},{97,1},{129,97},{161,65},{193,161},{225,1... | collective-permute-start | bytes 393224 | tf_op jit(solution)/shard_map/cond/branch_1_fun/ppermute | solution.py:77
  80.5 1.8 %collective-permute-start.4 = (bf16[4,16,2048]{2,1,0:T(8,128)(2,1)S(1)}, bf16[4,16,2048]{2,1,0:T(8,128)(2,1)S(1)}, u32[]{:S(2)}, u32[]{:S(2)}) collective-permute-start(bf16[4,16,2048]{2,1,0:T(8,128)(2,1)S(1)} %pad_maximum_fusion.9), channel_id=1, source_target_pairs={{0,1},{1,0},{2,3},{3,2},{4,5},{5,4},{6,7},{7,6},{8,9},{9,8},{10,11... | collective-permute-start | bytes 786440 | tf_op jit(solution)/shard_map/cond/branch_1_fun/ppermute | solution.py:51
  90.2 2.0 %collective-permute-start.5 = (f32[4,256,128]{2,1,0:T(8,128)S(1)}, f32[4,256,128]{2,1,0:T(8,128)S(1)}, u32[]{:S(2)}, u32[]{:S(2)}) collective-permute-start(f32[4,256,128]{2,1,0:T(8,128)S(1)} %fusion), channel_id=1, source_target_pairs={{0,1},{1,0},{2,3},{3,2},{4,5},{5,4},{6,7},{7,6},{8,9},{9,8},{10,11... | collective-permute-start | bytes 1572872 | tf_op jit(solution)/shard_map/cond/branch_1_fun/ppermute | solution.py:51
  96.1 1.0 copy-start.1
  97.1 4.0 %copy-start.4 = (f32[32,1024]{1,0:T(8,128)S(1)}, f32[32,1024]{1,0:T(8,128)}, u32[]{:S(2)}) copy-start(f32[32,1024]{1,0:T(8,128)} %multiply_reduce_fusion.block_ref) | copy-start | bytes 393220
  97.1 4.6 %copy-start.5 = (bf16[4,256,128]{2,1,0:T(8,128)(2,1)S(1)}, bf16[4,256,128]{2,1,0:T(8,128)(2,1)}, u32[]{:S(2)}) copy-start(bf16[4,256,128]{2,1,0:T(8,128)(2,1)} %get-tuple-element.43) | copy-start | bytes 786436
  97.1 24.7 %all-to-all-start.2 = ((bf16[8,2,64,512]{3,2,1,0:T(8,128)(2,1)}), bf16[8,2,64,512]{3,2,1,0:T(8,128)(2,1)S(1)}, u32[]{:S(2)}, u32[]{:S(2)}) async-start(bf16[8,2,64,512]{3,2,1,0:T(8,128)(2,1)} %copy-done.1), calls=%async_computation.2 | async-start | bytes 2097152 | tf_op jit(solution)/shard_map/all_to_all | solution.py:22
  101.7 11.0 %collective-permute-start.6 = (bf16[256,128]{1,0:T(8,128)(2,1)S(1)}, bf16[256,128]{1,0:T(8,128)(2,1)S(1)}, u32[]{:S(2)}, u32[]{:S(2)}) collective-permute-start(bf16[256,128]{1,0:T(8,128)(2,1)S(1)} %get-tuple-element.81), channel_id=1, source_target_pairs={{0,4},{4,8},{8,12},{12,16},{16,20},{20,24},{24,28},{28,0},{1,17},{... | collective-permute-start | bytes 196616 | tf_op jit(solution)/shard_map/cond/branch_1_fun/ppermute | solution.py:77
  107.7 5.2 %collective-permute-start.7 = (bf16[256,128]{1,0:T(8,128)(2,1)S(1)}, bf16[256,128]{1,0:T(8,128)(2,1)S(1)}, u32[]{:S(2)}, u32[]{:S(2)}) collective-permute-start(bf16[256,128]{1,0:T(8,128)(2,1)S(1)} %get-tuple-element.84), channel_id=1, source_target_pairs={{0,8},{4,12},{8,16},{12,20},{16,24},{20,28},{24,0},{28,4},{1,21},{... | collective-permute-start | bytes 196616 | tf_op jit(solution)/shard_map/cond/branch_1_fun/ppermute | solution.py:77
  107.8 6.5 %collective-permute-start.8 = (bf16[256,128]{1,0:T(8,128)(2,1)S(1)}, bf16[256,128]{1,0:T(8,128)(2,1)S(1)}, u32[]{:S(2)}, u32[]{:S(2)}) collective-permute-start(bf16[256,128]{1,0:T(8,128)(2,1)S(1)} %get-tuple-element.83), channel_id=1, source_target_pairs={{0,12},{4,16},{8,20},{12,24},{16,28},{20,0},{24,4},{28,8},{1,25},{... | collective-permute-start | bytes 196616 | tf_op jit(solution)/shard_map/cond/branch_1_fun/ppermute | solution.py:77
  110.1 5.3 %collective-permute-start.9 = (bf16[256,128]{1,0:T(8,128)(2,1)S(1)}, bf16[256,128]{1,0:T(8,128)(2,1)S(1)}, u32[]{:S(2)}, u32[]{:S(2)}) collective-permute-start(bf16[256,128]{1,0:T(8,128)(2,1)S(1)} %get-tuple-element.82), channel_id=1, source_target_pairs={{1,29},{5,1},{9,5},{13,9},{17,13},{21,17},{25,21},{29,25},{3,31},{... | collective-permute-start | bytes 196616 | tf_op jit(solution)/shard_map/cond/branch_1_fun/ppermute | solution.py:77
  116.4 1.3 %collective-permute-start.10 = (f32[2,64,128]{2,1,0:T(8,128)S(1)}, f32[2,64,128]{2,1,0:T(8,128)S(1)}, u32[]{:S(2)}, u32[]{:S(2)}) collective-permute-start(f32[2,64,128]{2,1,0:T(8,128)S(1)} %dynamic-slice_bitcast_fusion), channel_id=1, source_target_pairs={{0,1},{1,0},{2,3},{3,2},{4,5},{5,4},{6,7},{7,6},{8,9},{9,8},{10,11... | collective-permute-start | bytes 196616 | tf_op jit(solution)/shard_map/cond/branch_1_fun/ppermute | solution.py:51
  117.7 2.9 %collective-permute-start.11 = (f32[1,64,128]{2,1,0:T(8,128)S(1)}, f32[1,64,128]{2,1,0:T(8,128)S(1)}, u32[]{:S(2)}, u32[]{:S(2)}) collective-permute-start(f32[1,64,128]{2,1,0:T(8,128)S(1)} %constant_dynamic-slice_fusion.16), channel_id=1, source_target_pairs={{0,2},{2,0},{1,3},{3,1},{4,6},{6,4},{5,7},{7,5},{8,10},{10,8},{9,1... | collective-permute-start | bytes 98312 | tf_op jit(solution)/shard_map/cond/branch_1_fun/ppermute | solution.py:51
  120.6 4.0 %copy-start.6 = (f32[64,128]{1,0:T(8,128)}, f32[64,128]{1,0:T(8,128)S(1)}, u32[]{:S(2)}) copy-start(f32[64,128]{1,0:T(8,128)S(1)} %get-tuple-element.114) | copy-start | bytes 98308
  122.0 2.4 %collective-permute-start.22 = (f32[64,512]{1,0:T(8,128)S(1)}, f32[64,512]{1,0:T(8,128)S(1)}, u32[]{:S(2)}, u32[]{:S(2)}) collective-permute-start(f32[64,512]{1,0:T(8,128)S(1)} %get-tuple-element.108), channel_id=1, source_target_pairs={{0,1},{1,0},{2,3},{3,2},{4,5},{5,4},{6,7},{7,6},{8,9},{9,8},{10,11... | collective-permute-start | bytes 393224 | tf_op jit(solution)/shard_map/ppermute | solution.py:51
  (1 other events, 1.0 us)

commit v12 on v11

--- a/solution.py
+++ b/solution.py
@@ -51,11 +51,13 @@
     return lax.ppermute(block, axis, [(0, 1), (1, 0)])
 
 
-def pair_sum(pieces, axis):
-    me = lax.axis_index(axis)
-    keep = lax.dynamic_index_in_dim(pieces, me, 1, keepdims=False)
-    send = lax.dynamic_index_in_dim(pieces, 1 - me, 1, keepdims=False)
-    return keep + other(send, axis)
+def direct_sum(pieces, axes, sizes):
+    own = (0,) * len(sizes)
+    total = lax.dynamic_index_in_dim(pieces, peer(axes, sizes, own), 0, keepdims=False)
+    for shift in shifts(sizes):
+        piece = lax.dynamic_index_in_dim(pieces, peer(axes, sizes, shift), 0, keepdims=False)
+        total = total + lax.ppermute(piece, axes, moved(sizes, shift))
+    return total
 
 
 def in_order(mine, others, axis):
@@ -196,16 +198,16 @@
 
 
 def spread(pair, block, count):
-    whole = pl.BlockSpec(pair.shape, lambda i: (0, 0))
+    whole = pl.BlockSpec(memory_space=pltpu.VMEM)
     return pl.pallas_call(
         spread_kernel,
-        grid=(1,),
-        in_specs=[whole, pl.BlockSpec(block.shape, lambda i: (0, 0))],
-        out_specs=[pl.BlockSpec((count,) + block.shape, lambda i: (0, 0, 0)), whole],
+        in_specs=[whole, whole],
+        out_specs=[whole, whole],
         out_shape=[
             jax.ShapeDtypeStruct((count,) + block.shape, BF16),
             jax.ShapeDtypeStruct(pair.shape, pair.dtype),
         ],
+        compiler_params=pltpu.CompilerParams(vmem_limit_bytes=VMEM),
         cost_estimate=pl.CostEstimate(flops=0, bytes_accessed=0, transcendentals=0),
         name="spread",
     )(pair, block)
@@ -307,8 +309,7 @@
         total = jnp.where(core == 0, back_b[-1], 0.0)
         for j, (first, second) in enumerate(zip(*halves((n_z,)))):
             total = total + joint(sent[j], ("z",), (n_z,), first, second).astype(F32)
-        total = pair_sum(total.reshape(n_yl, 2, rows_b, lig_total), "c")
-        return pair_sum(total.reshape(1, n_yl, rows_b, lig_total), "yl").reshape(rows_b, lig_total)
+        return direct_sum(total.reshape(n_yl * 2, rows_b, lig_total), ("yl", "c"), (n_yl, 2))
 
     ligand_back = together(sum_back, core, back_b, sent)
     back_a = exchange(back_a, AA)

time: 126 us -> 128 us (1.016)
  local copies, waits for them, and re-layouts: 5.95 us -> 7.49 us
    ppermute x0 -> x3, waiting for transfers between devices: none -> 3.06 us  [direct_sum(): total = total + lax.ppermute(piece, axes, moved(sizes, shift))]
    ppermute x11 -> x9, waiting for transfers between devices: 9.26 us -> 6.36 us  [other(): return lax.ppermute(block, axis, [(0, 1), (1, 0)])]
    ppermute x0 -> x3, starting transfers between devices: none -> 2.22 us  [direct_sum(): total = total + lax.ppermute(piece, axes, moved(sizes, shift))]
    ppermute x11 -> x9, starting transfers between devices: 8.05 us -> 5.86 us  [other(): return lax.ppermute(block, axis, [(0, 1), (1, 0)])]
    unnamed x16 -> x18, local copies, waits for them, and re-layouts: 2.98 us -> 4.52 us
  transfers between devices with their start and end apart: 26 -> 27, of which waited for: 16 -> 16; matrix products, arithmetic and copies ran while one was open for 10% -> 11% of each run, Pallas kernels for 12% -> 12%
where the time goes in v12:
time: 128 us; the launch traced here: 127 us
  starting transfers between devices  59.9 us (47%)
  waiting for transfers between devices  23.1 us (18%)
  Pallas kernels  20.2 us (16%)
  other arithmetic  13.1 us (10%)
  local copies, waits for them, and re-layouts  7.49 us (6%)
  between operations  1.53 us (1%)
  matrix products  1.49 us (1%)
    ppermute x12, starting transfers between devices, joint(): return lax.ppermute(block, axes + ('c',), pairs)  31 us
    all_to_all x3, starting transfers between devices, exchange(): return lax.all_to_all(pieces, axes, 0, 0, tiled=True)  20.8 us
    ppermute x12, waiting for transfers between devices, joint(): return lax.ppermute(block, axes + ('c',), pairs)  13.7 us
    pallas_call x1, Pallas kernels, cross_part(): pl.pallas_call(cross_kernel, grid=(rows // step,), in_specs=[pl.BlockSpec...  7.78 us
    pallas_call x1, Pallas kernels, back_part(): pl.pallas_call(lambda *refs: back_kernel(*refs, count=count, scale=scale)...  7.67 us
    ppermute x9, waiting for transfers between devices, other(): return lax.ppermute(block, axis, [(0, 1), (1, 0)])  6.36 us
    ppermute x9, starting transfers between devices, other(): return lax.ppermute(block, axis, [(0, 1), (1, 0)])  5.86 us
    unnamed x18, local copies, waits for them, and re-layouts  4.52 us
  transfers between devices with their start and end apart: 27, of which 16 were waited for; matrix products, arithmetic and copies ran while one was open for 11% of the time, Pallas kernels for 12%

profile of v12, /device:TPU:1, one launch (start us, length us, event | category | flops | bytes accessed | tf_op | source)
XLA Modules:
  0.0 127.1 jit_solution(17874109451791094994)
XLA Ops:
  0.7 1.4 %constant_dynamic-slice_fusion.16 = (bf16[16,1,32,512]{3,2,1,0:T(8,128)(2,1)S(1)}, bf16[16,1,32,512]{3,2,1,0:T(8,128)(2,1)S(1)}) fusion(bf16[16,2,32,512]{3,2,1,0:T(8,128)(2,1)} %bitcast.112, s32[]{:T(128)S(6)} %select_n.266, s32[]{:T(128)S(6)} %select_n.265), kind=kLoop, calls=%fused_computation.96 | loop fusion | bytes 2097160 | tf_op jit(solution)/shard_map/jit(dynamic_index_in_dim)/dynamic_slice | solution.py:261
  2.1 3.3 %collective-permute-start.20 = (bf16[512,512]{1,0:T(8,128)(2,1)S(1)}, bf16[512,512]{1,0:T(8,128)(2,1)S(1)}, u32[]{:S(2)}, u32[]{:S(2)}) collective-permute-start(bf16[512,512]{1,0:T(8,128)(2,1)S(1)} %bitcast.121), channel_id=1, source_target_pairs={{0,1},{1,0},{2,3},{3,2},{4,5},{5,4},{6,7},{7,6},{8,9},{9,8},{10,11... | collective-permute-start | bytes 1572872 | tf_op jit(solution)/shard_map/ppermute | solution.py:51
  7.0 1.4 %maximum_convert_fusion = f32[2]{0:T(128)S(1)} fusion(bf16[1]{0:T(256)(128)(2,1)} %bitcast.41, bf16[1]{0:T(256)(128)(2,1)} %bitcast.40), kind=kLoop, calls=%fused_computation.94 | loop fusion | flops 8 | bytes 12 | tf_op jit(solution)/shard_map/stack | solution.py:264
  11.6 1.3 %pad_maximum_fusion.10 = f16[512,1152]{1,0:T(8,128)(2,1)} fusion(f16[512,1024]{1,0:T(8,128)(2,1)S(1)} %multiply_convert_fusion, f16[1152]{0:T(1024)(128)(2,1)S(1)} %pad.35.clone), kind=kLoop, calls=%fused_computation.74 | loop fusion | flops 589824 | bytes 2230528 | tf_op jit(solution)/shard_map/concatenate | solution.py:272
  12.9 7.6 %all-to-all-start = ((f16[16,32,1152]{2,1,0:T(8,128)(2,1)}), f16[16,32,1152]{2,1,0:T(8,128)(2,1)S(1)}, u32[]{:S(2)}, u32[]{:S(2)}) async-start(f16[16,32,1152]{2,1,0:T(8,128)(2,1)} %bitcast.44), calls=%async_computation | async-start | bytes 2359296 | tf_op jit(solution)/shard_map/all_to_all | solution.py:22
  21.2 31.9 %conditional.3 = (f32[16,2048]{1,0:T(8,128)S(1)}, bf16[32,2048]{1,0:T(8,128)(2,1)S(1)}) conditional(s32[]{:T(128)} %convert_element_type.59, () %tuple.28, (f32[8,128]{1,0:T(8,128)S(1)}, bf16[128,2048]{1,0:T(8,128)(2,1)}, bf16[2048,2048]{1,0:T(8,128)(2,1)}) %tuple.83), branch_computations={%region_3.4_spmd, %region_4.5_spmd} | conditional | flops 2359381 | bytes 10487028 | solution.py:192
  21.2 7.8 %cross_part.1 = bf16[128,2048]{1,0:T(8,128)(2,1)S(1)} custom-call(f32[8,128]{1,0:T(8,128)S(1)} %get-tuple-element.18.token_ref, bf16[128,2048]{1,0:T(8,128)(2,1)} %get-tuple-element.46.left_ref, bf16[2048,2048]{1,0:T(8,128)(2,1)} %get-tuple-element.24.right_ref), custom_call_target="tpu_custom_call" | custom-call | tf_op jit(solution)/shard_map/cond/branch_1_fun/cross_part/pallas_call | solution.py:137
  31.1 2.8 %collective-permute-start.14 = (bf16[2,16,2048]{2,1,0:T(8,128)(2,1)S(1)}, bf16[2,16,2048]{2,1,0:T(8,128)(2,1)S(1)}, u32[]{:S(2)}, u32[]{:S(2)}) collective-permute-start(bf16[2,16,2048]{2,1,0:T(8,128)(2,1)S(1)} %pad_maximum_fusion.2), channel_id=1, source_target_pairs={{0,32},{32,0},{64,96},{96,64},{128,160},{160,128},{192,224},{224,1... | collective-permute-start | bytes 393224 | tf_op jit(solution)/shard_map/cond/branch_1_fun/ppermute | solution.py:79
  33.9 2.6 %collective-permute-start.15 = (bf16[2,16,2048]{2,1,0:T(8,128)(2,1)S(1)}, bf16[2,16,2048]{2,1,0:T(8,128)(2,1)S(1)}, u32[]{:S(2)}, u32[]{:S(2)}) collective-permute-start(bf16[2,16,2048]{2,1,0:T(8,128)(2,1)S(1)} %pad_maximum_fusion.3), channel_id=1, source_target_pairs={{0,64},{32,96},{64,128},{96,160},{128,192},{160,224},{192,0},{224,... | collective-permute-start | bytes 393224 | tf_op jit(solution)/shard_map/cond/branch_1_fun/ppermute | solution.py:79
  36.6 2.6 %collective-permute-start.16 = (bf16[2,16,2048]{2,1,0:T(8,128)(2,1)S(1)}, bf16[2,16,2048]{2,1,0:T(8,128)(2,1)S(1)}, u32[]{:S(2)}, u32[]{:S(2)}) collective-permute-start(bf16[2,16,2048]{2,1,0:T(8,128)(2,1)S(1)} %pad_maximum_fusion.4), channel_id=1, source_target_pairs={{0,96},{32,64},{64,160},{96,128},{128,224},{160,192},{192,32},{224... | collective-permute-start | bytes 393224 | tf_op jit(solution)/shard_map/cond/branch_1_fun/ppermute | solution.py:79
  39.1 2.5 %collective-permute-start.17 = (bf16[2,16,2048]{2,1,0:T(8,128)(2,1)S(1)}, bf16[2,16,2048]{2,1,0:T(8,128)(2,1)S(1)}, u32[]{:S(2)}, u32[]{:S(2)}) collective-permute-start(bf16[2,16,2048]{2,1,0:T(8,128)(2,1)S(1)} %pad_maximum_fusion.5), channel_id=1, source_target_pairs={{1,225},{33,193},{65,33},{97,1},{129,97},{161,65},{193,161},{225,1... | collective-permute-start | bytes 393224 | tf_op jit(solution)/shard_map/cond/branch_1_fun/ppermute | solution.py:79
  41.7 1.6 %collective-permute-done.15 = bf16[2,16,2048]{2,1,0:T(8,128)(2,1)S(1)} collective-permute-done((bf16[2,16,2048]{2,1,0:T(8,128)(2,1)S(1)}, bf16[2,16,2048]{2,1,0:T(8,128)(2,1)S(1)}, u32[]{:S(2)}, u32[]{:S(2)}) %collective-permute-start.15) | collective-permute-done | bytes 131104 | tf_op jit(solution)/shard_map/cond/branch_1_fun/ppermute | solution.py:79
  43.3 6.9 %collective-permute-done.17 = bf16[2,16,2048]{2,1,0:T(8,128)(2,1)S(1)} collective-permute-done((bf16[2,16,2048]{2,1,0:T(8,128)(2,1)S(1)}, bf16[2,16,2048]{2,1,0:T(8,128)(2,1)S(1)}, u32[]{:S(2)}, u32[]{:S(2)}) %collective-permute-start.17) | collective-permute-done | bytes 131104 | tf_op jit(solution)/shard_map/cond/branch_1_fun/ppermute | solution.py:79
  50.4 1.3 %collective-permute-done.18 = f32[16,2048]{1,0:T(8,128)S(1)} collective-permute-done((f32[16,2048]{1,0:T(8,128)S(1)}, f32[16,2048]{1,0:T(8,128)S(1)}, u32[]{:S(2)}, u32[]{:S(2)}) %collective-permute-start.18) | collective-permute-done | bytes 131104 | tf_op jit(solution)/shard_map/cond/branch_1_fun/ppermute | solution.py:51
  54.1 1.7 %spread.1 = (bf16[16,32,1024]{2,1,0:T(8,128)(2,1)S(1)}, bf16[32,2048]{1,0:T(8,128)(2,1)}) custom-call(bf16[32,2048]{1,0:T(8,128)(2,1)} %copy-done.5, f32[32,1024]{1,0:T(8,128)S(1)} %multiply_reduce_fusion.block_ref), custom_call_target="tpu_custom_call" | custom-call | tf_op jit(solution)/shard_map/spread/pallas_call | solution.py:202
  56.7 9.4 %all-to-all-start.1 = ((bf16[16,32,1024]{2,1,0:T(8,128)(2,1)}), bf16[16,32,1024]{2,1,0:T(8,128)(2,1)S(1)}, u32[]{:S(2)}, u32[]{:S(2)}) async-start(bf16[16,32,1024]{2,1,0:T(8,128)(2,1)} %copy-done.1), calls=%async_computation.1 | async-start | bytes 2097152 | tf_op jit(solution)/shard_map/all_to_all | solution.py:22
  66.1 28.3 %conditional.4 = (f32[4,256,128]{2,1,0:T(8,128)}) conditional(s32[]{:T(128)} %convert_element_type.59, () %tuple.31, (bf16[32,2048]{1,0:T(8,128)(2,1)}, bf16[2048,2048]{1,0:T(8,128)(2,1)}) %tuple.84), branch_computations={%region_6.7_spmd, %region_7.8_spmd} | conditional | flops 2654375 | bytes 13306000 | solution.py:192
  66.2 1.8 %collective-permute-start = (bf16[2,16,2048]{2,1,0:T(8,128)(2,1)}, bf16[2,16,2048]{2,1,0:T(8,128)(2,1)}, u32[]{:S(2)}, u32[]{:S(2)}) collective-permute-start(bf16[2,16,2048]{2,1,0:T(8,128)(2,1)} %bitcast.16), channel_id=1, source_target_pairs={{0,32},{32,0},{64,96},{96,64},{128,160},{160,128},{192,224},{224,1... | collective-permute-start | bytes 393224 | tf_op jit(solution)/shard_map/cond/branch_1_fun/ppermute | solution.py:79
  67.9 3.0 %collective-permute-start.1 = (bf16[2,16,2048]{2,1,0:T(8,128)(2,1)}, bf16[2,16,2048]{2,1,0:T(8,128)(2,1)}, u32[]{:S(2)}, u32[]{:S(2)}) collective-permute-start(bf16[2,16,2048]{2,1,0:T(8,128)(2,1)} %bitcast.16), channel_id=1, source_target_pairs={{0,64},{32,96},{64,128},{96,160},{128,192},{160,224},{192,0},{224,... | collective-permute-start | bytes 393224 | tf_op jit(solution)/shard_map/cond/branch_1_fun/ppermute | solution.py:79
  71.0 1.3 %collective-permute-start.2 = (bf16[2,16,2048]{2,1,0:T(8,128)(2,1)}, bf16[2,16,2048]{2,1,0:T(8,128)(2,1)}, u32[]{:S(2)}, u32[]{:S(2)}) collective-permute-start(bf16[2,16,2048]{2,1,0:T(8,128)(2,1)} %bitcast.16), channel_id=1, source_target_pairs={{0,96},{32,64},{64,160},{96,128},{128,224},{160,192},{192,32},{224... | collective-permute-start | bytes 393224 | tf_op jit(solution)/shard_map/cond/branch_1_fun/ppermute | solution.py:79
  72.2 3.3 %collective-permute-start.3 = (bf16[2,16,2048]{2,1,0:T(8,128)(2,1)}, bf16[2,16,2048]{2,1,0:T(8,128)(2,1)}, u32[]{:S(2)}, u32[]{:S(2)}) collective-permute-start(bf16[2,16,2048]{2,1,0:T(8,128)(2,1)} %bitcast.16), channel_id=1, source_target_pairs={{1,225},{33,193},{65,33},{97,1},{129,97},{161,65},{193,161},{225,1... | collective-permute-start | bytes 393224 | tf_op jit(solution)/shard_map/cond/branch_1_fun/ppermute | solution.py:79
  79.2 1.8 %collective-permute-done.3 = bf16[2,16,2048]{2,1,0:T(8,128)(2,1)} collective-permute-done((bf16[2,16,2048]{2,1,0:T(8,128)(2,1)}, bf16[2,16,2048]{2,1,0:T(8,128)(2,1)}, u32[]{:S(2)}, u32[]{:S(2)}) %collective-permute-start.3) | collective-permute-done | bytes 131104 | tf_op jit(solution)/shard_map/cond/branch_1_fun/ppermute | solution.py:79
  83.7 7.7 %back_part.1 = f32[2048,128]{1,0:T(8,128)S(1)} custom-call(s32[9]{0:T(128)S(1)} %stack.72.refs_0_, bf16[2048,2048]{1,0:T(8,128)(2,1)} %get-tuple-element.25.refs_1_, bf16[16,2048]{1,0:T(8,128)(2,1)S(1)} %get-tuple-element.74.refs_2_, bf16[16,2048]{1,0:T(8,128)(2,1)S(1)} %get-tuple-element.76.refs_3_, bf16[16,2048]{1,0:T(8,128)(2,1)S(1)} %get-tuple-element.78.refs_4_, ...), custom_call_target="tpu_custom_call" | custom-call | tf_op jit(solution)/shard_map/cond/branch_1_fun/back_part/pallas_call | solution.py:169
  91.8 1.8 %collective-permute-done.5 = f32[4,256,128]{2,1,0:T(8,128)S(1)} collective-permute-done((f32[4,256,128]{2,1,0:T(8,128)S(1)}, f32[4,256,128]{2,1,0:T(8,128)S(1)}, u32[]{:S(2)}, u32[]{:S(2)}) %collective-permute-start.5) | collective-permute-done | bytes 524320 | tf_op jit(solution)/shard_map/cond/branch_1_fun/ppermute | solution.py:51
  94.4 3.1 %product.1 = (bf16[8,2,64,512]{3,2,1,0:T(8,128)(2,1)S(1)}, bf16[4,256,128]{2,1,0:T(8,128)(2,1)}) custom-call(f32[4,256,128]{2,1,0:T(8,128)} %get-tuple-element.116.refs_0_, bf16[1024,512]{1,0:T(8,128)(2,1)S(1)} %bitcast.106, bf16[1024,512]{1,0:T(8,128)(2,1)S(1)} %collective-permute-done.21.refs_2_, bf16[512,1024]{1,0:T(8,128)(2,1)S(1)} %bitcast.107), custom_call_target="tpu_custom_call" | custom-call | tf_op jit(solution)/shard_map/product/pallas_call | solution.py:231
  98.5 3.9 %all-to-all-start.2 = ((bf16[8,2,64,512]{3,2,1,0:T(8,128)(2,1)}), bf16[8,2,64,512]{3,2,1,0:T(8,128)(2,1)S(1)}, u32[]{:S(2)}, u32[]{:S(2)}) async-start(bf16[8,2,64,512]{3,2,1,0:T(8,128)(2,1)} %copy-done.2), calls=%async_computation.2 | async-start | bytes 2097152 | tf_op jit(solution)/shard_map/all_to_all | solution.py:22
  103.1 20.1 %conditional.5 = (f32[64,128]{1,0:T(8,128)S(1)}) conditional(s32[]{:T(128)} %convert_element_type.59, () %tuple.30, (s32[]{:T(128)}, f32[4,256,128]{2,1,0:T(8,128)}, bf16[4,256,128]{2,1,0:T(8,128)(2,1)S(1)}) %tuple.85), branch_computations={%region_8.9_spmd, %region_9.10_spmd} | conditional | flops 319538 | bytes 2851666 | solution.py:192
  103.1 6.1 %collective-permute-start.6 = (bf16[256,128]{1,0:T(8,128)(2,1)S(1)}, bf16[256,128]{1,0:T(8,128)(2,1)S(1)}, u32[]{:S(2)}, u32[]{:S(2)}) collective-permute-start(bf16[256,128]{1,0:T(8,128)(2,1)S(1)} %get-tuple-element.81), channel_id=1, source_target_pairs={{0,4},{4,8},{8,12},{12,16},{16,20},{20,24},{24,28},{28,0},{1,17},{... | collective-permute-start | bytes 196616 | tf_op jit(solution)/shard_map/cond/branch_1_fun/ppermute | solution.py:79
  109.3 2.3 %collective-permute-start.8 = (bf16[256,128]{1,0:T(8,128)(2,1)S(1)}, bf16[256,128]{1,0:T(8,128)(2,1)S(1)}, u32[]{:S(2)}, u32[]{:S(2)}) collective-permute-start(bf16[256,128]{1,0:T(8,128)(2,1)S(1)} %get-tuple-element.83), channel_id=1, source_target_pairs={{0,12},{4,16},{8,20},{12,24},{16,28},{20,0},{24,4},{28,8},{1,25},{... | collective-permute-start | bytes 196616 | tf_op jit(solution)/shard_map/cond/branch_1_fun/ppermute | solution.py:79
  111.6 2.6 %collective-permute-start.9 = (bf16[256,128]{1,0:T(8,128)(2,1)S(1)}, bf16[256,128]{1,0:T(8,128)(2,1)S(1)}, u32[]{:S(2)}, u32[]{:S(2)}) collective-permute-start(bf16[256,128]{1,0:T(8,128)(2,1)S(1)} %get-tuple-element.82), channel_id=1, source_target_pairs={{1,29},{5,1},{9,5},{13,9},{17,13},{21,17},{25,21},{29,25},{3,31},{... | collective-permute-start | bytes 196616 | tf_op jit(solution)/shard_map/cond/branch_1_fun/ppermute | solution.py:79
  114.4 1.4 %collective-permute-done.8 = bf16[256,128]{1,0:T(8,128)(2,1)S(1)} collective-permute-done((bf16[256,128]{1,0:T(8,128)(2,1)S(1)}, bf16[256,128]{1,0:T(8,128)(2,1)S(1)}, u32[]{:S(2)}, u32[]{:S(2)}) %collective-permute-start.8) | collective-permute-done | bytes 65568 | tf_op jit(solution)/shard_map/cond/branch_1_fun/ppermute | solution.py:79
  120.8 2.3 %collective-permute-done.12 = f32[64,128]{1,0:T(8,128)S(1)} collective-permute-done((f32[64,128]{1,0:T(8,128)S(1)}, f32[64,128]{1,0:T(8,128)S(1)}, u32[]{:S(2)}, u32[]{:S(2)}) %collective-permute-start.12) | collective-permute-done | bytes 32800 | tf_op jit(solution)/shard_map/cond/branch_1_fun/ppermute | solution.py:59
  (102 shorter events, 28.8 us)
Async XLA Ops:
  0.6 5.7 %copy-start.4 = (bf16[1024,512]{1,0:T(8,128)(2,1)S(1)}, bf16[1024,512]{1,0:T(8,128)(2,1)}, u32[]{:S(2)}) copy-start(bf16[1024,512]{1,0:T(8,128)(2,1)} %param.12) | copy-start | bytes 3145732
  0.6 4.8 %copy-start = (bf16[64,16,512]{2,1,0:T(8,128)(2,1)S(1)}, bf16[64,16,512]{2,1,0:T(8,128)(2,1)}, u32[]{:S(2)}) copy-start(bf16[64,16,512]{2,1,0:T(8,128)(2,1)} %param.10) | copy-start | bytes 3145732
  2.1 7.8 %collective-permute-start.20 = (bf16[512,512]{1,0:T(8,128)(2,1)S(1)}, bf16[512,512]{1,0:T(8,128)(2,1)S(1)}, u32[]{:S(2)}, u32[]{:S(2)}) collective-permute-start(bf16[512,512]{1,0:T(8,128)(2,1)S(1)} %bitcast.121), channel_id=1, source_target_pairs={{0,1},{1,0},{2,3},{3,2},{4,5},{5,4},{6,7},{7,6},{8,9},{9,8},{10,11... | collective-permute-start | bytes 1572872 | tf_op jit(solution)/shard_map/ppermute | solution.py:51
  5.4 4.4 %collective-permute-start.21 = (bf16[1024,512]{1,0:T(8,128)(2,1)S(1)}, bf16[1024,512]{1,0:T(8,128)(2,1)S(1)}, u32[]{:S(2)}, u32[]{:S(2)}) collective-permute-start(bf16[1024,512]{1,0:T(8,128)(2,1)S(1)} %bitcast.104), channel_id=1, source_target_pairs={{0,1},{1,0},{2,3},{3,2},{4,5},{5,4},{6,7},{7,6},{8,9},{9,8},{10,11... | collective-permute-start | bytes 3145736 | tf_op jit(solution)/shard_map/ppermute | solution.py:51
  8.5 1.2 collective-permute-start.22
  12.9 40.2 %all-to-all-start = ((f16[16,32,1152]{2,1,0:T(8,128)(2,1)}), f16[16,32,1152]{2,1,0:T(8,128)(2,1)S(1)}, u32[]{:S(2)}, u32[]{:S(2)}) async-start(f16[16,32,1152]{2,1,0:T(8,128)(2,1)} %bitcast.44), calls=%async_computation | async-start | bytes 2359296 | tf_op jit(solution)/shard_map/all_to_all | solution.py:22
  29.1 1.9 %collective-permute-start.13 = (bf16[4,16,2048]{2,1,0:T(8,128)(2,1)S(1)}, bf16[4,16,2048]{2,1,0:T(8,128)(2,1)S(1)}, u32[]{:S(2)}, u32[]{:S(2)}) collective-permute-start(bf16[4,16,2048]{2,1,0:T(8,128)(2,1)S(1)} %get-tuple-element.97), channel_id=1, source_target_pairs={{0,1},{1,0},{2,3},{3,2},{4,5},{5,4},{6,7},{7,6},{8,9},{9,8},{10,11... | collective-permute-start | bytes 786440 | tf_op jit(solution)/shard_map/cond/branch_1_fun/ppermute | solution.py:51
  31.1 10.6 %collective-permute-start.14 = (bf16[2,16,2048]{2,1,0:T(8,128)(2,1)S(1)}, bf16[2,16,2048]{2,1,0:T(8,128)(2,1)S(1)}, u32[]{:S(2)}, u32[]{:S(2)}) collective-permute-start(bf16[2,16,2048]{2,1,0:T(8,128)(2,1)S(1)} %pad_maximum_fusion.2), channel_id=1, source_target_pairs={{0,32},{32,0},{64,96},{96,64},{128,160},{160,128},{192,224},{224,1... | collective-permute-start | bytes 393224 | tf_op jit(solution)/shard_map/cond/branch_1_fun/ppermute | solution.py:79
  33.9 9.4 %collective-permute-start.15 = (bf16[2,16,2048]{2,1,0:T(8,128)(2,1)S(1)}, bf16[2,16,2048]{2,1,0:T(8,128)(2,1)S(1)}, u32[]{:S(2)}, u32[]{:S(2)}) collective-permute-start(bf16[2,16,2048]{2,1,0:T(8,128)(2,1)S(1)} %pad_maximum_fusion.3), channel_id=1, source_target_pairs={{0,64},{32,96},{64,128},{96,160},{128,192},{160,224},{192,0},{224,... | collective-permute-start | bytes 393224 | tf_op jit(solution)/shard_map/cond/branch_1_fun/ppermute | solution.py:79
  36.6 6.7 %collective-permute-start.16 = (bf16[2,16,2048]{2,1,0:T(8,128)(2,1)S(1)}, bf16[2,16,2048]{2,1,0:T(8,128)(2,1)S(1)}, u32[]{:S(2)}, u32[]{:S(2)}) collective-permute-start(bf16[2,16,2048]{2,1,0:T(8,128)(2,1)S(1)} %pad_maximum_fusion.4), channel_id=1, source_target_pairs={{0,96},{32,64},{64,160},{96,128},{128,224},{160,192},{192,32},{224... | collective-permute-start | bytes 393224 | tf_op jit(solution)/shard_map/cond/branch_1_fun/ppermute | solution.py:79
  39.1 11.0 %collective-permute-start.17 = (bf16[2,16,2048]{2,1,0:T(8,128)(2,1)S(1)}, bf16[2,16,2048]{2,1,0:T(8,128)(2,1)S(1)}, u32[]{:S(2)}, u32[]{:S(2)}) collective-permute-start(bf16[2,16,2048]{2,1,0:T(8,128)(2,1)S(1)} %pad_maximum_fusion.5), channel_id=1, source_target_pairs={{1,225},{33,193},{65,33},{97,1},{129,97},{161,65},{193,161},{225,1... | collective-permute-start | bytes 393224 | tf_op jit(solution)/shard_map/cond/branch_1_fun/ppermute | solution.py:79
  50.3 1.4 %collective-permute-start.18 = (f32[16,2048]{1,0:T(8,128)S(1)}, f32[16,2048]{1,0:T(8,128)S(1)}, u32[]{:S(2)}, u32[]{:S(2)}) collective-permute-start(f32[16,2048]{1,0:T(8,128)S(1)} %select_bitcast_fusion), channel_id=1, source_target_pairs={{0,1},{1,0},{2,3},{3,2},{4,5},{5,4},{6,7},{7,6},{8,9},{9,8},{10,11... | collective-permute-start | bytes 393224 | tf_op jit(solution)/shard_map/cond/branch_1_fun/ppermute | solution.py:51
  51.7 1.3 %collective-permute-start.19 = (bf16[16,2048]{1,0:T(8,128)(2,1)S(1)}, bf16[16,2048]{1,0:T(8,128)(2,1)S(1)}, u32[]{:S(2)}, u32[]{:S(2)}) collective-permute-start(bf16[16,2048]{1,0:T(8,128)(2,1)S(1)} %get-tuple-element.59), channel_id=1, source_target_pairs={{0,1},{1,0},{2,3},{3,2},{4,5},{5,4},{6,7},{7,6},{8,9},{9,8},{10,11... | collective-permute-start | bytes 196616 | tf_op jit(solution)/shard_map/cond/branch_1_fun/ppermute | solution.py:51
  56.7 37.7 %all-to-all-start.1 = ((bf16[16,32,1024]{2,1,0:T(8,128)(2,1)}), bf16[16,32,1024]{2,1,0:T(8,128)(2,1)S(1)}, u32[]{:S(2)}, u32[]{:S(2)}) async-start(bf16[16,32,1024]{2,1,0:T(8,128)(2,1)} %copy-done.1), calls=%async_computation.1 | async-start | bytes 2097152 | tf_op jit(solution)/shard_map/all_to_all | solution.py:22
  66.2 9.5 %collective-permute-start = (bf16[2,16,2048]{2,1,0:T(8,128)(2,1)}, bf16[2,16,2048]{2,1,0:T(8,128)(2,1)}, u32[]{:S(2)}, u32[]{:S(2)}) collective-permute-start(bf16[2,16,2048]{2,1,0:T(8,128)(2,1)} %bitcast.16), channel_id=1, source_target_pairs={{0,32},{32,0},{64,96},{96,64},{128,160},{160,128},{192,224},{224,1... | collective-permute-start | bytes 393224 | tf_op jit(solution)/shard_map/cond/branch_1_fun/ppermute | solution.py:79
  67.9 9.5 %collective-permute-start.1 = (bf16[2,16,2048]{2,1,0:T(8,128)(2,1)}, bf16[2,16,2048]{2,1,0:T(8,128)(2,1)}, u32[]{:S(2)}, u32[]{:S(2)}) collective-permute-start(bf16[2,16,2048]{2,1,0:T(8,128)(2,1)} %bitcast.16), channel_id=1, source_target_pairs={{0,64},{32,96},{64,128},{96,160},{128,192},{160,224},{192,0},{224,... | collective-permute-start | bytes 393224 | tf_op jit(solution)/shard_map/cond/branch_1_fun/ppermute | solution.py:79
  71.0 7.3 %collective-permute-start.2 = (bf16[2,16,2048]{2,1,0:T(8,128)(2,1)}, bf16[2,16,2048]{2,1,0:T(8,128)(2,1)}, u32[]{:S(2)}, u32[]{:S(2)}) collective-permute-start(bf16[2,16,2048]{2,1,0:T(8,128)(2,1)} %bitcast.16), channel_id=1, source_target_pairs={{0,96},{32,64},{64,160},{96,128},{128,224},{160,192},{192,32},{224... | collective-permute-start | bytes 393224 | tf_op jit(solution)/shard_map/cond/branch_1_fun/ppermute | solution.py:79
  72.2 8.7 %collective-permute-start.3 = (bf16[2,16,2048]{2,1,0:T(8,128)(2,1)}, bf16[2,16,2048]{2,1,0:T(8,128)(2,1)}, u32[]{:S(2)}, u32[]{:S(2)}) collective-permute-start(bf16[2,16,2048]{2,1,0:T(8,128)(2,1)} %bitcast.16), channel_id=1, source_target_pairs={{1,225},{33,193},{65,33},{97,1},{129,97},{161,65},{193,161},{225,1... | collective-permute-start | bytes 393224 | tf_op jit(solution)/shard_map/cond/branch_1_fun/ppermute | solution.py:79
  81.9 1.8 %collective-permute-start.4 = (bf16[4,16,2048]{2,1,0:T(8,128)(2,1)S(1)}, bf16[4,16,2048]{2,1,0:T(8,128)(2,1)S(1)}, u32[]{:S(2)}, u32[]{:S(2)}) collective-permute-start(bf16[4,16,2048]{2,1,0:T(8,128)(2,1)S(1)} %pad_maximum_fusion.9), channel_id=1, source_target_pairs={{0,1},{1,0},{2,3},{3,2},{4,5},{5,4},{6,7},{7,6},{8,9},{9,8},{10,11... | collective-permute-start | bytes 786440 | tf_op jit(solution)/shard_map/cond/branch_1_fun/ppermute | solution.py:51
  91.6 2.0 %collective-permute-start.5 = (f32[4,256,128]{2,1,0:T(8,128)S(1)}, f32[4,256,128]{2,1,0:T(8,128)S(1)}, u32[]{:S(2)}, u32[]{:S(2)}) collective-permute-start(f32[4,256,128]{2,1,0:T(8,128)S(1)} %fusion), channel_id=1, source_target_pairs={{0,1},{1,0},{2,3},{3,2},{4,5},{5,4},{6,7},{7,6},{8,9},{9,8},{10,11... | collective-permute-start | bytes 1572872 | tf_op jit(solution)/shard_map/cond/branch_1_fun/ppermute | solution.py:51
  97.5 1.0 copy-start.2
  98.5 4.6 %copy-start.6 = (bf16[4,256,128]{2,1,0:T(8,128)(2,1)S(1)}, bf16[4,256,128]{2,1,0:T(8,128)(2,1)}, u32[]{:S(2)}) copy-start(bf16[4,256,128]{2,1,0:T(8,128)(2,1)} %get-tuple-element.43) | copy-start | bytes 786436
  98.5 25.8 %all-to-all-start.2 = ((bf16[8,2,64,512]{3,2,1,0:T(8,128)(2,1)}), bf16[8,2,64,512]{3,2,1,0:T(8,128)(2,1)S(1)}, u32[]{:S(2)}, u32[]{:S(2)}) async-start(bf16[8,2,64,512]{3,2,1,0:T(8,128)(2,1)} %copy-done.2), calls=%async_computation.2 | async-start | bytes 2097152 | tf_op jit(solution)/shard_map/all_to_all | solution.py:22
  103.1 11.1 %collective-permute-start.6 = (bf16[256,128]{1,0:T(8,128)(2,1)S(1)}, bf16[256,128]{1,0:T(8,128)(2,1)S(1)}, u32[]{:S(2)}, u32[]{:S(2)}) collective-permute-start(bf16[256,128]{1,0:T(8,128)(2,1)S(1)} %get-tuple-element.81), channel_id=1, source_target_pairs={{0,4},{4,8},{8,12},{12,16},{16,20},{20,24},{24,28},{28,0},{1,17},{... | collective-permute-start | bytes 196616 | tf_op jit(solution)/shard_map/cond/branch_1_fun/ppermute | solution.py:79
  109.2 5.2 %collective-permute-start.7 = (bf16[256,128]{1,0:T(8,128)(2,1)S(1)}, bf16[256,128]{1,0:T(8,128)(2,1)S(1)}, u32[]{:S(2)}, u32[]{:S(2)}) collective-permute-start(bf16[256,128]{1,0:T(8,128)(2,1)S(1)} %get-tuple-element.84), channel_id=1, source_target_pairs={{0,8},{4,12},{8,16},{12,20},{16,24},{20,28},{24,0},{28,4},{1,21},{... | collective-permute-start | bytes 196616 | tf_op jit(solution)/shard_map/cond/branch_1_fun/ppermute | solution.py:79
  109.3 6.5 %collective-permute-start.8 = (bf16[256,128]{1,0:T(8,128)(2,1)S(1)}, bf16[256,128]{1,0:T(8,128)(2,1)S(1)}, u32[]{:S(2)}, u32[]{:S(2)}) collective-permute-start(bf16[256,128]{1,0:T(8,128)(2,1)S(1)} %get-tuple-element.83), channel_id=1, source_target_pairs={{0,12},{4,16},{8,20},{12,24},{16,28},{20,0},{24,4},{28,8},{1,25},{... | collective-permute-start | bytes 196616 | tf_op jit(solution)/shard_map/cond/branch_1_fun/ppermute | solution.py:79
  111.6 5.3 %collective-permute-start.9 = (bf16[256,128]{1,0:T(8,128)(2,1)S(1)}, bf16[256,128]{1,0:T(8,128)(2,1)S(1)}, u32[]{:S(2)}, u32[]{:S(2)}) collective-permute-start(bf16[256,128]{1,0:T(8,128)(2,1)S(1)} %get-tuple-element.82), channel_id=1, source_target_pairs={{1,29},{5,1},{9,5},{13,9},{17,13},{21,17},{25,21},{29,25},{3,31},{... | collective-permute-start | bytes 196616 | tf_op jit(solution)/shard_map/cond/branch_1_fun/ppermute | solution.py:79
  117.9 2.2 %collective-permute-start.10 = (f32[64,128]{1,0:T(8,128)S(1)}, f32[64,128]{1,0:T(8,128)S(1)}, u32[]{:S(2)}, u32[]{:S(2)}) collective-permute-start(f32[64,128]{1,0:T(8,128)S(1)} %get-tuple-element.85), channel_id=1, source_target_pairs={{0,1},{1,0},{2,3},{3,2},{4,5},{5,4},{6,7},{7,6},{8,9},{9,8},{10,11... | collective-permute-start | bytes 98312 | tf_op jit(solution)/shard_map/cond/branch_1_fun/ppermute | solution.py:59
  118.0 2.9 %collective-permute-start.11 = (f32[64,128]{1,0:T(8,128)S(1)}, f32[64,128]{1,0:T(8,128)S(1)}, u32[]{:S(2)}, u32[]{:S(2)}) collective-permute-start(f32[64,128]{1,0:T(8,128)S(1)} %get-tuple-element.87), channel_id=1, source_target_pairs={{0,2},{1,3},{2,0},{3,1},{4,6},{5,7},{6,4},{7,5},{8,10},{9,11},{10,... | collective-permute-start | bytes 98312 | tf_op jit(solution)/shard_map/cond/branch_1_fun/ppermute | solution.py:59
  119.2 4.0 %collective-permute-start.12 = (f32[64,128]{1,0:T(8,128)S(1)}, f32[64,128]{1,0:T(8,128)S(1)}, u32[]{:S(2)}, u32[]{:S(2)}) collective-permute-start(f32[64,128]{1,0:T(8,128)S(1)} %get-tuple-element.86), channel_id=1, source_target_pairs={{0,3},{1,2},{2,1},{3,0},{4,7},{5,6},{6,5},{7,4},{8,11},{9,10},{10,... | collective-permute-start | bytes 98312 | tf_op jit(solution)/shard_map/cond/branch_1_fun/ppermute | solution.py:59
  123.2 3.1 %copy-start.7 = (f32[64,128]{1,0:T(8,128)}, f32[64,128]{1,0:T(8,128)S(1)}, u32[]{:S(2)}) copy-start(f32[64,128]{1,0:T(8,128)S(1)} %get-tuple-element.117) | copy-start | bytes 98308
  124.5 1.5 %collective-permute-start.23 = (f32[64,512]{1,0:T(8,128)S(1)}, f32[64,512]{1,0:T(8,128)S(1)}, u32[]{:S(2)}, u32[]{:S(2)}) collective-permute-start(f32[64,512]{1,0:T(8,128)S(1)} %get-tuple-element.111), channel_id=1, source_target_pairs={{0,1},{1,0},{2,3},{3,2},{4,5},{5,4},{6,7},{7,6},{8,9},{9,8},{10,11... | collective-permute-start | bytes 393224 | tf_op jit(solution)/shard_map/ppermute | solution.py:51
  (3 other events, 2.6 us)
